TPU v7x, 128 devices: a whole 4x4x4 slice. The times are simulated.
128 devices in a mesh: ctx: 32 (over z, x, core), tp: 4 (over y).
Axes of the slice: x: 4, y: 4, z: 4, core: 2. Of those that a mesh axis runs over, the one named last changes fastest.
Arguments:
- query: bfloat16 [16384, 8192], P('ctx', 'tp'), may hold values from -12 to 12, as said below
- keys: bfloat16 [16384, 8192], P('ctx', 'tp'), may hold values from -5 to 5
- values: bfloat16 [16384, 8192], P('ctx', 'tp'), may hold values from -18 to 18, as said below
- gate_input: bfloat16 [16384, 8192], P('ctx', 'tp'), may hold values from -6 to 6
- grad_output: bfloat16 [16384, 8192], P('ctx', 'tp'), may hold values from -6 to 6
- norm_gain: float32 [8192], P('tp'), may hold values from 0.1 to 1.9
- segment_ids: int32 [16384], P('ctx'), may hold values from 0 to 5, never falling along the last dimension, each value on 1 to 8192 neighbouring positions
Outputs:
- layer_out: bfloat16 [16384, 8192], P('ctx', 'tp')
- grad_query: bfloat16 [16384, 8192], P('ctx', 'tp')
- grad_keys: bfloat16 [16384, 8192], P('ctx', 'tp')
- grad_values: bfloat16 [16384, 8192], P('ctx', 'tp')
- grad_gate: bfloat16 [16384, 8192], P('ctx', 'tp')
- grad_gain: float32 [8192], P('tp')
Inputs may be any that keep to these rules, and one draw needn't show every extreme that they name: `query`: real values. Real values. `segment_ids`: segment ids never fall along the window; each of the 6 documents holds 1 to 8192 tokens, one exactly 8192.
All inputs are finite; a program needn't handle non-finite values.
Results may differ from a plain program's by a relative error of at most 0.013.
Values may be sent and summed in bfloat16 or wider, within the bound.
No kernel may reach another device: no remote copies, remote signals or barrier semaphores. Data moves between devices by JAX's collectives and lax.ppermute only.
A program may use at most 192 MiB of HBM per device.

v0:
```python
import jax
import jax.numpy as jnp
from jax import lax
from jax.sharding import PartitionSpec as P

HD = 128
ATT = 8192


EPSILON = 1e-06


def carried_in(part, axis, combine, identity):
    place = lax.axis_index(axis)
    gathered = jax.tree.map(lambda a: lax.all_gather(a, axis), part)
    state = jax.tree.map(lambda a, e: jnp.zeros_like(a) + jnp.asarray(e, a.dtype), part, identity)

    def carried_one(hop, state):
        return combine(
            state, jax.tree.map(lambda a: lax.dynamic_index_in_dim(a, hop, 0, False), gathered)
        )

    return lax.fori_loop(0, place, carried_one, state)


def entering(x, axis, join, neutral):
    count = lax.axis_size(axis)
    place = lax.axis_index(axis)
    ahead = count - 1 - place
    gathered = jax.tree.map(
        lambda a, kind: lax.all_gather(a.astype(kind), axis),
        x,
        (jnp.bfloat16, jnp.int32, jnp.int32),
    )
    state = jax.tree.map(lambda a, e: jnp.zeros_like(a) + jnp.asarray(e, a.dtype), x, neutral)

    def entering_one(hop, state):
        source = count - 1 - hop
        return join(
            state,
            jax.tree.map(
                lambda a, own: lax.dynamic_index_in_dim(a, source, 0, False).astype(own.dtype),
                gathered,
                x,
            ),
        )

    return lax.fori_loop(0, ahead, entering_one, state)


def forward_join(earlier, later_part):
    state_a, low_a, high_a = earlier
    state_b, low_b, high_b = later_part
    joined = (high_a == low_b) & (low_b == high_b)
    merged = state_b + jnp.where(joined, state_a, 0.0)
    empty_a = low_a < 0
    empty_b = low_b < 0
    state_out = jnp.where(empty_b, state_a, jnp.where(empty_a, state_b, merged))
    low_out = jnp.where(empty_a, low_b, low_a)
    high_out = jnp.where(empty_b, high_a, high_b)
    return (state_out, low_out, high_out)


def backward_join(earlier, later_part):
    state_a, low_a, high_a = earlier
    state_b, low_b, high_b = later_part
    joined = (low_a == high_b) & (low_b == high_b)
    merged = state_b + jnp.where(joined, state_a, 0.0)
    empty_a = low_a < 0
    empty_b = low_b < 0
    state_out = jnp.where(empty_b, state_a, jnp.where(empty_a, state_b, merged))
    low_out = jnp.where(empty_b, low_a, low_b)
    high_out = jnp.where(empty_a, high_b, high_a)
    return (state_out, low_out, high_out)


def masked_product(left_rows, right_rows, allowed):
    scores = jnp.einsum("thd,shd->hts", left_rows, right_rows, preferred_element_type=jnp.float32)
    return jnp.where(allowed[None], scores, 0.0).astype(jnp.bfloat16)


def on_device(query, keys, values, gate_input, grad_output, norm_gain, segment_ids):
    tok_count = query.shape[0]
    head_count = query.shape[1] // HD
    query_heads = query.reshape(tok_count, head_count, HD)
    keys_heads = keys.reshape(tok_count, head_count, HD)
    values_heads = values.reshape(tok_count, head_count, HD)
    position = jnp.arange(tok_count)
    allowed = (position[:, None] >= position[None, :]) & (
        segment_ids[:, None] == segment_ids[None, :]
    )
    first_seg = segment_ids[0]
    last_seg = segment_ids[-1]
    no_state = jnp.zeros((head_count, HD, HD), jnp.float32)
    no_seg = jnp.full((), -1, jnp.int32)
    weights = masked_product(query_heads, keys_heads, allowed)
    intra = jnp.einsum("hts,shd->thd", weights, values_heads, preferred_element_type=jnp.float32)
    tail_keys = jnp.where(
        (segment_ids == last_seg)[:, None, None], keys_heads, jnp.zeros_like(keys_heads)
    )
    local_state = jnp.einsum(
        "thd,the->hde", tail_keys, values_heads, preferred_element_type=jnp.float32
    )
    earlier_state, prefix_low, prefix_high = carried_in(
        (local_state, first_seg, last_seg), "ctx", forward_join, (no_state, no_seg, no_seg)
    )
    from_before = segment_ids == prefix_high
    state_bf = earlier_state.astype(jnp.bfloat16)
    cross = jnp.einsum("thd,hde->the", query_heads, state_bf, preferred_element_type=jnp.float32)
    attn = (intra + jnp.where(from_before[:, None, None], cross, 0.0)).reshape(
        tok_count, head_count * HD
    )
    square_total = lax.psum(jnp.sum(attn * attn, axis=1), "tp")
    rinv = lax.rsqrt(square_total / ATT + EPSILON)
    normed = attn * rinv[:, None]
    sig = jax.nn.sigmoid(gate_input.astype(jnp.float32))
    layer_out = (normed * norm_gain[None, :] * sig).astype(jnp.bfloat16)
    grad_y = grad_output.astype(jnp.float32)
    grad_gain = lax.psum(jnp.sum(grad_y * normed * sig, axis=0), "ctx")
    grad_gate = (grad_y * normed * norm_gain[None, :] * sig * (1.0 - sig)).astype(jnp.bfloat16)
    dnorm = grad_y * norm_gain[None, :] * sig
    inner_total = lax.psum(jnp.sum(dnorm * normed, axis=1), "tp")
    grad_attn = (rinv[:, None] * (dnorm - normed * (inner_total / ATT)[:, None])).astype(
        jnp.bfloat16
    )
    grad_heads = grad_attn.reshape(tok_count, head_count, HD)
    head_query = jnp.where(
        (segment_ids == first_seg)[:, None, None], query_heads, jnp.zeros_like(query_heads)
    )
    local_later = jnp.einsum(
        "thd,the->hde", head_query, grad_heads, preferred_element_type=jnp.float32
    )
    grad_weights = masked_product(grad_heads, values_heads, allowed)
    grad_query = jnp.einsum(
        "hts,shd->thd", grad_weights, keys_heads, preferred_element_type=jnp.float32
    )
    grad_query = grad_query + jnp.where(
        from_before[:, None, None],
        jnp.einsum("the,hde->thd", grad_heads, state_bf, preferred_element_type=jnp.float32),
        0.0,
    )
    grad_keys = jnp.einsum(
        "hts,thd->shd", grad_weights, query_heads, preferred_element_type=jnp.float32
    )
    grad_values = jnp.einsum(
        "hts,the->she", weights, grad_heads, preferred_element_type=jnp.float32
    )
    later_state, suffix_low, suffix_high = entering(
        (local_later, first_seg, last_seg), "ctx", backward_join, (no_state, no_seg, no_seg)
    )
    to_after = segment_ids == suffix_low
    later_bf = later_state.astype(jnp.bfloat16)
    grad_keys = grad_keys + jnp.where(
        to_after[:, None, None],
        jnp.einsum("she,hde->shd", values_heads, later_bf, preferred_element_type=jnp.float32),
        0.0,
    )
    grad_values = grad_values + jnp.where(
        to_after[:, None, None],
        jnp.einsum("shd,hde->she", keys_heads, later_bf, preferred_element_type=jnp.float32),
        0.0,
    )
    flat_shape = (tok_count, head_count * HD)
    return (
        layer_out,
        grad_query.reshape(flat_shape).astype(jnp.bfloat16),
        grad_keys.reshape(flat_shape).astype(jnp.bfloat16),
        grad_values.reshape(flat_shape).astype(jnp.bfloat16),
        grad_gate,
        grad_gain,
    )


def solution(mesh):
    in_specs = (
        P("ctx", "tp"),
        P("ctx", "tp"),
        P("ctx", "tp"),
        P("ctx", "tp"),
        P("ctx", "tp"),
        P("tp"),
        P("ctx"),
    )
    out_specs = (
        P("ctx", "tp"),
        P("ctx", "tp"),
        P("ctx", "tp"),
        P("ctx", "tp"),
        P("ctx", "tp"),
        P("tp"),
    )
    return jax.shard_map(
        on_device, mesh=mesh, in_specs=in_specs, out_specs=out_specs, check_vma=False
    )
```

profile of v0, /device:TPU:1, one launch (start us, length us, event | category | flops | bytes accessed | tf_op | source)
XLA Modules:
  0.0 695.1 jit_solution(4210195639208704911)
XLA Ops:
  7.3 3.7 copy.63
  10.9 4.3 copy.38
  15.8 1.2 fusion.37
  16.9 1.3 broadcast_compare_fusion.1
  18.3 3.3 fusion.10
  21.6 3.9 copy.59
  26.3 15.6 %all-reduce.2 = (s32[32]{0:T(128)S(1)}, s32[32]{0:T(128)S(1)}) all-reduce(s32[32]{0:T(128)S(1)} %get-tuple-element.219, s32[32]{0:T(128)S(1)} %slice_dynamic-update-slice_fusion), channel_id=1, replica_groups=mesh['ctx'=32,'tp'=4] {'ctx'}, use_global_device_ids=true, to_apply=%add | all-reduce | flops 64 | bytes 512
  42.1 4.8 select_convert_fusion.1
  46.9 3.2 copy-done.1
  50.1 4.8 fusion.5
  54.9 84.5 %all-gather.5.cloned.1.call-done = f32[512,128,128]{2,1,0:T(8,128)} async-done(((f32[16,128,128]{2,1,0:T(8,128)}), f32[512,128,128]{2,1,0:T(8,128)}) %all-gather.5.cloned.1.call-update) | async-done | bytes 33554448 | tf_op jit(solution)/shard_map/all_gather | solution.py:15
  139.5 6.8 while.30
  143.3 1.7 fusion.60
  146.3 5.5 multiply_reduce_fusion.2
  151.9 5.4 copy.42
  157.2 8.4 %psum.21 = f32[512]{0:T(512)S(1)} all-reduce(f32[512]{0:T(512)S(1)} %get-tuple-element.221), channel_id=1, replica_groups=mesh['ctx'=32,'tp'=4] {'tp'}, use_global_device_ids=true, to_apply=%region_3.4 | all-reduce | flops 512 | bytes 4096 | tf_op jit(solution)/shard_map/psum | solution.py:113
  165.7 6.2 multiply_reduce_fusion
  171.9 6.2 psum.22
  178.1 6.0 multiply_convert_fusion.1
  184.1 3.9 copy.60
  188.0 3.7 fusion.25
  191.8 4.2 select_convert_fusion
  196.1 4.8 fusion.38
  200.8 4.3 fusion.4
  205.2 3.9 copy.54
  209.1 267.7 %psum.23 = f32[2048]{0:T(1024)} all-reduce(f32[2048]{0:T(1024)S(1)} %get-tuple-element.179), channel_id=1, replica_groups=mesh['ctx'=32,'tp'=4] {'ctx'}, use_global_device_ids=true, to_apply=%region_9.10 | all-reduce | flops 2048 | bytes 16384 | tf_op jit(solution)/shard_map/psum | solution.py:119
  476.8 7.2 %fusion.39 = f32[16,128,512]{2,1,0:T(8,128)} fusion(bf16[512,16,128]{0,2,1:T(8,128)(2,1)} %bitcast.100, bf16[16,512,512]{2,1,0:T(8,128)(2,1)} %copy-done.1), kind=kOutput, calls=%fused_computation.63 | convolution fusion | flops 1073741824 | bytes 14680064 | tf_op jit(solution)/shard_map/hts,the->she/dot_general | solution.py:145
  484.1 181.9 %while.31 = (s32[]{:T(128)}, f32[16,128,128]{2,1,0:T(8,128)S(1)}, s32[]{:T(128)}, s32[]{:T(128)}, s32[32]{0:T(128)S(1)}, /*index=5*/bf16[32,16,128,128]{3,2,1,0:...) while((s32[]{:T(128)}, f32[16,128,128]{2,1,0:T(8,128)S(1)}, ...), condition=%wide.region_7.8_spmd, body=%wide.region_6.7_spmd.sunk | while | flops 1310732 | bytes 2621678 | solution.py:48
  487.9 1.7 fusion.61
  493.9 1.7 fusion.61
  500.0 1.7 fusion.61
  506.0 1.7 fusion.61
  512.1 1.7 fusion.61
  518.1 1.7 fusion.61
  524.2 1.7 fusion.61
  530.3 1.7 fusion.61
  536.3 1.7 fusion.61
  542.4 1.7 fusion.61
  548.4 1.7 fusion.61
  554.5 1.7 fusion.61
  560.5 1.7 fusion.61
  566.6 1.7 fusion.61
  572.7 1.7 fusion.61
  578.7 1.7 fusion.61
  584.8 1.7 fusion.61
  590.8 1.7 fusion.61
  596.9 1.7 fusion.61
  602.9 1.7 fusion.61
  609.0 1.7 fusion.61
  615.1 1.7 fusion.61
  621.1 1.7 fusion.61
  627.2 1.7 fusion.61
  633.2 1.7 fusion.61
  639.3 1.7 fusion.61
  645.3 1.7 fusion.61
  651.4 1.7 fusion.61
  657.5 1.7 fusion.61
  663.5 1.7 fusion.61
  666.1 2.9 fusion.7
  669.5 1.0 copy-done.5
  670.4 2.3 add_convert_fusion
  672.7 3.9 copy.56
  676.6 7.8 %fusion.3 = bf16[512,16,128]{0,2,1:T(8,128)(2,1)} fusion(f32[16,128,512]{2,1,0:T(8,128)} %fusion.7, bf16[512,16,128]{0,2,1:T(8,128)(2,1)} %bitcast.105, bf16[16,512,512]{2,1,0:T(8,128)(2,1)} %copy-done.2, pred[512]{0:T(512)(128)(4,1)S(1)} %broadcast_compare_fusion), kind=kOutput, calls=%fused_computation.10 | convolution fusion | flops 1076887552 | bytes 16777728 | tf_op jit(solution)/shard_map/hts,thd->shd/dot_general | solution.py:142
  684.4 3.9 copy.55
  (96 shorter events, 39.0 us)
Async XLA Ops:
  7.2 11.1 %copy-start = (bf16[512,2048]{1,0:T(8,128)(2,1)S(1)}, bf16[512,2048]{1,0:T(8,128)(2,1)}, u32[]{:S(2)}) copy-start(bf16[512,2048]{1,0:T(8,128)(2,1)} %param.13) | copy-start | bytes 6291460
  7.2 132.2 %all-gather.5.cloned.1.call-start = ((), (), s32[]{:S(2)}) async-start(), calls=%async_computation | async-start | bytes 34603008 | tf_op jit(solution)/shard_map/all_gather | solution.py:15
  7.2 8.0 %copy-start.9 = (u32[128]{0:T(128)S(1)}, u32[128]{0:T(128)}, u32[]{:S(2)}) copy-start(u32[128]{0:T(128)} %constant.85) | copy-start | bytes 1540
  7.2 8.5 %copy-start.7 = (s32[512]{0:T(512)S(1)}, s32[512]{0:T(512)}, u32[]{:S(2)}) copy-start(s32[512]{0:T(512)} %param.17) | copy-start | bytes 6148
  21.6 462.4 %all-gather.7.cloned.1.call-start = ((), (), s32[]{:S(2)}) async-start(), calls=%async_computation.1 | async-start | bytes 17301504 | tf_op jit(solution)/shard_map/all_gather | solution.py:31
  46.9 3.2 copy-start.1
  151.9 13.8 %copy-start.8 = (f32[2048]{0:T(1024)S(1)}, f32[2048]{0:T(1024)}, u32[]{:S(2)}) copy-start(f32[2048]{0:T(1024)} %param.16) | copy-start | bytes 24580
  191.8 4.3 copy-start.6
  196.0 4.8 copy-start.2
  196.0 4.8 copy-start.4
  666.1 3.4 copy-start.3
  666.1 4.4 copy-start.5
Sparse Core Ops, SparseCore 0:
  21.7 117.6 all-gather.4
  191.9 274.7 all-gather.6
where the time goes:
time: 709 us; the launch traced here: 695 us
  blocking collectives  298 us (42%)
  loops' own time  100 us (14%)
  waiting for transfers between devices  84.5 us (12%)
  local copies, waits for them, and re-layouts  76.8 us (11%)
  other arithmetic  65.7 us (9%)
  matrix products  55.6 us (8%)
  between operations  14.2 us (2%)
    psum x1, blocking collectives, on_device(): grad_gain = lax.psum(jnp.sum(grad_y * normed * sig, axis=0), 'ctx')  268 us
    another operation x1, loops' own time, entering(): return lax.fori_loop(0, ahead, entering_one, state)  96.4 us
    all_gather x1, waiting for transfers between devices, carried_in(): gathered = jax.tree.map(lambda a: lax.all_gather(a, axis), part)  84.5 us
    select_n x30, other arithmetic, backward_join(): state_out = jnp.where(empty_b, state_a, jnp.where(empty_a, state_b, merged))  50.1 us
    dynamic_slice x60, local copies, waits for them, and re-layouts, entering_one(): lax.dynamic_index_in_dim(a, source, 0, False).astype(own.dtype)  35.4 us
    unnamed x28, local copies, waits for them, and re-layouts  21.5 us
    unnamed x1, blocking collectives  15.6 us
  transfers between devices with their start and end apart: 2, of which 1 were waited for; matrix products, arithmetic and copies ran while one was open for 6% of the time, Pallas kernels for 0%

commit v1 on v0

v1 whole, which is shorter than its diff:
```python
import functools

import jax
import jax.numpy as jnp
from jax import lax
from jax.experimental import pallas as pl
from jax.experimental.pallas import tpu as pltpu
from jax.sharding import PartitionSpec as P

HD = 128
ATT = 8192
EPSILON = 1e-06
TOK = 512
HALF = 256
PAIR = 2 * HD
PAIRS = 8
STATE_ROWS = 8 * HD
QUARTER = 2 * HD
TILE = 16
F32 = jnp.float32
BF16 = jnp.bfloat16
VMEM_LIMIT = 48 * 1024 * 1024


def dot(a, b, da, db):
    return lax.dot_general(a, b, (((da,), (db,)), ((), ())), preferred_element_type=F32)


def params():
    return pltpu.CompilerParams(vmem_limit_bytes=VMEM_LIMIT)


def estimate(flops, nbytes):
    return pl.CostEstimate(flops=int(flops), bytes_accessed=int(nbytes), transcendentals=0)


def column_block(first_pair):
    def index(i, ids):
        return (0, lax.rem(i + first_pair + 4 * ids[0], PAIRS))

    return pl.BlockSpec((TOK, PAIR), index)


def gain_block(first_pair):
    def index(i, ids):
        return (0, lax.rem(i + first_pair + 4 * ids[0], PAIRS))

    return pl.BlockSpec((1, PAIR), index)


def whole(shape):
    return pl.BlockSpec(shape, lambda i, ids: (0,) * len(shape))


def state_block(offset):
    return pl.BlockSpec((PAIR, HD), lambda i, ids: (i + offset, 0))


ANY = pl.BlockSpec(memory_space=pl.ANY)


def full(shape):
    return jax.ShapeDtypeStruct(shape, BF16)


def full32(shape):
    return jax.ShapeDtypeStruct(shape, F32)


def ends(seg_ref):
    seg = seg_ref[...].astype(F32)
    return seg, seg[:, 0:1], seg[:, TOK - 1 : TOK]


def count(flags):
    return jnp.sum(flags.astype(F32), axis=1, keepdims=True)


def token_rows(width=HD):
    return lax.broadcasted_iota(jnp.int32, (TOK, width), 0).astype(F32)


def head_mask(seg_ref):
    seg, first, _ = ends(seg_ref)
    return token_rows() < count(seg == first)


def tail_mask(seg_ref):
    seg, _, last = ends(seg_ref)
    return token_rows() >= (TOK - count(seg == last))


def info_tile(low, high):
    row = lax.broadcasted_iota(jnp.int32, (TILE, HD), 0)
    return jnp.where(
        row < 8, jnp.broadcast_to(low, (TILE, HD)), jnp.broadcast_to(high, (TILE, HD))
    ).astype(BF16)


def split_tile(x):
    high = x.astype(BF16).astype(F32)
    return jnp.concatenate([high, x - high], axis=0).astype(BF16)


def joined_tile(tile):
    t = tile.astype(F32)
    return t[0:8] + t[8:16]


def state_kernel(ids, seg_ref, k_ref, v_ref, out_ref, mask):
    i = pl.program_id(0)

    @pl.when(i == 0)
    def _():
        _, first, last = ends(seg_ref)
        mask[...] = tail_mask(seg_ref).astype(F32).astype(BF16)
        out_ref[STATE_ROWS : STATE_ROWS + TILE, :] = info_tile(first, last)

    for j in range(2):
        cols = slice(j * HD, (j + 1) * HD)
        part = dot(k_ref[:, cols] * mask[...], v_ref[:, cols], 0, 0)
        out_ref[pl.ds((2 * i + j) * HD, HD), :] = part.astype(BF16)


def local_state(ids, seg, k, v, first_pair):
    return pl.pallas_call(
        state_kernel,
        grid_spec=pltpu.PrefetchScalarGridSpec(
            num_scalar_prefetch=1,
            grid=(4,),
            in_specs=[whole((1, TOK)), column_block(first_pair), column_block(first_pair)],
            out_specs=whole((STATE_ROWS + TILE, HD)),
            scratch_shapes=[pltpu.VMEM((TOK, HD), BF16)],
        ),
        out_shape=full((STATE_ROWS + TILE, HD)),
        compiler_params=params(),
        cost_estimate=estimate(2.7e8, 2.3e6),
        name="local_state",
    )(ids, seg, k, v)


def pair_masks(seg_ref, m00, m1):
    seg, _, _ = ends(seg_ref)
    col = jnp.transpose(jnp.broadcast_to(seg, (8, TOK)))[:, 0:1]
    for start, ref in ((0, m00), (HALF, m1)):
        width = ref.shape[1]
        same = col[start : start + HALF] == seg[:, 0:width]
        t = lax.broadcasted_iota(jnp.int32, (HALF, width), 0) + start
        s = lax.broadcasted_iota(jnp.int32, (HALF, width), 1)
        ref[...] = jnp.where(same & (s <= t), 1.0, 0.0).astype(BF16)


def masked_pair(left, right, m00, m1):
    w0 = dot(left[0:HALF], right[0:HALF], 1, 1).astype(BF16) * m00[...]
    w1 = dot(left[HALF:TOK], right, 1, 1).astype(BF16) * m1[...]
    return w0, w1


def intra_kernel(ids, seg_ref, q_ref, k_ref, v_ref, *rest):
    out_ref, m00, m1 = rest[-3:]

    @pl.when(pl.program_id(0) == 0)
    def _():
        pair_masks(seg_ref, m00, m1)

    for j in range(2):
        cols = slice(j * HD, (j + 1) * HD)
        v = v_ref[:, cols]
        w0, w1 = masked_pair(q_ref[:, cols], k_ref[:, cols], m00, m1)
        out_ref[0:HALF, cols] = dot(w0, v[0:HALF], 1, 0)
        out_ref[HALF:TOK, cols] = dot(w1, v, 1, 0)


def intra(ids, seg, q, k, v, attn, first_pair, pairs):
    block = column_block(first_pair)
    more = () if attn is None else (attn,)
    return pl.pallas_call(
        intra_kernel,
        grid_spec=pltpu.PrefetchScalarGridSpec(
            num_scalar_prefetch=1,
            grid=(pairs,),
            in_specs=[whole((1, TOK)), block, block, block] + [ANY] * len(more),
            out_specs=block,
            scratch_shapes=[pltpu.VMEM((HALF, HALF), BF16), pltpu.VMEM((HALF, TOK), BF16)],
        ),
        out_shape=full32((TOK, 2048)),
        input_output_aliases={5: 0} if more else {},
        compiler_params=params(),
        cost_estimate=estimate(pairs * 4e8, pairs * 1.3e6),
        name="intra",
    )(ids, seg, q, k, v, *more)


def cross_kernel(ids, seg_ref, attn_in, q_ref, s_ref, go_ref, gi_ref, gain_ref, *rest):
    prev_ref = rest[0] if len(rest) == 5 else None
    attn_ref, sums_ref, squares, inners = rest[-4:]
    i = pl.program_id(0)

    @pl.when(i == 0)
    def _():
        squares[...] = jnp.zeros_like(squares)
        inners[...] = jnp.zeros_like(inners)

    allowed = head_mask(seg_ref)
    for j in range(2):
        cols = slice(j * HD, (j + 1) * HD)
        cross = dot(q_ref[:, cols], s_ref[j * HD : (j + 1) * HD, :], 1, 0)
        attn = attn_in[:, cols] + jnp.where(allowed, cross, 0.0)
        attn_ref[:, cols] = attn
        sig = 0.5 * jnp.tanh(0.5 * gi_ref[:, cols].astype(F32)) + 0.5
        dnorm = go_ref[:, cols].astype(F32) * sig * gain_ref[:, cols]
        squares[...] += attn * attn
        inners[...] += dnorm * attn

    @pl.when(i == pl.num_programs(0) - 1)
    def _():
        ones = jnp.ones((8, HD), F32)
        high = lax.Precision.HIGHEST
        dims = (((1,), (1,)), ((), ()))
        ss = lax.dot_general(ones, squares[...], dims, precision=high, preferred_element_type=F32)
        dd = lax.dot_general(ones, inners[...], dims, precision=high, preferred_element_type=F32)
        total = jnp.where(lax.broadcasted_iota(jnp.int32, (8, TOK), 0) < 4, ss, dd)
        if prev_ref is not None:
            total = total + prev_ref[...]
        sums_ref[...] = total


def cross(ids, seg, attn, q, state, go, gi, gain, prev, first_pair):
    block = column_block(first_pair)
    more = () if prev is None else (prev,)
    return pl.pallas_call(
        cross_kernel,
        grid_spec=pltpu.PrefetchScalarGridSpec(
            num_scalar_prefetch=1,
            grid=(4,),
            in_specs=[whole((1, TOK)), block, block, state_block(0), block, block]
            + [gain_block(first_pair)]
            + [whole((8, TOK))] * len(more),
            out_specs=[block, whole((8, TOK))],
            scratch_shapes=[pltpu.VMEM((TOK, HD), F32), pltpu.VMEM((TOK, HD), F32)],
        ),
        out_shape=[full32((TOK, 2048)), full32((8, TOK))],
        input_output_aliases={2: 0},
        compiler_params=params(),
        cost_estimate=estimate(2e8, 7e6),
        name="cross",
    )(ids, seg, attn, q, state, go, gi, gain, *more)


def scales(sums, rinv_ref, back_ref):
    own, one, two, three = [r[...] for r in sums]
    total = (own + one) + (two + three)
    rinv = lax.rsqrt(total * (1.0 / ATT) + EPSILON)
    rinv = rinv[0:1]
    back = rinv * rinv * rinv * total[4:5] * (1.0 / ATT)
    row = lax.broadcasted_iota(jnp.int32, (8, TOK), 0)
    both = jnp.where(
        row < 4, jnp.broadcast_to(rinv, (8, TOK)), jnp.broadcast_to(back, (8, TOK))
    )
    cols = jnp.transpose(both)
    rinv_ref[...] = jnp.broadcast_to(cols[:, 0:1], (TOK, HD))
    back_ref[...] = jnp.broadcast_to(cols[:, 4:5], (TOK, HD))


def grad_kernel(ids, seg_ref, s0, s1, s2, s3, attn_ref, q_ref, go_ref, gi_ref, gain_ref, *rest):
    g_ref, out_ref, mask, rinv, back, gains = rest[-6:]
    i = pl.program_id(0)

    @pl.when(i == 0)
    def _():
        _, first, last = ends(seg_ref)
        mask[...] = head_mask(seg_ref).astype(F32).astype(BF16)
        out_ref[STATE_ROWS : STATE_ROWS + TILE, :] = info_tile(8.0 - last, 8.0 - first)
        scales((s0, s1, s2, s3), rinv, back)

    for j in range(2):
        cols = slice(j * HD, (j + 1) * HD)
        attn = attn_ref[:, cols]
        sig = 0.5 * jnp.tanh(0.5 * gi_ref[:, cols].astype(F32)) + 0.5
        gated = go_ref[:, cols].astype(F32) * sig * rinv[...]
        gains[pl.ds(2 * i + j, 1), :] = jnp.sum(gated * attn, axis=0, keepdims=True)
        g = (gated * gain_ref[:, cols] - attn * back[...]).astype(BF16)
        g_ref[:, cols] = g
        part = dot(q_ref[:, cols] * mask[...], g, 0, 0)
        out_ref[pl.ds((2 * i + j) * HD, HD), :] = part.astype(BF16)

    @pl.when(i == pl.num_programs(0) - 1)
    def _():
        out_ref[STATE_ROWS + TILE : STATE_ROWS + 2 * TILE, :] = split_tile(gains[...])


def grad_attn(ids, seg, sums, attn, q, go, gi, gain, g, first_pair):
    block = column_block(first_pair)
    more = () if g is None else (g,)
    rows = STATE_ROWS + 2 * TILE
    return pl.pallas_call(
        grad_kernel,
        grid_spec=pltpu.PrefetchScalarGridSpec(
            num_scalar_prefetch=1,
            grid=(4,),
            in_specs=[whole((1, TOK))]
            + [whole((8, TOK))] * 4
            + [block] * 4
            + [gain_block(first_pair)]
            + [ANY] * len(more),
            out_specs=[block, whole((rows, HD))],
            scratch_shapes=[
                pltpu.VMEM((TOK, HD), BF16),
                pltpu.VMEM((TOK, HD), F32),
                pltpu.VMEM((TOK, HD), F32),
                pltpu.VMEM((8, HD), F32),
            ],
        ),
        out_shape=[full((TOK, 2048)), full((rows, HD))],
        input_output_aliases={11: 0} if more else {},
        compiler_params=params(),
        cost_estimate=estimate(2.7e8, 6e6),
        name="grad_attn",
    )(ids, seg, *sums, attn, q, go, gi, gain, *more)


def local_grads_kernel(
    ids, seg_ref, s0, s1, s2, s3, q_ref, k_ref, v_ref, g_ref, go_ref, gi_ref, attn_ref, gain_ref,
    state_ref, *rest
):
    lo_ref, gg_ref, dq_ref, dk_ref, dv_ref, m00, m1, rinv, back = rest[-9:]

    @pl.when(pl.program_id(0) == 0)
    def _():
        pair_masks(seg_ref, m00, m1)
        scales((s0, s1, s2, s3), rinv, back)

    allowed = head_mask(seg_ref)
    for j in range(2):
        cols = slice(j * HD, (j + 1) * HD)
        q, k, v, g = q_ref[:, cols], k_ref[:, cols], v_ref[:, cols], g_ref[:, cols]
        w0, w1 = masked_pair(q, k, m00, m1)
        dw0, dw1 = masked_pair(g, v, m00, m1)
        hop = jnp.where(allowed, dot(g, state_ref[j * HD : (j + 1) * HD, :], 1, 1), 0.0)
        dq_ref[0:HALF, cols] = (dot(dw0, k[0:HALF], 1, 0) + hop[0:HALF]).astype(BF16)
        dq_ref[HALF:TOK, cols] = (dot(dw1, k, 1, 0) + hop[HALF:TOK]).astype(BF16)
        for ref, a0, a1, rows in ((dk_ref, dw0, dw1, q), (dv_ref, w0, w1, g)):
            late = dot(a1, rows[HALF:TOK], 0, 0)
            ref[0:HALF, cols] = late[0:HALF] + dot(a0, rows[0:HALF], 0, 0)
            ref[HALF:TOK, cols] = late[HALF:TOK]
        bend = 0.5 * jnp.tanh(0.5 * gi_ref[:, cols].astype(F32))
        gated = attn_ref[:, cols] * rinv[...] * gain_ref[:, cols] * (0.5 + bend)
        lo_ref[:, cols] = gated.astype(BF16)
        gg_ref[:, cols] = (go_ref[:, cols].astype(F32) * gated * (0.5 - bend)).astype(BF16)


def local_grads(ids, seg, sums, q, k, v, g, go, gi, attn, gain, state, outs, first_pair, pairs):
    block = column_block(first_pair)
    more = () if outs is None else tuple(outs)
    return pl.pallas_call(
        local_grads_kernel,
        grid_spec=pltpu.PrefetchScalarGridSpec(
            num_scalar_prefetch=1,
            grid=(pairs,),
            in_specs=[whole((1, TOK))]
            + [whole((8, TOK))] * 4
            + [block] * 7
            + [gain_block(first_pair), state_block(first_pair % 4)]
            + [ANY] * len(more),
            out_specs=[block] * 5,
            scratch_shapes=[
                pltpu.VMEM((HALF, HALF), BF16),
                pltpu.VMEM((HALF, TOK), BF16),
                pltpu.VMEM((TOK, HD), F32),
                pltpu.VMEM((TOK, HD), F32),
            ],
        ),
        out_shape=[full((TOK, 2048))] * 3 + [full32((TOK, 2048))] * 2,
        input_output_aliases={15 + n: n for n in range(5)} if more else {},
        compiler_params=params(),
        cost_estimate=estimate(pairs * 1.1e9, pairs * 3.9e6),
        name="local_grads",
    )(ids, seg, *sums, q, k, v, g, go, gi, attn, gain, state, *more)


def finish_kernel(ids, seg_ref, dk_in, dv_in, k_ref, v_ref, l_ref, *rest):
    dk_ref, dv_ref = rest[-2:]
    allowed = tail_mask(seg_ref)
    for j in range(2):
        cols = slice(j * HD, (j + 1) * HD)
        later = l_ref[j * HD : (j + 1) * HD, :]
        dk = dot(v_ref[:, cols], later, 1, 1)
        dv = dot(k_ref[:, cols], later, 1, 0)
        dk_ref[:, cols] = (dk_in[:, cols] + jnp.where(allowed, dk, 0.0)).astype(BF16)
        dv_ref[:, cols] = (dv_in[:, cols] + jnp.where(allowed, dv, 0.0)).astype(BF16)


def finish(ids, seg, dk, dv, k, v, later, outs, first_pair):
    block = column_block(first_pair)
    more = () if outs is None else tuple(outs)
    return pl.pallas_call(
        finish_kernel,
        grid_spec=pltpu.PrefetchScalarGridSpec(
            num_scalar_prefetch=1,
            grid=(4,),
            in_specs=[whole((1, TOK))] + [block] * 4 + [state_block(0)] + [ANY] * len(more),
            out_specs=[block] * 2,
        ),
        out_shape=[full((TOK, 2048))] * 2,
        input_output_aliases={7 + n: n for n in range(2)} if more else {},
        compiler_params=params(),
        cost_estimate=estimate(2.7e8, 8e6),
        name="finish",
    )(ids, seg, dk, dv, k, v, later, *more)


def place(ids, reverse):
    core, x, z = ids[0], ids[1], ids[2]
    return (1 - core, 3 - x, 3 - z) if reverse else (core, x, z)


def info_rows(ref, at):
    tile = ref[at : at + TILE, :].astype(F32)
    return tile[0:1], tile[8:9]


def flag(cond):
    return jnp.where(cond, 1.0, 0.0)


def sorted_cores(first_core, own, other):
    return jnp.where(first_core, own, other), jnp.where(first_core, other, own)


def chip_kernel(reverse, gain, ids, own_ref, other_ref, *outs):
    vcore, _, _ = place(ids, reverse)
    first_core = vcore == 0
    low_own, high_own = info_rows(own_ref, STATE_ROWS)
    low_other, high_other = info_rows(other_ref, STATE_ROWS)
    low_a, _ = sorted_cores(first_core, low_own, low_other)
    high_a, high_b = sorted_cores(first_core, high_own, high_other)
    join = flag(high_a == high_b)
    own_weight = jnp.where(first_core, join, 1.0)
    other_weight = jnp.where(first_core, 1.0, join)
    for m, out in enumerate(outs):
        rows = pl.ds(pl.multiple_of((ids[1] ^ m) * QUARTER, QUARTER), QUARTER)
        total = own_ref[rows, :].astype(F32) * own_weight
        total = total + other_ref[rows, :].astype(F32) * other_weight
        out[0:QUARTER, :] = total.astype(BF16)
        out[QUARTER : QUARTER + TILE, :] = info_tile(low_a, high_b)
        if gain:
            at = slice(STATE_ROWS + TILE, STATE_ROWS + 2 * TILE)
            both = joined_tile(own_ref[at, :]) + joined_tile(other_ref[at, :])
            out[QUARTER + TILE : QUARTER + 2 * TILE, :] = split_tile(both)


def row_kernel(gain, ids, p0, p1, p2, p3, out):
    parts = (p0, p1, p2, p3)
    info = [info_rows(p, QUARTER) for p in parts]
    low = jnp.minimum(jnp.minimum(info[0][0], info[1][0]), jnp.minimum(info[2][0], info[3][0]))
    high = jnp.maximum(jnp.maximum(info[0][1], info[1][1]), jnp.maximum(info[2][1], info[3][1]))
    total = None
    for p, (_, own_high) in zip(parts, info):
        term = p[0:QUARTER, :].astype(F32) * flag(own_high == high)
        total = term if total is None else total + term
    out[0:QUARTER, :] = total.astype(BF16)
    out[QUARTER : QUARTER + TILE, :] = info_tile(low, high)
    if gain:
        g = [joined_tile(p[QUARTER + TILE : QUARTER + 2 * TILE, :]) for p in parts]
        out[QUARTER + TILE : QUARTER + 2 * TILE, :] = split_tile((g[0] + g[1]) + (g[2] + g[3]))


def entry_kernel(reverse, gain, ids, p0, p1, p2, p3, t0, t1, t2, t3, *outs):
    _, vx, vz = place(ids, reverse)
    parts = (p0, p1, p2, p3)
    rows = (t0, t1, t2, t3)
    info = [info_rows(p, QUARTER) for p in parts]
    row_high = [info_rows(t, QUARTER)[1] for t in rows]
    for m in range(4):
        low = info[m][0]
        total = jnp.zeros((QUARTER, HD), F32)
        for n in range(4):
            if n != m:
                before = flag((vx ^ n) < (vx ^ m))
                total = total + parts[n][0:QUARTER, :].astype(F32) * (flag(info[n][1] == low) * before)
        for n in range(1, 4):
            before = flag((vz ^ n) < vz)
            total = total + rows[n][0:QUARTER, :].astype(F32) * (flag(row_high[n] == low) * before)
        outs[m][...] = total.astype(BF16)
    if gain:
        g = [joined_tile(t[QUARTER + TILE : QUARTER + 2 * TILE, :]) for t in rows]
        outs[4][...] = split_tile((g[0] + g[1]) + (g[2] + g[3]))


def device_kernel(reverse, gain, ids, own_ref, other_ref, e0, e1, e2, e3, *rest):
    keep, send = rest[-2:]
    vcore, _, _ = place(ids, reverse)
    first_core = vcore == 0
    low_own, high_own = info_rows(own_ref, STATE_ROWS)
    low_other, high_other = info_rows(other_ref, STATE_ROWS)
    low_a, low_b = sorted_cores(first_core, low_own, low_other)
    high_a, _ = sorted_cores(first_core, high_own, high_other)
    from_a = flag(high_a == low_b)
    from_chip = flag(low_a == low_b)
    for m, ref in enumerate((e0, e1, e2, e3)):
        rows = pl.ds(pl.multiple_of((ids[1] ^ m) * QUARTER, QUARTER), QUARTER)
        entry = ref[...].astype(F32)
        a = jnp.where(first_core, own_ref[rows, :].astype(F32), other_ref[rows, :].astype(F32))
        second = a * from_a + entry * from_chip
        keep[rows, :] = jnp.where(first_core, entry, second).astype(BF16)
        send[rows, :] = jnp.where(first_core, second, entry).astype(BF16)
    if gain:
        send[STATE_ROWS : STATE_ROWS + TILE, :] = rest[0][...]


def small(kernel, out_rows, nbytes, name, ids, *args):
    block = pl.BlockSpec(memory_space=pltpu.VMEM)
    return pl.pallas_call(
        kernel,
        in_specs=[pl.BlockSpec(memory_space=pltpu.SMEM)] + [block] * len(args),
        out_specs=[block] * len(out_rows),
        out_shape=[full((r, HD)) for r in out_rows],
        compiler_params=params(),
        cost_estimate=estimate(1e6, nbytes),
        name=name,
    )(ids, *args)


def swap(x, axis, size, bits):
    return lax.ppermute(x, axis, [(i, i ^ bits) for i in range(size)])


def chip_swap(x):
    return swap(x, "ctx", 32, 1)


def row_swap(x, m):
    return swap(x, "ctx", 32, m << 1)


def plane_swap(x, m):
    return swap(x, "ctx", 32, m << 3)


def scan(ids, own, other, reverse, gain):
    extra = TILE if gain else 0
    rows = QUARTER + TILE + extra
    parts = small(
        functools.partial(chip_kernel, reverse, gain), [rows] * 4, 1.1e6, "chip_sum", ids, own, other
    )
    parts = [parts[0]] + [row_swap(parts[m], m) for m in range(1, 4)]
    total = small(functools.partial(row_kernel, gain), [rows], 3e5, "row_sum", ids, *parts)[0]
    totals = [total] + [plane_swap(total, m) for m in range(1, 4)]
    entries = small(
        functools.partial(entry_kernel, reverse, gain),
        [QUARTER] * 4 + ([TILE] if gain else []),
        8e5,
        "entry",
        ids,
        *parts,
        *totals,
    )
    tail = entries[4:]
    entries = [entries[0]] + [row_swap(entries[m], m) for m in range(1, 4)]
    keep, send = small(
        functools.partial(device_kernel, reverse, gain),
        [STATE_ROWS, STATE_ROWS + extra],
        1.3e6,
        "device_entry",
        ids,
        own,
        other,
        *entries,
        *tail,
    )
    return keep, chip_swap(send), tail


def on_device(query, keys, values, gate_input, grad_output, norm_gain, segment_ids):
    where = lax.axis_index("ctx")
    core = where & 1
    ids = jnp.stack([core, (where >> 1) & 3, where >> 3]).astype(jnp.int32)
    seg = segment_ids.reshape(1, TOK)
    gain = norm_gain.reshape(1, -1)

    sent = local_state(ids, seg, keys, values, 4)
    other = chip_swap(sent)
    own = local_state(ids, seg, keys, values, 0)
    attn = intra(ids, seg, query, keys, values, None, 0, 4)
    attn = intra(ids, seg, query, keys, values, attn, 4, 4)
    keep, received, _ = scan(ids, own, other, False, False)
    attn, sums = cross(
        ids, seg, attn, query, keep, grad_output, gate_input, gain, None, 0
    )
    attn, sums = cross(
        ids, seg, attn, query, received, grad_output, gate_input, gain, sums, 4
    )
    sums = [sums] + [swap(sums, "tp", 4, m) for m in range(1, 4)]

    g, sent = grad_attn(ids, seg, sums, attn, query, grad_output, gate_input, gain, None, 4)
    other = chip_swap(sent)
    g, own = grad_attn(ids, seg, sums, attn, query, grad_output, gate_input, gain, g, 0)
    outs = None
    for first_pair, state in ((0, keep), (2, keep), (4, received), (6, received)):
        outs = local_grads(
            ids, seg, sums, query, keys, values, g, grad_output, gate_input, attn, gain, state,
            outs, first_pair, 2,
        )
    layer_out, grad_gate, grad_query, grad_keys, grad_values = outs
    later_keep, later_received, tail = scan(ids, own, other, True, True)
    done = finish(ids, seg, grad_keys, grad_values, keys, values, later_keep, None, 0)
    grad_keys, grad_values = finish(
        ids, seg, grad_keys, grad_values, keys, values, later_received, done, 4
    )
    gain_keep = joined_tile(tail[0])
    gain_other = joined_tile(later_received[STATE_ROWS : STATE_ROWS + TILE])
    grad_gain = jnp.where(
        core == 0,
        jnp.concatenate([gain_keep, gain_other]),
        jnp.concatenate([gain_other, gain_keep]),
    ).reshape(-1)
    return layer_out, grad_query, grad_keys, grad_values, grad_gate, grad_gain


def solution(mesh):
    in_specs = (P("ctx", "tp"),) * 5 + (P("tp"), P("ctx"))
    out_specs = (P("ctx", "tp"),) * 5 + (P("tp"),)
    return jax.shard_map(
        on_device, mesh=mesh, in_specs=in_specs, out_specs=out_specs, check_vma=False
    )
```

time: 709 us -> 148 us (0.21); the launches traced: 695 us -> 147 us
  blocking collectives: 298 us -> 0 us
  loops' own time: 100 us -> 0 us
  Pallas kernels: 0 us -> 83.7 us
  waiting for transfers between devices: 84.5 us -> 15.5 us
  local copies, waits for them, and re-layouts: 76.8 us -> 9.7 us
  other arithmetic: 65.7 us -> 0.7 us
  matrix products: 55.6 us -> 0 us
  starting transfers between devices: 0.08 us -> 36.7 us
  between operations: 14.2 us -> 0.91 us
    psum x3 -> x0, blocking collectives: 282 us -> none  [the longest x1 268 us: on_device(): grad_gain = lax.psum(jnp.sum(grad_y * normed * sig, axis=0), 'ctx')]
    another operation x2 -> x0, loops' own time: 100 us -> none  [the longest x1 96.4 us: entering(): return lax.fori_loop(0, ahead, entering_one, state)]
    all_gather x2 -> x0, waiting for transfers between devices: 84.5 us -> none  [the longest x1 84.5 us: carried_in(): gathered = jax.tree.map(lambda a: lax.all_gather(a, axis), part)]
    pallas_call x0 -> x22, Pallas kernels: none -> 83.7 us  [the longest x4 29.2 us: local_grads(): pl.pallas_call(local_grads_kernel, grid_spec=pltpu.PrefetchScalarGridSpec...]
    dot_general x12 -> x0, matrix products: 55.6 us -> none  [the longest x2 9.04 us: masked_product(): jnp.einsum('thd,shd->hts', left_rows, right_rows, preferred_element_type=...]
    select_n x31 -> x1, other arithmetic: 51.9 us -> 0.61 us  [on_device(): jnp.where(core == 0, jnp.concatenate([gain_keep, gain_other]), jnp.concat...]
    ppermute x0 -> x25, starting transfers between devices: none -> 36.7 us  [swap(): return lax.ppermute(x, axis, [(i, i ^ bits) for i in range(size)])]
    dynamic_slice x62 -> x0, local copies, waits for them, and re-layouts: 36.6 us -> none  [the longest x60 35.4 us: entering_one(): lax.dynamic_index_in_dim(a, source, 0, False).astype(own.dtype)]
  transfers between devices with their start and end apart: 2 -> 25, of which waited for: 1 -> 8; matrix products, arithmetic and copies ran while one was open for 6% -> 0% of each run, Pallas kernels for 0% -> 40%
where the time goes in v1:
time: 148 us; the launch traced here: 147 us
  Pallas kernels  83.7 us (57%)
  starting transfers between devices  36.7 us (25%)
  waiting for transfers between devices  15.5 us (10%)
  local copies, waits for them, and re-layouts  9.7 us (7%)
    ppermute x25, starting transfers between devices, swap(): return lax.ppermute(x, axis, [(i, i ^ bits) for i in range(size)])  36.7 us
    pallas_call x4, Pallas kernels, local_grads(): pl.pallas_call(local_grads_kernel, grid_spec=pltpu.PrefetchScalarGridSpec...  29.2 us
    ppermute x25, waiting for transfers between devices, swap(): return lax.ppermute(x, axis, [(i, i ^ bits) for i in range(size)])  15.5 us
    pallas_call x2, Pallas kernels, intra(): pl.pallas_call(intra_kernel, grid_spec=pltpu.PrefetchScalarGridSpec(num_s...  11.8 us
    pallas_call x2, Pallas kernels, cross(): pl.pallas_call(cross_kernel, grid_spec=pltpu.PrefetchScalarGridSpec(num_s...  11.7 us
    pallas_call x2, Pallas kernels, finish(): pl.pallas_call(finish_kernel, grid_spec=pltpu.PrefetchScalarGridSpec(num_...  10.5 us
    pallas_call x2, Pallas kernels, grad_attn(): pl.pallas_call(grad_kernel, grid_spec=pltpu.PrefetchScalarGridSpec(num_sc...  10.3 us
    unnamed x28, local copies, waits for them, and re-layouts  9.7 us
  transfers between devices with their start and end apart: 25, of which 8 were waited for; matrix products, arithmetic and copies ran while one was open for 0% of the time, Pallas kernels for 40%

profile of v1, /device:TPU:1, one launch (start us, length us, event | category | flops | bytes accessed | tf_op | source)
XLA Modules:
  0.0 147.2 jit_solution(8185963186974562727)
XLA Ops:
  0.6 0.1 pad_add_fusion.ids
  0.7 1.6 %copy-done = bf16[512,2048]{1,0:T(8,128)(2,1)S(1)} copy-done((bf16[512,2048]{1,0:T(8,128)(2,1)S(1)}, bf16[512,2048]{1,0:T(8,128)(2,1)}, u32[]{:S(2)}) %copy-start) | copy-done | bytes 2097176
  2.3 1.6 %copy-done.2 = bf16[512,2048]{1,0:T(8,128)(2,1)S(1)} copy-done((bf16[512,2048]{1,0:T(8,128)(2,1)S(1)}, bf16[512,2048]{1,0:T(8,128)(2,1)}, u32[]{:S(2)}) %copy-start.2) | copy-done | bytes 2097176
  3.9 0.7 copy-done.12
  4.6 2.3 %local_state.3 = bf16[1040,128]{1,0:T(8,128)(2,1)S(1)} custom-call(s32[3]{0:T(128)S(1)} %pad_add_fusion.ids, s32[1,512]{1,0:T(1,128)S(1)} %bitcast.15, bf16[512,2048]{1,0:T(8,128)(2,1)S(1)} %copy-done, bf16[512,2048]{1,0:T(8,128)(2,1)S(1)} %copy-done.2), custom_call_target="tpu_custom_call" | custom-call | flops 270000000 | bytes 2300000 | tf_op jit(solution)/shard_map/local_state/pallas_call | solution.py:126
  6.9 1.5 %collective-permute-start = (bf16[1040,128]{1,0:T(8,128)(2,1)S(1)}, bf16[1040,128]{1,0:T(8,128)(2,1)S(1)}, u32[]{:S(2)}, u32[]{:S(2)}) collective-permute-start(bf16[1040,128]{1,0:T(8,128)(2,1)S(1)} %local_state.3), channel_id=1, source_target_pairs={{0,4},{4,0},{8,12},{12,8},{16,20},{20,16},{24,28},{28,24},{32,36},... | collective-permute-start | bytes 798728 | tf_op jit(solution)/shard_map/ppermute | solution.py:525
  8.4 2.3 %local_state.2.own_ref = bf16[1040,128]{1,0:T(8,128)(2,1)S(1)} custom-call(s32[3]{0:T(128)S(1)} %pad_add_fusion.ids, s32[1,512]{1,0:T(1,128)S(1)} %bitcast.16, bf16[512,2048]{1,0:T(8,128)(2,1)S(1)} %copy-done, bf16[512,2048]{1,0:T(8,128)(2,1)S(1)} %copy-done.2), custom_call_target="tpu_custom_call" | custom-call | flops 270000000 | bytes 2300000 | tf_op jit(solution)/shard_map/local_state/pallas_call | solution.py:126
  10.7 0.0 copy-start.1
  10.7 0.6 chip_sum.2
  11.4 1.4 collective-permute-start.1
  12.8 2.4 %collective-permute-start.2 = (bf16[272,128]{1,0:T(8,128)(2,1)S(1)}, bf16[272,128]{1,0:T(8,128)(2,1)S(1)}, u32[]{:S(2)}, u32[]{:S(2)}) collective-permute-start(bf16[272,128]{1,0:T(8,128)(2,1)S(1)} %get-tuple-element.61), channel_id=1, source_target_pairs={{0,16},{4,20},{8,24},{12,28},{16,0},{20,4},{24,8},{28,12},{32,48},... | collective-permute-start | bytes 208904 | tf_op jit(solution)/shard_map/ppermute | solution.py:525
  15.2 0.1 collective-permute-start.3
  15.3 3.7 %collective-permute-done.2.p2 = bf16[272,128]{1,0:T(8,128)(2,1)S(1)} collective-permute-done((bf16[272,128]{1,0:T(8,128)(2,1)S(1)}, bf16[272,128]{1,0:T(8,128)(2,1)S(1)}, u32[]{:S(2)}, u32[]{:S(2)}) %collective-permute-start.2) | collective-permute-done | bytes 69664 | tf_op jit(solution)/shard_map/ppermute | solution.py:525
  19.0 0.9 collective-permute-done.3.p3
  19.9 0.6 row_sum.2.t0
  20.5 3.8 %collective-permute-start.6 = (bf16[272,128]{1,0:T(8,128)(2,1)S(1)}, bf16[272,128]{1,0:T(8,128)(2,1)S(1)}, u32[]{:S(2)}, u32[]{:S(2)}) collective-permute-start(bf16[272,128]{1,0:T(8,128)(2,1)S(1)} %row_sum.2.t0), channel_id=1, source_target_pairs={{0,96},{4,100},{8,104},{12,108},{16,112},{20,116},{24,120},{28,124... | collective-permute-start | bytes 208904 | tf_op jit(solution)/shard_map/ppermute | solution.py:525
  24.4 0.7 collective-permute-start.4
  25.0 1.3 collective-permute-done.6.t3
  26.3 2.7 %collective-permute-done.5.t2 = bf16[272,128]{1,0:T(8,128)(2,1)S(1)} collective-permute-done((bf16[272,128]{1,0:T(8,128)(2,1)S(1)}, bf16[272,128]{1,0:T(8,128)(2,1)S(1)}, u32[]{:S(2)}, u32[]{:S(2)}) %collective-permute-start.5) | collective-permute-done | bytes 69664 | tf_op jit(solution)/shard_map/ppermute | solution.py:525
  29.0 0.9 entry.2
  29.9 0.5 collective-permute-start.7
  30.4 2.5 %collective-permute-start.8 = (bf16[256,128]{1,0:T(8,128)(2,1)S(1)}, bf16[256,128]{1,0:T(8,128)(2,1)S(1)}, u32[]{:S(2)}, u32[]{:S(2)}) collective-permute-start(bf16[256,128]{1,0:T(8,128)(2,1)S(1)} %get-tuple-element.65), channel_id=1, source_target_pairs={{0,16},{4,20},{8,24},{12,28},{16,0},{20,4},{24,8},{28,12},{32,48},... | collective-permute-start | bytes 196616 | tf_op jit(solution)/shard_map/ppermute | solution.py:525
  32.9 0.9 collective-permute-start.9
  33.8 1.5 collective-permute-done.8.e2
  35.3 2.0 %collective-permute-done.9.e3 = bf16[256,128]{1,0:T(8,128)(2,1)S(1)} collective-permute-done((bf16[256,128]{1,0:T(8,128)(2,1)S(1)}, bf16[256,128]{1,0:T(8,128)(2,1)S(1)}, u32[]{:S(2)}, u32[]{:S(2)}) %collective-permute-start.9) | collective-permute-done | bytes 65568 | tf_op jit(solution)/shard_map/ppermute | solution.py:525
  37.3 0.7 device_entry.2
  38.0 4.0 %collective-permute-start.10 = (bf16[1024,128]{1,0:T(8,128)(2,1)S(1)}, bf16[1024,128]{1,0:T(8,128)(2,1)S(1)}, u32[]{:S(2)}, u32[]{:S(2)}) collective-permute-start(bf16[1024,128]{1,0:T(8,128)(2,1)S(1)} %get-tuple-element.69), channel_id=1, source_target_pairs={{0,4},{4,0},{8,12},{12,8},{16,20},{20,16},{24,28},{28,24},{32,36},... | collective-permute-start | bytes 786440 | tf_op jit(solution)/shard_map/ppermute | solution.py:525
  42.0 5.8 %intra.2.rest_0_ = f32[512,2048]{1,0:T(8,128)} custom-call(s32[3]{0:T(128)S(1)} %pad_add_fusion.ids, s32[1,512]{1,0:T(1,128)S(1)} %bitcast.17, bf16[512,2048]{1,0:T(8,128)(2,1)S(1)} %copy-done.4, bf16[512,2048]{1,0:T(8,128)(2,1)S(1)} %copy-done.1, bf16[512,2048]{1,0:T(8,128)(2,1)} %v_ref.19), custom_call_target="tpu_custom_call" | custom-call | flops 1600000000 | bytes 5200000 | tf_op jit(solution)/shard_map/intra/pallas_call | solution.py:177
  47.8 5.9 %intra.3.attn_in = f32[512,2048]{1,0:T(8,128)} custom-call(s32[3]{0:T(128)S(1)} %pad_add_fusion.ids, s32[1,512]{1,0:T(1,128)S(1)} %bitcast.18, bf16[512,2048]{1,0:T(8,128)(2,1)S(1)} %copy-done.4, bf16[512,2048]{1,0:T(8,128)(2,1)S(1)} %copy-done.1, bf16[512,2048]{1,0:T(8,128)(2,1)} %v_ref.19, f32[512,2048]{1,0:T(8,128)} %intra.2.rest_0_), custom_call_target="tpu_custom_call", output_to_operand_aliasing={{}: (5, {})} | custom-call | flops 1600000000 | bytes 5200000 | tf_op jit(solution)/shard_map/intra/pallas_call | solution.py:177
  53.7 5.8 %cross.2 = (f32[512,2048]{1,0:T(8,128)}, f32[8,512]{1,0:T(8,128)S(1)}) custom-call(s32[3]{0:T(128)S(1)} %pad_add_fusion.ids, s32[1,512]{1,0:T(1,128)S(1)} %bitcast.19, f32[512,2048]{1,0:T(8,128)} %intra.3.attn_in, bf16[512,2048]{1,0:T(8,128)(2,1)S(1)} %copy-done.4, ...), custom_call_target="tpu_custom_call", output_to_operand_aliasing={{0}: (2, {})} | custom-call | flops 200000000 | bytes 7000000 | tf_op jit(solution)/shard_map/cross/pallas_call | solution.py:231
  59.6 5.9 %cross.3 = (f32[512,2048]{1,0:T(8,128)}, f32[8,512]{1,0:T(8,128)S(1)}) custom-call(s32[3]{0:T(128)S(1)} %pad_add_fusion.ids, s32[1,512]{1,0:T(1,128)S(1)} %bitcast.20, f32[512,2048]{1,0:T(8,128)} %get-tuple-element.68.attn_in, bf16[512,2048]{1,0:T(8,128)(2,1)S(1)} %copy-done.4, ...), custom_call_target="tpu_custom_call", output_to_operand_aliasing={{0}: (2, {})} | custom-call | flops 200000000 | bytes 7000000 | tf_op jit(solution)/shard_map/cross/pallas_call | solution.py:231
  65.4 2.7 %collective-permute-start.13 = (f32[8,512]{1,0:T(8,128)S(1)}, f32[8,512]{1,0:T(8,128)S(1)}, u32[]{:S(2)}, u32[]{:S(2)}) collective-permute-start(f32[8,512]{1,0:T(8,128)S(1)} %get-tuple-element.71.s0), channel_id=1, source_target_pairs={{0,3},{1,2},{2,1},{3,0},{4,7},{5,6},{6,5},{7,4},{8,11},{9,10},{10,... | collective-permute-start | bytes 49160 | tf_op jit(solution)/shard_map/ppermute | solution.py:525
  68.2 0.3 collective-permute-start.12
  68.5 0.2 collective-permute-start.11
  68.7 0.5 collective-permute-done.13.s3
  69.3 3.0 %collective-permute-done.12.s2 = f32[8,512]{1,0:T(8,128)S(1)} collective-permute-done((f32[8,512]{1,0:T(8,128)S(1)}, f32[8,512]{1,0:T(8,128)S(1)}, u32[]{:S(2)}, u32[]{:S(2)}) %collective-permute-start.12) | collective-permute-done | bytes 16416 | tf_op jit(solution)/shard_map/ppermute | solution.py:525
  72.2 5.1 %grad_attn.2 = (bf16[512,2048]{1,0:T(8,128)(2,1)S(1)}, bf16[1056,128]{1,0:T(8,128)(2,1)S(1)}) custom-call(s32[3]{0:T(128)S(1)} %pad_add_fusion.ids, s32[1,512]{1,0:T(1,128)S(1)} %bitcast.21, f32[8,512]{1,0:T(8,128)S(1)} %get-tuple-element.71.s0, f32[8,512]{1,0:T(8,128)S(1)} %collective-permute-done.11.s1, f32[8,512]{1,0:T(8,128)S(1)} %collective-permute-done.12.s2, ...), custom_call_target="tpu_custom_call" | custom-call | flops 270000000 | bytes 6000000 | tf_op jit(solution)/shard_map/grad_attn/pallas_call | solution.py:296
  77.4 1.3 copy-done.8
  78.7 1.4 collective-permute-start.14
  80.2 1.6 %copy-done.5 = bf16[512,2048]{1,0:T(8,128)(2,1)S(1)} copy-done((bf16[512,2048]{1,0:T(8,128)(2,1)S(1)}, bf16[512,2048]{1,0:T(8,128)(2,1)}, u32[]{:S(2)}) %copy-start.5) | copy-done | bytes 2097176
  81.8 1.6 %copy-done.9 = bf16[512,2048]{1,0:T(8,128)(2,1)S(1)} copy-done((bf16[512,2048]{1,0:T(8,128)(2,1)S(1)}, bf16[512,2048]{1,0:T(8,128)(2,1)}, u32[]{:S(2)}) %copy-start.9) | copy-done | bytes 2097176
  83.4 5.2 %grad_attn.3 = (bf16[512,2048]{1,0:T(8,128)(2,1)S(1)}, bf16[1056,128]{1,0:T(8,128)(2,1)S(1)}) custom-call(s32[3]{0:T(128)S(1)} %pad_add_fusion.ids, s32[1,512]{1,0:T(1,128)S(1)} %bitcast.22, f32[8,512]{1,0:T(8,128)S(1)} %get-tuple-element.71.s0, f32[8,512]{1,0:T(8,128)S(1)} %collective-permute-done.11.s1, ...), custom_call_target="tpu_custom_call", output_to_operand_aliasing={{0}: (11, {})} | custom-call | flops 270000000 | bytes 6000000 | tf_op jit(solution)/shard_map/grad_attn/pallas_call | solution.py:296
  88.6 1.3 copy-done.10
  89.9 0.6 chip_sum.3
  90.5 0.1 collective-permute-start.15
  90.6 2.8 %collective-permute-start.16 = (bf16[288,128]{1,0:T(8,128)(2,1)S(1)}, bf16[288,128]{1,0:T(8,128)(2,1)S(1)}, u32[]{:S(2)}, u32[]{:S(2)}) collective-permute-start(bf16[288,128]{1,0:T(8,128)(2,1)S(1)} %get-tuple-element.98), channel_id=1, source_target_pairs={{0,16},{4,20},{8,24},{12,28},{16,0},{20,4},{24,8},{28,12},{32,48},... | collective-permute-start | bytes 221192 | tf_op jit(solution)/shard_map/ppermute | solution.py:525
  93.4 1.1 collective-permute-start.17
  94.5 7.3 %local_grads.4 = (bf16[512,2048]{1,0:T(8,128)(2,1)}, bf16[512,2048]{1,0:T(8,128)(2,1)}, bf16[512,2048]{1,0:T(8,128)(2,1)}, f32[512,2048]{1,0:T(8,128)}, f32[512,2048]{1,0:T(8,128)}) custom-call(s32[3]{0:T(128)S(1)} %pad_add_fusion.ids, s32[1,512]{1,0:T(1,128)S(1)} %bitcast.23, f32[8,512]{1,0:T(8,128)S(1)} %get-tuple-element.71.s0, ...), custom_call_target="tpu_custom_call" | custom-call | flops 2200000000 | bytes 7800000 | tf_op jit(solution)/shard_map/local_grads/pallas_call | solution.py:355
  101.8 0.6 row_sum.3.t0
  102.4 1.1 collective-permute-start.20
  103.5 0.7 collective-permute-start.19
  104.2 1.5 %collective-permute-start.18 = (bf16[288,128]{1,0:T(8,128)(2,1)S(1)}, bf16[288,128]{1,0:T(8,128)(2,1)S(1)}, u32[]{:S(2)}, u32[]{:S(2)}) collective-permute-start(bf16[288,128]{1,0:T(8,128)(2,1)S(1)} %row_sum.3.t0), channel_id=1, source_target_pairs={{0,32},{4,36},{8,40},{12,44},{16,48},{20,52},{24,56},{28,60},{32,0... | collective-permute-start | bytes 221192 | tf_op jit(solution)/shard_map/ppermute | solution.py:525
  105.8 7.3 %local_grads.5 = (bf16[512,2048]{1,0:T(8,128)(2,1)}, bf16[512,2048]{1,0:T(8,128)(2,1)}, bf16[512,2048]{1,0:T(8,128)(2,1)}, f32[512,2048]{1,0:T(8,128)}, f32[512,2048]{1,0:T(8,128)}) custom-call(s32[3]{0:T(128)S(1)} %pad_add_fusion.ids, s32[1,512]{1,0:T(1,128)S(1)} %bitcast.24, ...), custom_call_target="tpu_custom_call", output_to_operand_aliasing={{0}: (15, {}), {1}: (16, {}), {2}: (17, {}), {3}: (18, {}),... | custom-call | flops 2200000000 | bytes 7800000 | tf_op jit(solution)/shard_map/local_grads/pallas_call | solution.py:355
  113.1 0.9 entry.3
  114.0 0.1 collective-permute-start.21
  114.0 2.8 %collective-permute-start.22 = (bf16[256,128]{1,0:T(8,128)(2,1)S(1)}, bf16[256,128]{1,0:T(8,128)(2,1)S(1)}, u32[]{:S(2)}, u32[]{:S(2)}) collective-permute-start(bf16[256,128]{1,0:T(8,128)(2,1)S(1)} %get-tuple-element.102), channel_id=1, source_target_pairs={{0,16},{4,20},{8,24},{12,28},{16,0},{20,4},{24,8},{28,12},{32,48},... | collective-permute-start | bytes 196616 | tf_op jit(solution)/shard_map/ppermute | solution.py:525
  116.8 1.1 collective-permute-start.23
  117.9 7.3 %local_grads.6 = (bf16[512,2048]{1,0:T(8,128)(2,1)}, bf16[512,2048]{1,0:T(8,128)(2,1)}, bf16[512,2048]{1,0:T(8,128)(2,1)}, f32[512,2048]{1,0:T(8,128)}, f32[512,2048]{1,0:T(8,128)}) custom-call(s32[3]{0:T(128)S(1)} %pad_add_fusion.ids, s32[1,512]{1,0:T(1,128)S(1)} %bitcast.25, ...), custom_call_target="tpu_custom_call", output_to_operand_aliasing={{0}: (15, {}), {1}: (16, {}), {2}: (17, {}), {3}: (18, {}),... | custom-call | flops 2200000000 | bytes 7800000 | tf_op jit(solution)/shard_map/local_grads/pallas_call | solution.py:355
  125.2 0.7 device_entry.3
  126.0 2.8 %collective-permute-start.24 = (bf16[1040,128]{1,0:T(8,128)(2,1)S(1)}, bf16[1040,128]{1,0:T(8,128)(2,1)S(1)}, u32[]{:S(2)}, u32[]{:S(2)}) collective-permute-start(bf16[1040,128]{1,0:T(8,128)(2,1)S(1)} %get-tuple-element.105), channel_id=1, source_target_pairs={{0,4},{4,0},{8,12},{12,8},{16,20},{20,16},{24,28},{28,24},{32,36},... | collective-permute-start | bytes 798728 | tf_op jit(solution)/shard_map/ppermute | solution.py:525
  128.8 7.3 %local_grads.7 = (bf16[512,2048]{1,0:T(8,128)(2,1)}, bf16[512,2048]{1,0:T(8,128)(2,1)}, bf16[512,2048]{1,0:T(8,128)(2,1)}, f32[512,2048]{1,0:T(8,128)}, f32[512,2048]{1,0:T(8,128)}) custom-call(s32[3]{0:T(128)S(1)} %pad_add_fusion.ids, s32[1,512]{1,0:T(1,128)S(1)} %bitcast.26, ...), custom_call_target="tpu_custom_call", output_to_operand_aliasing={{0}: (15, {}), {1}: (16, {}), {2}: (17, {}), {3}: (18, {}),... | custom-call | flops 2200000000 | bytes 7800000 | tf_op jit(solution)/shard_map/local_grads/pallas_call | solution.py:355
  136.2 5.2 %finish.2 = (bf16[512,2048]{1,0:T(8,128)(2,1)}, bf16[512,2048]{1,0:T(8,128)(2,1)}) custom-call(s32[3]{0:T(128)S(1)} %pad_add_fusion.ids, s32[1,512]{1,0:T(1,128)S(1)} %bitcast.27, f32[512,2048]{1,0:T(8,128)} %get-tuple-element.92.dk_in, f32[512,2048]{1,0:T(8,128)} %get-tuple-element.93.dv_in, bf16[512,2048]{1,0:T(8,128)(2,1)S(1)} %copy-done.1, ...), custom_call_target="tpu_custom_call" | custom-call | flops 270000000 | bytes 8000000 | tf_op jit(solution)/shard_map/finish/pallas_call | solution.py:396
  141.4 0.6 fusion
  142.0 5.2 %finish.3 = (bf16[512,2048]{1,0:T(8,128)(2,1)}, bf16[512,2048]{1,0:T(8,128)(2,1)}) custom-call(s32[3]{0:T(128)S(1)} %pad_add_fusion.ids, s32[1,512]{1,0:T(1,128)S(1)} %bitcast.28, f32[512,2048]{1,0:T(8,128)} %get-tuple-element.92.dk_in, f32[512,2048]{1,0:T(8,128)} %get-tuple-element.93.dv_in, ...), custom_call_target="tpu_custom_call", output_to_operand_aliasing={{0}: (7, {}), {1}: (8, {})} | custom-call | flops 270000000 | bytes 8000000 | tf_op jit(solution)/shard_map/finish/pallas_call | solution.py:396
  (42 shorter events, 0.1 us)
Async XLA Ops:
  0.7 1.6 %copy-start = (bf16[512,2048]{1,0:T(8,128)(2,1)S(1)}, bf16[512,2048]{1,0:T(8,128)(2,1)}, u32[]{:S(2)}) copy-start(bf16[512,2048]{1,0:T(8,128)(2,1)} %k_ref.19) | copy-start | bytes 6291460
  2.3 1.6 %copy-start.2 = (bf16[512,2048]{1,0:T(8,128)(2,1)S(1)}, bf16[512,2048]{1,0:T(8,128)(2,1)}, u32[]{:S(2)}) copy-start(bf16[512,2048]{1,0:T(8,128)(2,1)} %v_ref.19) | copy-start | bytes 6291460
  3.9 0.7 copy-start.12
  6.9 3.9 %collective-permute-start = (bf16[1040,128]{1,0:T(8,128)(2,1)S(1)}, bf16[1040,128]{1,0:T(8,128)(2,1)S(1)}, u32[]{:S(2)}, u32[]{:S(2)}) collective-permute-start(bf16[1040,128]{1,0:T(8,128)(2,1)S(1)} %local_state.3), channel_id=1, source_target_pairs={{0,4},{4,0},{8,12},{12,8},{16,20},{20,16},{24,28},{28,24},{32,36},... | collective-permute-start | bytes 798728 | tf_op jit(solution)/shard_map/ppermute | solution.py:525
  8.4 33.6 %copy-start.4 = (bf16[512,2048]{1,0:T(8,128)(2,1)S(1)}, bf16[512,2048]{1,0:T(8,128)(2,1)}, u32[]{:S(2)}) copy-start(bf16[512,2048]{1,0:T(8,128)(2,1)} %q_ref.19) | copy-start | bytes 6291460
  10.7 31.3 %copy-start.1 = (bf16[512,2048]{1,0:T(8,128)(2,1)S(1)}, bf16[512,2048]{1,0:T(8,128)(2,1)}, u32[]{:S(2)}) copy-start(bf16[512,2048]{1,0:T(8,128)(2,1)} %k_ref.19) | copy-start | bytes 6291460
  10.7 31.2 %copy-start.13 = (s32[512]{0:T(512)S(1)}, s32[512]{0:T(512)}, u32[]{:S(2)}) copy-start(s32[512]{0:T(512)} %param.13) | copy-start | bytes 6148
  11.4 3.9 %collective-permute-start.1 = (bf16[272,128]{1,0:T(8,128)(2,1)S(1)}, bf16[272,128]{1,0:T(8,128)(2,1)S(1)}, u32[]{:S(2)}, u32[]{:S(2)}) collective-permute-start(bf16[272,128]{1,0:T(8,128)(2,1)S(1)} %get-tuple-element.60), channel_id=1, source_target_pairs={{0,8},{4,12},{8,0},{12,4},{16,24},{20,28},{24,16},{28,20},{32,40},... | collective-permute-start | bytes 208904 | tf_op jit(solution)/shard_map/ppermute | solution.py:525
  12.8 6.2 %collective-permute-start.2 = (bf16[272,128]{1,0:T(8,128)(2,1)S(1)}, bf16[272,128]{1,0:T(8,128)(2,1)S(1)}, u32[]{:S(2)}, u32[]{:S(2)}) collective-permute-start(bf16[272,128]{1,0:T(8,128)(2,1)S(1)} %get-tuple-element.61), channel_id=1, source_target_pairs={{0,16},{4,20},{8,24},{12,28},{16,0},{20,4},{24,8},{28,12},{32,48},... | collective-permute-start | bytes 208904 | tf_op jit(solution)/shard_map/ppermute | solution.py:525
  15.2 4.7 %collective-permute-start.3 = (bf16[272,128]{1,0:T(8,128)(2,1)S(1)}, bf16[272,128]{1,0:T(8,128)(2,1)S(1)}, u32[]{:S(2)}, u32[]{:S(2)}) collective-permute-start(bf16[272,128]{1,0:T(8,128)(2,1)S(1)} %get-tuple-element.62), channel_id=1, source_target_pairs={{0,24},{4,28},{8,16},{12,20},{16,8},{20,12},{24,0},{28,4},{32,56},... | collective-permute-start | bytes 208904 | tf_op jit(solution)/shard_map/ppermute | solution.py:525
  20.5 5.8 %collective-permute-start.6 = (bf16[272,128]{1,0:T(8,128)(2,1)S(1)}, bf16[272,128]{1,0:T(8,128)(2,1)S(1)}, u32[]{:S(2)}, u32[]{:S(2)}) collective-permute-start(bf16[272,128]{1,0:T(8,128)(2,1)S(1)} %row_sum.2.t0), channel_id=1, source_target_pairs={{0,96},{4,100},{8,104},{12,108},{16,112},{20,116},{24,120},{28,124... | collective-permute-start | bytes 208904 | tf_op jit(solution)/shard_map/ppermute | solution.py:525
  24.3 4.7 %collective-permute-start.5 = (bf16[272,128]{1,0:T(8,128)(2,1)S(1)}, bf16[272,128]{1,0:T(8,128)(2,1)S(1)}, u32[]{:S(2)}, u32[]{:S(2)}) collective-permute-start(bf16[272,128]{1,0:T(8,128)(2,1)S(1)} %row_sum.2.t0), channel_id=1, source_target_pairs={{0,64},{4,68},{8,72},{12,76},{16,80},{20,84},{24,88},{28,92},{32,9... | collective-permute-start | bytes 208904 | tf_op jit(solution)/shard_map/ppermute | solution.py:525
  24.4 4.7 %collective-permute-start.4 = (bf16[272,128]{1,0:T(8,128)(2,1)S(1)}, bf16[272,128]{1,0:T(8,128)(2,1)S(1)}, u32[]{:S(2)}, u32[]{:S(2)}) collective-permute-start(bf16[272,128]{1,0:T(8,128)(2,1)S(1)} %row_sum.2.t0), channel_id=1, source_target_pairs={{0,32},{4,36},{8,40},{12,44},{16,48},{20,52},{24,56},{28,60},{32,0... | collective-permute-start | bytes 208904 | tf_op jit(solution)/shard_map/ppermute | solution.py:525
  29.9 3.9 %collective-permute-start.7 = (bf16[256,128]{1,0:T(8,128)(2,1)S(1)}, bf16[256,128]{1,0:T(8,128)(2,1)S(1)}, u32[]{:S(2)}, u32[]{:S(2)}) collective-permute-start(bf16[256,128]{1,0:T(8,128)(2,1)S(1)} %get-tuple-element.64), channel_id=1, source_target_pairs={{0,8},{4,12},{8,0},{12,4},{16,24},{20,28},{24,16},{28,20},{32,40},... | collective-permute-start | bytes 196616 | tf_op jit(solution)/shard_map/ppermute | solution.py:525
  30.4 4.9 %collective-permute-start.8 = (bf16[256,128]{1,0:T(8,128)(2,1)S(1)}, bf16[256,128]{1,0:T(8,128)(2,1)S(1)}, u32[]{:S(2)}, u32[]{:S(2)}) collective-permute-start(bf16[256,128]{1,0:T(8,128)(2,1)S(1)} %get-tuple-element.65), channel_id=1, source_target_pairs={{0,16},{4,20},{8,24},{12,28},{16,0},{20,4},{24,8},{28,12},{32,48},... | collective-permute-start | bytes 196616 | tf_op jit(solution)/shard_map/ppermute | solution.py:525
  32.9 4.3 %collective-permute-start.9 = (bf16[256,128]{1,0:T(8,128)(2,1)S(1)}, bf16[256,128]{1,0:T(8,128)(2,1)S(1)}, u32[]{:S(2)}, u32[]{:S(2)}) collective-permute-start(bf16[256,128]{1,0:T(8,128)(2,1)S(1)} %get-tuple-element.66), channel_id=1, source_target_pairs={{0,24},{4,28},{8,16},{12,20},{16,8},{20,12},{24,0},{28,4},{32,56},... | collective-permute-start | bytes 196616 | tf_op jit(solution)/shard_map/ppermute | solution.py:525
  38.0 21.6 %collective-permute-start.10 = (bf16[1024,128]{1,0:T(8,128)(2,1)S(1)}, bf16[1024,128]{1,0:T(8,128)(2,1)S(1)}, u32[]{:S(2)}, u32[]{:S(2)}) collective-permute-start(bf16[1024,128]{1,0:T(8,128)(2,1)S(1)} %get-tuple-element.69), channel_id=1, source_target_pairs={{0,4},{4,0},{8,12},{12,8},{16,20},{20,16},{24,28},{28,24},{32,36},... | collective-permute-start | bytes 786440 | tf_op jit(solution)/shard_map/ppermute | solution.py:525
  47.8 5.9 %copy-start.7 = (bf16[512,2048]{1,0:T(8,128)(2,1)S(1)}, bf16[512,2048]{1,0:T(8,128)(2,1)}, u32[]{:S(2)}) copy-start(bf16[512,2048]{1,0:T(8,128)(2,1)} %go_ref.15) | copy-start | bytes 6291460
  47.8 5.9 %copy-start.11 = (f32[2048]{0:T(1024)S(1)}, f32[2048]{0:T(1024)}, u32[]{:S(2)}) copy-start(f32[2048]{0:T(1024)} %param.12) | copy-start | bytes 24580
  65.4 3.9 %collective-permute-start.13 = (f32[8,512]{1,0:T(8,128)S(1)}, f32[8,512]{1,0:T(8,128)S(1)}, u32[]{:S(2)}, u32[]{:S(2)}) collective-permute-start(f32[8,512]{1,0:T(8,128)S(1)} %get-tuple-element.71.s0), channel_id=1, source_target_pairs={{0,3},{1,2},{2,1},{3,0},{4,7},{5,6},{6,5},{7,4},{8,11},{9,10},{10,... | collective-permute-start | bytes 49160 | tf_op jit(solution)/shard_map/ppermute | solution.py:525
  68.2 4.1 %collective-permute-start.12 = (f32[8,512]{1,0:T(8,128)S(1)}, f32[8,512]{1,0:T(8,128)S(1)}, u32[]{:S(2)}, u32[]{:S(2)}) collective-permute-start(f32[8,512]{1,0:T(8,128)S(1)} %get-tuple-element.71.s0), channel_id=1, source_target_pairs={{0,2},{1,3},{2,0},{3,1},{4,6},{5,7},{6,4},{7,5},{8,10},{9,11},{10,... | collective-permute-start | bytes 49160 | tf_op jit(solution)/shard_map/ppermute | solution.py:525
  68.5 3.7 %collective-permute-start.11 = (f32[8,512]{1,0:T(8,128)S(1)}, f32[8,512]{1,0:T(8,128)S(1)}, u32[]{:S(2)}, u32[]{:S(2)}) collective-permute-start(f32[8,512]{1,0:T(8,128)S(1)} %get-tuple-element.71.s0), channel_id=1, source_target_pairs={{0,1},{1,0},{2,3},{3,2},{4,5},{5,4},{6,7},{7,6},{8,9},{9,8},{10,11... | collective-permute-start | bytes 49160 | tf_op jit(solution)/shard_map/ppermute | solution.py:525
  77.4 1.3 copy-start.8
  78.7 11.2 %collective-permute-start.14 = (bf16[1056,128]{1,0:T(8,128)(2,1)S(1)}, bf16[1056,128]{1,0:T(8,128)(2,1)S(1)}, u32[]{:S(2)}, u32[]{:S(2)}) collective-permute-start(bf16[1056,128]{1,0:T(8,128)(2,1)S(1)} %get-tuple-element.95), channel_id=1, source_target_pairs={{0,4},{4,0},{8,12},{12,8},{16,20},{20,16},{24,28},{28,24},{32,36},... | collective-permute-start | bytes 811016 | tf_op jit(solution)/shard_map/ppermute | solution.py:525
  80.2 1.6 %copy-start.5 = (bf16[512,2048]{1,0:T(8,128)(2,1)S(1)}, bf16[512,2048]{1,0:T(8,128)(2,1)}, u32[]{:S(2)}) copy-start(bf16[512,2048]{1,0:T(8,128)(2,1)} %q_ref.19) | copy-start | bytes 6291460
  81.8 1.6 %copy-start.9 = (bf16[512,2048]{1,0:T(8,128)(2,1)S(1)}, bf16[512,2048]{1,0:T(8,128)(2,1)}, u32[]{:S(2)}) copy-start(bf16[512,2048]{1,0:T(8,128)(2,1)} %copy-done.8) | copy-start | bytes 6291460
  83.4 11.1 %copy-start.6 = (bf16[512,2048]{1,0:T(8,128)(2,1)S(1)}, bf16[512,2048]{1,0:T(8,128)(2,1)}, u32[]{:S(2)}) copy-start(bf16[512,2048]{1,0:T(8,128)(2,1)} %q_ref.19) | copy-start | bytes 6291460
  88.6 1.3 copy-start.10
  90.5 11.2 %collective-permute-start.15 = (bf16[288,128]{1,0:T(8,128)(2,1)S(1)}, bf16[288,128]{1,0:T(8,128)(2,1)S(1)}, u32[]{:S(2)}, u32[]{:S(2)}) collective-permute-start(bf16[288,128]{1,0:T(8,128)(2,1)S(1)} %get-tuple-element.97), channel_id=1, source_target_pairs={{0,8},{4,12},{8,0},{12,4},{16,24},{20,28},{24,16},{28,20},{32,40},... | collective-permute-start | bytes 221192 | tf_op jit(solution)/shard_map/ppermute | solution.py:525
  90.6 11.2 %collective-permute-start.16 = (bf16[288,128]{1,0:T(8,128)(2,1)S(1)}, bf16[288,128]{1,0:T(8,128)(2,1)S(1)}, u32[]{:S(2)}, u32[]{:S(2)}) collective-permute-start(bf16[288,128]{1,0:T(8,128)(2,1)S(1)} %get-tuple-element.98), channel_id=1, source_target_pairs={{0,16},{4,20},{8,24},{12,28},{16,0},{20,4},{24,8},{28,12},{32,48},... | collective-permute-start | bytes 221192 | tf_op jit(solution)/shard_map/ppermute | solution.py:525
  93.4 8.4 %collective-permute-start.17 = (bf16[288,128]{1,0:T(8,128)(2,1)S(1)}, bf16[288,128]{1,0:T(8,128)(2,1)S(1)}, u32[]{:S(2)}, u32[]{:S(2)}) collective-permute-start(bf16[288,128]{1,0:T(8,128)(2,1)S(1)} %get-tuple-element.99), channel_id=1, source_target_pairs={{0,24},{4,28},{8,16},{12,20},{16,8},{20,12},{24,0},{28,4},{32,56},... | collective-permute-start | bytes 221192 | tf_op jit(solution)/shard_map/ppermute | solution.py:525
  102.4 10.6 %collective-permute-start.20 = (bf16[288,128]{1,0:T(8,128)(2,1)S(1)}, bf16[288,128]{1,0:T(8,128)(2,1)S(1)}, u32[]{:S(2)}, u32[]{:S(2)}) collective-permute-start(bf16[288,128]{1,0:T(8,128)(2,1)S(1)} %row_sum.3.t0), channel_id=1, source_target_pairs={{0,96},{4,100},{8,104},{12,108},{16,112},{20,116},{24,120},{28,124... | collective-permute-start | bytes 221192 | tf_op jit(solution)/shard_map/ppermute | solution.py:525
  103.5 9.5 %collective-permute-start.19 = (bf16[288,128]{1,0:T(8,128)(2,1)S(1)}, bf16[288,128]{1,0:T(8,128)(2,1)S(1)}, u32[]{:S(2)}, u32[]{:S(2)}) collective-permute-start(bf16[288,128]{1,0:T(8,128)(2,1)S(1)} %row_sum.3.t0), channel_id=1, source_target_pairs={{0,64},{4,68},{8,72},{12,76},{16,80},{20,84},{24,88},{28,92},{32,9... | collective-permute-start | bytes 221192 | tf_op jit(solution)/shard_map/ppermute | solution.py:525
  104.2 8.8 %collective-permute-start.18 = (bf16[288,128]{1,0:T(8,128)(2,1)S(1)}, bf16[288,128]{1,0:T(8,128)(2,1)S(1)}, u32[]{:S(2)}, u32[]{:S(2)}) collective-permute-start(bf16[288,128]{1,0:T(8,128)(2,1)S(1)} %row_sum.3.t0), channel_id=1, source_target_pairs={{0,32},{4,36},{8,40},{12,44},{16,48},{20,52},{24,56},{28,60},{32,0... | collective-permute-start | bytes 221192 | tf_op jit(solution)/shard_map/ppermute | solution.py:525
  114.0 11.2 %collective-permute-start.21 = (bf16[256,128]{1,0:T(8,128)(2,1)S(1)}, bf16[256,128]{1,0:T(8,128)(2,1)S(1)}, u32[]{:S(2)}, u32[]{:S(2)}) collective-permute-start(bf16[256,128]{1,0:T(8,128)(2,1)S(1)} %get-tuple-element.101), channel_id=1, source_target_pairs={{0,8},{4,12},{8,0},{12,4},{16,24},{20,28},{24,16},{28,20},{32,40},... | collective-permute-start | bytes 196616 | tf_op jit(solution)/shard_map/ppermute | solution.py:525
  114.0 11.2 %collective-permute-start.22 = (bf16[256,128]{1,0:T(8,128)(2,1)S(1)}, bf16[256,128]{1,0:T(8,128)(2,1)S(1)}, u32[]{:S(2)}, u32[]{:S(2)}) collective-permute-start(bf16[256,128]{1,0:T(8,128)(2,1)S(1)} %get-tuple-element.102), channel_id=1, source_target_pairs={{0,16},{4,20},{8,24},{12,28},{16,0},{20,4},{24,8},{28,12},{32,48},... | collective-permute-start | bytes 196616 | tf_op jit(solution)/shard_map/ppermute | solution.py:525
  116.8 8.4 %collective-permute-start.23 = (bf16[256,128]{1,0:T(8,128)(2,1)S(1)}, bf16[256,128]{1,0:T(8,128)(2,1)S(1)}, u32[]{:S(2)}, u32[]{:S(2)}) collective-permute-start(bf16[256,128]{1,0:T(8,128)(2,1)S(1)} %get-tuple-element.103), channel_id=1, source_target_pairs={{0,24},{4,28},{8,16},{12,20},{16,8},{20,12},{24,0},{28,4},{32,56},... | collective-permute-start | bytes 196616 | tf_op jit(solution)/shard_map/ppermute | solution.py:525
  126.0 15.4 %collective-permute-start.24 = (bf16[1040,128]{1,0:T(8,128)(2,1)S(1)}, bf16[1040,128]{1,0:T(8,128)(2,1)S(1)}, u32[]{:S(2)}, u32[]{:S(2)}) collective-permute-start(bf16[1040,128]{1,0:T(8,128)(2,1)S(1)} %get-tuple-element.105), channel_id=1, source_target_pairs={{0,4},{4,0},{8,12},{12,8},{16,20},{20,16},{24,28},{28,24},{32,36},... | collective-permute-start | bytes 798728 | tf_op jit(solution)/shard_map/ppermute | solution.py:525
  128.8 7.3 %copy-start.3 = (bf16[512,2048]{1,0:T(8,128)(2,1)S(1)}, bf16[512,2048]{1,0:T(8,128)(2,1)}, u32[]{:S(2)}) copy-start(bf16[512,2048]{1,0:T(8,128)(2,1)} %v_ref.19) | copy-start | bytes 6291460

commit v2 on v0

v2 whole, which is shorter than its diff:
```python
import functools

import jax
import jax.numpy as jnp
from jax import lax
from jax.experimental import pallas as pl
from jax.experimental.pallas import tpu as pltpu
from jax.sharding import PartitionSpec as P

HD = 128
ATT = 8192
EPSILON = 1e-06
TOK = 512
BLOCK = 256
HEADS = 8
WIDE = HEADS * HD
GROUP = 4
GROUPS = HEADS // GROUP
SPAN = GROUP * HD
STATE_ROWS = HEADS * HD
QUARTER = 2 * HD
TILE = 16
F32 = jnp.float32
BF16 = jnp.bfloat16
VMEM_LIMIT = 16 * 1024 * 1024
VM = pl.BlockSpec(memory_space=pltpu.VMEM)
SM = pl.BlockSpec(memory_space=pltpu.SMEM)
ANY = pl.BlockSpec(memory_space=pl.ANY)


def dot(a, b, da, db):
    return lax.dot_general(a, b, (((da,), (db,)), ((), ())), preferred_element_type=F32)


def vmem(shape, dtype):
    return pltpu.VMEM(shape, dtype)


def half_shape(dtype):
    return vmem((TOK, WIDE), dtype)


def far(dtype=BF16):
    return jax.ShapeDtypeStruct((TOK, 2 * WIDE), dtype)


def call(kernel, name, flops, near, outs, distant=(), scratch=(), aliases=None):
    near = [pltpu.with_memory_space_constraint(a, pltpu.VMEM) for a in near]
    distant = [pltpu.with_memory_space_constraint(a, pltpu.HBM) for a in distant]
    out_specs = [ANY if isinstance(o, jax.ShapeDtypeStruct) else VM for o in outs]

    def placed(*refs):
        where = lax.axis_index("ctx")
        kernel((where & 1, (where >> 1) & 3, where >> 3), *refs)

    return pl.pallas_call(
        placed,
        in_specs=[VM] * len(near) + [ANY] * len(distant),
        out_specs=out_specs,
        out_shape=list(outs),
        scratch_shapes=list(scratch),
        input_output_aliases=aliases or {},
        compiler_params=pltpu.CompilerParams(vmem_limit_bytes=VMEM_LIMIT),
        cost_estimate=pl.CostEstimate(
            flops=int(flops), bytes_accessed=int(flops / 300), transcendentals=0
        ),
        name=name,
    )(*near, *distant)


def base_column(ids, flip):
    return pl.multiple_of((ids[0] ^ flip) * WIDE, WIDE)


def each_group(body):
    def step(g, carry):
        body(g)
        return carry

    lax.fori_loop(0, GROUPS, step, 0)


def head_columns(g, j):
    return pl.ds(pl.multiple_of(g * SPAN + j * HD, HD), HD)


def head_rows(g, j, rows=HD):
    return pl.ds(pl.multiple_of((g * GROUP + j) * rows, rows), rows)


def group_columns(g):
    return pl.ds(pl.multiple_of(g * SPAN, SPAN), SPAN)


def far_columns(base, g):
    return pl.ds(pl.multiple_of(base + g * SPAN, SPAN), SPAN)


def load(source, base, g, target, sem):
    return pltpu.make_async_copy(
        source.at[:, far_columns(base, g)], target.at[:, group_columns(g)], sem
    )


def store(source, base, g, target, sem):
    return pltpu.make_async_copy(
        source.at[:, group_columns(g)], target.at[:, far_columns(base, g)], sem
    )


def load_all(base, pairs, sems):
    for g in range(GROUPS):
        for n, (source, target) in enumerate(pairs):
            load(source, base, g, target, sems.at[n, g]).start()


def ends(seg_ref):
    seg = seg_ref[...].astype(F32)
    return seg, seg[:, 0:1], seg[:, TOK - 1 : TOK]


def count(flags):
    return jnp.sum(flags.astype(F32), axis=1, keepdims=True)


def info_tile(low, high):
    row = lax.broadcasted_iota(jnp.int32, (TILE, HD), 0)
    return jnp.where(
        row < 8, jnp.broadcast_to(low, (TILE, HD)), jnp.broadcast_to(high, (TILE, HD))
    ).astype(BF16)


def split_tile(x):
    high = x.astype(BF16).astype(F32)
    return jnp.concatenate([high, x - high], axis=0).astype(BF16)


def joined_tile(tile):
    t = tile.astype(F32)
    return t[0:8] + t[8:16]


def state_kernel(flip, ids, *refs):
    if flip:
        k_far, v_far, seg_far, k, v, out, seg, head, tail, sems, seg_sem, mask = refs
    else:
        seg, tail, k_far, v_far, k, v, out, sems, mask = refs
    base = base_column(ids, flip)
    load_all(base, ((k_far, k), (v_far, v)), sems)
    if flip:
        copy = pltpu.make_async_copy(seg_far, seg, seg_sem)
        copy.start()
        copy.wait()
        row, first, last = ends(seg)
        token = lax.broadcasted_iota(jnp.int32, (TOK, HD), 0).astype(F32)
        head[...] = jnp.where(token < count(row == first), 1.0, 0.0)
        tail[...] = jnp.where(token >= TOK - count(row == last), 1.0, 0.0)
    _, first, last = ends(seg)
    mask[...] = tail[...].astype(BF16)
    out[STATE_ROWS : STATE_ROWS + TILE, :] = info_tile(first, last)

    def body(g):
        load(k_far, base, g, k, sems.at[0, g]).wait()
        load(v_far, base, g, v, sems.at[1, g]).wait()
        for j in range(GROUP):
            c = head_columns(g, j)
            out[head_rows(g, j), :] = dot(k[:, c] * mask[...], v[:, c], 0, 0).astype(BF16)

    each_group(body)


def local_state(k, v, seg, seg_vmem=None, tail=None):
    flip = seg_vmem is None
    outs = [half_shape(BF16), half_shape(BF16), vmem((STATE_ROWS + TILE, HD), BF16)]
    scratch = [pltpu.SemaphoreType.DMA((2, GROUPS))]
    near, distant = [seg_vmem, tail], [k, v]
    if flip:
        outs += [vmem((1, TOK), jnp.int32), vmem((TOK, HD), F32), vmem((TOK, HD), F32)]
        scratch += [pltpu.SemaphoreType.DMA]
        near, distant = [], [k, v, seg]
    return call(
        functools.partial(state_kernel, int(flip)), "local_state", 1e9, near, outs, distant,
        scratch + [pltpu.VMEM((TOK, HD), BF16)],
    )


def fill_masks(seg_ref, m0, m1):
    seg, _, _ = ends(seg_ref)
    col = jnp.transpose(jnp.broadcast_to(seg, (8, TOK)))[:, 0:1]
    for start, ref in ((0, m0), (BLOCK, m1)):
        width = ref.shape[1]
        same = col[start : start + BLOCK] == seg[:, 0:width]
        t = lax.broadcasted_iota(jnp.int32, (BLOCK, width), 0) + start
        s = lax.broadcasted_iota(jnp.int32, (BLOCK, width), 1)
        ref[...] = jnp.where(same & (s <= t), 1.0, 0.0).astype(BF16)


def masked_pair(left, right, m0, m1):
    w0 = dot(left[0:BLOCK], right[0:BLOCK], 1, 1).astype(BF16) * m0[...]
    w1 = dot(left[BLOCK:TOK], right, 1, 1).astype(BF16) * m1[...]
    return w0, w1


def intra_kernel(flip, ids, *refs):
    if flip:
        k, v, m0, m1, _, q_far, q, attn, w0, w1, token, sems = refs
    else:
        k, v, seg, _, q_far, q, attn, w0, w1, token, m0, m1, sems = refs
    base = base_column(ids, flip)
    load_all(base, ((q_far, q),), sems)
    if not flip:
        fill_masks(seg, m0, m1)
    token[...] = jnp.zeros_like(token)

    def body(g):
        load(q_far, base, g, q, sems.at[0, g]).wait()
        for j in range(GROUP):
            c = head_columns(g, j)
            value = v[:, c]
            a0, a1 = masked_pair(q[:, c], k[:, c], m0, m1)
            w0[head_rows(g, j, BLOCK), :] = a0
            w1[head_rows(g, j, BLOCK), :] = a1
            attn[0:BLOCK, c] = dot(a0, value[0:BLOCK], 1, 0)
            attn[BLOCK:TOK, c] = dot(a1, value, 1, 0)

    each_group(body)


TOKEN = vmem((8, HD), F32)


def intra(k, v, q, after, seg=None, masks=None):
    outs = [
        half_shape(BF16),
        half_shape(F32),
        vmem((HEADS * BLOCK, BLOCK), BF16),
        vmem((HEADS * BLOCK, TOK), BF16),
        TOKEN,
    ]
    if masks is None:
        near = [k, v, seg, after]
        outs += [vmem((BLOCK, BLOCK), BF16), vmem((BLOCK, TOK), BF16)]
    else:
        near = [k, v, *masks, after]
    return call(
        functools.partial(intra_kernel, int(masks is not None)), "intra", 3e9, near, outs, [q],
        [pltpu.SemaphoreType.DMA((1, GROUPS))],
    )


def sigmoid_parts(gi):
    bend = 0.5 * jnp.tanh(0.5 * gi.astype(F32))
    return 0.5 + bend, 0.5 - bend


def prepare_kernel(flip, ids, q, head, _, go_far, gi_far, w, gi, qt, token, go, sems, mask):
    base = base_column(ids, flip)
    load_all(base, ((go_far, go), (gi_far, gi)), sems)
    mask[...] = head[...].astype(BF16)
    token[...] = jnp.zeros_like(token)

    def body(g):
        for j in range(GROUP):
            qt[head_rows(g, j), :] = jnp.transpose(q[:, head_columns(g, j)] * mask[...])
        load(go_far, base, g, go, sems.at[0, g]).wait()
        load(gi_far, base, g, gi, sems.at[1, g]).wait()
        for j in range(GROUP):
            c = head_columns(g, j)
            w[:, c] = go[:, c].astype(F32) * sigmoid_parts(gi[:, c])[0]

    each_group(body)


def prepare(flip, q, head, after, go, gi):
    return call(
        functools.partial(prepare_kernel, flip), "prepare", 1.5e9, [q, head, after],
        [half_shape(F32), half_shape(BF16), vmem((STATE_ROWS, TOK), BF16), TOKEN], [go, gi],
        [
            pltpu.VMEM((TOK, WIDE), BF16),
            pltpu.SemaphoreType.DMA((2, GROUPS)),
            pltpu.VMEM((TOK, HD), BF16),
        ],
    )


def cross_kernel(flip, ids, attn_in, q, s, w, head, gain, *rest):
    previous = rest[0] if flip else None
    attn, sums, squares, inners = rest[-4:]
    base = base_column(ids, flip)
    squares[...] = jnp.zeros_like(squares)
    inners[...] = jnp.zeros_like(inners)

    def body(g):
        for j in range(GROUP):
            c = head_columns(g, j)
            a = attn_in[:, c] + dot(q[:, c], s[head_rows(g, j), :], 1, 0) * head[...]
            attn[:, c] = a
            squares[...] += a * a
            scale = gain[:, pl.ds(pl.multiple_of(base + g * SPAN + j * HD, HD), HD)]
            inners[...] += w[:, c] * a * scale

    each_group(body)
    ones = jnp.ones((8, HD), F32)
    dims = (((1,), (1,)), ((), ()))
    ss, dd = [
        lax.dot_general(
            ones, x[...], dims, precision=lax.Precision.HIGHEST, preferred_element_type=F32
        )
        for x in (squares, inners)
    ]
    total = jnp.where(lax.broadcasted_iota(jnp.int32, (8, TOK), 0) < 4, ss, dd)
    if flip:
        total = total + previous[...]
    sums[...] = total


def cross(flip, attn, q, state, w, head, gain, previous=()):
    return call(
        functools.partial(cross_kernel, flip), "cross", 1.2e9,
        [attn, q, state, w, head, gain, *previous], [half_shape(F32), vmem((8, TOK), F32)], (),
        [pltpu.VMEM((TOK, HD), F32), pltpu.VMEM((TOK, HD), F32)],
    )


def scales(sums, rinv_ref, back_ref):
    own, one, two, three = [r[...] for r in sums]
    total = (own + one) + (two + three)
    rinv = lax.rsqrt(total[0:1] * (1.0 / ATT) + EPSILON)
    back = rinv * rinv * rinv * total[4:5] * (1.0 / ATT)
    row = lax.broadcasted_iota(jnp.int32, (8, TOK), 0)
    both = jnp.where(
        row < 4, jnp.broadcast_to(rinv, (8, TOK)), jnp.broadcast_to(back, (8, TOK))
    )
    cols = jnp.transpose(both)
    rinv_ref[...] = jnp.broadcast_to(cols[:, 0:1], (TOK, HD))
    back_ref[...] = jnp.broadcast_to(cols[:, 4:5], (TOK, HD))


def grad_kernel(flip, ids, seg, attn, w, qt, gain, *rest):
    if flip:
        s0, s1, s2, s3, grad, out, rinv, back, gains = rest
        scales((s0, s1, s2, s3), rinv, back)
    else:
        rinv, back, grad, out, gains = rest
    base = base_column(ids, flip)
    _, first, last = ends(seg)
    out[STATE_ROWS : STATE_ROWS + TILE, :] = info_tile(8.0 - last, 8.0 - first)

    def body(g):
        for j in range(GROUP):
            c = head_columns(g, j)
            a = attn[:, c]
            gated = w[:, c] * rinv[...]
            gains[pl.ds(g * GROUP + j, 1), :] = jnp.sum(gated * a, axis=0, keepdims=True)
            scale = gain[:, pl.ds(pl.multiple_of(base + g * SPAN + j * HD, HD), HD)]
            x = (gated * scale - a * back[...]).astype(BF16)
            grad[:, c] = x
            out[head_rows(g, j), :] = dot(qt[head_rows(g, j), :], x, 1, 0).astype(BF16)

    each_group(body)
    out[STATE_ROWS + TILE : STATE_ROWS + 2 * TILE, :] = split_tile(gains[...])


def grad_attn(flip, seg, attn, w, qt, gain, extra):
    outs = [half_shape(BF16), vmem((STATE_ROWS + 2 * TILE, HD), BF16)]
    if flip:
        outs += [vmem((TOK, HD), F32), vmem((TOK, HD), F32)]
    return call(
        functools.partial(grad_kernel, flip), "grad_attn", 1.2e9,
        [seg, attn, w, qt, gain, *extra], outs, (), [pltpu.VMEM((8, HD), F32)],
    )


def local_grads_kernel(flip, ids, q, k, v, grad, s, w0, w1, m0, m1, head, _, *rest):
    dq_far, dk, dv, token, dq, sems = rest[-6:]
    base = base_column(ids, flip)
    token[...] = jnp.zeros_like(token)

    def body(g):
        for j in range(GROUP):
            c = head_columns(g, j)
            qh, kh, vh, gh = q[:, c], k[:, c], v[:, c], grad[:, c]
            d0, d1 = masked_pair(gh, vh, m0, m1)
            hop = dot(gh, s[head_rows(g, j), :], 1, 1) * head[...]
            dq[0:BLOCK, c] = (dot(d0, kh[0:BLOCK], 1, 0) + hop[0:BLOCK]).astype(BF16)
            dq[BLOCK:TOK, c] = (dot(d1, kh, 1, 0) + hop[BLOCK:TOK]).astype(BF16)
            a0, a1 = w0[head_rows(g, j, BLOCK), :], w1[head_rows(g, j, BLOCK), :]
            for ref, b0, b1, rows in ((dk, d0, d1, qh), (dv, a0, a1, gh)):
                late = dot(b1, rows[BLOCK:TOK], 0, 0)
                ref[0:BLOCK, c] = late[0:BLOCK] + dot(b0, rows[0:BLOCK], 0, 0)
                ref[BLOCK:TOK, c] = late[BLOCK:TOK]
        store(dq, base, g, dq_far, sems.at[g]).start()

    each_group(body)
    for g in range(GROUPS):
        store(dq, base, g, dq_far, sems.at[g]).wait()


def local_grads(flip, q, k, v, g, state, w0, w1, masks, head, after, before=()):
    return call(
        functools.partial(local_grads_kernel, flip), "local_grads", 5e9,
        [q, k, v, g, state, w0, w1, *masks, head, after],
        [far(), half_shape(F32), half_shape(F32), TOKEN], before,
        [pltpu.VMEM((TOK, WIDE), BF16), pltpu.SemaphoreType.DMA((GROUPS,))],
        {11: 0} if before else None,
    )


def gates_kernel(flip, ids, attn, gi, w, rinv, gain, _, *rest):
    lo_far, gg_far, token, lo, gg, sems = rest[-6:]
    base = base_column(ids, flip)
    token[...] = jnp.zeros_like(token)

    def body(g):
        for j in range(GROUP):
            c = head_columns(g, j)
            sig, other = sigmoid_parts(gi[:, c])
            scale = gain[:, pl.ds(pl.multiple_of(base + g * SPAN + j * HD, HD), HD)]
            scaled = attn[:, c] * rinv[...] * scale
            lo[:, c] = (scaled * sig).astype(BF16)
            gg[:, c] = (scaled * w[:, c] * other).astype(BF16)
        store(lo, base, g, lo_far, sems.at[0, g]).start()
        store(gg, base, g, gg_far, sems.at[1, g]).start()

    each_group(body)
    for g in range(GROUPS):
        store(lo, base, g, lo_far, sems.at[0, g]).wait()
        store(gg, base, g, gg_far, sems.at[1, g]).wait()


def gates(flip, attn, gi, w, rinv, gain, after, before=()):
    return call(
        functools.partial(gates_kernel, flip), "gates", 1.2e9, [attn, gi, w, rinv, gain, after],
        [far(), far(), TOKEN], before,
        [
            pltpu.VMEM((TOK, WIDE), BF16),
            pltpu.VMEM((TOK, WIDE), BF16),
            pltpu.SemaphoreType.DMA((2, GROUPS)),
        ],
        {6: 0, 7: 1} if before else None,
    )


def finish_kernel(flip, ids, dk_in, dv_in, k, v, later, tail, *rest):
    if flip:
        total, _, _, dk_far, dv_far, gain_far, dk, dv, sems, gain, gain_sem = rest
        core = ids[0]
        at = [pl.ds(pl.multiple_of(n * 8, 8), 8) for n in (core, 1 - core)]
        gain[at[0], :] = joined_tile(total[...])
        gain[at[1], :] = joined_tile(later[STATE_ROWS : STATE_ROWS + TILE, :])
        gain_copy = pltpu.make_async_copy(gain, gain_far, gain_sem)
        gain_copy.start()
    else:
        dk_far, dv_far, dk, dv, sems = rest
    base = base_column(ids, flip)

    def body(g):
        for j in range(GROUP):
            c = head_columns(g, j)
            m = later[head_rows(g, j), :]
            dk[:, c] = (dk_in[:, c] + dot(v[:, c], m, 1, 1) * tail[...]).astype(BF16)
            dv[:, c] = (dv_in[:, c] + dot(k[:, c], m, 1, 0) * tail[...]).astype(BF16)
        store(dk, base, g, dk_far, sems.at[0, g]).start()
        store(dv, base, g, dv_far, sems.at[1, g]).start()

    each_group(body)
    for g in range(GROUPS):
        store(dk, base, g, dk_far, sems.at[0, g]).wait()
        store(dv, base, g, dv_far, sems.at[1, g]).wait()
    if flip:
        gain_copy.wait()


def finish(flip, dk, dv, k, v, later, tail, total=(), before=()):
    near = [dk, dv, k, v, later, tail, *total]
    outs = [far(), far()]
    scratch = [
        pltpu.VMEM((TOK, WIDE), BF16),
        pltpu.VMEM((TOK, WIDE), BF16),
        pltpu.SemaphoreType.DMA((2, GROUPS)),
    ]
    if flip:
        outs += [jax.ShapeDtypeStruct((TILE, HD), F32)]
        scratch += [pltpu.VMEM((TILE, HD), F32), pltpu.SemaphoreType.DMA]
    return call(
        functools.partial(finish_kernel, flip), "finish", 1.2e9, near, outs, before, scratch,
        {len(near): 0, len(near) + 1: 1} if flip else None,
    )


def place(ids, reverse):
    core, x, z = ids[0], ids[1], ids[2]
    return (1 - core, 3 - x, 3 - z) if reverse else (core, x, z)


def info_rows(ref, at):
    tile = ref[at : at + TILE, :].astype(F32)
    return tile[0:1], tile[8:9]


def flag(cond):
    return jnp.where(cond, 1.0, 0.0)


def sorted_cores(first_core, own, other):
    return jnp.where(first_core, own, other), jnp.where(first_core, other, own)


def quarter_rows(ids, m):
    return pl.ds(pl.multiple_of((ids[1] ^ m) * QUARTER, QUARTER), QUARTER)


def chip_kernel(reverse, gain, ids, own_ref, other_ref, *outs):
    vcore, _, _ = place(ids, reverse)
    first_core = vcore == 0
    low_own, high_own = info_rows(own_ref, STATE_ROWS)
    low_other, high_other = info_rows(other_ref, STATE_ROWS)
    low_a, _ = sorted_cores(first_core, low_own, low_other)
    high_a, high_b = sorted_cores(first_core, high_own, high_other)
    join = flag(high_a == high_b)
    own_weight = jnp.where(first_core, join, 1.0)
    other_weight = jnp.where(first_core, 1.0, join)
    for m, out in enumerate(outs):
        rows = quarter_rows(ids, m)
        total = own_ref[rows, :].astype(F32) * own_weight
        total = total + other_ref[rows, :].astype(F32) * other_weight
        out[0:QUARTER, :] = total.astype(BF16)
        out[QUARTER : QUARTER + TILE, :] = info_tile(low_a, high_b)
        if gain:
            at = slice(STATE_ROWS + TILE, STATE_ROWS + 2 * TILE)
            both = joined_tile(own_ref[at, :]) + joined_tile(other_ref[at, :])
            out[QUARTER + TILE : QUARTER + 2 * TILE, :] = split_tile(both)


def row_kernel(gain, ids, p0, p1, p2, p3, _, out):
    parts = (p0, p1, p2, p3)
    info = [info_rows(p, QUARTER) for p in parts]
    low = jnp.minimum(jnp.minimum(info[0][0], info[1][0]), jnp.minimum(info[2][0], info[3][0]))
    high = jnp.maximum(jnp.maximum(info[0][1], info[1][1]), jnp.maximum(info[2][1], info[3][1]))
    total = None
    for p, (_, own_high) in zip(parts, info):
        term = p[0:QUARTER, :].astype(F32) * flag(own_high == high)
        total = term if total is None else total + term
    out[0:QUARTER, :] = total.astype(BF16)
    out[QUARTER : QUARTER + TILE, :] = info_tile(low, high)
    if gain:
        g = [joined_tile(p[QUARTER + TILE : QUARTER + 2 * TILE, :]) for p in parts]
        out[QUARTER + TILE : QUARTER + 2 * TILE, :] = split_tile((g[0] + g[1]) + (g[2] + g[3]))


def entry_kernel(reverse, gain, ids, p0, p1, p2, p3, t0, t1, t2, t3, _, *outs):
    _, vx, vz = place(ids, reverse)
    parts = (p0, p1, p2, p3)
    rows = (t0, t1, t2, t3)
    info = [info_rows(p, QUARTER) for p in parts]
    row_high = [info_rows(t, QUARTER)[1] for t in rows]
    for m in range(4):
        low = info[m][0]
        total = jnp.zeros((QUARTER, HD), F32)
        for n in range(4):
            if n != m:
                weight = flag(info[n][1] == low) * flag((vx ^ n) < (vx ^ m))
                total = total + parts[n][0:QUARTER, :].astype(F32) * weight
        for n in range(1, 4):
            weight = flag(row_high[n] == low) * flag((vz ^ n) < vz)
            total = total + rows[n][0:QUARTER, :].astype(F32) * weight
        outs[m][...] = total.astype(BF16)
    if gain:
        g = [joined_tile(t[QUARTER + TILE : QUARTER + 2 * TILE, :]) for t in rows]
        outs[4][...] = split_tile((g[0] + g[1]) + (g[2] + g[3]))


def device_kernel(reverse, gain, ids, own_ref, other_ref, e0, e1, e2, e3, _, *rest):
    keep, send = rest[-2:]
    vcore, _, _ = place(ids, reverse)
    first_core = vcore == 0
    low_own, high_own = info_rows(own_ref, STATE_ROWS)
    low_other, high_other = info_rows(other_ref, STATE_ROWS)
    low_a, low_b = sorted_cores(first_core, low_own, low_other)
    high_a, _ = sorted_cores(first_core, high_own, high_other)
    from_a = flag(high_a == low_b)
    from_chip = flag(low_a == low_b)
    for m, ref in enumerate((e0, e1, e2, e3)):
        rows = quarter_rows(ids, m)
        entry = ref[...].astype(F32)
        a = jnp.where(first_core, own_ref[rows, :].astype(F32), other_ref[rows, :].astype(F32))
        second = a * from_a + entry * from_chip
        keep[rows, :] = jnp.where(first_core, entry, second).astype(BF16)
        send[rows, :] = jnp.where(first_core, second, entry).astype(BF16)
    if gain:
        send[STATE_ROWS : STATE_ROWS + TILE, :] = rest[0][...]


def glue(kernel, name, rows, *args):
    return call(kernel, name, 5e8, args, [vmem((r, HD), BF16) for r in rows])


def swap(x, axis, size, bits):
    return lax.ppermute(x, axis, [(i, i ^ bits) for i in range(size)])


def chip_swap(x):
    return swap(x, "ctx", 32, 1)


def row_swap(x, m):
    return swap(x, "ctx", 32, m << 1)


def plane_swap(x, m):
    return swap(x, "ctx", 32, m << 3)


def scan(own, other, reverse, gain, beside_x, beside_z, beside_back):
    extra = TILE if gain else 0
    rows = QUARTER + TILE + extra
    sent = glue(
        functools.partial(chip_kernel, reverse, gain), "chip_sum", [rows] * 4, own, other
    )
    parts = [sent[0]] + [row_swap(sent[m], m) for m in range(1, 4)]
    token = beside_x(sent[0])
    total = glue(functools.partial(row_kernel, gain), "row_sum", [rows], *parts, token)[0]
    totals = [total] + [plane_swap(total, m) for m in range(1, 4)]
    token = beside_z(total)
    entries = glue(
        functools.partial(entry_kernel, reverse, gain),
        "entry",
        [QUARTER] * 4 + ([TILE] if gain else []),
        *parts,
        *totals,
        token,
    )
    tail = entries[4:]
    back = [entries[0]] + [row_swap(entries[m], m) for m in range(1, 4)]
    token = beside_back(entries[0])
    keep, send = glue(
        functools.partial(device_kernel, reverse, gain),
        "device_entry",
        [STATE_ROWS, STATE_ROWS + extra],
        own,
        other,
        *back,
        token,
        *tail,
    )
    return keep, chip_swap(send), tail


def on_device(query, keys, values, gate_input, grad_output, norm_gain, segment_ids):
    gain = norm_gain.reshape(1, -1)

    k_send, v_send, sent, seg, head, tail = local_state(keys, values, segment_ids.reshape(1, TOK)
    )
    other = chip_swap(sent)
    k_keep, v_keep, own = local_state(keys, values, None, seg, tail)
    made = {}

    def intra_keep(after):
        made["keep"] = intra(k_keep, v_keep, query, after, seg=seg)
        return made["keep"][4]

    def intra_send(after):
        made["send"] = intra(k_send, v_send, query, after, masks=made["keep"][5:7])
        return made["send"][4]

    def prepare_both(after):
        made["pk"] = prepare(0, made["keep"][0], head, after, grad_output, gate_input)
        made["ps"] = prepare(1, made["send"][0], head, made["pk"][3], grad_output, gate_input
        )
        return made["ps"][3]

    state_keep, state_send, _ = scan(own, other, False, False, intra_keep, intra_send, prepare_both
    )
    q_keep, attn_keep, w0_keep, w1_keep, _, m0, m1 = made["keep"]
    q_send, attn_send, w0_send, w1_send, _ = made["send"]
    gated_keep, gi_keep, qt_keep, _ = made["pk"]
    gated_send, gi_send, qt_send, _ = made["ps"]

    attn_keep, sums = cross(0, attn_keep, q_keep, state_keep, gated_keep, head, gain
    )
    attn_send, sums = cross(1, attn_send, q_send, state_send, gated_send, head, gain, (sums,)
    )
    sums = [sums] + [swap(sums, "tp", 4, m) for m in range(1, 4)]

    g_send, sent, rinv, back = grad_attn(1, seg, attn_send, gated_send, qt_send, gain, sums
    )
    other = chip_swap(sent)
    g_keep, own = grad_attn(0, seg, attn_keep, gated_keep, qt_keep, gain, (rinv, back)
    )

    def grads_keep(after):
        made["gk"] = local_grads(0, q_keep, k_keep, v_keep, g_keep, state_keep, w0_keep, w1_keep, (m0, m1),
            head, after,
        )
        return made["gk"][3]

    def grads_send(after):
        made["gs"] = local_grads(1, q_send, k_send, v_send, g_send, state_send, w0_send, w1_send, (m0, m1),
            head, after, (made["gk"][0],),
        )
        return made["gs"][3]

    def gates_both(after):
        first = gates(0, attn_keep, gi_keep, gated_keep, rinv, gain, after)
        made["out"] = gates(1, attn_send, gi_send, gated_send, rinv, gain, first[2], tuple(first[:2])
        )
        return made["out"][2]

    later_keep, later_send, total = scan(own, other, True, True, grads_keep, grads_send, gates_both
    )
    _, dk_keep, dv_keep, _ = made["gk"]
    grad_query, dk_send, dv_send, _ = made["gs"]
    layer_out, grad_gate, _ = made["out"]
    done = finish(0, dk_keep, dv_keep, k_keep, v_keep, later_keep, tail)
    grad_keys, grad_values, grad_gain = finish(
        1, dk_send, dv_send, k_send, v_send, later_send, tail, (total[0],), tuple(done)
    )
    grad_gain = grad_gain.reshape(-1)
    return layer_out, grad_query, grad_keys, grad_values, grad_gate, grad_gain


def solution(mesh):
    in_specs = (P("ctx", "tp"),) * 5 + (P("tp"), P("ctx"))
    out_specs = (P("ctx", "tp"),) * 5 + (P("tp"),)
    return jax.shard_map(
        on_device, mesh=mesh, in_specs=in_specs, out_specs=out_specs, check_vma=False
    )
```

time: 709 us -> 85.4 us (0.12); the launches traced: 695 us -> 85.2 us
  blocking collectives: 298 us -> 0 us
  loops' own time: 100 us -> 0 us
  waiting for transfers between devices: 84.5 us -> 5.87 us
  local copies, waits for them, and re-layouts: 76.8 us -> 0.01 us
  other arithmetic: 65.7 us -> 0 us
  matrix products: 55.6 us -> 0 us
  Pallas kernels: 0 us -> 41.8 us
  starting transfers between devices: 0.08 us -> 36.4 us
  between operations: 14.2 us -> 1.09 us
    psum x3 -> x0, blocking collectives: 282 us -> none  [the longest x1 268 us: on_device(): grad_gain = lax.psum(jnp.sum(grad_y * normed * sig, axis=0), 'ctx')]
    another operation x2 -> x0, loops' own time: 100 us -> none  [the longest x1 96.4 us: entering(): return lax.fori_loop(0, ahead, entering_one, state)]
    all_gather x2 -> x0, waiting for transfers between devices: 84.5 us -> none  [the longest x1 84.5 us: carried_in(): gathered = jax.tree.map(lambda a: lax.all_gather(a, axis), part)]
    dot_general x12 -> x0, matrix products: 55.6 us -> none  [the longest x2 9.04 us: masked_product(): jnp.einsum('thd,shd->hts', left_rows, right_rows, preferred_element_type=...]
    select_n x31 -> x0, other arithmetic: 51.9 us -> none  [the longest x30 50.1 us: backward_join(): state_out = jnp.where(empty_b, state_a, jnp.where(empty_a, state_b, merged))]
    pallas_call x0 -> x24, Pallas kernels: none -> 41.8 us  [call(): pl.pallas_call(placed, in_specs=[VM] * len(near) + [ANY] * len(distant),...]
    dynamic_slice x62 -> x0, local copies, waits for them, and re-layouts: 36.6 us -> none  [the longest x60 35.4 us: entering_one(): lax.dynamic_index_in_dim(a, source, 0, False).astype(own.dtype)]
    ppermute x0 -> x25, starting transfers between devices: none -> 36.4 us  [swap(): return lax.ppermute(x, axis, [(i, i ^ bits) for i in range(size)])]
  transfers between devices with their start and end apart: 2 -> 25, of which waited for: 1 -> 5; matrix products, arithmetic and copies ran while one was open for 6% -> 0% of each run, Pallas kernels for 0% -> 38%
where the time goes in v2:
time: 85.4 us; the launch traced here: 85.2 us
  Pallas kernels  41.8 us (49%)
  starting transfers between devices  36.4 us (43%)
  waiting for transfers between devices  5.87 us (7%)
  between operations  1.09 us (1%)
    pallas_call x24, Pallas kernels, call(): pl.pallas_call(placed, in_specs=[VM] * len(near) + [ANY] * len(distant),...  41.8 us
    ppermute x25, starting transfers between devices, swap(): return lax.ppermute(x, axis, [(i, i ^ bits) for i in range(size)])  36.4 us
    ppermute x25, waiting for transfers between devices, swap(): return lax.ppermute(x, axis, [(i, i ^ bits) for i in range(size)])  5.87 us
  transfers between devices with their start and end apart: 25, of which 5 were waited for; matrix products, arithmetic and copies ran while one was open for 0% of the time, Pallas kernels for 38%

profile of v2, /device:TPU:1, one launch (start us, length us, event | category | flops | bytes accessed | tf_op | source)
XLA Modules:
  0.0 85.2 jit_solution(17867040498551265752)
XLA Ops:
  0.6 2.3 %local_state.2 = (bf16[512,1024]{1,0:T(8,128)(2,1)S(1)}, bf16[512,1024]{1,0:T(8,128)(2,1)S(1)}, bf16[1040,128]{1,0:T(8,128)(2,1)S(1)}, s32[1,512]{1,0:T(1,128)S(...) custom-call(bf16[512,2048]{1,0:T(8,128)(2,1)} %refs_2_.1, bf16[512,2048]{1,0:T(8,128)(2,1)} %refs_3_.3, s32[1,512]{1,0:T(1,128)} %bitcast.9), custom_call_target="tpu_custom_call" | custom-call | flops 1000000000 | bytes 3333333 | tf_op jit(solution)/shard_map/local_state/pallas_call | solution.py:56
  2.9 1.5 %collective-permute-start = (bf16[1040,128]{1,0:T(8,128)(2,1)S(1)}, bf16[1040,128]{1,0:T(8,128)(2,1)S(1)}, u32[]{:S(2)}, u32[]{:S(2)}) collective-permute-start(bf16[1040,128]{1,0:T(8,128)(2,1)S(1)} %get-tuple-element.92), channel_id=1, source_target_pairs={{0,4},{4,0},{8,12},{12,8},{16,20},{20,16},{24,28},{28,24},{32,36},... | collective-permute-start | bytes 798728 | tf_op jit(solution)/shard_map/ppermute | solution.py:599
  4.4 2.3 %local_state.3 = (bf16[512,1024]{1,0:T(8,128)(2,1)S(1)}, bf16[512,1024]{1,0:T(8,128)(2,1)S(1)}, bf16[1040,128]{1,0:T(8,128)(2,1)S(1)}) custom-call(s32[1,512]{1,0:T(1,128)S(1)} %get-tuple-element.87.refs_0_.refs_2_, f32[512,128]{1,0:T(8,128)S(1)} %get-tuple-element.88.refs_1_.refs_5_, bf16[512,2048]{1,0:T(8,128)(2,1)} %refs_2_.1, bf16[512,2048]{1,0:T(8,128)(2,1)} %refs_3_.3), custom_call_target="tpu_custom_call" | custom-call | flops 1000000000 | bytes 3333333 | tf_op jit(solution)/shard_map/local_state/pallas_call | solution.py:56
  6.7 0.1 chip_sum.2
  6.8 1.4 %collective-permute-start.1 = (bf16[272,128]{1,0:T(8,128)(2,1)S(1)}, bf16[272,128]{1,0:T(8,128)(2,1)S(1)}, u32[]{:S(2)}, u32[]{:S(2)}) collective-permute-start(bf16[272,128]{1,0:T(8,128)(2,1)S(1)} %get-tuple-element.96), channel_id=1, source_target_pairs={{0,8},{4,12},{8,0},{12,4},{16,24},{20,28},{24,16},{28,20},{32,40},... | collective-permute-start | bytes 208904 | tf_op jit(solution)/shard_map/ppermute | solution.py:599
  8.2 2.5 %collective-permute-start.2 = (bf16[272,128]{1,0:T(8,128)(2,1)S(1)}, bf16[272,128]{1,0:T(8,128)(2,1)S(1)}, u32[]{:S(2)}, u32[]{:S(2)}) collective-permute-start(bf16[272,128]{1,0:T(8,128)(2,1)S(1)} %get-tuple-element.97), channel_id=1, source_target_pairs={{0,16},{4,20},{8,24},{12,28},{16,0},{20,4},{24,8},{28,12},{32,48},... | collective-permute-start | bytes 208904 | tf_op jit(solution)/shard_map/ppermute | solution.py:599
  10.6 0.1 collective-permute-start.3
  10.8 3.2 %intra.2 = (bf16[512,1024]{1,0:T(8,128)(2,1)S(1)}, f32[512,1024]{1,0:T(8,128)S(1)}, bf16[2048,256]{1,0:T(8,128)(2,1)S(1)}, bf16[2048,512]{1,0:T(8,128)(2,1)S(1)}...) custom-call(bf16[512,1024]{1,0:T(8,128)(2,1)S(1)} %get-tuple-element.89.refs_0_.refs_1_.refs_2_, ...), custom_call_target="tpu_custom_call" | custom-call | flops 3000000000 | bytes 10000000 | tf_op jit(solution)/shard_map/intra/pallas_call | solution.py:56
  14.0 0.0 collective-permute-done.1.refs_1_
  14.0 0.5 collective-permute-done.2.refs_2_
  14.5 1.2 %collective-permute-done.3.refs_3_ = bf16[272,128]{1,0:T(8,128)(2,1)S(1)} collective-permute-done((bf16[272,128]{1,0:T(8,128)(2,1)S(1)}, bf16[272,128]{1,0:T(8,128)(2,1)S(1)}, u32[]{:S(2)}, u32[]{:S(2)}) %collective-permute-start.3) | collective-permute-done | bytes 69664 | tf_op jit(solution)/shard_map/ppermute | solution.py:599
  15.6 0.1 row_sum.2.refs_4_
  15.7 3.9 %collective-permute-start.6 = (bf16[272,128]{1,0:T(8,128)(2,1)S(1)}, bf16[272,128]{1,0:T(8,128)(2,1)S(1)}, u32[]{:S(2)}, u32[]{:S(2)}) collective-permute-start(bf16[272,128]{1,0:T(8,128)(2,1)S(1)} %row_sum.2.refs_4_), channel_id=1, source_target_pairs={{0,96},{4,100},{8,104},{12,108},{16,112},{20,116},{24,120},{28,124... | collective-permute-start | bytes 208904 | tf_op jit(solution)/shard_map/ppermute | solution.py:599
  19.5 0.0 collective-permute-start.5
  19.5 0.7 collective-permute-start.4
  20.2 3.2 %intra.3 = (bf16[512,1024]{1,0:T(8,128)(2,1)S(1)}, f32[512,1024]{1,0:T(8,128)S(1)}, bf16[2048,256]{1,0:T(8,128)(2,1)S(1)}, bf16[2048,512]{1,0:T(8,128)(2,1)S(1)}, f32[8,128]{1,0:T(8,128)S(1)}) custom-call(bf16[512,1024]{1,0:T(8,128)(2,1)S(1)} %get-tuple-element.85.refs_0_.refs_1_.refs_2_, bf16[512,1024]{1,0:T(8,128)(2,1)S(1)} %get-tuple-element.86.refs_1_.refs_2_.refs_3_, ...), custom_call_target="tpu_custom_call" | custom-call | flops 3000000000 | bytes 10000000 | tf_op jit(solution)/shard_map/intra/pallas_call | solution.py:56
  23.4 0.0 collective-permute-done.6.refs_7_
  23.5 0.7 collective-permute-done.5.refs_6_
  24.2 0.0 collective-permute-done.4.refs_5_
  24.2 0.3 entry.2
  24.5 0.2 collective-permute-start.7
  24.8 2.5 %collective-permute-start.8 = (bf16[256,128]{1,0:T(8,128)(2,1)S(1)}, bf16[256,128]{1,0:T(8,128)(2,1)S(1)}, u32[]{:S(2)}, u32[]{:S(2)}) collective-permute-start(bf16[256,128]{1,0:T(8,128)(2,1)S(1)} %get-tuple-element.105), channel_id=1, source_target_pairs={{0,16},{4,20},{8,24},{12,28},{16,0},{20,4},{24,8},{28,12},{32,48},... | collective-permute-start | bytes 196616 | tf_op jit(solution)/shard_map/ppermute | solution.py:599
  27.3 1.2 %collective-permute-start.9 = (bf16[256,128]{1,0:T(8,128)(2,1)S(1)}, bf16[256,128]{1,0:T(8,128)(2,1)S(1)}, u32[]{:S(2)}, u32[]{:S(2)}) collective-permute-start(bf16[256,128]{1,0:T(8,128)(2,1)S(1)} %get-tuple-element.106), channel_id=1, source_target_pairs={{0,24},{4,28},{8,16},{12,20},{16,8},{20,12},{24,0},{28,4},{32,56},... | collective-permute-start | bytes 196616 | tf_op jit(solution)/shard_map/ppermute | solution.py:599
  28.5 2.1 %prepare.2 = (f32[512,1024]{1,0:T(8,128)S(1)}, bf16[512,1024]{1,0:T(8,128)(2,1)S(1)}, bf16[1024,512]{1,0:T(8,128)(2,1)S(1)}, f32[8,128]{1,0:T(8,128)S(1)}) custom-call(bf16[512,1024]{1,0:T(8,128)(2,1)S(1)} %get-tuple-element.108.refs_0_.refs_1_, f32[512,128]{1,0:T(8,128)S(1)} %get-tuple-element.107.refs_1_.refs_4_.refs_9_, ...), custom_call_target="tpu_custom_call" | custom-call | flops 1500000000 | bytes 5000000 | tf_op jit(solution)/shard_map/prepare/pallas_call | solution.py:56
  30.6 0.0 copy-start
  30.6 2.1 %prepare.3 = (f32[512,1024]{1,0:T(8,128)S(1)}, bf16[512,1024]{1,0:T(8,128)(2,1)S(1)}, bf16[1024,512]{1,0:T(8,128)(2,1)S(1)}, f32[8,128]{1,0:T(8,128)S(1)}) custom-call(bf16[512,1024]{1,0:T(8,128)(2,1)S(1)} %get-tuple-element.101.refs_0_.refs_1_, f32[512,128]{1,0:T(8,128)S(1)} %get-tuple-element.107.refs_1_.refs_4_.refs_9_, ...), custom_call_target="tpu_custom_call" | custom-call | flops 1500000000 | bytes 5000000 | tf_op jit(solution)/shard_map/prepare/pallas_call | solution.py:56
  32.7 0.0 collective-permute-done.7.refs_3_
  32.7 0.0 collective-permute-done.9.refs_5_
  32.7 0.2 device_entry.2
  32.9 3.5 %collective-permute-start.10 = (bf16[1024,128]{1,0:T(8,128)(2,1)S(1)}, bf16[1024,128]{1,0:T(8,128)(2,1)S(1)}, u32[]{:S(2)}, u32[]{:S(2)}) collective-permute-start(bf16[1024,128]{1,0:T(8,128)(2,1)S(1)} %get-tuple-element.111), channel_id=1, source_target_pairs={{0,4},{4,0},{8,12},{12,8},{16,20},{20,16},{24,28},{28,24},{32,36},... | collective-permute-start | bytes 786440 | tf_op jit(solution)/shard_map/ppermute | solution.py:599
  36.4 1.8 %cross.2 = (f32[512,1024]{1,0:T(8,128)S(1)}, f32[8,512]{1,0:T(8,128)S(1)}) custom-call(f32[512,1024]{1,0:T(8,128)S(1)} %get-tuple-element.113.refs_0_, bf16[512,1024]{1,0:T(8,128)(2,1)S(1)} %get-tuple-element.108.refs_0_.refs_1_, bf16[1024,128]{1,0:T(8,128)(2,1)S(1)} %get-tuple-element.114.refs_2_.refs_4_, ...), custom_call_target="tpu_custom_call" | custom-call | flops 1200000000 | bytes 4000000 | tf_op jit(solution)/shard_map/cross/pallas_call | solution.py:56
  38.2 0.0 collective-permute-done.10.refs_2_.refs_4_
  38.2 1.8 %cross.3 = (f32[512,1024]{1,0:T(8,128)S(1)}, f32[8,512]{1,0:T(8,128)S(1)}) custom-call(f32[512,1024]{1,0:T(8,128)S(1)} %get-tuple-element.100.refs_0_, bf16[512,1024]{1,0:T(8,128)(2,1)S(1)} %get-tuple-element.101.refs_0_.refs_1_, bf16[1024,128]{1,0:T(8,128)(2,1)S(1)} %collective-permute-done.10.refs_2_.refs_4_, ...), custom_call_target="tpu_custom_call" | custom-call | flops 1200000000 | bytes 4000000 | tf_op jit(solution)/shard_map/cross/pallas_call | solution.py:56
  40.0 2.7 %collective-permute-start.13 = (f32[8,512]{1,0:T(8,128)S(1)}, f32[8,512]{1,0:T(8,128)S(1)}, u32[]{:S(2)}, u32[]{:S(2)}) collective-permute-start(f32[8,512]{1,0:T(8,128)S(1)} %get-tuple-element.120.refs_5_), channel_id=1, source_target_pairs={{0,3},{1,2},{2,1},{3,0},{4,7},{5,6},{6,5},{7,4},{8,11},{9,10},{10,... | collective-permute-start | bytes 49160 | tf_op jit(solution)/shard_map/ppermute | solution.py:599
  42.8 0.3 collective-permute-start.12
  43.1 0.3 collective-permute-start.11
  43.4 0.5 collective-permute-done.13.refs_8_
  43.9 3.0 %collective-permute-done.12.refs_7_ = f32[8,512]{1,0:T(8,128)S(1)} collective-permute-done((f32[8,512]{1,0:T(8,128)S(1)}, f32[8,512]{1,0:T(8,128)S(1)}, u32[]{:S(2)}, u32[]{:S(2)}) %collective-permute-start.12) | collective-permute-done | bytes 16416 | tf_op jit(solution)/shard_map/ppermute | solution.py:599
  46.9 1.7 %grad_attn.2 = (bf16[512,1024]{1,0:T(8,128)(2,1)S(1)}, bf16[1056,128]{1,0:T(8,128)(2,1)S(1)}, f32[512,128]{1,0:T(8,128)S(1)}, f32[512,128]{1,0:T(8,128)S(1)}) custom-call(s32[1,512]{1,0:T(1,128)S(1)} %get-tuple-element.87.refs_0_.refs_2_, f32[512,1024]{1,0:T(8,128)S(1)} %get-tuple-element.117.refs_1_.refs_0_, ...), custom_call_target="tpu_custom_call" | custom-call | flops 1200000000 | bytes 4000000 | tf_op jit(solution)/shard_map/grad_attn/pallas_call | solution.py:56
  48.6 1.7 %collective-permute-start.14 = (bf16[1056,128]{1,0:T(8,128)(2,1)S(1)}, bf16[1056,128]{1,0:T(8,128)(2,1)S(1)}, u32[]{:S(2)}, u32[]{:S(2)}) collective-permute-start(bf16[1056,128]{1,0:T(8,128)(2,1)S(1)} %get-tuple-element.127), channel_id=1, source_target_pairs={{0,4},{4,0},{8,12},{12,8},{16,20},{20,16},{24,28},{28,24},{32,36},... | collective-permute-start | bytes 811016 | tf_op jit(solution)/shard_map/ppermute | solution.py:599
  50.3 1.5 %grad_attn.3 = (bf16[512,1024]{1,0:T(8,128)(2,1)S(1)}, bf16[1056,128]{1,0:T(8,128)(2,1)S(1)}) custom-call(s32[1,512]{1,0:T(1,128)S(1)} %get-tuple-element.87.refs_0_.refs_2_, f32[512,1024]{1,0:T(8,128)S(1)} %get-tuple-element.122.refs_1_.refs_0_, f32[512,1024]{1,0:T(8,128)S(1)} %get-tuple-element.115.refs_3_.refs_2_, ...), custom_call_target="tpu_custom_call" | custom-call | flops 1200000000 | bytes 4000000 | tf_op jit(solution)/shard_map/grad_attn/pallas_call | solution.py:56
  51.8 0.1 chip_sum.3
  51.9 0.1 collective-permute-start.15
  52.0 2.3 %collective-permute-start.16 = (bf16[288,128]{1,0:T(8,128)(2,1)S(1)}, bf16[288,128]{1,0:T(8,128)(2,1)S(1)}, u32[]{:S(2)}, u32[]{:S(2)}) collective-permute-start(bf16[288,128]{1,0:T(8,128)(2,1)S(1)} %get-tuple-element.130), channel_id=1, source_target_pairs={{0,16},{4,20},{8,24},{12,28},{16,0},{20,4},{24,8},{28,12},{32,48},... | collective-permute-start | bytes 221192 | tf_op jit(solution)/shard_map/ppermute | solution.py:599
  54.3 1.6 %collective-permute-start.17 = (bf16[288,128]{1,0:T(8,128)(2,1)S(1)}, bf16[288,128]{1,0:T(8,128)(2,1)S(1)}, u32[]{:S(2)}, u32[]{:S(2)}) collective-permute-start(bf16[288,128]{1,0:T(8,128)(2,1)S(1)} %get-tuple-element.131), channel_id=1, source_target_pairs={{0,24},{4,28},{8,16},{12,20},{16,8},{20,12},{24,0},{28,4},{32,56},... | collective-permute-start | bytes 221192 | tf_op jit(solution)/shard_map/ppermute | solution.py:599
  55.9 4.7 %local_grads.2 = (bf16[512,2048]{1,0:T(8,128)(2,1)}, f32[512,1024]{1,0:T(8,128)S(1)}, f32[512,1024]{1,0:T(8,128)S(1)}, f32[8,128]{1,0:T(8,128)S(1)}) custom-call(bf16[512,1024]{1,0:T(8,128)(2,1)S(1)} %get-tuple-element.108.refs_0_.refs_1_, bf16[512,1024]{1,0:T(8,128)(2,1)S(1)} %get-tuple-element.89.refs_0_.refs_1_.refs_2_, ...), custom_call_target="tpu_custom_call" | custom-call | flops 5000000000 | bytes 16666666 | tf_op jit(solution)/shard_map/local_grads/pallas_call | solution.py:56
  60.6 0.0 collective-permute-done.15.refs_1_
  60.6 0.0 collective-permute-done.17.refs_3_
  60.6 0.1 row_sum.3.refs_10_.refs_4_
  60.7 1.3 %collective-permute-start.20 = (bf16[288,128]{1,0:T(8,128)(2,1)S(1)}, bf16[288,128]{1,0:T(8,128)(2,1)S(1)}, u32[]{:S(2)}, u32[]{:S(2)}) collective-permute-start(bf16[288,128]{1,0:T(8,128)(2,1)S(1)} %row_sum.3.refs_10_.refs_4_), channel_id=1, source_target_pairs={{0,96},{4,100},{8,104},{12,108},{16,112},{20,116},{24,120},{28,124... | collective-permute-start | bytes 221192 | tf_op jit(solution)/shard_map/ppermute | solution.py:599
  62.0 0.6 collective-permute-start.19
  62.6 1.4 %collective-permute-start.18 = (bf16[288,128]{1,0:T(8,128)(2,1)S(1)}, bf16[288,128]{1,0:T(8,128)(2,1)S(1)}, u32[]{:S(2)}, u32[]{:S(2)}) collective-permute-start(bf16[288,128]{1,0:T(8,128)(2,1)S(1)} %row_sum.3.refs_10_.refs_4_), channel_id=1, source_target_pairs={{0,32},{4,36},{8,40},{12,44},{16,48},{20,52},{24,56},{28,60},{32,0... | collective-permute-start | bytes 221192 | tf_op jit(solution)/shard_map/ppermute | solution.py:599
  64.0 4.8 %local_grads.3 = (bf16[512,2048]{1,0:T(8,128)(2,1)}, f32[512,1024]{1,0:T(8,128)S(1)}, f32[512,1024]{1,0:T(8,128)S(1)}, f32[8,128]{1,0:T(8,128)S(1)}) custom-call(bf16[512,1024]{1,0:T(8,128)(2,1)S(1)} %get-tuple-element.101.refs_0_.refs_1_, bf16[512,1024]{1,0:T(8,128)(2,1)S(1)} %get-tuple-element.85.refs_0_.refs_1_.refs_2_, ...), custom_call_target="tpu_custom_call", output_to_operand_aliasing={{0}: (11, {})} | custom-call | flops 5000000000 | bytes 16666666 | tf_op jit(solution)/shard_map/local_grads/pallas_call | solution.py:56
  68.9 0.0 collective-permute-done.19.refs_6_
  68.9 0.3 entry.3
  69.3 0.1 collective-permute-start.21
  69.4 2.3 %collective-permute-start.22 = (bf16[256,128]{1,0:T(8,128)(2,1)S(1)}, bf16[256,128]{1,0:T(8,128)(2,1)S(1)}, u32[]{:S(2)}, u32[]{:S(2)}) collective-permute-start(bf16[256,128]{1,0:T(8,128)(2,1)S(1)} %get-tuple-element.150), channel_id=1, source_target_pairs={{0,16},{4,20},{8,24},{12,28},{16,0},{20,4},{24,8},{28,12},{32,48},... | collective-permute-start | bytes 196616 | tf_op jit(solution)/shard_map/ppermute | solution.py:599
  71.6 1.6 %collective-permute-start.23 = (bf16[256,128]{1,0:T(8,128)(2,1)S(1)}, bf16[256,128]{1,0:T(8,128)(2,1)S(1)}, u32[]{:S(2)}, u32[]{:S(2)}) collective-permute-start(bf16[256,128]{1,0:T(8,128)(2,1)S(1)} %get-tuple-element.151), channel_id=1, source_target_pairs={{0,24},{4,28},{8,16},{12,20},{16,8},{20,12},{24,0},{28,4},{32,56},... | collective-permute-start | bytes 196616 | tf_op jit(solution)/shard_map/ppermute | solution.py:599
  73.2 2.1 %gates.2 = (bf16[512,2048]{1,0:T(8,128)(2,1)}, bf16[512,2048]{1,0:T(8,128)(2,1)}, f32[8,128]{1,0:T(8,128)S(1)}) custom-call(f32[512,1024]{1,0:T(8,128)S(1)} %get-tuple-element.122.refs_1_.refs_0_, bf16[512,1024]{1,0:T(8,128)(2,1)S(1)} %get-tuple-element.123.refs_1_, f32[512,1024]{1,0:T(8,128)S(1)} %get-tuple-element.115.refs_3_.refs_2_, ...), custom_call_target="tpu_custom_call" | custom-call | flops 1200000000 | bytes 4000000 | tf_op jit(solution)/shard_map/gates/pallas_call | solution.py:56
  75.3 2.1 %gates.3 = (bf16[512,2048]{1,0:T(8,128)(2,1)}, bf16[512,2048]{1,0:T(8,128)(2,1)}, f32[8,128]{1,0:T(8,128)S(1)}) custom-call(f32[512,1024]{1,0:T(8,128)S(1)} %get-tuple-element.117.refs_1_.refs_0_, bf16[512,1024]{1,0:T(8,128)(2,1)S(1)} %get-tuple-element.118.refs_1_, ...), custom_call_target="tpu_custom_call", output_to_operand_aliasing={{0}: (6, {}), {1}: (7, {})} | custom-call | flops 1200000000 | bytes 4000000 | tf_op jit(solution)/shard_map/gates/pallas_call | solution.py:56
  77.4 0.2 device_entry.3
  77.7 2.7 %collective-permute-start.24 = (bf16[1040,128]{1,0:T(8,128)(2,1)S(1)}, bf16[1040,128]{1,0:T(8,128)(2,1)S(1)}, u32[]{:S(2)}, u32[]{:S(2)}) collective-permute-start(bf16[1040,128]{1,0:T(8,128)(2,1)S(1)} %get-tuple-element.154), channel_id=1, source_target_pairs={{0,4},{4,0},{8,12},{12,8},{16,20},{20,16},{24,28},{28,24},{32,36},... | collective-permute-start | bytes 798728 | tf_op jit(solution)/shard_map/ppermute | solution.py:599
  80.3 2.3 %finish.2 = (bf16[512,2048]{1,0:T(8,128)(2,1)}, bf16[512,2048]{1,0:T(8,128)(2,1)}) custom-call(f32[512,1024]{1,0:T(8,128)S(1)} %get-tuple-element.155.refs_0_, f32[512,1024]{1,0:T(8,128)S(1)} %get-tuple-element.156.refs_1_, bf16[512,1024]{1,0:T(8,128)(2,1)S(1)} %get-tuple-element.89.refs_0_.refs_1_.refs_2_, ...), custom_call_target="tpu_custom_call" | custom-call | flops 1200000000 | bytes 4000000 | tf_op jit(solution)/shard_map/finish/pallas_call | solution.py:56
  82.7 2.3 %finish.3 = (bf16[512,2048]{1,0:T(8,128)(2,1)}, bf16[512,2048]{1,0:T(8,128)(2,1)}, f32[16,128]{1,0:T(8,128)}) custom-call(f32[512,1024]{1,0:T(8,128)S(1)} %get-tuple-element.147.refs_0_, f32[512,1024]{1,0:T(8,128)S(1)} %get-tuple-element.148.refs_1_, ...), custom_call_target="tpu_custom_call", output_to_operand_aliasing={{0}: (7, {}), {1}: (8, {})} | custom-call | flops 1200000000 | bytes 4000000 | tf_op jit(solution)/shard_map/finish/pallas_call | solution.py:56
  (12 shorter events, 0.0 us)
Async XLA Ops:
  2.9 3.8 %collective-permute-start = (bf16[1040,128]{1,0:T(8,128)(2,1)S(1)}, bf16[1040,128]{1,0:T(8,128)(2,1)S(1)}, u32[]{:S(2)}, u32[]{:S(2)}) collective-permute-start(bf16[1040,128]{1,0:T(8,128)(2,1)S(1)} %get-tuple-element.92), channel_id=1, source_target_pairs={{0,4},{4,0},{8,12},{12,8},{16,20},{20,16},{24,28},{28,24},{32,36},... | collective-permute-start | bytes 798728 | tf_op jit(solution)/shard_map/ppermute | solution.py:599
  6.8 7.2 %collective-permute-start.1 = (bf16[272,128]{1,0:T(8,128)(2,1)S(1)}, bf16[272,128]{1,0:T(8,128)(2,1)S(1)}, u32[]{:S(2)}, u32[]{:S(2)}) collective-permute-start(bf16[272,128]{1,0:T(8,128)(2,1)S(1)} %get-tuple-element.96), channel_id=1, source_target_pairs={{0,8},{4,12},{8,0},{12,4},{16,24},{20,28},{24,16},{28,20},{32,40},... | collective-permute-start | bytes 208904 | tf_op jit(solution)/shard_map/ppermute | solution.py:599
  8.2 6.3 %collective-permute-start.2 = (bf16[272,128]{1,0:T(8,128)(2,1)S(1)}, bf16[272,128]{1,0:T(8,128)(2,1)S(1)}, u32[]{:S(2)}, u32[]{:S(2)}) collective-permute-start(bf16[272,128]{1,0:T(8,128)(2,1)S(1)} %get-tuple-element.97), channel_id=1, source_target_pairs={{0,16},{4,20},{8,24},{12,28},{16,0},{20,4},{24,8},{28,12},{32,48},... | collective-permute-start | bytes 208904 | tf_op jit(solution)/shard_map/ppermute | solution.py:599
  10.6 5.0 %collective-permute-start.3 = (bf16[272,128]{1,0:T(8,128)(2,1)S(1)}, bf16[272,128]{1,0:T(8,128)(2,1)S(1)}, u32[]{:S(2)}, u32[]{:S(2)}) collective-permute-start(bf16[272,128]{1,0:T(8,128)(2,1)S(1)} %get-tuple-element.98), channel_id=1, source_target_pairs={{0,24},{4,28},{8,16},{12,20},{16,8},{20,12},{24,0},{28,4},{32,56},... | collective-permute-start | bytes 208904 | tf_op jit(solution)/shard_map/ppermute | solution.py:599
  15.7 7.8 %collective-permute-start.6 = (bf16[272,128]{1,0:T(8,128)(2,1)S(1)}, bf16[272,128]{1,0:T(8,128)(2,1)S(1)}, u32[]{:S(2)}, u32[]{:S(2)}) collective-permute-start(bf16[272,128]{1,0:T(8,128)(2,1)S(1)} %row_sum.2.refs_4_), channel_id=1, source_target_pairs={{0,96},{4,100},{8,104},{12,108},{16,112},{20,116},{24,120},{28,124... | collective-permute-start | bytes 208904 | tf_op jit(solution)/shard_map/ppermute | solution.py:599
  19.5 4.7 %collective-permute-start.5 = (bf16[272,128]{1,0:T(8,128)(2,1)S(1)}, bf16[272,128]{1,0:T(8,128)(2,1)S(1)}, u32[]{:S(2)}, u32[]{:S(2)}) collective-permute-start(bf16[272,128]{1,0:T(8,128)(2,1)S(1)} %row_sum.2.refs_4_), channel_id=1, source_target_pairs={{0,64},{4,68},{8,72},{12,76},{16,80},{20,84},{24,88},{28,92},{32,9... | collective-permute-start | bytes 208904 | tf_op jit(solution)/shard_map/ppermute | solution.py:599
  19.5 4.7 %collective-permute-start.4 = (bf16[272,128]{1,0:T(8,128)(2,1)S(1)}, bf16[272,128]{1,0:T(8,128)(2,1)S(1)}, u32[]{:S(2)}, u32[]{:S(2)}) collective-permute-start(bf16[272,128]{1,0:T(8,128)(2,1)S(1)} %row_sum.2.refs_4_), channel_id=1, source_target_pairs={{0,32},{4,36},{8,40},{12,44},{16,48},{20,52},{24,56},{28,60},{32,0... | collective-permute-start | bytes 208904 | tf_op jit(solution)/shard_map/ppermute | solution.py:599
  24.5 8.1 %collective-permute-start.7 = (bf16[256,128]{1,0:T(8,128)(2,1)S(1)}, bf16[256,128]{1,0:T(8,128)(2,1)S(1)}, u32[]{:S(2)}, u32[]{:S(2)}) collective-permute-start(bf16[256,128]{1,0:T(8,128)(2,1)S(1)} %get-tuple-element.104), channel_id=1, source_target_pairs={{0,8},{4,12},{8,0},{12,4},{16,24},{20,28},{24,16},{28,20},{32,40},... | collective-permute-start | bytes 196616 | tf_op jit(solution)/shard_map/ppermute | solution.py:599
  24.8 7.9 %collective-permute-start.8 = (bf16[256,128]{1,0:T(8,128)(2,1)S(1)}, bf16[256,128]{1,0:T(8,128)(2,1)S(1)}, u32[]{:S(2)}, u32[]{:S(2)}) collective-permute-start(bf16[256,128]{1,0:T(8,128)(2,1)S(1)} %get-tuple-element.105), channel_id=1, source_target_pairs={{0,16},{4,20},{8,24},{12,28},{16,0},{20,4},{24,8},{28,12},{32,48},... | collective-permute-start | bytes 196616 | tf_op jit(solution)/shard_map/ppermute | solution.py:599
  27.3 5.4 %collective-permute-start.9 = (bf16[256,128]{1,0:T(8,128)(2,1)S(1)}, bf16[256,128]{1,0:T(8,128)(2,1)S(1)}, u32[]{:S(2)}, u32[]{:S(2)}) collective-permute-start(bf16[256,128]{1,0:T(8,128)(2,1)S(1)} %get-tuple-element.106), channel_id=1, source_target_pairs={{0,24},{4,28},{8,16},{12,20},{16,8},{20,12},{24,0},{28,4},{32,56},... | collective-permute-start | bytes 196616 | tf_op jit(solution)/shard_map/ppermute | solution.py:599
  30.6 5.9 %copy-start = (f32[2048]{0:T(1024)S(1)}, f32[2048]{0:T(1024)}, u32[]{:S(2)}) copy-start(f32[2048]{0:T(1024)} %param.12) | copy-start | bytes 24580
  32.9 5.3 %collective-permute-start.10 = (bf16[1024,128]{1,0:T(8,128)(2,1)S(1)}, bf16[1024,128]{1,0:T(8,128)(2,1)S(1)}, u32[]{:S(2)}, u32[]{:S(2)}) collective-permute-start(bf16[1024,128]{1,0:T(8,128)(2,1)S(1)} %get-tuple-element.111), channel_id=1, source_target_pairs={{0,4},{4,0},{8,12},{12,8},{16,20},{20,16},{24,28},{28,24},{32,36},... | collective-permute-start | bytes 786440 | tf_op jit(solution)/shard_map/ppermute | solution.py:599
  40.0 3.9 %collective-permute-start.13 = (f32[8,512]{1,0:T(8,128)S(1)}, f32[8,512]{1,0:T(8,128)S(1)}, u32[]{:S(2)}, u32[]{:S(2)}) collective-permute-start(f32[8,512]{1,0:T(8,128)S(1)} %get-tuple-element.120.refs_5_), channel_id=1, source_target_pairs={{0,3},{1,2},{2,1},{3,0},{4,7},{5,6},{6,5},{7,4},{8,11},{9,10},{10,... | collective-permute-start | bytes 49160 | tf_op jit(solution)/shard_map/ppermute | solution.py:599
  42.8 4.1 %collective-permute-start.12 = (f32[8,512]{1,0:T(8,128)S(1)}, f32[8,512]{1,0:T(8,128)S(1)}, u32[]{:S(2)}, u32[]{:S(2)}) collective-permute-start(f32[8,512]{1,0:T(8,128)S(1)} %get-tuple-element.120.refs_5_), channel_id=1, source_target_pairs={{0,2},{1,3},{2,0},{3,1},{4,6},{5,7},{6,4},{7,5},{8,10},{9,11},{10,... | collective-permute-start | bytes 49160 | tf_op jit(solution)/shard_map/ppermute | solution.py:599
  43.1 3.7 %collective-permute-start.11 = (f32[8,512]{1,0:T(8,128)S(1)}, f32[8,512]{1,0:T(8,128)S(1)}, u32[]{:S(2)}, u32[]{:S(2)}) collective-permute-start(f32[8,512]{1,0:T(8,128)S(1)} %get-tuple-element.120.refs_5_), channel_id=1, source_target_pairs={{0,1},{1,0},{2,3},{3,2},{4,5},{5,4},{6,7},{7,6},{8,9},{9,8},{10,11... | collective-permute-start | bytes 49160 | tf_op jit(solution)/shard_map/ppermute | solution.py:599
  48.6 3.2 %collective-permute-start.14 = (bf16[1056,128]{1,0:T(8,128)(2,1)S(1)}, bf16[1056,128]{1,0:T(8,128)(2,1)S(1)}, u32[]{:S(2)}, u32[]{:S(2)}) collective-permute-start(bf16[1056,128]{1,0:T(8,128)(2,1)S(1)} %get-tuple-element.127), channel_id=1, source_target_pairs={{0,4},{4,0},{8,12},{12,8},{16,20},{20,16},{24,28},{28,24},{32,36},... | collective-permute-start | bytes 811016 | tf_op jit(solution)/shard_map/ppermute | solution.py:599
  51.9 8.7 %collective-permute-start.15 = (bf16[288,128]{1,0:T(8,128)(2,1)S(1)}, bf16[288,128]{1,0:T(8,128)(2,1)S(1)}, u32[]{:S(2)}, u32[]{:S(2)}) collective-permute-start(bf16[288,128]{1,0:T(8,128)(2,1)S(1)} %get-tuple-element.129), channel_id=1, source_target_pairs={{0,8},{4,12},{8,0},{12,4},{16,24},{20,28},{24,16},{28,20},{32,40},... | collective-permute-start | bytes 221192 | tf_op jit(solution)/shard_map/ppermute | solution.py:599
  52.0 8.6 %collective-permute-start.16 = (bf16[288,128]{1,0:T(8,128)(2,1)S(1)}, bf16[288,128]{1,0:T(8,128)(2,1)S(1)}, u32[]{:S(2)}, u32[]{:S(2)}) collective-permute-start(bf16[288,128]{1,0:T(8,128)(2,1)S(1)} %get-tuple-element.130), channel_id=1, source_target_pairs={{0,16},{4,20},{8,24},{12,28},{16,0},{20,4},{24,8},{28,12},{32,48},... | collective-permute-start | bytes 221192 | tf_op jit(solution)/shard_map/ppermute | solution.py:599
  54.3 6.3 %collective-permute-start.17 = (bf16[288,128]{1,0:T(8,128)(2,1)S(1)}, bf16[288,128]{1,0:T(8,128)(2,1)S(1)}, u32[]{:S(2)}, u32[]{:S(2)}) collective-permute-start(bf16[288,128]{1,0:T(8,128)(2,1)S(1)} %get-tuple-element.131), channel_id=1, source_target_pairs={{0,24},{4,28},{8,16},{12,20},{16,8},{20,12},{24,0},{28,4},{32,56},... | collective-permute-start | bytes 221192 | tf_op jit(solution)/shard_map/ppermute | solution.py:599
  60.7 8.2 %collective-permute-start.20 = (bf16[288,128]{1,0:T(8,128)(2,1)S(1)}, bf16[288,128]{1,0:T(8,128)(2,1)S(1)}, u32[]{:S(2)}, u32[]{:S(2)}) collective-permute-start(bf16[288,128]{1,0:T(8,128)(2,1)S(1)} %row_sum.3.refs_10_.refs_4_), channel_id=1, source_target_pairs={{0,96},{4,100},{8,104},{12,108},{16,112},{20,116},{24,120},{28,124... | collective-permute-start | bytes 221192 | tf_op jit(solution)/shard_map/ppermute | solution.py:599
  62.0 6.9 %collective-permute-start.19 = (bf16[288,128]{1,0:T(8,128)(2,1)S(1)}, bf16[288,128]{1,0:T(8,128)(2,1)S(1)}, u32[]{:S(2)}, u32[]{:S(2)}) collective-permute-start(bf16[288,128]{1,0:T(8,128)(2,1)S(1)} %row_sum.3.refs_10_.refs_4_), channel_id=1, source_target_pairs={{0,64},{4,68},{8,72},{12,76},{16,80},{20,84},{24,88},{28,92},{32,9... | collective-permute-start | bytes 221192 | tf_op jit(solution)/shard_map/ppermute | solution.py:599
  62.6 6.3 %collective-permute-start.18 = (bf16[288,128]{1,0:T(8,128)(2,1)S(1)}, bf16[288,128]{1,0:T(8,128)(2,1)S(1)}, u32[]{:S(2)}, u32[]{:S(2)}) collective-permute-start(bf16[288,128]{1,0:T(8,128)(2,1)S(1)} %row_sum.3.refs_10_.refs_4_), channel_id=1, source_target_pairs={{0,32},{4,36},{8,40},{12,44},{16,48},{20,52},{24,56},{28,60},{32,0... | collective-permute-start | bytes 221192 | tf_op jit(solution)/shard_map/ppermute | solution.py:599
  69.3 8.1 %collective-permute-start.21 = (bf16[256,128]{1,0:T(8,128)(2,1)S(1)}, bf16[256,128]{1,0:T(8,128)(2,1)S(1)}, u32[]{:S(2)}, u32[]{:S(2)}) collective-permute-start(bf16[256,128]{1,0:T(8,128)(2,1)S(1)} %get-tuple-element.149), channel_id=1, source_target_pairs={{0,8},{4,12},{8,0},{12,4},{16,24},{20,28},{24,16},{28,20},{32,40},... | collective-permute-start | bytes 196616 | tf_op jit(solution)/shard_map/ppermute | solution.py:599
  69.4 8.1 %collective-permute-start.22 = (bf16[256,128]{1,0:T(8,128)(2,1)S(1)}, bf16[256,128]{1,0:T(8,128)(2,1)S(1)}, u32[]{:S(2)}, u32[]{:S(2)}) collective-permute-start(bf16[256,128]{1,0:T(8,128)(2,1)S(1)} %get-tuple-element.150), channel_id=1, source_target_pairs={{0,16},{4,20},{8,24},{12,28},{16,0},{20,4},{24,8},{28,12},{32,48},... | collective-permute-start | bytes 196616 | tf_op jit(solution)/shard_map/ppermute | solution.py:599
  71.6 5.8 %collective-permute-start.23 = (bf16[256,128]{1,0:T(8,128)(2,1)S(1)}, bf16[256,128]{1,0:T(8,128)(2,1)S(1)}, u32[]{:S(2)}, u32[]{:S(2)}) collective-permute-start(bf16[256,128]{1,0:T(8,128)(2,1)S(1)} %get-tuple-element.151), channel_id=1, source_target_pairs={{0,24},{4,28},{8,16},{12,20},{16,8},{20,12},{24,0},{28,4},{32,56},... | collective-permute-start | bytes 196616 | tf_op jit(solution)/shard_map/ppermute | solution.py:599
  77.7 5.0 %collective-permute-start.24 = (bf16[1040,128]{1,0:T(8,128)(2,1)S(1)}, bf16[1040,128]{1,0:T(8,128)(2,1)S(1)}, u32[]{:S(2)}, u32[]{:S(2)}) collective-permute-start(bf16[1040,128]{1,0:T(8,128)(2,1)S(1)} %get-tuple-element.154), channel_id=1, source_target_pairs={{0,4},{4,0},{8,12},{12,8},{16,20},{20,16},{24,28},{28,24},{32,36},... | collective-permute-start | bytes 798728 | tf_op jit(solution)/shard_map/ppermute | solution.py:599

commit v3 on v2

v3 whole, which is shorter than its diff:
```python
import functools

import jax
import jax.numpy as jnp
from jax import lax
from jax.experimental import pallas as pl
from jax.experimental.pallas import tpu as pltpu
from jax.sharding import PartitionSpec as P

HD = 128
ATT = 8192
EPSILON = 1e-06
TOK = 512
BLOCK = 256
HEADS = 8
WIDE = HEADS * HD
GROUP = 4
GROUPS = HEADS // GROUP
SPAN = GROUP * HD
STATE_ROWS = HEADS * HD
QUARTER = 2 * HD
TILE = 16
F32 = jnp.float32
BF16 = jnp.bfloat16
VMEM_LIMIT = 16 * 1024 * 1024
VM = pl.BlockSpec(memory_space=pltpu.VMEM)
SM = pl.BlockSpec(memory_space=pltpu.SMEM)
ANY = pl.BlockSpec(memory_space=pl.ANY)


def dot(a, b, da, db):
    return lax.dot_general(a, b, (((da,), (db,)), ((), ())), preferred_element_type=F32)


def vmem(shape, dtype):
    return pltpu.VMEM(shape, dtype)


def half_shape(dtype):
    return vmem((TOK, WIDE), dtype)


def far(dtype=BF16):
    return jax.ShapeDtypeStruct((TOK, 2 * WIDE), dtype)


def call(kernel, name, flops, near, outs, distant=(), scratch=(), aliases=None):
    near = [pltpu.with_memory_space_constraint(a, pltpu.VMEM) for a in near]
    distant = [pltpu.with_memory_space_constraint(a, pltpu.HBM) for a in distant]
    out_specs = [ANY if isinstance(o, jax.ShapeDtypeStruct) else VM for o in outs]

    def placed(*refs):
        where = lax.axis_index("ctx")
        kernel((where & 1, (where >> 1) & 3, where >> 3), *refs)

    return pl.pallas_call(
        placed,
        in_specs=[VM] * len(near) + [ANY] * len(distant),
        out_specs=out_specs,
        out_shape=list(outs),
        scratch_shapes=list(scratch),
        input_output_aliases=aliases or {},
        compiler_params=pltpu.CompilerParams(vmem_limit_bytes=VMEM_LIMIT),
        cost_estimate=pl.CostEstimate(
            flops=int(flops), bytes_accessed=int(flops / 300), transcendentals=0
        ),
        name=name,
    )(*near, *distant)


def base_column(ids, flip):
    return pl.multiple_of((ids[0] ^ flip) * WIDE, WIDE)


def each_group(body, groups=GROUPS):
    def step(g, carry):
        body(g)
        return carry

    lax.fori_loop(0, groups, step, 0)


def head_columns(h):
    return pl.ds(pl.multiple_of(h * HD, HD), HD)


def head_rows(h, rows=HD):
    return pl.ds(pl.multiple_of(h * rows, rows), rows)


def span(start, width):
    return pl.ds(pl.multiple_of(start, width), width)


def load(source, base, at, target, sem, width=SPAN):
    return pltpu.make_async_copy(
        source.at[:, span(base + at, width)], target.at[:, span(at, width)], sem
    )


def store(source, at, base, target, sem, width=SPAN):
    return pltpu.make_async_copy(
        source.at[:, span(at, width)], target.at[:, span(base, width)], sem
    )


def info_tile(low, high):
    row = lax.broadcasted_iota(jnp.int32, (TILE, HD), 0)
    return jnp.where(
        row < 8, jnp.broadcast_to(low, (TILE, HD)), jnp.broadcast_to(high, (TILE, HD))
    ).astype(BF16)


def split_tile(x):
    high = x.astype(BF16).astype(F32)
    return jnp.concatenate([high, x - high], axis=0).astype(BF16)


def joined_tile(tile):
    t = tile.astype(F32)
    return t[0:8] + t[8:16]


def split_ends(seg_ref):
    seg = seg_ref[...].astype(F32)
    return seg[:, 0:1], seg[:, BLOCK - 1 : BLOCK], seg[:, BLOCK : BLOCK + 1], seg[:, TOK - 1 : TOK]


def flag(cond):
    return jnp.where(cond, 1.0, 0.0)


def fill_token_masks(seg_ref, before, after, last, first):
    start0, end0, start1, end1 = split_ends(seg_ref)
    col = jnp.transpose(jnp.broadcast_to(seg_ref[...].astype(F32), (8, TOK)))[:, 0:1]
    col = jnp.broadcast_to(col, (TOK, HD))
    for ref, id0, id1 in (
        (last, end0, end1), (before, start0, end0), (after, start1, end1), (first, start0, start1)
    ):
        ref[0:BLOCK, :] = flag(col[0:BLOCK] == id0).astype(BF16)
        ref[BLOCK:TOK, :] = flag(col[BLOCK:TOK] == id1).astype(BF16)


FINE = 2
FINE_SPAN = FINE * HD


def state_kernel(flip, ids, *refs):
    if flip:
        k_far, v_far, seg_far, k, v, out, early, seg, before, after, last, first, sems, seg_sem = refs
    else:
        seg, last, k_far, v_far, k, v, out, early, sems = refs
    base = base_column(ids, flip)
    groups = HEADS // FINE
    copies = [
        [
            load(far_ref, base, g * FINE_SPAN, ref, sems.at[n, g], FINE_SPAN)
            for n, (far_ref, ref) in enumerate(((k_far, k), (v_far, v)))
        ]
        for g in range(groups)
    ]
    if flip:
        copy = pltpu.make_async_copy(seg_far, seg, seg_sem)
        copy.start()
    for pair in copies:
        for c in pair:
            c.start()
    if flip:
        copy.wait()
        fill_token_masks(seg, before, after, last, first)
    start0, end0, _, end1 = split_ends(seg)
    join = flag(end0 == end1)
    out[STATE_ROWS : STATE_ROWS + TILE, :] = info_tile(start0, end1)
    for g in range(groups):
        for c in copies[g]:
            c.wait()
        for h in range(g * FINE, (g + 1) * FINE):
            kh = k[:, head_columns(h)] * last[...]
            vh = v[:, head_columns(h)]
            one = dot(kh[0:BLOCK], vh[0:BLOCK], 0, 0)
            two = dot(kh[BLOCK:TOK], vh[BLOCK:TOK], 0, 0)
            early[head_rows(h), :] = one
            out[head_rows(h), :] = (two + one * join).astype(BF16)


def local_state(k, v, seg, seg_vmem=None, last=None):
    flip = seg_vmem is None
    outs = [
        half_shape(BF16), half_shape(BF16), vmem((STATE_ROWS + TILE, HD), BF16),
        vmem((STATE_ROWS, HD), F32),
    ]
    scratch = [pltpu.SemaphoreType.DMA((2, HEADS // FINE))]
    near, distant = [seg_vmem, last], [k, v]
    if flip:
        outs += [vmem((1, TOK), jnp.int32)] + [vmem((TOK, HD), BF16)] * 4
        scratch += [pltpu.SemaphoreType.DMA]
        near, distant = [], [k, v, seg]
    return call(
        functools.partial(state_kernel, int(flip)), "local_state", 1e9, near, outs, distant, scratch
    )


def fill_masks(seg_ref, m0, m1):
    seg = seg_ref[...].astype(F32)
    col = jnp.transpose(jnp.broadcast_to(seg, (8, TOK)))[:, 0:1]
    t = lax.broadcasted_iota(jnp.int32, (BLOCK, BLOCK), 0)
    s = lax.broadcasted_iota(jnp.int32, (BLOCK, BLOCK), 1)
    for start, ref in ((0, m0), (BLOCK, m1)):
        same = col[start : start + BLOCK] == seg[:, start : start + BLOCK]
        ref[...] = flag(same & (s <= t)).astype(BF16)


def masked(left, right, mask):
    return dot(left, right, 1, 1).astype(BF16) * mask[...]


BLOCKS = ((0, slice(0, BLOCK)), (1, slice(BLOCK, TOK)))


def intra_kernel(flip, ids, *refs):
    if flip:
        k, v, first, m0, m1, _, q_far, q, attn, w0, w1, qt, token, sems = refs
    else:
        k, v, first, seg, _, q_far, q, attn, w0, w1, qt, token, m0, m1, sems = refs
    base = base_column(ids, flip)
    for g in range(GROUPS):
        load(q_far, base, g * SPAN, q, sems.at[g]).start()
    if not flip:
        fill_masks(seg, m0, m1)
    token[...] = jnp.zeros_like(token)

    def body(g):
        load(q_far, base, g * SPAN, q, sems.at[g]).wait()
        for j in range(GROUP):
            h = g * GROUP + j
            c = head_columns(h)
            qh, kh, vh = q[:, c], k[:, c], v[:, c]
            for n, t in BLOCKS:
                w = masked(qh[t], kh[t], (m0, m1)[n])
                (w0, w1)[n][head_rows(h, BLOCK), :] = w
                attn[t, c] = dot(w, vh[t], 1, 0)
            qt[head_rows(h), :] = jnp.transpose(qh * first[...])

    each_group(body)


TOKEN = vmem((8, HD), F32)


def intra(k, v, first, q, after, seg=None, masks=None):
    outs = [
        half_shape(BF16),
        half_shape(F32),
        vmem((HEADS * BLOCK, BLOCK), BF16),
        vmem((HEADS * BLOCK, BLOCK), BF16),
        vmem((STATE_ROWS, TOK), BF16),
        TOKEN,
    ]
    if masks is None:
        near = [k, v, first, seg, after]
        outs += [vmem((BLOCK, BLOCK), BF16), vmem((BLOCK, BLOCK), BF16)]
    else:
        near = [k, v, first, *masks, after]
    return call(
        functools.partial(intra_kernel, int(masks is not None)), "intra", 3e9, near, outs, [q],
        [pltpu.SemaphoreType.DMA((GROUPS,))],
    )


def sigmoid_parts(gi):
    bend = 0.5 * jnp.tanh(0.5 * gi.astype(F32))
    return 0.5 + bend, 0.5 - bend


def prepare_kernel(ids, _, go_far, gi_far, w, gi, token, go, sems):
    pairs = ((go_far, go), (gi_far, gi))
    for g in range(2 * GROUPS):
        for n, (far_ref, ref) in enumerate(pairs):
            load(far_ref, 0, g * SPAN, ref, sems.at[n, g]).start()
    token[...] = jnp.zeros_like(token)

    def body(g):
        for n, (far_ref, ref) in enumerate(pairs):
            load(far_ref, 0, g * SPAN, ref, sems.at[n, g]).wait()
        for j in range(GROUP):
            c = head_columns(g * GROUP + j)
            w[:, c] = go[:, c].astype(F32) * sigmoid_parts(gi[:, c])[0]

    each_group(body, 2 * GROUPS)


def prepare(after, go, gi):
    return call(
        prepare_kernel, "prepare", 3e9, [after],
        [vmem((TOK, 2 * WIDE), F32), vmem((TOK, 2 * WIDE), BF16), TOKEN], [go, gi],
        [pltpu.VMEM((TOK, 2 * WIDE), BF16), pltpu.SemaphoreType.DMA((2, 2 * GROUPS))],
    )


def cross_kernel(flip, ids, attn_in, q, s, early, w, before, seg, gain, *rest):
    previous = rest[0] if flip else None
    attn, second, sums, squares, inners = rest[-5:]
    base = base_column(ids, flip)
    squares[...] = jnp.zeros_like(squares)
    inners[...] = jnp.zeros_like(inners)
    start0, end0, _, _ = split_ends(seg)
    join = flag(start0 == end0)

    def body(g):
        for j in range(GROUP):
            h = g * GROUP + j
            c, rows = head_columns(h), head_rows(h)
            far_c = span(base + h * HD, HD)
            one = s[rows, :]
            two = (early[rows, :] + one.astype(F32) * join).astype(BF16)
            second[rows, :] = two
            qh = q[:, c] * before[...]
            scale = gain[:, far_c]
            for n, t in BLOCKS:
                a = attn_in[t, c] + dot(qh[t], (one, two)[n], 1, 0)
                attn[t, c] = a
                squares[t, :] += a * a
                inners[t, :] += w[t, far_c] * a * scale

    each_group(body)
    ones = jnp.ones((8, HD), F32)
    dims = (((1,), (1,)), ((), ()))
    ss, dd = [
        lax.dot_general(
            ones, x[...], dims, precision=lax.Precision.HIGHEST, preferred_element_type=F32
        )
        for x in (squares, inners)
    ]
    total = jnp.where(lax.broadcasted_iota(jnp.int32, (8, TOK), 0) < 4, ss, dd)
    if flip:
        total = total + previous[...]
    sums[...] = total


def cross(flip, attn, q, state, early, w, before, seg, gain, previous=()):
    return call(
        functools.partial(cross_kernel, flip), "cross", 1.2e9,
        [attn, q, state, early, w, before, seg, gain, *previous],
        [half_shape(F32), vmem((STATE_ROWS, HD), BF16), vmem((8, TOK), F32)], (),
        [pltpu.VMEM((TOK, HD), F32), pltpu.VMEM((TOK, HD), F32)],
    )


def scales(sums, rinv_ref, back_ref):
    own, one, two, three = [r[...] for r in sums]
    total = (own + one) + (two + three)
    rinv = lax.rsqrt(total[0:1] * (1.0 / ATT) + EPSILON)
    back = rinv * rinv * rinv * total[4:5] * (1.0 / ATT)
    row = lax.broadcasted_iota(jnp.int32, (8, TOK), 0)
    both = jnp.where(
        row < 4, jnp.broadcast_to(rinv, (8, TOK)), jnp.broadcast_to(back, (8, TOK))
    )
    cols = jnp.transpose(both)
    rinv_ref[...] = jnp.broadcast_to(cols[:, 0:1], (TOK, HD))
    back_ref[...] = jnp.broadcast_to(cols[:, 4:5], (TOK, HD))


def grad_kernel(flip, ids, seg, attn, w, qt, gain, *rest):
    if flip:
        s0, s1, s2, s3, grad, out, late, rinv, back, gains = rest
        scales((s0, s1, s2, s3), rinv, back)
    else:
        rinv, back, grad, out, late, gains = rest
    base = base_column(ids, flip)
    start0, _, start1, end1 = split_ends(seg)
    join = flag(start0 == start1)
    out[STATE_ROWS : STATE_ROWS + TILE, :] = info_tile(8.0 - end1, 8.0 - start0)

    def body(g):
        for j in range(GROUP):
            h = g * GROUP + j
            c, rows = head_columns(h), head_rows(h)
            far_c = span(base + h * HD, HD)
            a = attn[:, c]
            gated = w[:, far_c] * rinv[...]
            gains[pl.ds(h, 1), :] = jnp.sum(gated * a, axis=0, keepdims=True)
            x = (gated * gain[:, far_c] - a * back[...]).astype(BF16)
            grad[:, c] = x
            one = dot(qt[rows, 0:BLOCK], x[0:BLOCK], 1, 0)
            two = dot(qt[rows, BLOCK:TOK], x[BLOCK:TOK], 1, 0)
            late[rows, :] = two
            out[rows, :] = (one + two * join).astype(BF16)

    each_group(body)
    out[STATE_ROWS + TILE : STATE_ROWS + 2 * TILE, :] = split_tile(gains[...])


def grad_attn(flip, seg, attn, w, qt, gain, extra):
    outs = [
        half_shape(BF16), vmem((STATE_ROWS + 2 * TILE, HD), BF16), vmem((STATE_ROWS, HD), F32)
    ]
    if flip:
        outs += [vmem((TOK, HD), F32), vmem((TOK, HD), F32)]
    return call(
        functools.partial(grad_kernel, flip), "grad_attn", 1.2e9,
        [seg, attn, w, qt, gain, *extra], outs, (), [pltpu.VMEM((8, HD), F32)],
    )


def local_grads_kernel(flip, ids, q, k, v, grad, s0, s1, w0, w1, m0, m1, before, _, *rest):
    dq_far, dk, dv, token, dq, sems = rest[-6:]
    base = base_column(ids, flip)
    token[...] = jnp.zeros_like(token)

    def body(g):
        for j in range(GROUP):
            h = g * GROUP + j
            c = head_columns(h)
            qh, kh, vh, gh = q[:, c], k[:, c], v[:, c], grad[:, c]
            cut = gh * before[...]
            for n, t in BLOCKS:
                d = masked(gh[t], vh[t], (m0, m1)[n])
                w = (w0, w1)[n][head_rows(h, BLOCK), :]
                hop = dot(cut[t], (s0, s1)[n][head_rows(h), :], 1, 1)
                dq[t, c] = (dot(d, kh[t], 1, 0) + hop).astype(BF16)
                dk[t, c] = dot(d, qh[t], 0, 0)
                dv[t, c] = dot(w, gh[t], 0, 0)
        store(dq, g * SPAN, base + g * SPAN, dq_far, sems.at[g]).start()

    each_group(body)
    for g in range(GROUPS):
        store(dq, g * SPAN, base + g * SPAN, dq_far, sems.at[g]).wait()


def local_grads(flip, q, k, v, g, states, weights, masks, before, after, done=()):
    near = [q, k, v, g, *states, *weights, *masks, before, after]
    return call(
        functools.partial(local_grads_kernel, flip), "local_grads", 5e9, near,
        [far(), half_shape(F32), half_shape(F32), TOKEN], done,
        [pltpu.VMEM((TOK, WIDE), BF16), pltpu.SemaphoreType.DMA((GROUPS,))],
        {len(near): 0} if done else None,
    )


def gates_kernel(ids, keep, send, gi, w, rinv, gain, _, lo_far, gg_far, token, lo, gg, sems):
    token[...] = jnp.zeros_like(token)
    copies = []
    for flip, attn in enumerate((keep, send)):
        base = base_column(ids, flip)

        def body(g, flip=flip, attn=attn, base=base):
            for j in range(GROUP):
                h = g * GROUP + j
                far_c = span(base + h * HD, HD)
                out_c = head_columns(flip * HEADS + h)
                sig, other = sigmoid_parts(gi[:, far_c])
                scaled = attn[:, head_columns(h)] * rinv[...] * gain[:, far_c]
                lo[:, out_c] = (scaled * sig).astype(BF16)
                gg[:, out_c] = (scaled * w[:, far_c] * other).astype(BF16)
            at, to = flip * WIDE + g * SPAN, base + g * SPAN
            store(lo, at, to, lo_far, sems.at[0, flip, g]).start()
            store(gg, at, to, gg_far, sems.at[1, flip, g]).start()

        each_group(body)
        for g in range(GROUPS):
            at, to = flip * WIDE + g * SPAN, base + g * SPAN
            copies.append(store(lo, at, to, lo_far, sems.at[0, flip, g]))
            copies.append(store(gg, at, to, gg_far, sems.at[1, flip, g]))
    for copy in copies:
        copy.wait()


def gates(keep, send, gi, w, rinv, gain, after):
    return call(
        gates_kernel, "gates", 3e9, [keep, send, gi, w, rinv, gain, after],
        [far(), far(), TOKEN], (),
        [
            pltpu.VMEM((TOK, 2 * WIDE), BF16),
            pltpu.VMEM((TOK, 2 * WIDE), BF16),
            pltpu.SemaphoreType.DMA((2, 2, GROUPS)),
        ],
    )


def finish_kernel(flip, ids, dk_in, dv_in, k, v, later, late, seg, after, *rest):
    if flip:
        total, _, _, dk_far, dv_far, gain_far, dk, dv, sems, gain, gain_sem = rest
        core = ids[0]
        at = [pl.ds(pl.multiple_of(n * 8, 8), 8) for n in (core, 1 - core)]
        gain[at[0], :] = joined_tile(total[...])
        gain[at[1], :] = joined_tile(later[STATE_ROWS : STATE_ROWS + TILE, :])
        gain_copy = pltpu.make_async_copy(gain, gain_far, gain_sem)
        gain_copy.start()
    else:
        dk_far, dv_far, dk, dv, sems = rest
    base = base_column(ids, flip)
    _, _, start1, end1 = split_ends(seg)
    join = flag(start1 == end1)
    copies = []
    for g in range(HEADS // FINE):
        for h in range(g * FINE, (g + 1) * FINE):
            c, rows = head_columns(h), head_rows(h)
            one = later[rows, :]
            both = ((late[rows, :] + one.astype(F32) * join).astype(BF16), one)
            kh, vh = k[:, c] * after[...], v[:, c] * after[...]
            for n, t in BLOCKS:
                dk[t, c] = (dk_in[t, c] + dot(vh[t], both[n], 1, 1)).astype(BF16)
                dv[t, c] = (dv_in[t, c] + dot(kh[t], both[n], 1, 0)).astype(BF16)
        for n, (ref, far_ref) in enumerate(((dk, dk_far), (dv, dv_far))):
            at = g * FINE_SPAN
            copy = store(ref, at, base + at, far_ref, sems.at[n, g], FINE_SPAN)
            copy.start()
            copies.append(copy)
    for copy in copies:
        copy.wait()
    if flip:
        gain_copy.wait()


def finish(flip, dk, dv, k, v, later, late, seg, after, total=(), done=()):
    near = [dk, dv, k, v, later, late, seg, after, *total]
    outs = [far(), far()]
    scratch = [
        pltpu.VMEM((TOK, WIDE), BF16),
        pltpu.VMEM((TOK, WIDE), BF16),
        pltpu.SemaphoreType.DMA((2, HEADS // FINE)),
    ]
    if flip:
        outs += [jax.ShapeDtypeStruct((TILE, HD), F32)]
        scratch += [pltpu.VMEM((TILE, HD), F32), pltpu.SemaphoreType.DMA]
    return call(
        functools.partial(finish_kernel, flip), "finish", 1.2e9, near, outs, done, scratch,
        {len(near): 0, len(near) + 1: 1} if flip else None,
    )


def place(ids, reverse):
    core, x, z = ids[0], ids[1], ids[2]
    return (1 - core, 3 - x, 3 - z) if reverse else (core, x, z)


def info_rows(ref, at):
    tile = ref[at : at + TILE, :].astype(F32)
    return tile[0:1], tile[8:9]


def sorted_cores(first_core, own, other):
    return jnp.where(first_core, own, other), jnp.where(first_core, other, own)


def quarter_rows(ids, m):
    return pl.ds(pl.multiple_of((ids[1] ^ m) * QUARTER, QUARTER), QUARTER)


def chip_kernel(reverse, gain, ids, own_ref, other_ref, *outs):
    vcore, _, _ = place(ids, reverse)
    first_core = vcore == 0
    low_own, high_own = info_rows(own_ref, STATE_ROWS)
    low_other, high_other = info_rows(other_ref, STATE_ROWS)
    low_a, _ = sorted_cores(first_core, low_own, low_other)
    high_a, high_b = sorted_cores(first_core, high_own, high_other)
    join = flag(high_a == high_b)
    own_weight = jnp.where(first_core, join, 1.0)
    other_weight = jnp.where(first_core, 1.0, join)
    for m, out in enumerate(outs):
        rows = quarter_rows(ids, m)
        total = own_ref[rows, :].astype(F32) * own_weight
        total = total + other_ref[rows, :].astype(F32) * other_weight
        out[0:QUARTER, :] = total.astype(BF16)
        out[QUARTER : QUARTER + TILE, :] = info_tile(low_a, high_b)
        if gain:
            at = slice(STATE_ROWS + TILE, STATE_ROWS + 2 * TILE)
            both = joined_tile(own_ref[at, :]) + joined_tile(other_ref[at, :])
            out[QUARTER + TILE : QUARTER + 2 * TILE, :] = split_tile(both)


def row_kernel(gain, ids, p0, p1, p2, p3, _, out):
    parts = (p0, p1, p2, p3)
    info = [info_rows(p, QUARTER) for p in parts]
    low = jnp.minimum(jnp.minimum(info[0][0], info[1][0]), jnp.minimum(info[2][0], info[3][0]))
    high = jnp.maximum(jnp.maximum(info[0][1], info[1][1]), jnp.maximum(info[2][1], info[3][1]))
    total = None
    for p, (_, own_high) in zip(parts, info):
        term = p[0:QUARTER, :].astype(F32) * flag(own_high == high)
        total = term if total is None else total + term
    out[0:QUARTER, :] = total.astype(BF16)
    out[QUARTER : QUARTER + TILE, :] = info_tile(low, high)
    if gain:
        g = [joined_tile(p[QUARTER + TILE : QUARTER + 2 * TILE, :]) for p in parts]
        out[QUARTER + TILE : QUARTER + 2 * TILE, :] = split_tile((g[0] + g[1]) + (g[2] + g[3]))


def entry_kernel(reverse, gain, ids, p0, p1, p2, p3, *rest):
    _, vx, vz = place(ids, reverse)
    parts = (p0, p1, p2, p3)
    outs = rest[-5 if gain else -4 :]
    if gain:
        rows = rest[1:4]
        earlier = [(vz ^ n) < vz for n in range(1, 4)]
    else:
        rows = rest[1:3]
        earlier = [vz >= 1, vz >= 2]
    info = [info_rows(p, QUARTER) for p in parts]
    row_high = [info_rows(t, QUARTER)[1] for t in rows]
    for m in range(4):
        low = info[m][0]
        total = jnp.zeros((QUARTER, HD), F32)
        for n in range(4):
            if n != m:
                weight = flag(info[n][1] == low) * flag((vx ^ n) < (vx ^ m))
                total = total + parts[n][0:QUARTER, :].astype(F32) * weight
        for row, high, before in zip(rows, row_high, earlier):
            weight = flag(high == low) * flag(before)
            total = total + row[0:QUARTER, :].astype(F32) * weight
        outs[m][...] = total.astype(BF16)
    if gain:
        g = [joined_tile(t[QUARTER + TILE : QUARTER + 2 * TILE, :]) for t in rest[0:4]]
        outs[4][...] = split_tile((g[0] + g[1]) + (g[2] + g[3]))


def device_kernel(reverse, gain, ids, own_ref, other_ref, e0, e1, e2, e3, _, *rest):
    keep, send = rest[-2:]
    vcore, _, _ = place(ids, reverse)
    first_core = vcore == 0
    low_own, high_own = info_rows(own_ref, STATE_ROWS)
    low_other, high_other = info_rows(other_ref, STATE_ROWS)
    low_a, low_b = sorted_cores(first_core, low_own, low_other)
    high_a, _ = sorted_cores(first_core, high_own, high_other)
    from_a = flag(high_a == low_b)
    from_chip = flag(low_a == low_b)
    for m, ref in enumerate((e0, e1, e2, e3)):
        rows = quarter_rows(ids, m)
        entry = ref[...].astype(F32)
        a = jnp.where(first_core, own_ref[rows, :].astype(F32), other_ref[rows, :].astype(F32))
        second = a * from_a + entry * from_chip
        keep[rows, :] = jnp.where(first_core, entry, second).astype(BF16)
        send[rows, :] = jnp.where(first_core, second, entry).astype(BF16)
    if gain:
        send[STATE_ROWS : STATE_ROWS + TILE, :] = rest[0][...]


def glue(kernel, name, rows, *args):
    return call(kernel, name, 5e8, args, [vmem((r, HD), BF16) for r in rows])


def swap(x, axis, size, bits):
    return lax.ppermute(x, axis, [(i, i ^ bits) for i in range(size)])


def chip_swap(x):
    return swap(x, "ctx", 32, 1)


def row_swap(x, m):
    return swap(x, "ctx", 32, m << 1)


def plane_swap(x, m):
    return swap(x, "ctx", 32, m << 3)


def plane_shift(x):
    return lax.ppermute(x, "ctx", [(i, (i + 8) % 32) for i in range(32)])


def scan(own, other, reverse, gain, beside_x, beside_z, beside_back):
    extra = TILE if gain else 0
    rows = QUARTER + TILE + extra
    sent = glue(
        functools.partial(chip_kernel, reverse, gain), "chip_sum", [rows] * 4, own, other
    )
    parts = [sent[0]] + [row_swap(sent[m], m) for m in range(1, 4)]
    token = beside_x(sent[0])
    total = glue(functools.partial(row_kernel, gain), "row_sum", [rows], *parts, token)[0]
    if gain:
        totals = [total] + [plane_swap(total, m) for m in range(1, 4)]
    else:
        totals = [total, plane_shift(total), plane_swap(total, 2)]
    token = beside_z(total)
    entries = glue(
        functools.partial(entry_kernel, reverse, gain),
        "entry",
        [QUARTER] * 4 + ([TILE] if gain else []),
        *parts,
        *totals,
        token,
    )
    tail = entries[4:]
    back = [entries[0]] + [row_swap(entries[m], m) for m in range(1, 4)]
    token = beside_back(entries[0])
    keep, send = glue(
        functools.partial(device_kernel, reverse, gain),
        "device_entry",
        [STATE_ROWS, STATE_ROWS + extra],
        own,
        other,
        *back,
        token,
        *tail,
    )
    return keep, chip_swap(send), tail


def on_device(query, keys, values, gate_input, grad_output, norm_gain, segment_ids):
    gain = norm_gain.reshape(1, -1)

    k_send, v_send, sent, early_send, seg, before, after, last, first = local_state(
        keys, values, segment_ids.reshape(1, TOK)
    )
    other = chip_swap(sent)
    k_keep, v_keep, own, early_keep = local_state(keys, values, None, seg, last)
    made = {}

    def intra_keep(token):
        made["keep"] = intra(k_keep, v_keep, first, query, token, seg=seg)
        return made["keep"][5]

    def intra_send(token):
        made["send"] = intra(k_send, v_send, first, query, token, masks=made["keep"][6:8])
        return made["send"][5]

    def prepare_both(token):
        made["gate"] = prepare(token, grad_output, gate_input)
        return made["gate"][2]

    state_keep, state_send, _ = scan(own, other, False, False, intra_keep, intra_send, prepare_both)
    q_keep, attn_keep, w0_keep, w1_keep, qt_keep, _, *masks = made["keep"]
    q_send, attn_send, w0_send, w1_send, qt_send, _ = made["send"]
    gated, gate, _ = made["gate"]

    attn_keep, second_keep, sums = cross(
        0, attn_keep, q_keep, state_keep, early_keep, gated, before, seg, gain
    )
    attn_send, second_send, sums = cross(
        1, attn_send, q_send, state_send, early_send, gated, before, seg, gain, (sums,)
    )
    sums = [sums] + [swap(sums, "tp", 4, m) for m in range(1, 4)]

    g_send, sent, late_send, rinv, back = grad_attn(
        1, seg, attn_send, gated, qt_send, gain, sums
    )
    other = chip_swap(sent)
    g_keep, own, late_keep = grad_attn(0, seg, attn_keep, gated, qt_keep, gain, (rinv, back))

    def grads_keep(token):
        made["gk"] = local_grads(
            0, q_keep, k_keep, v_keep, g_keep, (state_keep, second_keep), (w0_keep, w1_keep),
            masks, before, token,
        )
        return made["gk"][3]

    def grads_send(token):
        made["gs"] = local_grads(
            1, q_send, k_send, v_send, g_send, (state_send, second_send), (w0_send, w1_send),
            masks, before, token, (made["gk"][0],),
        )
        return made["gs"][3]

    def gates_both(token):
        made["out"] = gates(attn_keep, attn_send, gate, gated, rinv, gain, token)
        return made["out"][2]

    later_keep, later_send, total = scan(
        own, other, True, True, grads_keep, grads_send, gates_both
    )
    _, dk_keep, dv_keep, _ = made["gk"]
    grad_query, dk_send, dv_send, _ = made["gs"]
    layer_out, grad_gate, _ = made["out"]
    done = finish(0, dk_keep, dv_keep, k_keep, v_keep, later_keep, late_keep, seg, after)
    grad_keys, grad_values, grad_gain = finish(
        1, dk_send, dv_send, k_send, v_send, later_send, late_send, seg, after, (total[0],),
        tuple(done),
    )
    grad_gain = grad_gain.reshape(-1)
    return layer_out, grad_query, grad_keys, grad_values, grad_gate, grad_gain


def solution(mesh):
    in_specs = (P("ctx", "tp"),) * 5 + (P("tp"), P("ctx"))
    out_specs = (P("ctx", "tp"),) * 5 + (P("tp"),)
    return jax.shard_map(
        on_device, mesh=mesh, in_specs=in_specs, out_specs=out_specs, check_vma=False
    )
```

time: 85.4 us -> 86.5 us (1.013)
  waiting for transfers between devices: 5.87 us -> 7.35 us
    ppermute x25 -> x23, waiting for transfers between devices: 5.87 us -> 6.77 us  [swap(): return lax.ppermute(x, axis, [(i, i ^ bits) for i in range(size)])]
    pallas_call x24 -> x22, Pallas kernels: 41.8 us -> 41.1 us  [call(): pl.pallas_call(placed, in_specs=[VM] * len(near) + [ANY] * len(distant),...]
    ppermute x25 -> x23, starting transfers between devices: 36.4 us -> 36 us  [swap(): return lax.ppermute(x, axis, [(i, i ^ bits) for i in range(size)])]
  transfers between devices with their start and end apart: 25 -> 24, of which waited for: 5 -> 7; matrix products, arithmetic and copies ran while one was open for 0% -> 0% of each run, Pallas kernels for 38% -> 36%
where the time goes in v3:
time: 86.5 us; the launch traced here: 86.3 us
  Pallas kernels  41.1 us (48%)
  starting transfers between devices  36.8 us (43%)
  waiting for transfers between devices  7.35 us (8%)
  between operations  1.05 us (1%)
    pallas_call x22, Pallas kernels, call(): pl.pallas_call(placed, in_specs=[VM] * len(near) + [ANY] * len(distant),...  41.1 us
    ppermute x23, starting transfers between devices, swap(): return lax.ppermute(x, axis, [(i, i ^ bits) for i in range(size)])  36 us
    ppermute x23, waiting for transfers between devices, swap(): return lax.ppermute(x, axis, [(i, i ^ bits) for i in range(size)])  6.77 us
  transfers between devices with their start and end apart: 24, of which 7 were waited for; matrix products, arithmetic and copies ran while one was open for 0% of the time, Pallas kernels for 36%

profile of v3, /device:TPU:1, one launch (start us, length us, event | category | flops | bytes accessed | tf_op | source)
XLA Modules:
  0.0 86.3 jit_solution(11782435951393023304)
XLA Ops:
  0.6 2.8 %local_state.2 = (bf16[512,1024]{1,0:T(8,128)(2,1)S(1)}, bf16[512,1024]{1,0:T(8,128)(2,1)S(1)}, bf16[1040,128]{1,0:T(8,128)(2,1)S(1)}, f32[1024,128]{1,0:T(8,128...) custom-call(bf16[512,2048]{1,0:T(8,128)(2,1)} %refs_2_.2, ...), custom_call_target="tpu_custom_call" | custom-call | flops 1000000000 | bytes 3333333 | tf_op jit(solution)/shard_map/local_state/pallas_call | solution.py:56
  3.5 1.7 %collective-permute-start = (bf16[1040,128]{1,0:T(8,128)(2,1)S(1)}, bf16[1040,128]{1,0:T(8,128)(2,1)S(1)}, u32[]{:S(2)}, u32[]{:S(2)}) collective-permute-start(bf16[1040,128]{1,0:T(8,128)(2,1)S(1)} %get-tuple-element.93), channel_id=1, source_target_pairs={{0,4},{4,0},{8,12},{12,8},{16,20},{20,16},{24,28},{28,24},{32,36},... | collective-permute-start | bytes 798728 | tf_op jit(solution)/shard_map/ppermute | solution.py:642
  5.1 2.3 %local_state.3 = (bf16[512,1024]{1,0:T(8,128)(2,1)S(1)}, bf16[512,1024]{1,0:T(8,128)(2,1)S(1)}, bf16[1040,128]{1,0:T(8,128)(2,1)S(1)}, f32[1024,128]{1,0:T(8,128)S(1)}) custom-call(s32[1,512]{1,0:T(1,128)S(1)} %get-tuple-element.87.refs_0_.refs_3_.refs_6_, bf16[512,128]{1,0:T(8,128)(2,1)S(1)} %get-tuple-element.88.refs_1_, bf16[512,2048]{1,0:T(8,128)(2,1)} %refs_2_.2, ...), custom_call_target="tpu_custom_call" | custom-call | flops 1000000000 | bytes 3333333 | tf_op jit(solution)/shard_map/local_state/pallas_call | solution.py:56
  7.4 0.0 collective-permute-done.refs_1_
  7.4 0.1 chip_sum.2
  7.5 1.4 %collective-permute-start.1 = (bf16[272,128]{1,0:T(8,128)(2,1)S(1)}, bf16[272,128]{1,0:T(8,128)(2,1)S(1)}, u32[]{:S(2)}, u32[]{:S(2)}) collective-permute-start(bf16[272,128]{1,0:T(8,128)(2,1)S(1)} %get-tuple-element.97), channel_id=1, source_target_pairs={{0,8},{4,12},{8,0},{12,4},{16,24},{20,28},{24,16},{28,20},{32,40},... | collective-permute-start | bytes 208904 | tf_op jit(solution)/shard_map/ppermute | solution.py:642
  8.9 2.4 %collective-permute-start.2 = (bf16[272,128]{1,0:T(8,128)(2,1)S(1)}, bf16[272,128]{1,0:T(8,128)(2,1)S(1)}, u32[]{:S(2)}, u32[]{:S(2)}) collective-permute-start(bf16[272,128]{1,0:T(8,128)(2,1)S(1)} %get-tuple-element.98), channel_id=1, source_target_pairs={{0,16},{4,20},{8,24},{12,28},{16,0},{20,4},{24,8},{28,12},{32,48},... | collective-permute-start | bytes 208904 | tf_op jit(solution)/shard_map/ppermute | solution.py:642
  11.3 0.1 collective-permute-start.3
  11.5 3.0 %intra.2 = (bf16[512,1024]{1,0:T(8,128)(2,1)S(1)}, f32[512,1024]{1,0:T(8,128)S(1)}, bf16[2048,256]{1,0:T(8,128)(2,1)S(1)}, bf16[2048,256]{1,0:T(8,128)(2,1)S(1)}...) custom-call(bf16[512,1024]{1,0:T(8,128)(2,1)S(1)} %get-tuple-element, ...), custom_call_target="tpu_custom_call" | custom-call | flops 3000000000 | bytes 10000000 | tf_op jit(solution)/shard_map/intra/pallas_call | solution.py:56
  14.5 0.7 collective-permute-done.2.refs_2_
  15.2 1.2 %collective-permute-done.3.refs_3_ = bf16[272,128]{1,0:T(8,128)(2,1)S(1)} collective-permute-done((bf16[272,128]{1,0:T(8,128)(2,1)S(1)}, bf16[272,128]{1,0:T(8,128)(2,1)S(1)}, u32[]{:S(2)}, u32[]{:S(2)}) %collective-permute-start.3) | collective-permute-done | bytes 69664 | tf_op jit(solution)/shard_map/ppermute | solution.py:642
  16.3 0.1 row_sum.2.refs_5_.refs_4_
  16.4 3.7 %collective-permute-start.5 = (bf16[272,128]{1,0:T(8,128)(2,1)S(1)}, bf16[272,128]{1,0:T(8,128)(2,1)S(1)}, u32[]{:S(2)}, u32[]{:S(2)}) collective-permute-start(bf16[272,128]{1,0:T(8,128)(2,1)S(1)} %row_sum.2.refs_5_.refs_4_), channel_id=1, source_target_pairs={{0,64},{4,68},{8,72},{12,76},{16,80},{20,84},{24,88},{28,92},{32,9... | collective-permute-start | bytes 208904 | tf_op jit(solution)/shard_map/ppermute | solution.py:642
  20.1 0.7 collective-permute-start.4
  20.8 3.0 %intra.3 = (bf16[512,1024]{1,0:T(8,128)(2,1)S(1)}, f32[512,1024]{1,0:T(8,128)S(1)}, bf16[2048,256]{1,0:T(8,128)(2,1)S(1)}, bf16[2048,256]{1,0:T(8,128)(2,1)S(1)}...) custom-call(bf16[512,1024]{1,0:T(8,128)(2,1)S(1)} %get-tuple-element.101.refs_0_.refs_1_.refs_2_, ...), custom_call_target="tpu_custom_call" | custom-call | flops 3000000000 | bytes 10000000 | tf_op jit(solution)/shard_map/intra/pallas_call | solution.py:56
  23.8 0.0 collective-permute-done.5.refs_6_
  23.8 0.6 collective-permute-done.4.refs_5_
  24.4 0.3 entry.2
  24.7 0.2 collective-permute-start.6
  24.9 2.5 %collective-permute-start.7 = (bf16[256,128]{1,0:T(8,128)(2,1)S(1)}, bf16[256,128]{1,0:T(8,128)(2,1)S(1)}, u32[]{:S(2)}, u32[]{:S(2)}) collective-permute-start(bf16[256,128]{1,0:T(8,128)(2,1)S(1)} %get-tuple-element.108), channel_id=1, source_target_pairs={{0,16},{4,20},{8,24},{12,28},{16,0},{20,4},{24,8},{28,12},{32,48},... | collective-permute-start | bytes 196616 | tf_op jit(solution)/shard_map/ppermute | solution.py:642
  27.5 1.2 %collective-permute-start.8 = (bf16[256,128]{1,0:T(8,128)(2,1)S(1)}, bf16[256,128]{1,0:T(8,128)(2,1)S(1)}, u32[]{:S(2)}, u32[]{:S(2)}) collective-permute-start(bf16[256,128]{1,0:T(8,128)(2,1)S(1)} %get-tuple-element.109), channel_id=1, source_target_pairs={{0,24},{4,28},{8,16},{12,20},{16,8},{20,12},{24,0},{28,4},{32,56},... | collective-permute-start | bytes 196616 | tf_op jit(solution)/shard_map/ppermute | solution.py:642
  28.7 2.5 %prepare.1 = (f32[512,2048]{1,0:T(8,128)S(1)}, bf16[512,2048]{1,0:T(8,128)(2,1)S(1)}, f32[8,128]{1,0:T(8,128)S(1)}) custom-call(bf16[256,128]{1,0:T(8,128)(2,1)S(1)} %get-tuple-element.106.refs_0_.refs_2_, bf16[512,2048]{1,0:T(8,128)(2,1)} %refs_1_.3, bf16[512,2048]{1,0:T(8,128)(2,1)} %refs_2_.3), custom_call_target="tpu_custom_call" | custom-call | flops 3000000000 | bytes 10000000 | tf_op jit(solution)/shard_map/prepare/pallas_call | solution.py:56
  31.2 0.6 collective-permute-done.8.refs_5_
  31.8 0.2 device_entry.2
  32.0 3.7 %collective-permute-start.9 = (bf16[1024,128]{1,0:T(8,128)(2,1)S(1)}, bf16[1024,128]{1,0:T(8,128)(2,1)S(1)}, u32[]{:S(2)}, u32[]{:S(2)}) collective-permute-start(bf16[1024,128]{1,0:T(8,128)(2,1)S(1)} %get-tuple-element.118), channel_id=1, source_target_pairs={{0,4},{4,0},{8,12},{12,8},{16,20},{20,16},{24,28},{28,24},{32,36},... | collective-permute-start | bytes 786440 | tf_op jit(solution)/shard_map/ppermute | solution.py:642
  35.8 1.9 %cross.2 = (f32[512,1024]{1,0:T(8,128)S(1)}, bf16[1024,128]{1,0:T(8,128)(2,1)S(1)}, f32[8,512]{1,0:T(8,128)S(1)}) custom-call(f32[512,1024]{1,0:T(8,128)S(1)} %get-tuple-element.95.refs_0_, bf16[512,1024]{1,0:T(8,128)(2,1)S(1)} %get-tuple-element.96.refs_1_.refs_0_, bf16[1024,128]{1,0:T(8,128)(2,1)S(1)} %get-tuple-element.111.refs_2_.refs_4_, ...), custom_call_target="tpu_custom_call" | custom-call | flops 1200000000 | bytes 4000000 | tf_op jit(solution)/shard_map/cross/pallas_call | solution.py:56
  37.7 0.0 collective-permute-done.9.refs_2_.refs_4_
  37.7 1.9 %cross.3 = (f32[512,1024]{1,0:T(8,128)S(1)}, bf16[1024,128]{1,0:T(8,128)(2,1)S(1)}, f32[8,512]{1,0:T(8,128)S(1)}) custom-call(f32[512,1024]{1,0:T(8,128)S(1)} %get-tuple-element.116.refs_0_, bf16[512,1024]{1,0:T(8,128)(2,1)S(1)} %get-tuple-element.117.refs_1_.refs_0_, bf16[1024,128]{1,0:T(8,128)(2,1)S(1)} %collective-permute-done.9.refs_2_.refs_4_, ...), custom_call_target="tpu_custom_call" | custom-call | flops 1200000000 | bytes 4000000 | tf_op jit(solution)/shard_map/cross/pallas_call | solution.py:56
  39.6 2.8 %collective-permute-start.12 = (f32[8,512]{1,0:T(8,128)S(1)}, f32[8,512]{1,0:T(8,128)S(1)}, u32[]{:S(2)}, u32[]{:S(2)}) collective-permute-start(f32[8,512]{1,0:T(8,128)S(1)} %get-tuple-element.124.refs_5_), channel_id=1, source_target_pairs={{0,3},{1,2},{2,1},{3,0},{4,7},{5,6},{6,5},{7,4},{8,11},{9,10},{10,... | collective-permute-start | bytes 49160 | tf_op jit(solution)/shard_map/ppermute | solution.py:642
  42.4 0.4 collective-permute-start.11
  42.7 0.3 collective-permute-start.10
  43.0 0.5 collective-permute-done.12.refs_8_
  43.5 3.0 %collective-permute-done.11.refs_7_ = f32[8,512]{1,0:T(8,128)S(1)} collective-permute-done((f32[8,512]{1,0:T(8,128)S(1)}, f32[8,512]{1,0:T(8,128)S(1)}, u32[]{:S(2)}, u32[]{:S(2)}) %collective-permute-start.11) | collective-permute-done | bytes 16416 | tf_op jit(solution)/shard_map/ppermute | solution.py:642
  46.5 0.0 collective-permute-done.10.refs_6_
  46.5 1.7 %grad_attn.2 = (bf16[512,1024]{1,0:T(8,128)(2,1)S(1)}, bf16[1056,128]{1,0:T(8,128)(2,1)S(1)}, f32[1024,128]{1,0:T(8,128)S(1)}, f32[512,128]{1,0:T(8,128)S(1)}, f32[512,128]{1,0:T(8,128)S(1)}) custom-call(s32[1,512]{1,0:T(1,128)S(1)} %get-tuple-element.87.refs_0_.refs_3_.refs_6_, f32[512,1024]{1,0:T(8,128)S(1)} %get-tuple-element.121.refs_1_, ...), custom_call_target="tpu_custom_call" | custom-call | flops 1200000000 | bytes 4000000 | tf_op jit(solution)/shard_map/grad_attn/pallas_call | solution.py:56
  48.2 1.7 %collective-permute-start.13 = (bf16[1056,128]{1,0:T(8,128)(2,1)S(1)}, bf16[1056,128]{1,0:T(8,128)(2,1)S(1)}, u32[]{:S(2)}, u32[]{:S(2)}) collective-permute-start(bf16[1056,128]{1,0:T(8,128)(2,1)S(1)} %get-tuple-element.129), channel_id=1, source_target_pairs={{0,4},{4,0},{8,12},{12,8},{16,20},{20,16},{24,28},{28,24},{32,36},... | collective-permute-start | bytes 811016 | tf_op jit(solution)/shard_map/ppermute | solution.py:642
  49.9 1.5 %grad_attn.3 = (bf16[512,1024]{1,0:T(8,128)(2,1)S(1)}, bf16[1056,128]{1,0:T(8,128)(2,1)S(1)}, f32[1024,128]{1,0:T(8,128)S(1)}) custom-call(s32[1,512]{1,0:T(1,128)S(1)} %get-tuple-element.87.refs_0_.refs_3_.refs_6_, f32[512,1024]{1,0:T(8,128)S(1)} %get-tuple-element.115.refs_1_.refs_0_, f32[512,2048]{1,0:T(8,128)S(1)} %get-tuple-element.113.refs_4_.refs_2_.refs_3_, ...), custom_call_target="tpu_custom_call" | custom-call | flops 1200000000 | bytes 4000000 | tf_op jit(solution)/shard_map/grad_attn/pallas_call | solution.py:56
  51.4 0.0 collective-permute-done.13.refs_1_
  51.4 0.1 chip_sum.3
  51.5 0.1 collective-permute-start.14
  51.6 3.0 %collective-permute-start.15 = (bf16[288,128]{1,0:T(8,128)(2,1)S(1)}, bf16[288,128]{1,0:T(8,128)(2,1)S(1)}, u32[]{:S(2)}, u32[]{:S(2)}) collective-permute-start(bf16[288,128]{1,0:T(8,128)(2,1)S(1)} %get-tuple-element.132), channel_id=1, source_target_pairs={{0,16},{4,20},{8,24},{12,28},{16,0},{20,4},{24,8},{28,12},{32,48},... | collective-permute-start | bytes 221192 | tf_op jit(solution)/shard_map/ppermute | solution.py:642
  54.6 0.8 collective-permute-start.16
  55.5 5.8 %local_grads.2 = (bf16[512,2048]{1,0:T(8,128)(2,1)}, f32[512,1024]{1,0:T(8,128)S(1)}, f32[512,1024]{1,0:T(8,128)S(1)}, f32[8,128]{1,0:T(8,128)S(1)}) custom-call(bf16[512,1024]{1,0:T(8,128)(2,1)S(1)} %get-tuple-element.96.refs_1_.refs_0_, bf16[512,1024]{1,0:T(8,128)(2,1)S(1)} %get-tuple-element.89.refs_0_.refs_1_.refs_2_, ...), custom_call_target="tpu_custom_call" | custom-call | flops 5000000000 | bytes 16666666 | tf_op jit(solution)/shard_map/local_grads/pallas_call | solution.py:56
  61.3 0.0 collective-permute-done.15.refs_2_
  61.3 0.0 collective-permute-done.16.refs_3_
  61.3 0.1 row_sum.3.refs_11_.refs_4_
  61.4 0.6 collective-permute-start.19
  61.9 1.1 %collective-permute-start.18 = (bf16[288,128]{1,0:T(8,128)(2,1)S(1)}, bf16[288,128]{1,0:T(8,128)(2,1)S(1)}, u32[]{:S(2)}, u32[]{:S(2)}) collective-permute-start(bf16[288,128]{1,0:T(8,128)(2,1)S(1)} %row_sum.3.refs_11_.refs_4_), channel_id=1, source_target_pairs={{0,64},{4,68},{8,72},{12,76},{16,80},{20,84},{24,88},{28,92},{32,9... | collective-permute-start | bytes 221192 | tf_op jit(solution)/shard_map/ppermute | solution.py:642
  63.0 1.7 %collective-permute-start.17 = (bf16[288,128]{1,0:T(8,128)(2,1)S(1)}, bf16[288,128]{1,0:T(8,128)(2,1)S(1)}, u32[]{:S(2)}, u32[]{:S(2)}) collective-permute-start(bf16[288,128]{1,0:T(8,128)(2,1)S(1)} %row_sum.3.refs_11_.refs_4_), channel_id=1, source_target_pairs={{0,32},{4,36},{8,40},{12,44},{16,48},{20,52},{24,56},{28,60},{32,0... | collective-permute-start | bytes 221192 | tf_op jit(solution)/shard_map/ppermute | solution.py:642
  64.7 5.8 %local_grads.3 = (bf16[512,2048]{1,0:T(8,128)(2,1)}, f32[512,1024]{1,0:T(8,128)S(1)}, f32[512,1024]{1,0:T(8,128)S(1)}, f32[8,128]{1,0:T(8,128)S(1)}) custom-call(bf16[512,1024]{1,0:T(8,128)(2,1)S(1)} %get-tuple-element.117.refs_1_.refs_0_, bf16[512,1024]{1,0:T(8,128)(2,1)S(1)} %get-tuple-element.101.refs_0_.refs_1_.refs_2_, ...), custom_call_target="tpu_custom_call", output_to_operand_aliasing={{0}: (12, {})} | custom-call | flops 5000000000 | bytes 16666666 | tf_op jit(solution)/shard_map/local_grads/pallas_call | solution.py:56
  70.5 0.0 collective-permute-done.19.refs_7_
  70.5 0.0 collective-permute-done.18.refs_6_
  70.5 0.3 entry.3
  70.8 0.1 collective-permute-start.20
  70.9 3.0 %collective-permute-start.21 = (bf16[256,128]{1,0:T(8,128)(2,1)S(1)}, bf16[256,128]{1,0:T(8,128)(2,1)S(1)}, u32[]{:S(2)}, u32[]{:S(2)}) collective-permute-start(bf16[256,128]{1,0:T(8,128)(2,1)S(1)} %get-tuple-element.151), channel_id=1, source_target_pairs={{0,16},{4,20},{8,24},{12,28},{16,0},{20,4},{24,8},{28,12},{32,48},... | collective-permute-start | bytes 196616 | tf_op jit(solution)/shard_map/ppermute | solution.py:642
  73.9 0.9 collective-permute-start.22
  74.8 3.3 %gates.1 = (bf16[512,2048]{1,0:T(8,128)(2,1)}, bf16[512,2048]{1,0:T(8,128)(2,1)}, f32[8,128]{1,0:T(8,128)S(1)}) custom-call(f32[512,1024]{1,0:T(8,128)S(1)} %get-tuple-element.115.refs_1_.refs_0_, f32[512,1024]{1,0:T(8,128)S(1)} %get-tuple-element.121.refs_1_, bf16[512,2048]{1,0:T(8,128)(2,1)S(1)} %get-tuple-element.122.refs_2_, ...), custom_call_target="tpu_custom_call" | custom-call | flops 3000000000 | bytes 10000000 | tf_op jit(solution)/shard_map/gates/pallas_call | solution.py:56
  78.0 0.0 collective-permute-done.20.refs_3_
  78.1 0.0 collective-permute-done.21.refs_4_
  78.1 0.9 %collective-permute-done.22.refs_5_ = bf16[256,128]{1,0:T(8,128)(2,1)S(1)} collective-permute-done((bf16[256,128]{1,0:T(8,128)(2,1)S(1)}, bf16[256,128]{1,0:T(8,128)(2,1)S(1)}, u32[]{:S(2)}, u32[]{:S(2)}) %collective-permute-start.22) | collective-permute-done | bytes 65568 | tf_op jit(solution)/shard_map/ppermute | solution.py:642
  79.0 0.2 device_entry.3
  79.2 2.8 %collective-permute-start.23 = (bf16[1040,128]{1,0:T(8,128)(2,1)S(1)}, bf16[1040,128]{1,0:T(8,128)(2,1)S(1)}, u32[]{:S(2)}, u32[]{:S(2)}) collective-permute-start(bf16[1040,128]{1,0:T(8,128)(2,1)S(1)} %get-tuple-element.155), channel_id=1, source_target_pairs={{0,4},{4,0},{8,12},{12,8},{16,20},{20,16},{24,28},{28,24},{32,36},... | collective-permute-start | bytes 798728 | tf_op jit(solution)/shard_map/ppermute | solution.py:642
  82.0 2.0 %finish.2 = (bf16[512,2048]{1,0:T(8,128)(2,1)}, bf16[512,2048]{1,0:T(8,128)(2,1)}) custom-call(f32[512,1024]{1,0:T(8,128)S(1)} %get-tuple-element.158.refs_0_, f32[512,1024]{1,0:T(8,128)S(1)} %get-tuple-element.159.refs_1_, bf16[512,1024]{1,0:T(8,128)(2,1)S(1)} %get-tuple-element.89.refs_0_.refs_1_.refs_2_, ...), custom_call_target="tpu_custom_call" | custom-call | flops 1200000000 | bytes 4000000 | tf_op jit(solution)/shard_map/finish/pallas_call | solution.py:56
  84.0 2.1 %finish.3 = (bf16[512,2048]{1,0:T(8,128)(2,1)}, bf16[512,2048]{1,0:T(8,128)(2,1)}, f32[16,128]{1,0:T(8,128)}) custom-call(f32[512,1024]{1,0:T(8,128)S(1)} %get-tuple-element.148.refs_0_, f32[512,1024]{1,0:T(8,128)S(1)} %get-tuple-element.149.refs_1_, ...), custom_call_target="tpu_custom_call", output_to_operand_aliasing={{0}: (9, {}), {1}: (10, {})} | custom-call | flops 1200000000 | bytes 4000000 | tf_op jit(solution)/shard_map/finish/pallas_call | solution.py:56
  (8 shorter events, 0.0 us)
Async XLA Ops:
  3.5 3.9 %collective-permute-start = (bf16[1040,128]{1,0:T(8,128)(2,1)S(1)}, bf16[1040,128]{1,0:T(8,128)(2,1)S(1)}, u32[]{:S(2)}, u32[]{:S(2)}) collective-permute-start(bf16[1040,128]{1,0:T(8,128)(2,1)S(1)} %get-tuple-element.93), channel_id=1, source_target_pairs={{0,4},{4,0},{8,12},{12,8},{16,20},{20,16},{24,28},{28,24},{32,36},... | collective-permute-start | bytes 798728 | tf_op jit(solution)/shard_map/ppermute | solution.py:642
  7.5 7.0 %collective-permute-start.1 = (bf16[272,128]{1,0:T(8,128)(2,1)S(1)}, bf16[272,128]{1,0:T(8,128)(2,1)S(1)}, u32[]{:S(2)}, u32[]{:S(2)}) collective-permute-start(bf16[272,128]{1,0:T(8,128)(2,1)S(1)} %get-tuple-element.97), channel_id=1, source_target_pairs={{0,8},{4,12},{8,0},{12,4},{16,24},{20,28},{24,16},{28,20},{32,40},... | collective-permute-start | bytes 208904 | tf_op jit(solution)/shard_map/ppermute | solution.py:642
  8.9 6.3 %collective-permute-start.2 = (bf16[272,128]{1,0:T(8,128)(2,1)S(1)}, bf16[272,128]{1,0:T(8,128)(2,1)S(1)}, u32[]{:S(2)}, u32[]{:S(2)}) collective-permute-start(bf16[272,128]{1,0:T(8,128)(2,1)S(1)} %get-tuple-element.98), channel_id=1, source_target_pairs={{0,16},{4,20},{8,24},{12,28},{16,0},{20,4},{24,8},{28,12},{32,48},... | collective-permute-start | bytes 208904 | tf_op jit(solution)/shard_map/ppermute | solution.py:642
  11.3 5.0 %collective-permute-start.3 = (bf16[272,128]{1,0:T(8,128)(2,1)S(1)}, bf16[272,128]{1,0:T(8,128)(2,1)S(1)}, u32[]{:S(2)}, u32[]{:S(2)}) collective-permute-start(bf16[272,128]{1,0:T(8,128)(2,1)S(1)} %get-tuple-element.99), channel_id=1, source_target_pairs={{0,24},{4,28},{8,16},{12,20},{16,8},{20,12},{24,0},{28,4},{32,56},... | collective-permute-start | bytes 208904 | tf_op jit(solution)/shard_map/ppermute | solution.py:642
  16.4 7.5 %collective-permute-start.5 = (bf16[272,128]{1,0:T(8,128)(2,1)S(1)}, bf16[272,128]{1,0:T(8,128)(2,1)S(1)}, u32[]{:S(2)}, u32[]{:S(2)}) collective-permute-start(bf16[272,128]{1,0:T(8,128)(2,1)S(1)} %row_sum.2.refs_5_.refs_4_), channel_id=1, source_target_pairs={{0,64},{4,68},{8,72},{12,76},{16,80},{20,84},{24,88},{28,92},{32,9... | collective-permute-start | bytes 208904 | tf_op jit(solution)/shard_map/ppermute | solution.py:642
  20.1 4.4 %collective-permute-start.4 = (bf16[272,128]{1,0:T(8,128)(2,1)S(1)}, bf16[272,128]{1,0:T(8,128)(2,1)S(1)}, u32[]{:S(2)}, u32[]{:S(2)}) collective-permute-start(bf16[272,128]{1,0:T(8,128)(2,1)S(1)} %row_sum.2.refs_5_.refs_4_), channel_id=1, source_target_pairs={{0,32},{4,36},{8,40},{12,44},{16,48},{20,52},{24,56},{28,60},{32,6... | collective-permute-start | bytes 208904 | tf_op jit(solution)/shard_map/ppermute | solution.py:658
  24.7 6.5 %collective-permute-start.6 = (bf16[256,128]{1,0:T(8,128)(2,1)S(1)}, bf16[256,128]{1,0:T(8,128)(2,1)S(1)}, u32[]{:S(2)}, u32[]{:S(2)}) collective-permute-start(bf16[256,128]{1,0:T(8,128)(2,1)S(1)} %get-tuple-element.107), channel_id=1, source_target_pairs={{0,8},{4,12},{8,0},{12,4},{16,24},{20,28},{24,16},{28,20},{32,40},... | collective-permute-start | bytes 196616 | tf_op jit(solution)/shard_map/ppermute | solution.py:642
  24.9 6.3 %collective-permute-start.7 = (bf16[256,128]{1,0:T(8,128)(2,1)S(1)}, bf16[256,128]{1,0:T(8,128)(2,1)S(1)}, u32[]{:S(2)}, u32[]{:S(2)}) collective-permute-start(bf16[256,128]{1,0:T(8,128)(2,1)S(1)} %get-tuple-element.108), channel_id=1, source_target_pairs={{0,16},{4,20},{8,24},{12,28},{16,0},{20,4},{24,8},{28,12},{32,48},... | collective-permute-start | bytes 196616 | tf_op jit(solution)/shard_map/ppermute | solution.py:642
  27.5 4.3 %collective-permute-start.8 = (bf16[256,128]{1,0:T(8,128)(2,1)S(1)}, bf16[256,128]{1,0:T(8,128)(2,1)S(1)}, u32[]{:S(2)}, u32[]{:S(2)}) collective-permute-start(bf16[256,128]{1,0:T(8,128)(2,1)S(1)} %get-tuple-element.109), channel_id=1, source_target_pairs={{0,24},{4,28},{8,16},{12,20},{16,8},{20,12},{24,0},{28,4},{32,56},... | collective-permute-start | bytes 196616 | tf_op jit(solution)/shard_map/ppermute | solution.py:642
  28.7 7.1 %copy-start = (f32[2048]{0:T(1024)S(1)}, f32[2048]{0:T(1024)}, u32[]{:S(2)}) copy-start(f32[2048]{0:T(1024)} %param.12) | copy-start | bytes 24580
  32.0 5.6 %collective-permute-start.9 = (bf16[1024,128]{1,0:T(8,128)(2,1)S(1)}, bf16[1024,128]{1,0:T(8,128)(2,1)S(1)}, u32[]{:S(2)}, u32[]{:S(2)}) collective-permute-start(bf16[1024,128]{1,0:T(8,128)(2,1)S(1)} %get-tuple-element.118), channel_id=1, source_target_pairs={{0,4},{4,0},{8,12},{12,8},{16,20},{20,16},{24,28},{28,24},{32,36},... | collective-permute-start | bytes 786440 | tf_op jit(solution)/shard_map/ppermute | solution.py:642
  39.6 3.9 %collective-permute-start.12 = (f32[8,512]{1,0:T(8,128)S(1)}, f32[8,512]{1,0:T(8,128)S(1)}, u32[]{:S(2)}, u32[]{:S(2)}) collective-permute-start(f32[8,512]{1,0:T(8,128)S(1)} %get-tuple-element.124.refs_5_), channel_id=1, source_target_pairs={{0,3},{1,2},{2,1},{3,0},{4,7},{5,6},{6,5},{7,4},{8,11},{9,10},{10,... | collective-permute-start | bytes 49160 | tf_op jit(solution)/shard_map/ppermute | solution.py:642
  42.4 4.1 %collective-permute-start.11 = (f32[8,512]{1,0:T(8,128)S(1)}, f32[8,512]{1,0:T(8,128)S(1)}, u32[]{:S(2)}, u32[]{:S(2)}) collective-permute-start(f32[8,512]{1,0:T(8,128)S(1)} %get-tuple-element.124.refs_5_), channel_id=1, source_target_pairs={{0,2},{1,3},{2,0},{3,1},{4,6},{5,7},{6,4},{7,5},{8,10},{9,11},{10,... | collective-permute-start | bytes 49160 | tf_op jit(solution)/shard_map/ppermute | solution.py:642
  42.7 3.7 %collective-permute-start.10 = (f32[8,512]{1,0:T(8,128)S(1)}, f32[8,512]{1,0:T(8,128)S(1)}, u32[]{:S(2)}, u32[]{:S(2)}) collective-permute-start(f32[8,512]{1,0:T(8,128)S(1)} %get-tuple-element.124.refs_5_), channel_id=1, source_target_pairs={{0,1},{1,0},{2,3},{3,2},{4,5},{5,4},{6,7},{7,6},{8,9},{9,8},{10,11... | collective-permute-start | bytes 49160 | tf_op jit(solution)/shard_map/ppermute | solution.py:642
  48.2 3.2 %collective-permute-start.13 = (bf16[1056,128]{1,0:T(8,128)(2,1)S(1)}, bf16[1056,128]{1,0:T(8,128)(2,1)S(1)}, u32[]{:S(2)}, u32[]{:S(2)}) collective-permute-start(bf16[1056,128]{1,0:T(8,128)(2,1)S(1)} %get-tuple-element.129), channel_id=1, source_target_pairs={{0,4},{4,0},{8,12},{12,8},{16,20},{20,16},{24,28},{28,24},{32,36},... | collective-permute-start | bytes 811016 | tf_op jit(solution)/shard_map/ppermute | solution.py:642
  51.5 9.7 %collective-permute-start.14 = (bf16[288,128]{1,0:T(8,128)(2,1)S(1)}, bf16[288,128]{1,0:T(8,128)(2,1)S(1)}, u32[]{:S(2)}, u32[]{:S(2)}) collective-permute-start(bf16[288,128]{1,0:T(8,128)(2,1)S(1)} %get-tuple-element.131), channel_id=1, source_target_pairs={{0,8},{4,12},{8,0},{12,4},{16,24},{20,28},{24,16},{28,20},{32,40},... | collective-permute-start | bytes 221192 | tf_op jit(solution)/shard_map/ppermute | solution.py:642
  51.6 9.6 %collective-permute-start.15 = (bf16[288,128]{1,0:T(8,128)(2,1)S(1)}, bf16[288,128]{1,0:T(8,128)(2,1)S(1)}, u32[]{:S(2)}, u32[]{:S(2)}) collective-permute-start(bf16[288,128]{1,0:T(8,128)(2,1)S(1)} %get-tuple-element.132), channel_id=1, source_target_pairs={{0,16},{4,20},{8,24},{12,28},{16,0},{20,4},{24,8},{28,12},{32,48},... | collective-permute-start | bytes 221192 | tf_op jit(solution)/shard_map/ppermute | solution.py:642
  54.6 6.6 %collective-permute-start.16 = (bf16[288,128]{1,0:T(8,128)(2,1)S(1)}, bf16[288,128]{1,0:T(8,128)(2,1)S(1)}, u32[]{:S(2)}, u32[]{:S(2)}) collective-permute-start(bf16[288,128]{1,0:T(8,128)(2,1)S(1)} %get-tuple-element.133), channel_id=1, source_target_pairs={{0,24},{4,28},{8,16},{12,20},{16,8},{20,12},{24,0},{28,4},{32,56},... | collective-permute-start | bytes 221192 | tf_op jit(solution)/shard_map/ppermute | solution.py:642
  61.4 9.1 %collective-permute-start.19 = (bf16[288,128]{1,0:T(8,128)(2,1)S(1)}, bf16[288,128]{1,0:T(8,128)(2,1)S(1)}, u32[]{:S(2)}, u32[]{:S(2)}) collective-permute-start(bf16[288,128]{1,0:T(8,128)(2,1)S(1)} %row_sum.3.refs_11_.refs_4_), channel_id=1, source_target_pairs={{0,96},{4,100},{8,104},{12,108},{16,112},{20,116},{24,120},{28,124... | collective-permute-start | bytes 221192 | tf_op jit(solution)/shard_map/ppermute | solution.py:642
  61.9 8.5 %collective-permute-start.18 = (bf16[288,128]{1,0:T(8,128)(2,1)S(1)}, bf16[288,128]{1,0:T(8,128)(2,1)S(1)}, u32[]{:S(2)}, u32[]{:S(2)}) collective-permute-start(bf16[288,128]{1,0:T(8,128)(2,1)S(1)} %row_sum.3.refs_11_.refs_4_), channel_id=1, source_target_pairs={{0,64},{4,68},{8,72},{12,76},{16,80},{20,84},{24,88},{28,92},{32,9... | collective-permute-start | bytes 221192 | tf_op jit(solution)/shard_map/ppermute | solution.py:642
  63.0 7.5 %collective-permute-start.17 = (bf16[288,128]{1,0:T(8,128)(2,1)S(1)}, bf16[288,128]{1,0:T(8,128)(2,1)S(1)}, u32[]{:S(2)}, u32[]{:S(2)}) collective-permute-start(bf16[288,128]{1,0:T(8,128)(2,1)S(1)} %row_sum.3.refs_11_.refs_4_), channel_id=1, source_target_pairs={{0,32},{4,36},{8,40},{12,44},{16,48},{20,52},{24,56},{28,60},{32,0... | collective-permute-start | bytes 221192 | tf_op jit(solution)/shard_map/ppermute | solution.py:642
  70.8 7.2 %collective-permute-start.20 = (bf16[256,128]{1,0:T(8,128)(2,1)S(1)}, bf16[256,128]{1,0:T(8,128)(2,1)S(1)}, u32[]{:S(2)}, u32[]{:S(2)}) collective-permute-start(bf16[256,128]{1,0:T(8,128)(2,1)S(1)} %get-tuple-element.150), channel_id=1, source_target_pairs={{0,8},{4,12},{8,0},{12,4},{16,24},{20,28},{24,16},{28,20},{32,40},... | collective-permute-start | bytes 196616 | tf_op jit(solution)/shard_map/ppermute | solution.py:642
  70.9 7.1 %collective-permute-start.21 = (bf16[256,128]{1,0:T(8,128)(2,1)S(1)}, bf16[256,128]{1,0:T(8,128)(2,1)S(1)}, u32[]{:S(2)}, u32[]{:S(2)}) collective-permute-start(bf16[256,128]{1,0:T(8,128)(2,1)S(1)} %get-tuple-element.151), channel_id=1, source_target_pairs={{0,16},{4,20},{8,24},{12,28},{16,0},{20,4},{24,8},{28,12},{32,48},... | collective-permute-start | bytes 196616 | tf_op jit(solution)/shard_map/ppermute | solution.py:642
  73.9 5.0 %collective-permute-start.22 = (bf16[256,128]{1,0:T(8,128)(2,1)S(1)}, bf16[256,128]{1,0:T(8,128)(2,1)S(1)}, u32[]{:S(2)}, u32[]{:S(2)}) collective-permute-start(bf16[256,128]{1,0:T(8,128)(2,1)S(1)} %get-tuple-element.152), channel_id=1, source_target_pairs={{0,24},{4,28},{8,16},{12,20},{16,8},{20,12},{24,0},{28,4},{32,56},... | collective-permute-start | bytes 196616 | tf_op jit(solution)/shard_map/ppermute | solution.py:642
  79.2 4.9 %collective-permute-start.23 = (bf16[1040,128]{1,0:T(8,128)(2,1)S(1)}, bf16[1040,128]{1,0:T(8,128)(2,1)S(1)}, u32[]{:S(2)}, u32[]{:S(2)}) collective-permute-start(bf16[1040,128]{1,0:T(8,128)(2,1)S(1)} %get-tuple-element.155), channel_id=1, source_target_pairs={{0,4},{4,0},{8,12},{12,8},{16,20},{20,16},{24,28},{28,24},{32,36},... | collective-permute-start | bytes 798728 | tf_op jit(solution)/shard_map/ppermute | solution.py:642

commit v4 on v3

--- a/solution.py
+++ b/solution.py
@@ -130,24 +130,31 @@
     return jnp.where(cond, 1.0, 0.0)
 
 
-def fill_token_masks(seg_ref, before, after, last, first):
+def fill_last_mask(seg_ref, ref):
+    seg = seg_ref[...].astype(F32)
+    row = lax.broadcasted_iota(jnp.int32, (BLOCK, HD), 0).astype(F32)
+    for _, t in BLOCKS:
+        block = seg[:, t]
+        same = jnp.sum(flag(block == block[:, BLOCK - 1 : BLOCK]), axis=1, keepdims=True)
+        ref[t, :] = flag(row >= BLOCK - same).astype(BF16)
+
+
+def fill_token_masks(seg_ref, col, before, after, first):
     start0, end0, start1, end1 = split_ends(seg_ref)
-    col = jnp.transpose(jnp.broadcast_to(seg_ref[...].astype(F32), (8, TOK)))[:, 0:1]
-    col = jnp.broadcast_to(col, (TOK, HD))
-    for ref, id0, id1 in (
-        (last, end0, end1), (before, start0, end0), (after, start1, end1), (first, start0, start1)
-    ):
-        ref[0:BLOCK, :] = flag(col[0:BLOCK] == id0).astype(BF16)
-        ref[BLOCK:TOK, :] = flag(col[BLOCK:TOK] == id1).astype(BF16)
-
-
+    wide = jnp.broadcast_to(col, (TOK, HD))
+    for ref, ids in ((before, (start0, end0)), (after, (start1, end1)), (first, (start0, start1))):
+        for n, t in BLOCKS:
+            ref[t, :] = flag(wide[t] == ids[n]).astype(BF16)
+
+
+BLOCKS = ((0, slice(0, BLOCK)), (1, slice(BLOCK, TOK)))
 FINE = 2
 FINE_SPAN = FINE * HD
 
 
 def state_kernel(flip, ids, *refs):
     if flip:
-        k_far, v_far, seg_far, k, v, out, early, seg, before, after, last, first, sems, seg_sem = refs
+        k_far, v_far, seg_far, k, v, out, early, seg, last, sems, seg_sem = refs
     else:
         seg, last, k_far, v_far, k, v, out, early, sems = refs
     base = base_column(ids, flip)
@@ -167,18 +174,17 @@
             c.start()
     if flip:
         copy.wait()
-        fill_token_masks(seg, before, after, last, first)
+        fill_last_mask(seg, last)
     start0, end0, _, end1 = split_ends(seg)
     join = flag(end0 == end1)
     out[STATE_ROWS : STATE_ROWS + TILE, :] = info_tile(start0, end1)
     for g in range(groups):
         for c in copies[g]:
             c.wait()
-        for h in range(g * FINE, (g + 1) * FINE):
-            kh = k[:, head_columns(h)] * last[...]
-            vh = v[:, head_columns(h)]
-            one = dot(kh[0:BLOCK], vh[0:BLOCK], 0, 0)
-            two = dot(kh[BLOCK:TOK], vh[BLOCK:TOK], 0, 0)
+        group = range(g * FINE, (g + 1) * FINE)
+        rows = [(k[:, head_columns(h)] * last[...], v[:, head_columns(h)]) for h in group]
+        parts = [[dot(kh[t], vh[t], 0, 0) for _, t in BLOCKS] for kh, vh in rows]
+        for h, (one, two) in zip(group, parts):
             early[head_rows(h), :] = one
             out[head_rows(h), :] = (two + one * join).astype(BF16)
 
@@ -192,7 +198,7 @@
     scratch = [pltpu.SemaphoreType.DMA((2, HEADS // FINE))]
     near, distant = [seg_vmem, last], [k, v]
     if flip:
-        outs += [vmem((1, TOK), jnp.int32)] + [vmem((TOK, HD), BF16)] * 4
+        outs += [vmem((1, TOK), jnp.int32), vmem((TOK, HD), BF16)]
         scratch += [pltpu.SemaphoreType.DMA]
         near, distant = [], [k, v, seg]
     return call(
@@ -200,9 +206,10 @@
     )
 
 
-def fill_masks(seg_ref, m0, m1):
+def fill_masks(seg_ref, m0, m1, *masks):
     seg = seg_ref[...].astype(F32)
     col = jnp.transpose(jnp.broadcast_to(seg, (8, TOK)))[:, 0:1]
+    fill_token_masks(seg_ref, col, *masks)
     t = lax.broadcasted_iota(jnp.int32, (BLOCK, BLOCK), 0)
     s = lax.broadcasted_iota(jnp.int32, (BLOCK, BLOCK), 1)
     for start, ref in ((0, m0), (BLOCK, m1)):
@@ -214,32 +221,32 @@
     return dot(left, right, 1, 1).astype(BF16) * mask[...]
 
 
-BLOCKS = ((0, slice(0, BLOCK)), (1, slice(BLOCK, TOK)))
-
-
 def intra_kernel(flip, ids, *refs):
     if flip:
-        k, v, first, m0, m1, _, q_far, q, attn, w0, w1, qt, token, sems = refs
+        k, v, m0, m1, first, _, q_far, q, attn, w0, w1, qt, token, sems = refs
     else:
-        k, v, first, seg, _, q_far, q, attn, w0, w1, qt, token, m0, m1, sems = refs
+        k, v, seg, _, q_far, q, attn, w0, w1, qt, token, m0, m1, before, after, first, sems = refs
     base = base_column(ids, flip)
     for g in range(GROUPS):
         load(q_far, base, g * SPAN, q, sems.at[g]).start()
     if not flip:
-        fill_masks(seg, m0, m1)
+        fill_masks(seg, m0, m1, before, after, first)
     token[...] = jnp.zeros_like(token)
 
     def body(g):
         load(q_far, base, g * SPAN, q, sems.at[g]).wait()
-        for j in range(GROUP):
-            h = g * GROUP + j
-            c = head_columns(h)
-            qh, kh, vh = q[:, c], k[:, c], v[:, c]
+        group = [g * GROUP + j for j in range(GROUP)]
+        rows = [[ref[:, head_columns(h)] for ref in (q, k, v)] for h in group]
+        flipped = [jnp.transpose(qh * first[...]) for qh, _, _ in rows]
+        weights = [[masked(qh[t], kh[t], (m0, m1)[n]) for n, t in BLOCKS] for qh, kh, _ in rows]
+        sums = [
+            [dot(w[n], vh[t], 1, 0) for n, t in BLOCKS] for w, (_, _, vh) in zip(weights, rows)
+        ]
+        for h, turned, w, a in zip(group, flipped, weights, sums):
+            qt[head_rows(h), :] = turned
             for n, t in BLOCKS:
-                w = masked(qh[t], kh[t], (m0, m1)[n])
-                (w0, w1)[n][head_rows(h, BLOCK), :] = w
-                attn[t, c] = dot(w, vh[t], 1, 0)
-            qt[head_rows(h), :] = jnp.transpose(qh * first[...])
+                (w0, w1)[n][head_rows(h, BLOCK), :] = w[n]
+                attn[t, head_columns(h)] = a[n]
 
     each_group(body)
 
@@ -247,7 +254,7 @@
 TOKEN = vmem((8, HD), F32)
 
 
-def intra(k, v, first, q, after, seg=None, masks=None):
+def intra(k, v, q, after, seg=None, masks=None):
     outs = [
         half_shape(BF16),
         half_shape(F32),
@@ -257,10 +264,10 @@
         TOKEN,
     ]
     if masks is None:
-        near = [k, v, first, seg, after]
-        outs += [vmem((BLOCK, BLOCK), BF16), vmem((BLOCK, BLOCK), BF16)]
+        near = [k, v, seg, after]
+        outs += [vmem((BLOCK, BLOCK), BF16)] * 2 + [vmem((TOK, HD), BF16)] * 3
     else:
-        near = [k, v, first, *masks, after]
+        near = [k, v, *masks, after]
     return call(
         functools.partial(intra_kernel, int(masks is not None)), "intra", 3e9, near, outs, [q],
         [pltpu.SemaphoreType.DMA((GROUPS,))],
@@ -307,20 +314,27 @@
     join = flag(start0 == end0)
 
     def body(g):
-        for j in range(GROUP):
-            h = g * GROUP + j
-            c, rows = head_columns(h), head_rows(h)
-            far_c = span(base + h * HD, HD)
-            one = s[rows, :]
-            two = (early[rows, :] + one.astype(F32) * join).astype(BF16)
-            second[rows, :] = two
-            qh = q[:, c] * before[...]
-            scale = gain[:, far_c]
-            for n, t in BLOCKS:
-                a = attn_in[t, c] + dot(qh[t], (one, two)[n], 1, 0)
-                attn[t, c] = a
-                squares[t, :] += a * a
-                inners[t, :] += w[t, far_c] * a * scale
+        group = [g * GROUP + j for j in range(GROUP)]
+        ones = [s[head_rows(h), :] for h in group]
+        twos = [
+            (early[head_rows(h), :] + one.astype(F32) * join).astype(BF16)
+            for h, one in zip(group, ones)
+        ]
+        rows = [q[:, head_columns(h)] * before[...] for h in group]
+        for n, t in BLOCKS:
+            hops = [dot(qh[t], pair[n], 1, 0) for qh, pair in zip(rows, zip(ones, twos))]
+            sums = [attn_in[t, head_columns(h)] + hop for h, hop in zip(group, hops)]
+            square, inner = squares[t, :], inners[t, :]
+            for h, a in zip(group, sums):
+                far_c = span(base + h * HD, HD)
+                square = square + a * a
+                inner = inner + w[t, far_c] * a * gain[:, far_c]
+            squares[t, :] = square
+            inners[t, :] = inner
+            for h, a in zip(group, sums):
+                attn[t, head_columns(h)] = a
+        for h, two in zip(group, twos):
+            second[head_rows(h), :] = two
 
     each_group(body)
     ones = jnp.ones((8, HD), F32)
@@ -372,19 +386,21 @@
     out[STATE_ROWS : STATE_ROWS + TILE, :] = info_tile(8.0 - end1, 8.0 - start0)
 
     def body(g):
-        for j in range(GROUP):
-            h = g * GROUP + j
-            c, rows = head_columns(h), head_rows(h)
+        group = [g * GROUP + j for j in range(GROUP)]
+        turned = [qt[head_rows(h), :] for h in group]
+        totals, rows = [], []
+        for h in group:
             far_c = span(base + h * HD, HD)
-            a = attn[:, c]
+            a = attn[:, head_columns(h)]
             gated = w[:, far_c] * rinv[...]
-            gains[pl.ds(h, 1), :] = jnp.sum(gated * a, axis=0, keepdims=True)
-            x = (gated * gain[:, far_c] - a * back[...]).astype(BF16)
-            grad[:, c] = x
-            one = dot(qt[rows, 0:BLOCK], x[0:BLOCK], 1, 0)
-            two = dot(qt[rows, BLOCK:TOK], x[BLOCK:TOK], 1, 0)
-            late[rows, :] = two
-            out[rows, :] = (one + two * join).astype(BF16)
+            totals.append(jnp.sum(gated * a, axis=0, keepdims=True))
+            rows.append((gated * gain[:, far_c] - a * back[...]).astype(BF16))
+        parts = [[dot(qh[:, t], x[t], 1, 0) for _, t in BLOCKS] for qh, x in zip(turned, rows)]
+        for h, total, x, (one, two) in zip(group, totals, rows, parts):
+            gains[pl.ds(h, 1), :] = total
+            grad[:, head_columns(h)] = x
+            late[head_rows(h), :] = two
+            out[head_rows(h), :] = (one + two * join).astype(BF16)
 
     each_group(body)
     out[STATE_ROWS + TILE : STATE_ROWS + 2 * TILE, :] = split_tile(gains[...])
@@ -408,18 +424,32 @@
     token[...] = jnp.zeros_like(token)
 
     def body(g):
-        for j in range(GROUP):
-            h = g * GROUP + j
+        group = [g * GROUP + j for j in range(GROUP)]
+        rows = [[ref[:, head_columns(h)] for ref in (q, k, v, grad)] for h in group]
+        states = [[ref[head_rows(h), :] for ref in (s0, s1)] for h in group]
+        weights = [[ref[head_rows(h, BLOCK), :] for ref in (w0, w1)] for h in group]
+        inner = [
+            [masked(gh[t], vh[t], (m0, m1)[n]) for n, t in BLOCKS] for _, _, vh, gh in rows
+        ]
+        outs = []
+        for (qh, kh, _, gh), state, w, d in zip(rows, states, weights, inner):
+            cut = gh * before[...]
+            outs.append(
+                [
+                    (
+                        dot(d[n], kh[t], 1, 0) + dot(cut[t], state[n], 1, 1),
+                        dot(d[n], qh[t], 0, 0),
+                        dot(w[n], gh[t], 0, 0),
+                    )
+                    for n, t in BLOCKS
+                ]
+            )
+        for h, blocks in zip(group, outs):
             c = head_columns(h)
-            qh, kh, vh, gh = q[:, c], k[:, c], v[:, c], grad[:, c]
-            cut = gh * before[...]
-            for n, t in BLOCKS:
-                d = masked(gh[t], vh[t], (m0, m1)[n])
-                w = (w0, w1)[n][head_rows(h, BLOCK), :]
-                hop = dot(cut[t], (s0, s1)[n][head_rows(h), :], 1, 1)
-                dq[t, c] = (dot(d, kh[t], 1, 0) + hop).astype(BF16)
-                dk[t, c] = dot(d, qh[t], 0, 0)
-                dv[t, c] = dot(w, gh[t], 0, 0)
+            for (n, t), (x, y, z) in zip(BLOCKS, blocks):
+                dq[t, c] = x.astype(BF16)
+                dk[t, c] = y
+                dv[t, c] = z
         store(dq, g * SPAN, base + g * SPAN, dq_far, sems.at[g]).start()
 
     each_group(body)
@@ -493,14 +523,31 @@
     join = flag(start1 == end1)
     copies = []
     for g in range(HEADS // FINE):
-        for h in range(g * FINE, (g + 1) * FINE):
-            c, rows = head_columns(h), head_rows(h)
-            one = later[rows, :]
-            both = ((late[rows, :] + one.astype(F32) * join).astype(BF16), one)
-            kh, vh = k[:, c] * after[...], v[:, c] * after[...]
-            for n, t in BLOCKS:
-                dk[t, c] = (dk_in[t, c] + dot(vh[t], both[n], 1, 1)).astype(BF16)
-                dv[t, c] = (dv_in[t, c] + dot(kh[t], both[n], 1, 0)).astype(BF16)
+        group = range(g * FINE, (g + 1) * FINE)
+        states = []
+        for h in group:
+            one = later[head_rows(h), :]
+            states.append(
+                ((late[head_rows(h), :] + one.astype(F32) * join).astype(BF16), one)
+            )
+        rows = [
+            (k[:, head_columns(h)] * after[...], v[:, head_columns(h)] * after[...]) for h in group
+        ]
+        hops = [
+            [(dot(vh[t], state[n], 1, 1), dot(kh[t], state[n], 1, 0)) for n, t in BLOCKS]
+            for (kh, vh), state in zip(rows, states)
+        ]
+        sums = [
+            [
+                (dk_in[t, head_columns(h)] + hop[n][0], dv_in[t, head_columns(h)] + hop[n][1])
+                for n, t in BLOCKS
+            ]
+            for h, hop in zip(group, hops)
+        ]
+        for h, blocks in zip(group, sums):
+            for (_, t), (x, y) in zip(BLOCKS, blocks):
+                dk[t, head_columns(h)] = x.astype(BF16)
+                dv[t, head_columns(h)] = y.astype(BF16)
         for n, (ref, far_ref) in enumerate(((dk, dk_far), (dv, dv_far))):
             at = g * FINE_SPAN
             copy = store(ref, at, base + at, far_ref, sems.at[n, g], FINE_SPAN)
@@ -699,7 +746,7 @@
 def on_device(query, keys, values, gate_input, grad_output, norm_gain, segment_ids):
     gain = norm_gain.reshape(1, -1)
 
-    k_send, v_send, sent, early_send, seg, before, after, last, first = local_state(
+    k_send, v_send, sent, early_send, seg, last = local_state(
         keys, values, segment_ids.reshape(1, TOK)
     )
     other = chip_swap(sent)
@@ -707,11 +754,12 @@
     made = {}
 
     def intra_keep(token):
-        made["keep"] = intra(k_keep, v_keep, first, query, token, seg=seg)
+        made["keep"] = intra(k_keep, v_keep, query, token, seg=seg)
         return made["keep"][5]
 
     def intra_send(token):
-        made["send"] = intra(k_send, v_send, first, query, token, masks=made["keep"][6:8])
+        m0, m1, _, _, first = made["keep"][6:]
+        made["send"] = intra(k_send, v_send, query, token, masks=(m0, m1, first))
         return made["send"][5]
 
     def prepare_both(token):
@@ -719,7 +767,7 @@
         return made["gate"][2]
 
     state_keep, state_send, _ = scan(own, other, False, False, intra_keep, intra_send, prepare_both)
-    q_keep, attn_keep, w0_keep, w1_keep, qt_keep, _, *masks = made["keep"]
+    q_keep, attn_keep, w0_keep, w1_keep, qt_keep, _, *masks, before, after, _ = made["keep"]
     q_send, attn_send, w0_send, w1_send, qt_send, _ = made["send"]
     gated, gate, _ = made["gate"]
 

time: 86.5 us -> 83 us (0.960)
  Pallas kernels: 41.1 us -> 37.2 us
    pallas_call x22, Pallas kernels: 41.1 us -> 37.2 us  [call(): pl.pallas_call(placed, in_specs=[VM] * len(near) + [ANY] * len(distant),...]
  transfers between devices with their start and end apart: 24 -> 24, of which waited for: 7 -> 8; matrix products, arithmetic and copies ran while one was open for 0% -> 0% of each run, Pallas kernels for 36% -> 33%
where the time goes in v4:
time: 83 us; the launch traced here: 82.8 us
  Pallas kernels  37.2 us (45%)
  starting transfers between devices  36.7 us (44%)
  waiting for transfers between devices  7.72 us (9%)
  between operations  1.05 us (1%)
    pallas_call x22, Pallas kernels, call(): pl.pallas_call(placed, in_specs=[VM] * len(near) + [ANY] * len(distant),...  37.2 us
    ppermute x23, starting transfers between devices, swap(): return lax.ppermute(x, axis, [(i, i ^ bits) for i in range(size)])  35.7 us
    ppermute x23, waiting for transfers between devices, swap(): return lax.ppermute(x, axis, [(i, i ^ bits) for i in range(size)])  7.2 us
  transfers between devices with their start and end apart: 24, of which 8 were waited for; matrix products, arithmetic and copies ran while one was open for 0% of the time, Pallas kernels for 33%

profile of v4, /device:TPU:1, one launch (start us, length us, event | category | flops | bytes accessed | tf_op | source)
XLA Modules:
  0.0 82.8 jit_solution(5085201162565725246)
XLA Ops:
  0.6 2.7 %local_state.2 = (bf16[512,1024]{1,0:T(8,128)(2,1)S(1)}, bf16[512,1024]{1,0:T(8,128)(2,1)S(1)}, bf16[1040,128]{1,0:T(8,128)(2,1)S(1)}, f32[1024,128]{1,0:T(8,128...) custom-call(bf16[512,2048]{1,0:T(8,128)(2,1)} %refs_2_.2, bf16[512,2048]{1,0:T(8,128)(2,1)} %refs_3_.1, ...), custom_call_target="tpu_custom_call" | custom-call | flops 1000000000 | bytes 3333333 | tf_op jit(solution)/shard_map/local_state/pallas_call | solution.py:56
  3.3 1.6 %collective-permute-start = (bf16[1040,128]{1,0:T(8,128)(2,1)S(1)}, bf16[1040,128]{1,0:T(8,128)(2,1)S(1)}, u32[]{:S(2)}, u32[]{:S(2)}) collective-permute-start(bf16[1040,128]{1,0:T(8,128)(2,1)S(1)} %get-tuple-element.92), channel_id=1, source_target_pairs={{0,4},{4,0},{8,12},{12,8},{16,20},{20,16},{24,28},{28,24},{32,36},... | collective-permute-start | bytes 798728 | tf_op jit(solution)/shard_map/ppermute | solution.py:689
  4.9 2.2 %local_state.3 = (bf16[512,1024]{1,0:T(8,128)(2,1)S(1)}, bf16[512,1024]{1,0:T(8,128)(2,1)S(1)}, bf16[1040,128]{1,0:T(8,128)(2,1)S(1)}, f32[1024,128]{1,0:T(8,128)S(1)}) custom-call(s32[1,512]{1,0:T(1,128)S(1)} %get-tuple-element.87.refs_0_.refs_2_.refs_6_, bf16[512,128]{1,0:T(8,128)(2,1)S(1)} %get-tuple-element.88.refs_1_, bf16[512,2048]{1,0:T(8,128)(2,1)} %refs_2_.2, ...), custom_call_target="tpu_custom_call" | custom-call | flops 1000000000 | bytes 3333333 | tf_op jit(solution)/shard_map/local_state/pallas_call | solution.py:56
  7.2 0.1 chip_sum.2
  7.3 1.4 %collective-permute-start.1 = (bf16[272,128]{1,0:T(8,128)(2,1)S(1)}, bf16[272,128]{1,0:T(8,128)(2,1)S(1)}, u32[]{:S(2)}, u32[]{:S(2)}) collective-permute-start(bf16[272,128]{1,0:T(8,128)(2,1)S(1)} %get-tuple-element.96), channel_id=1, source_target_pairs={{0,8},{4,12},{8,0},{12,4},{16,24},{20,28},{24,16},{28,20},{32,40},... | collective-permute-start | bytes 208904 | tf_op jit(solution)/shard_map/ppermute | solution.py:689
  8.7 2.5 %collective-permute-start.2 = (bf16[272,128]{1,0:T(8,128)(2,1)S(1)}, bf16[272,128]{1,0:T(8,128)(2,1)S(1)}, u32[]{:S(2)}, u32[]{:S(2)}) collective-permute-start(bf16[272,128]{1,0:T(8,128)(2,1)S(1)} %get-tuple-element.97), channel_id=1, source_target_pairs={{0,16},{4,20},{8,24},{12,28},{16,0},{20,4},{24,8},{28,12},{32,48},... | collective-permute-start | bytes 208904 | tf_op jit(solution)/shard_map/ppermute | solution.py:689
  11.1 0.1 collective-permute-start.3
  11.3 2.9 %intra.2 = (bf16[512,1024]{1,0:T(8,128)(2,1)S(1)}, f32[512,1024]{1,0:T(8,128)S(1)}, bf16[2048,256]{1,0:T(8,128)(2,1)S(1)}, bf16[2048,256]{1,0:T(8,128)(2,1)S(1)}...) custom-call(bf16[512,1024]{1,0:T(8,128)(2,1)S(1)} %get-tuple-element, ...), custom_call_target="tpu_custom_call" | custom-call | flops 3000000000 | bytes 10000000 | tf_op jit(solution)/shard_map/intra/pallas_call | solution.py:56
  14.1 0.0 collective-permute-done.1.refs_1_
  14.1 0.8 %collective-permute-done.2.refs_2_ = bf16[272,128]{1,0:T(8,128)(2,1)S(1)} collective-permute-done((bf16[272,128]{1,0:T(8,128)(2,1)S(1)}, bf16[272,128]{1,0:T(8,128)(2,1)S(1)}, u32[]{:S(2)}, u32[]{:S(2)}) %collective-permute-start.2) | collective-permute-done | bytes 69664 | tf_op jit(solution)/shard_map/ppermute | solution.py:689
  15.0 1.2 %collective-permute-done.3.refs_3_ = bf16[272,128]{1,0:T(8,128)(2,1)S(1)} collective-permute-done((bf16[272,128]{1,0:T(8,128)(2,1)S(1)}, bf16[272,128]{1,0:T(8,128)(2,1)S(1)}, u32[]{:S(2)}, u32[]{:S(2)}) %collective-permute-start.3) | collective-permute-done | bytes 69664 | tf_op jit(solution)/shard_map/ppermute | solution.py:689
  16.1 0.1 row_sum.2.refs_5_.refs_4_
  16.2 3.4 %collective-permute-start.5 = (bf16[272,128]{1,0:T(8,128)(2,1)S(1)}, bf16[272,128]{1,0:T(8,128)(2,1)S(1)}, u32[]{:S(2)}, u32[]{:S(2)}) collective-permute-start(bf16[272,128]{1,0:T(8,128)(2,1)S(1)} %row_sum.2.refs_5_.refs_4_), channel_id=1, source_target_pairs={{0,64},{4,68},{8,72},{12,76},{16,80},{20,84},{24,88},{28,92},{32,9... | collective-permute-start | bytes 208904 | tf_op jit(solution)/shard_map/ppermute | solution.py:689
  19.6 1.0 %collective-permute-start.4 = (bf16[272,128]{1,0:T(8,128)(2,1)S(1)}, bf16[272,128]{1,0:T(8,128)(2,1)S(1)}, u32[]{:S(2)}, u32[]{:S(2)}) collective-permute-start(bf16[272,128]{1,0:T(8,128)(2,1)S(1)} %row_sum.2.refs_5_.refs_4_), channel_id=1, source_target_pairs={{0,32},{4,36},{8,40},{12,44},{16,48},{20,52},{24,56},{28,60},{32,6... | collective-permute-start | bytes 208904 | tf_op jit(solution)/shard_map/ppermute | solution.py:705
  20.6 2.9 %intra.3 = (bf16[512,1024]{1,0:T(8,128)(2,1)S(1)}, f32[512,1024]{1,0:T(8,128)S(1)}, bf16[2048,256]{1,0:T(8,128)(2,1)S(1)}, bf16[2048,256]{1,0:T(8,128)(2,1)S(1)}...) custom-call(bf16[512,1024]{1,0:T(8,128)(2,1)S(1)} %get-tuple-element.100.refs_0_.refs_1_.refs_2_, ...), custom_call_target="tpu_custom_call" | custom-call | flops 3000000000 | bytes 10000000 | tf_op jit(solution)/shard_map/intra/pallas_call | solution.py:56
  23.5 0.0 collective-permute-done.5.refs_6_
  23.5 0.5 collective-permute-done.4.refs_5_
  24.0 0.3 entry.2
  24.3 0.5 collective-permute-start.6
  24.7 2.5 %collective-permute-start.7 = (bf16[256,128]{1,0:T(8,128)(2,1)S(1)}, bf16[256,128]{1,0:T(8,128)(2,1)S(1)}, u32[]{:S(2)}, u32[]{:S(2)}) collective-permute-start(bf16[256,128]{1,0:T(8,128)(2,1)S(1)} %get-tuple-element.108), channel_id=1, source_target_pairs={{0,16},{4,20},{8,24},{12,28},{16,0},{20,4},{24,8},{28,12},{32,48},... | collective-permute-start | bytes 196616 | tf_op jit(solution)/shard_map/ppermute | solution.py:689
  27.3 1.0 %collective-permute-start.8 = (bf16[256,128]{1,0:T(8,128)(2,1)S(1)}, bf16[256,128]{1,0:T(8,128)(2,1)S(1)}, u32[]{:S(2)}, u32[]{:S(2)}) collective-permute-start(bf16[256,128]{1,0:T(8,128)(2,1)S(1)} %get-tuple-element.109), channel_id=1, source_target_pairs={{0,24},{4,28},{8,16},{12,20},{16,8},{20,12},{24,0},{28,4},{32,56},... | collective-permute-start | bytes 196616 | tf_op jit(solution)/shard_map/ppermute | solution.py:689
  28.2 2.5 %prepare.1 = (f32[512,2048]{1,0:T(8,128)S(1)}, bf16[512,2048]{1,0:T(8,128)(2,1)S(1)}, f32[8,128]{1,0:T(8,128)S(1)}) custom-call(bf16[256,128]{1,0:T(8,128)(2,1)S(1)} %get-tuple-element.106.refs_0_.refs_2_, bf16[512,2048]{1,0:T(8,128)(2,1)} %refs_1_.3, bf16[512,2048]{1,0:T(8,128)(2,1)} %refs_2_.3), custom_call_target="tpu_custom_call" | custom-call | flops 3000000000 | bytes 10000000 | tf_op jit(solution)/shard_map/prepare/pallas_call | solution.py:56
  30.8 0.0 collective-permute-done.6.refs_3_
  30.8 0.0 collective-permute-done.7.refs_4_
  30.8 0.8 collective-permute-done.8.refs_5_
  31.6 0.2 device_entry.2
  31.8 3.7 %collective-permute-start.9 = (bf16[1024,128]{1,0:T(8,128)(2,1)S(1)}, bf16[1024,128]{1,0:T(8,128)(2,1)S(1)}, u32[]{:S(2)}, u32[]{:S(2)}) collective-permute-start(bf16[1024,128]{1,0:T(8,128)(2,1)S(1)} %get-tuple-element.118), channel_id=1, source_target_pairs={{0,4},{4,0},{8,12},{12,8},{16,20},{20,16},{24,28},{28,24},{32,36},... | collective-permute-start | bytes 786440 | tf_op jit(solution)/shard_map/ppermute | solution.py:689
  35.5 1.9 %cross.2 = (f32[512,1024]{1,0:T(8,128)S(1)}, bf16[1024,128]{1,0:T(8,128)(2,1)S(1)}, f32[8,512]{1,0:T(8,128)S(1)}) custom-call(f32[512,1024]{1,0:T(8,128)S(1)} %get-tuple-element.94.refs_0_, bf16[512,1024]{1,0:T(8,128)(2,1)S(1)} %get-tuple-element.95.refs_1_.refs_0_, bf16[1024,128]{1,0:T(8,128)(2,1)S(1)} %get-tuple-element.111.refs_2_.refs_4_, ...), custom_call_target="tpu_custom_call" | custom-call | flops 1200000000 | bytes 4000000 | tf_op jit(solution)/shard_map/cross/pallas_call | solution.py:56
  37.4 0.0 collective-permute-done.9.refs_2_.refs_4_
  37.4 1.9 %cross.3 = (f32[512,1024]{1,0:T(8,128)S(1)}, bf16[1024,128]{1,0:T(8,128)(2,1)S(1)}, f32[8,512]{1,0:T(8,128)S(1)}) custom-call(f32[512,1024]{1,0:T(8,128)S(1)} %get-tuple-element.116.refs_0_, bf16[512,1024]{1,0:T(8,128)(2,1)S(1)} %get-tuple-element.117.refs_1_.refs_0_, bf16[1024,128]{1,0:T(8,128)(2,1)S(1)} %collective-permute-done.9.refs_2_.refs_4_, ...), custom_call_target="tpu_custom_call" | custom-call | flops 1200000000 | bytes 4000000 | tf_op jit(solution)/shard_map/cross/pallas_call | solution.py:56
  39.3 2.7 %collective-permute-start.12 = (f32[8,512]{1,0:T(8,128)S(1)}, f32[8,512]{1,0:T(8,128)S(1)}, u32[]{:S(2)}, u32[]{:S(2)}) collective-permute-start(f32[8,512]{1,0:T(8,128)S(1)} %get-tuple-element.124.refs_5_), channel_id=1, source_target_pairs={{0,3},{1,2},{2,1},{3,0},{4,7},{5,6},{6,5},{7,4},{8,11},{9,10},{10,... | collective-permute-start | bytes 49160 | tf_op jit(solution)/shard_map/ppermute | solution.py:689
  42.0 0.4 collective-permute-start.11
  42.4 0.3 collective-permute-start.10
  42.7 0.5 collective-permute-done.12.refs_8_
  43.2 3.0 %collective-permute-done.11.refs_7_ = f32[8,512]{1,0:T(8,128)S(1)} collective-permute-done((f32[8,512]{1,0:T(8,128)S(1)}, f32[8,512]{1,0:T(8,128)S(1)}, u32[]{:S(2)}, u32[]{:S(2)}) %collective-permute-start.11) | collective-permute-done | bytes 16416 | tf_op jit(solution)/shard_map/ppermute | solution.py:689
  46.1 1.9 %grad_attn.2 = (bf16[512,1024]{1,0:T(8,128)(2,1)S(1)}, bf16[1056,128]{1,0:T(8,128)(2,1)S(1)}, f32[1024,128]{1,0:T(8,128)S(1)}, f32[512,128]{1,0:T(8,128)S(1)}, f32[512,128]{1,0:T(8,128)S(1)}) custom-call(s32[1,512]{1,0:T(1,128)S(1)} %get-tuple-element.87.refs_0_.refs_2_.refs_6_, f32[512,1024]{1,0:T(8,128)S(1)} %get-tuple-element.121.refs_1_, ...), custom_call_target="tpu_custom_call" | custom-call | flops 1200000000 | bytes 4000000 | tf_op jit(solution)/shard_map/grad_attn/pallas_call | solution.py:56
  48.1 1.7 %collective-permute-start.13 = (bf16[1056,128]{1,0:T(8,128)(2,1)S(1)}, bf16[1056,128]{1,0:T(8,128)(2,1)S(1)}, u32[]{:S(2)}, u32[]{:S(2)}) collective-permute-start(bf16[1056,128]{1,0:T(8,128)(2,1)S(1)} %get-tuple-element.129), channel_id=1, source_target_pairs={{0,4},{4,0},{8,12},{12,8},{16,20},{20,16},{24,28},{28,24},{32,36},... | collective-permute-start | bytes 811016 | tf_op jit(solution)/shard_map/ppermute | solution.py:689
  49.8 1.7 %grad_attn.3 = (bf16[512,1024]{1,0:T(8,128)(2,1)S(1)}, bf16[1056,128]{1,0:T(8,128)(2,1)S(1)}, f32[1024,128]{1,0:T(8,128)S(1)}) custom-call(s32[1,512]{1,0:T(1,128)S(1)} %get-tuple-element.87.refs_0_.refs_2_.refs_6_, f32[512,1024]{1,0:T(8,128)S(1)} %get-tuple-element.115.refs_1_.refs_0_, f32[512,2048]{1,0:T(8,128)S(1)} %get-tuple-element.113.refs_4_.refs_2_.refs_3_, ...), custom_call_target="tpu_custom_call" | custom-call | flops 1200000000 | bytes 4000000 | tf_op jit(solution)/shard_map/grad_attn/pallas_call | solution.py:56
  51.5 0.0 collective-permute-done.13.refs_1_
  51.5 0.1 chip_sum.3
  51.6 0.1 collective-permute-start.14
  51.7 3.0 %collective-permute-start.15 = (bf16[288,128]{1,0:T(8,128)(2,1)S(1)}, bf16[288,128]{1,0:T(8,128)(2,1)S(1)}, u32[]{:S(2)}, u32[]{:S(2)}) collective-permute-start(bf16[288,128]{1,0:T(8,128)(2,1)S(1)} %get-tuple-element.132), channel_id=1, source_target_pairs={{0,16},{4,20},{8,24},{12,28},{16,0},{20,4},{24,8},{28,12},{32,48},... | collective-permute-start | bytes 221192 | tf_op jit(solution)/shard_map/ppermute | solution.py:689
  54.7 0.8 %collective-permute-start.16 = (bf16[288,128]{1,0:T(8,128)(2,1)S(1)}, bf16[288,128]{1,0:T(8,128)(2,1)S(1)}, u32[]{:S(2)}, u32[]{:S(2)}) collective-permute-start(bf16[288,128]{1,0:T(8,128)(2,1)S(1)} %get-tuple-element.133), channel_id=1, source_target_pairs={{0,24},{4,28},{8,16},{12,20},{16,8},{20,12},{24,0},{28,4},{32,56},... | collective-permute-start | bytes 221192 | tf_op jit(solution)/shard_map/ppermute | solution.py:689
  55.5 4.0 %local_grads.2 = (bf16[512,2048]{1,0:T(8,128)(2,1)}, f32[512,1024]{1,0:T(8,128)S(1)}, f32[512,1024]{1,0:T(8,128)S(1)}, f32[8,128]{1,0:T(8,128)S(1)}) custom-call(bf16[512,1024]{1,0:T(8,128)(2,1)S(1)} %get-tuple-element.95.refs_1_.refs_0_, bf16[512,1024]{1,0:T(8,128)(2,1)S(1)} %get-tuple-element.89.refs_0_.refs_1_.refs_2_, ...), custom_call_target="tpu_custom_call" | custom-call | flops 5000000000 | bytes 16666666 | tf_op jit(solution)/shard_map/local_grads/pallas_call | solution.py:56
  59.5 0.6 collective-permute-done.16.refs_3_
  60.1 0.1 row_sum.3.refs_11_.refs_4_
  60.2 0.4 collective-permute-start.19
  60.6 1.0 %collective-permute-start.18 = (bf16[288,128]{1,0:T(8,128)(2,1)S(1)}, bf16[288,128]{1,0:T(8,128)(2,1)S(1)}, u32[]{:S(2)}, u32[]{:S(2)}) collective-permute-start(bf16[288,128]{1,0:T(8,128)(2,1)S(1)} %row_sum.3.refs_11_.refs_4_), channel_id=1, source_target_pairs={{0,64},{4,68},{8,72},{12,76},{16,80},{20,84},{24,88},{28,92},{32,9... | collective-permute-start | bytes 221192 | tf_op jit(solution)/shard_map/ppermute | solution.py:689
  61.6 1.9 %collective-permute-start.17 = (bf16[288,128]{1,0:T(8,128)(2,1)S(1)}, bf16[288,128]{1,0:T(8,128)(2,1)S(1)}, u32[]{:S(2)}, u32[]{:S(2)}) collective-permute-start(bf16[288,128]{1,0:T(8,128)(2,1)S(1)} %row_sum.3.refs_11_.refs_4_), channel_id=1, source_target_pairs={{0,32},{4,36},{8,40},{12,44},{16,48},{20,52},{24,56},{28,60},{32,0... | collective-permute-start | bytes 221192 | tf_op jit(solution)/shard_map/ppermute | solution.py:689
  63.5 4.0 %local_grads.3 = (bf16[512,2048]{1,0:T(8,128)(2,1)}, f32[512,1024]{1,0:T(8,128)S(1)}, f32[512,1024]{1,0:T(8,128)S(1)}, f32[8,128]{1,0:T(8,128)S(1)}) custom-call(bf16[512,1024]{1,0:T(8,128)(2,1)S(1)} %get-tuple-element.117.refs_1_.refs_0_, bf16[512,1024]{1,0:T(8,128)(2,1)S(1)} %get-tuple-element.100.refs_0_.refs_1_.refs_2_, ...), custom_call_target="tpu_custom_call", output_to_operand_aliasing={{0}: (12, {})} | custom-call | flops 5000000000 | bytes 16666666 | tf_op jit(solution)/shard_map/local_grads/pallas_call | solution.py:56
  67.5 0.0 collective-permute-done.18.refs_6_
  67.5 0.0 collective-permute-done.17.refs_5_
  67.5 0.4 entry.3
  67.9 0.1 collective-permute-start.20
  68.0 2.4 %collective-permute-start.21 = (bf16[256,128]{1,0:T(8,128)(2,1)S(1)}, bf16[256,128]{1,0:T(8,128)(2,1)S(1)}, u32[]{:S(2)}, u32[]{:S(2)}) collective-permute-start(bf16[256,128]{1,0:T(8,128)(2,1)S(1)} %get-tuple-element.151), channel_id=1, source_target_pairs={{0,16},{4,20},{8,24},{12,28},{16,0},{20,4},{24,8},{28,12},{32,48},... | collective-permute-start | bytes 196616 | tf_op jit(solution)/shard_map/ppermute | solution.py:689
  70.4 1.4 %collective-permute-start.22 = (bf16[256,128]{1,0:T(8,128)(2,1)S(1)}, bf16[256,128]{1,0:T(8,128)(2,1)S(1)}, u32[]{:S(2)}, u32[]{:S(2)}) collective-permute-start(bf16[256,128]{1,0:T(8,128)(2,1)S(1)} %get-tuple-element.152), channel_id=1, source_target_pairs={{0,24},{4,28},{8,16},{12,20},{16,8},{20,12},{24,0},{28,4},{32,56},... | collective-permute-start | bytes 196616 | tf_op jit(solution)/shard_map/ppermute | solution.py:689
  71.8 3.3 %gates.1 = (bf16[512,2048]{1,0:T(8,128)(2,1)}, bf16[512,2048]{1,0:T(8,128)(2,1)}, f32[8,128]{1,0:T(8,128)S(1)}) custom-call(f32[512,1024]{1,0:T(8,128)S(1)} %get-tuple-element.115.refs_1_.refs_0_, f32[512,1024]{1,0:T(8,128)S(1)} %get-tuple-element.121.refs_1_, bf16[512,2048]{1,0:T(8,128)(2,1)S(1)} %get-tuple-element.122.refs_2_, ...), custom_call_target="tpu_custom_call" | custom-call | flops 3000000000 | bytes 10000000 | tf_op jit(solution)/shard_map/gates/pallas_call | solution.py:56
  75.1 0.0 collective-permute-done.20.refs_3_
  75.1 0.0 collective-permute-done.21.refs_4_
  75.1 0.3 collective-permute-done.22.refs_5_
  75.5 0.2 device_entry.3
  75.7 2.8 %collective-permute-start.23 = (bf16[1040,128]{1,0:T(8,128)(2,1)S(1)}, bf16[1040,128]{1,0:T(8,128)(2,1)S(1)}, u32[]{:S(2)}, u32[]{:S(2)}) collective-permute-start(bf16[1040,128]{1,0:T(8,128)(2,1)S(1)} %get-tuple-element.155), channel_id=1, source_target_pairs={{0,4},{4,0},{8,12},{12,8},{16,20},{20,16},{24,28},{28,24},{32,36},... | collective-permute-start | bytes 798728 | tf_op jit(solution)/shard_map/ppermute | solution.py:689
  78.5 2.0 %finish.2 = (bf16[512,2048]{1,0:T(8,128)(2,1)}, bf16[512,2048]{1,0:T(8,128)(2,1)}) custom-call(f32[512,1024]{1,0:T(8,128)S(1)} %get-tuple-element.158.refs_0_, f32[512,1024]{1,0:T(8,128)S(1)} %get-tuple-element.159.refs_1_, bf16[512,1024]{1,0:T(8,128)(2,1)S(1)} %get-tuple-element.89.refs_0_.refs_1_.refs_2_, ...), custom_call_target="tpu_custom_call" | custom-call | flops 1200000000 | bytes 4000000 | tf_op jit(solution)/shard_map/finish/pallas_call | solution.py:56
  80.5 2.1 %finish.3 = (bf16[512,2048]{1,0:T(8,128)(2,1)}, bf16[512,2048]{1,0:T(8,128)(2,1)}, f32[16,128]{1,0:T(8,128)}) custom-call(f32[512,1024]{1,0:T(8,128)S(1)} %get-tuple-element.148.refs_0_, f32[512,1024]{1,0:T(8,128)S(1)} %get-tuple-element.149.refs_1_, ...), custom_call_target="tpu_custom_call", output_to_operand_aliasing={{0}: (9, {}), {1}: (10, {})} | custom-call | flops 1200000000 | bytes 4000000 | tf_op jit(solution)/shard_map/finish/pallas_call | solution.py:56
  (8 shorter events, 0.0 us)
Async XLA Ops:
  3.3 3.9 %collective-permute-start = (bf16[1040,128]{1,0:T(8,128)(2,1)S(1)}, bf16[1040,128]{1,0:T(8,128)(2,1)S(1)}, u32[]{:S(2)}, u32[]{:S(2)}) collective-permute-start(bf16[1040,128]{1,0:T(8,128)(2,1)S(1)} %get-tuple-element.92), channel_id=1, source_target_pairs={{0,4},{4,0},{8,12},{12,8},{16,20},{20,16},{24,28},{28,24},{32,36},... | collective-permute-start | bytes 798728 | tf_op jit(solution)/shard_map/ppermute | solution.py:689
  7.3 6.8 %collective-permute-start.1 = (bf16[272,128]{1,0:T(8,128)(2,1)S(1)}, bf16[272,128]{1,0:T(8,128)(2,1)S(1)}, u32[]{:S(2)}, u32[]{:S(2)}) collective-permute-start(bf16[272,128]{1,0:T(8,128)(2,1)S(1)} %get-tuple-element.96), channel_id=1, source_target_pairs={{0,8},{4,12},{8,0},{12,4},{16,24},{20,28},{24,16},{28,20},{32,40},... | collective-permute-start | bytes 208904 | tf_op jit(solution)/shard_map/ppermute | solution.py:689
  8.7 6.3 %collective-permute-start.2 = (bf16[272,128]{1,0:T(8,128)(2,1)S(1)}, bf16[272,128]{1,0:T(8,128)(2,1)S(1)}, u32[]{:S(2)}, u32[]{:S(2)}) collective-permute-start(bf16[272,128]{1,0:T(8,128)(2,1)S(1)} %get-tuple-element.97), channel_id=1, source_target_pairs={{0,16},{4,20},{8,24},{12,28},{16,0},{20,4},{24,8},{28,12},{32,48},... | collective-permute-start | bytes 208904 | tf_op jit(solution)/shard_map/ppermute | solution.py:689
  11.1 5.0 %collective-permute-start.3 = (bf16[272,128]{1,0:T(8,128)(2,1)S(1)}, bf16[272,128]{1,0:T(8,128)(2,1)S(1)}, u32[]{:S(2)}, u32[]{:S(2)}) collective-permute-start(bf16[272,128]{1,0:T(8,128)(2,1)S(1)} %get-tuple-element.98), channel_id=1, source_target_pairs={{0,24},{4,28},{8,16},{12,20},{16,8},{20,12},{24,0},{28,4},{32,56},... | collective-permute-start | bytes 208904 | tf_op jit(solution)/shard_map/ppermute | solution.py:689
  16.2 7.3 %collective-permute-start.5 = (bf16[272,128]{1,0:T(8,128)(2,1)S(1)}, bf16[272,128]{1,0:T(8,128)(2,1)S(1)}, u32[]{:S(2)}, u32[]{:S(2)}) collective-permute-start(bf16[272,128]{1,0:T(8,128)(2,1)S(1)} %row_sum.2.refs_5_.refs_4_), channel_id=1, source_target_pairs={{0,64},{4,68},{8,72},{12,76},{16,80},{20,84},{24,88},{28,92},{32,9... | collective-permute-start | bytes 208904 | tf_op jit(solution)/shard_map/ppermute | solution.py:689
  19.6 4.4 %collective-permute-start.4 = (bf16[272,128]{1,0:T(8,128)(2,1)S(1)}, bf16[272,128]{1,0:T(8,128)(2,1)S(1)}, u32[]{:S(2)}, u32[]{:S(2)}) collective-permute-start(bf16[272,128]{1,0:T(8,128)(2,1)S(1)} %row_sum.2.refs_5_.refs_4_), channel_id=1, source_target_pairs={{0,32},{4,36},{8,40},{12,44},{16,48},{20,52},{24,56},{28,60},{32,6... | collective-permute-start | bytes 208904 | tf_op jit(solution)/shard_map/ppermute | solution.py:705
  24.3 6.5 %collective-permute-start.6 = (bf16[256,128]{1,0:T(8,128)(2,1)S(1)}, bf16[256,128]{1,0:T(8,128)(2,1)S(1)}, u32[]{:S(2)}, u32[]{:S(2)}) collective-permute-start(bf16[256,128]{1,0:T(8,128)(2,1)S(1)} %get-tuple-element.107), channel_id=1, source_target_pairs={{0,8},{4,12},{8,0},{12,4},{16,24},{20,28},{24,16},{28,20},{32,40},... | collective-permute-start | bytes 196616 | tf_op jit(solution)/shard_map/ppermute | solution.py:689
  24.7 6.0 %collective-permute-start.7 = (bf16[256,128]{1,0:T(8,128)(2,1)S(1)}, bf16[256,128]{1,0:T(8,128)(2,1)S(1)}, u32[]{:S(2)}, u32[]{:S(2)}) collective-permute-start(bf16[256,128]{1,0:T(8,128)(2,1)S(1)} %get-tuple-element.108), channel_id=1, source_target_pairs={{0,16},{4,20},{8,24},{12,28},{16,0},{20,4},{24,8},{28,12},{32,48},... | collective-permute-start | bytes 196616 | tf_op jit(solution)/shard_map/ppermute | solution.py:689
  27.3 4.3 %collective-permute-start.8 = (bf16[256,128]{1,0:T(8,128)(2,1)S(1)}, bf16[256,128]{1,0:T(8,128)(2,1)S(1)}, u32[]{:S(2)}, u32[]{:S(2)}) collective-permute-start(bf16[256,128]{1,0:T(8,128)(2,1)S(1)} %get-tuple-element.109), channel_id=1, source_target_pairs={{0,24},{4,28},{8,16},{12,20},{16,8},{20,12},{24,0},{28,4},{32,56},... | collective-permute-start | bytes 196616 | tf_op jit(solution)/shard_map/ppermute | solution.py:689
  28.2 7.3 %copy-start = (f32[2048]{0:T(1024)S(1)}, f32[2048]{0:T(1024)}, u32[]{:S(2)}) copy-start(f32[2048]{0:T(1024)} %param.12) | copy-start | bytes 24580
  31.8 5.6 %collective-permute-start.9 = (bf16[1024,128]{1,0:T(8,128)(2,1)S(1)}, bf16[1024,128]{1,0:T(8,128)(2,1)S(1)}, u32[]{:S(2)}, u32[]{:S(2)}) collective-permute-start(bf16[1024,128]{1,0:T(8,128)(2,1)S(1)} %get-tuple-element.118), channel_id=1, source_target_pairs={{0,4},{4,0},{8,12},{12,8},{16,20},{20,16},{24,28},{28,24},{32,36},... | collective-permute-start | bytes 786440 | tf_op jit(solution)/shard_map/ppermute | solution.py:689
  39.3 3.9 %collective-permute-start.12 = (f32[8,512]{1,0:T(8,128)S(1)}, f32[8,512]{1,0:T(8,128)S(1)}, u32[]{:S(2)}, u32[]{:S(2)}) collective-permute-start(f32[8,512]{1,0:T(8,128)S(1)} %get-tuple-element.124.refs_5_), channel_id=1, source_target_pairs={{0,3},{1,2},{2,1},{3,0},{4,7},{5,6},{6,5},{7,4},{8,11},{9,10},{10,... | collective-permute-start | bytes 49160 | tf_op jit(solution)/shard_map/ppermute | solution.py:689
  42.0 4.1 %collective-permute-start.11 = (f32[8,512]{1,0:T(8,128)S(1)}, f32[8,512]{1,0:T(8,128)S(1)}, u32[]{:S(2)}, u32[]{:S(2)}) collective-permute-start(f32[8,512]{1,0:T(8,128)S(1)} %get-tuple-element.124.refs_5_), channel_id=1, source_target_pairs={{0,2},{1,3},{2,0},{3,1},{4,6},{5,7},{6,4},{7,5},{8,10},{9,11},{10,... | collective-permute-start | bytes 49160 | tf_op jit(solution)/shard_map/ppermute | solution.py:689
  42.4 3.7 %collective-permute-start.10 = (f32[8,512]{1,0:T(8,128)S(1)}, f32[8,512]{1,0:T(8,128)S(1)}, u32[]{:S(2)}, u32[]{:S(2)}) collective-permute-start(f32[8,512]{1,0:T(8,128)S(1)} %get-tuple-element.124.refs_5_), channel_id=1, source_target_pairs={{0,1},{1,0},{2,3},{3,2},{4,5},{5,4},{6,7},{7,6},{8,9},{9,8},{10,11... | collective-permute-start | bytes 49160 | tf_op jit(solution)/shard_map/ppermute | solution.py:689
  48.1 3.4 %collective-permute-start.13 = (bf16[1056,128]{1,0:T(8,128)(2,1)S(1)}, bf16[1056,128]{1,0:T(8,128)(2,1)S(1)}, u32[]{:S(2)}, u32[]{:S(2)}) collective-permute-start(bf16[1056,128]{1,0:T(8,128)(2,1)S(1)} %get-tuple-element.129), channel_id=1, source_target_pairs={{0,4},{4,0},{8,12},{12,8},{16,20},{20,16},{24,28},{28,24},{32,36},... | collective-permute-start | bytes 811016 | tf_op jit(solution)/shard_map/ppermute | solution.py:689
  51.6 7.9 %collective-permute-start.14 = (bf16[288,128]{1,0:T(8,128)(2,1)S(1)}, bf16[288,128]{1,0:T(8,128)(2,1)S(1)}, u32[]{:S(2)}, u32[]{:S(2)}) collective-permute-start(bf16[288,128]{1,0:T(8,128)(2,1)S(1)} %get-tuple-element.131), channel_id=1, source_target_pairs={{0,8},{4,12},{8,0},{12,4},{16,24},{20,28},{24,16},{28,20},{32,40},... | collective-permute-start | bytes 221192 | tf_op jit(solution)/shard_map/ppermute | solution.py:689
  51.7 7.8 %collective-permute-start.15 = (bf16[288,128]{1,0:T(8,128)(2,1)S(1)}, bf16[288,128]{1,0:T(8,128)(2,1)S(1)}, u32[]{:S(2)}, u32[]{:S(2)}) collective-permute-start(bf16[288,128]{1,0:T(8,128)(2,1)S(1)} %get-tuple-element.132), channel_id=1, source_target_pairs={{0,16},{4,20},{8,24},{12,28},{16,0},{20,4},{24,8},{28,12},{32,48},... | collective-permute-start | bytes 221192 | tf_op jit(solution)/shard_map/ppermute | solution.py:689
  54.7 5.4 %collective-permute-start.16 = (bf16[288,128]{1,0:T(8,128)(2,1)S(1)}, bf16[288,128]{1,0:T(8,128)(2,1)S(1)}, u32[]{:S(2)}, u32[]{:S(2)}) collective-permute-start(bf16[288,128]{1,0:T(8,128)(2,1)S(1)} %get-tuple-element.133), channel_id=1, source_target_pairs={{0,24},{4,28},{8,16},{12,20},{16,8},{20,12},{24,0},{28,4},{32,56},... | collective-permute-start | bytes 221192 | tf_op jit(solution)/shard_map/ppermute | solution.py:689
  60.2 7.3 %collective-permute-start.19 = (bf16[288,128]{1,0:T(8,128)(2,1)S(1)}, bf16[288,128]{1,0:T(8,128)(2,1)S(1)}, u32[]{:S(2)}, u32[]{:S(2)}) collective-permute-start(bf16[288,128]{1,0:T(8,128)(2,1)S(1)} %row_sum.3.refs_11_.refs_4_), channel_id=1, source_target_pairs={{0,96},{4,100},{8,104},{12,108},{16,112},{20,116},{24,120},{28,124... | collective-permute-start | bytes 221192 | tf_op jit(solution)/shard_map/ppermute | solution.py:689
  60.6 6.9 %collective-permute-start.18 = (bf16[288,128]{1,0:T(8,128)(2,1)S(1)}, bf16[288,128]{1,0:T(8,128)(2,1)S(1)}, u32[]{:S(2)}, u32[]{:S(2)}) collective-permute-start(bf16[288,128]{1,0:T(8,128)(2,1)S(1)} %row_sum.3.refs_11_.refs_4_), channel_id=1, source_target_pairs={{0,64},{4,68},{8,72},{12,76},{16,80},{20,84},{24,88},{28,92},{32,9... | collective-permute-start | bytes 221192 | tf_op jit(solution)/shard_map/ppermute | solution.py:689
  61.6 6.0 %collective-permute-start.17 = (bf16[288,128]{1,0:T(8,128)(2,1)S(1)}, bf16[288,128]{1,0:T(8,128)(2,1)S(1)}, u32[]{:S(2)}, u32[]{:S(2)}) collective-permute-start(bf16[288,128]{1,0:T(8,128)(2,1)S(1)} %row_sum.3.refs_11_.refs_4_), channel_id=1, source_target_pairs={{0,32},{4,36},{8,40},{12,44},{16,48},{20,52},{24,56},{28,60},{32,0... | collective-permute-start | bytes 221192 | tf_op jit(solution)/shard_map/ppermute | solution.py:689
  67.9 7.2 %collective-permute-start.20 = (bf16[256,128]{1,0:T(8,128)(2,1)S(1)}, bf16[256,128]{1,0:T(8,128)(2,1)S(1)}, u32[]{:S(2)}, u32[]{:S(2)}) collective-permute-start(bf16[256,128]{1,0:T(8,128)(2,1)S(1)} %get-tuple-element.150), channel_id=1, source_target_pairs={{0,8},{4,12},{8,0},{12,4},{16,24},{20,28},{24,16},{28,20},{32,40},... | collective-permute-start | bytes 196616 | tf_op jit(solution)/shard_map/ppermute | solution.py:689
  68.0 7.1 %collective-permute-start.21 = (bf16[256,128]{1,0:T(8,128)(2,1)S(1)}, bf16[256,128]{1,0:T(8,128)(2,1)S(1)}, u32[]{:S(2)}, u32[]{:S(2)}) collective-permute-start(bf16[256,128]{1,0:T(8,128)(2,1)S(1)} %get-tuple-element.151), channel_id=1, source_target_pairs={{0,16},{4,20},{8,24},{12,28},{16,0},{20,4},{24,8},{28,12},{32,48},... | collective-permute-start | bytes 196616 | tf_op jit(solution)/shard_map/ppermute | solution.py:689
  70.4 5.0 %collective-permute-start.22 = (bf16[256,128]{1,0:T(8,128)(2,1)S(1)}, bf16[256,128]{1,0:T(8,128)(2,1)S(1)}, u32[]{:S(2)}, u32[]{:S(2)}) collective-permute-start(bf16[256,128]{1,0:T(8,128)(2,1)S(1)} %get-tuple-element.152), channel_id=1, source_target_pairs={{0,24},{4,28},{8,16},{12,20},{16,8},{20,12},{24,0},{28,4},{32,56},... | collective-permute-start | bytes 196616 | tf_op jit(solution)/shard_map/ppermute | solution.py:689
  75.7 4.8 %collective-permute-start.23 = (bf16[1040,128]{1,0:T(8,128)(2,1)S(1)}, bf16[1040,128]{1,0:T(8,128)(2,1)S(1)}, u32[]{:S(2)}, u32[]{:S(2)}) collective-permute-start(bf16[1040,128]{1,0:T(8,128)(2,1)S(1)} %get-tuple-element.155), channel_id=1, source_target_pairs={{0,4},{4,0},{8,12},{12,8},{16,20},{20,16},{24,28},{28,24},{32,36},... | collective-permute-start | bytes 798728 | tf_op jit(solution)/shard_map/ppermute | solution.py:689

commit v5 on v4

--- a/solution.py
+++ b/solution.py
@@ -92,6 +92,10 @@
     return pl.ds(pl.multiple_of(start, width), width)
 
 
+def store_half(source, base, target, sem):
+    return pltpu.make_async_copy(source, target.at[:, span(base, WIDE)], sem)
+
+
 def load(source, base, at, target, sem, width=SPAN):
     return pltpu.make_async_copy(
         source.at[:, span(base + at, width)], target.at[:, span(at, width)], sem
@@ -158,35 +162,36 @@
     else:
         seg, last, k_far, v_far, k, v, out, early, sems = refs
     base = base_column(ids, flip)
-    groups = HEADS // FINE
     copies = [
         [
-            load(far_ref, base, g * FINE_SPAN, ref, sems.at[n, g], FINE_SPAN)
-            for n, (far_ref, ref) in enumerate(((k_far, k), (v_far, v)))
+            pltpu.make_async_copy(far_ref.at[t, span(base, WIDE)], ref.at[t, :], sems.at[m, n])
+            for m, (far_ref, ref) in enumerate(((k_far, k), (v_far, v)))
         ]
-        for g in range(groups)
+        for n, t in BLOCKS
     ]
-    if flip:
-        copy = pltpu.make_async_copy(seg_far, seg, seg_sem)
-        copy.start()
     for pair in copies:
         for c in pair:
             c.start()
     if flip:
+        copy = pltpu.make_async_copy(seg_far, seg, seg_sem)
+        copy.start()
         copy.wait()
         fill_last_mask(seg, last)
     start0, end0, _, end1 = split_ends(seg)
     join = flag(end0 == end1)
     out[STATE_ROWS : STATE_ROWS + TILE, :] = info_tile(start0, end1)
-    for g in range(groups):
-        for c in copies[g]:
+    for n, t in BLOCKS:
+        for c in copies[n]:
             c.wait()
-        group = range(g * FINE, (g + 1) * FINE)
-        rows = [(k[:, head_columns(h)] * last[...], v[:, head_columns(h)]) for h in group]
-        parts = [[dot(kh[t], vh[t], 0, 0) for _, t in BLOCKS] for kh, vh in rows]
-        for h, (one, two) in zip(group, parts):
-            early[head_rows(h), :] = one
-            out[head_rows(h), :] = (two + one * join).astype(BF16)
+        rows = [(k[t, head_columns(h)] * last[t, :], v[t, head_columns(h)]) for h in range(HEADS)]
+        parts = [dot(kh, vh, 0, 0) for kh, vh in rows]
+        if n == 1:
+            parts = [two + early[head_rows(h), :] * join for h, two in enumerate(parts)]
+        for h, part in enumerate(parts):
+            if n == 0:
+                early[head_rows(h), :] = part
+            else:
+                out[head_rows(h), :] = part.astype(BF16)
 
 
 def local_state(k, v, seg, seg_vmem=None, last=None):
@@ -195,7 +200,7 @@
         half_shape(BF16), half_shape(BF16), vmem((STATE_ROWS + TILE, HD), BF16),
         vmem((STATE_ROWS, HD), F32),
     ]
-    scratch = [pltpu.SemaphoreType.DMA((2, HEADS // FINE))]
+    scratch = [pltpu.SemaphoreType.DMA((2, 2))]
     near, distant = [seg_vmem, last], [k, v]
     if flip:
         outs += [vmem((1, TOK), jnp.int32), vmem((TOK, HD), BF16)]
@@ -305,11 +310,15 @@
 
 
 def cross_kernel(flip, ids, attn_in, q, s, early, w, before, seg, gain, *rest):
-    previous = rest[0] if flip else None
-    attn, second, sums, squares, inners = rest[-5:]
+    if flip:
+        squares_in, inners_in, attn, second, sums, squares, inners = rest
+        squares[...] = squares_in[...]
+        inners[...] = inners_in[...]
+    else:
+        attn, second, squares, inners = rest
+        squares[...] = jnp.zeros_like(squares)
+        inners[...] = jnp.zeros_like(inners)
     base = base_column(ids, flip)
-    squares[...] = jnp.zeros_like(squares)
-    inners[...] = jnp.zeros_like(inners)
     start0, end0, _, _ = split_ends(seg)
     join = flag(start0 == end0)
 
@@ -337,26 +346,25 @@
             second[head_rows(h), :] = two
 
     each_group(body)
-    ones = jnp.ones((8, HD), F32)
-    dims = (((1,), (1,)), ((), ()))
-    ss, dd = [
-        lax.dot_general(
-            ones, x[...], dims, precision=lax.Precision.HIGHEST, preferred_element_type=F32
-        )
-        for x in (squares, inners)
-    ]
-    total = jnp.where(lax.broadcasted_iota(jnp.int32, (8, TOK), 0) < 4, ss, dd)
-    if flip:
-        total = total + previous[...]
-    sums[...] = total
+    if flip:
+        ones = jnp.ones((8, HD), BF16)
+        totals = []
+        for x in (squares[...], inners[...]):
+            high = x.astype(BF16)
+            low = (x - high.astype(F32)).astype(BF16)
+            totals.append(dot(ones, high, 1, 1) + dot(ones, low, 1, 1))
+        row = lax.broadcasted_iota(jnp.int32, (8, TOK), 0)
+        sums[...] = jnp.where(row < 4, totals[0], totals[1])
 
 
 def cross(flip, attn, q, state, early, w, before, seg, gain, previous=()):
+    total = vmem((TOK, HD), F32)
+    outs = [half_shape(F32), vmem((STATE_ROWS, HD), BF16)]
     return call(
         functools.partial(cross_kernel, flip), "cross", 1.2e9,
         [attn, q, state, early, w, before, seg, gain, *previous],
-        [half_shape(F32), vmem((STATE_ROWS, HD), BF16), vmem((8, TOK), F32)], (),
-        [pltpu.VMEM((TOK, HD), F32), pltpu.VMEM((TOK, HD), F32)],
+        outs + ([vmem((8, TOK), F32)] if flip else [total, total]), (),
+        [pltpu.VMEM((TOK, HD), F32)] * 2 if flip else [],
     )
 
 
@@ -419,8 +427,13 @@
 
 
 def local_grads_kernel(flip, ids, q, k, v, grad, s0, s1, w0, w1, m0, m1, before, _, *rest):
-    dq_far, dk, dv, token, dq, sems = rest[-6:]
-    base = base_column(ids, flip)
+    if flip:
+        dq_keep, dq_far, dq, dk, dv, token, sems = rest
+        keep_copy = store_half(dq_keep, base_column(ids, 0), dq_far, sems.at[1])
+        keep_copy.start()
+        first_copy = store(dq, 0, base_column(ids, 1), dq_far, sems.at[0])
+    else:
+        dq, dk, dv, token = rest
     token[...] = jnp.zeros_like(token)
 
     def body(g):
@@ -450,26 +463,32 @@
                 dq[t, c] = x.astype(BF16)
                 dk[t, c] = y
                 dv[t, c] = z
-        store(dq, g * SPAN, base + g * SPAN, dq_far, sems.at[g]).start()
+        if flip:
+            pl.when(g == 0)(first_copy.start)
 
     each_group(body)
-    for g in range(GROUPS):
-        store(dq, g * SPAN, base + g * SPAN, dq_far, sems.at[g]).wait()
-
-
-def local_grads(flip, q, k, v, g, states, weights, masks, before, after, done=()):
-    near = [q, k, v, g, *states, *weights, *masks, before, after]
+    if flip:
+        first_copy.wait()
+        keep_copy.wait()
+
+
+def local_grads(flip, q, k, v, g, states, weights, masks, before, after, dq_keep=()):
+    near = [q, k, v, g, *states, *weights, *masks, before, after, *dq_keep]
+    outs = [half_shape(BF16), half_shape(F32), half_shape(F32), TOKEN]
     return call(
         functools.partial(local_grads_kernel, flip), "local_grads", 5e9, near,
-        [far(), half_shape(F32), half_shape(F32), TOKEN], done,
-        [pltpu.VMEM((TOK, WIDE), BF16), pltpu.SemaphoreType.DMA((GROUPS,))],
-        {len(near): 0} if done else None,
-    )
-
-
-def gates_kernel(ids, keep, send, gi, w, rinv, gain, _, lo_far, gg_far, token, lo, gg, sems):
+        [far()] * flip + outs, (), [pltpu.SemaphoreType.DMA((2,))] * flip,
+    )
+
+
+def gates_kernel(
+    ids, keep, send, gi, w, rinv, gain, dq, _, dq_in, lo_far, gg_far, dq_far, token, lo, gg, sems,
+    dq_sem
+):
     token[...] = jnp.zeros_like(token)
-    copies = []
+    at = (GROUPS - 1) * SPAN
+    copies = [store(dq, at, base_column(ids, 1) + at, dq_far, dq_sem)]
+    copies[0].start()
     for flip, attn in enumerate((keep, send)):
         base = base_column(ids, flip)
 
@@ -495,15 +514,17 @@
         copy.wait()
 
 
-def gates(keep, send, gi, w, rinv, gain, after):
+def gates(keep, send, gi, w, rinv, gain, dq, after, dq_far):
+    near = [keep, send, gi, w, rinv, gain, dq, after]
     return call(
-        gates_kernel, "gates", 3e9, [keep, send, gi, w, rinv, gain, after],
-        [far(), far(), TOKEN], (),
+        gates_kernel, "gates", 3e9, near, [far(), far(), far(), TOKEN], [dq_far],
         [
             pltpu.VMEM((TOK, 2 * WIDE), BF16),
             pltpu.VMEM((TOK, 2 * WIDE), BF16),
             pltpu.SemaphoreType.DMA((2, 2, GROUPS)),
+            pltpu.SemaphoreType.DMA,
         ],
+        {len(near): 2},
     )
 
 
@@ -771,11 +792,11 @@
     q_send, attn_send, w0_send, w1_send, qt_send, _ = made["send"]
     gated, gate, _ = made["gate"]
 
-    attn_keep, second_keep, sums = cross(
+    attn_keep, second_keep, *sums = cross(
         0, attn_keep, q_keep, state_keep, early_keep, gated, before, seg, gain
     )
     attn_send, second_send, sums = cross(
-        1, attn_send, q_send, state_send, early_send, gated, before, seg, gain, (sums,)
+        1, attn_send, q_send, state_send, early_send, gated, before, seg, gain, sums
     )
     sums = [sums] + [swap(sums, "tp", 4, m) for m in range(1, 4)]
 
@@ -797,18 +818,20 @@
             1, q_send, k_send, v_send, g_send, (state_send, second_send), (w0_send, w1_send),
             masks, before, token, (made["gk"][0],),
         )
-        return made["gs"][3]
+        return made["gs"][4]
 
     def gates_both(token):
-        made["out"] = gates(attn_keep, attn_send, gate, gated, rinv, gain, token)
-        return made["out"][2]
+        made["out"] = gates(
+            attn_keep, attn_send, gate, gated, rinv, gain, made["gs"][1], token, made["gs"][0]
+        )
+        return made["out"][3]
 
     later_keep, later_send, total = scan(
         own, other, True, True, grads_keep, grads_send, gates_both
     )
     _, dk_keep, dv_keep, _ = made["gk"]
-    grad_query, dk_send, dv_send, _ = made["gs"]
-    layer_out, grad_gate, _ = made["out"]
+    _, _, dk_send, dv_send, _ = made["gs"]
+    layer_out, grad_gate, grad_query, _ = made["out"]
     done = finish(0, dk_keep, dv_keep, k_keep, v_keep, later_keep, late_keep, seg, after)
     grad_keys, grad_values, grad_gain = finish(
         1, dk_send, dv_send, k_send, v_send, later_send, late_send, seg, after, (total[0],),

time: 83 us -> 81.2 us (0.978)
  Pallas kernels: 37.2 us -> 33.8 us
  starting transfers between devices: 36.7 us -> 37.7 us
    pallas_call x22, Pallas kernels: 37.2 us -> 33.8 us  [call(): pl.pallas_call(placed, in_specs=[VM] * len(near) + [ANY] * len(distant),...]
    ppermute x23, waiting for transfers between devices: 7.2 us -> 8.42 us  [swap(): return lax.ppermute(x, axis, [(i, i ^ bits) for i in range(size)])]
  transfers between devices with their start and end apart: 24 -> 24, of which waited for: 8 -> 7; matrix products, arithmetic and copies ran while one was open for 0% -> 0% of each run, Pallas kernels for 33% -> 31%
where the time goes in v5:
time: 81.2 us; the launch traced here: 81 us
  starting transfers between devices  37.7 us (46%)
  Pallas kernels  33.8 us (42%)
  waiting for transfers between devices  8.42 us (10%)
  between operations  1.07 us (1%)
    ppermute x23, starting transfers between devices, swap(): return lax.ppermute(x, axis, [(i, i ^ bits) for i in range(size)])  36 us
    pallas_call x22, Pallas kernels, call(): pl.pallas_call(placed, in_specs=[VM] * len(near) + [ANY] * len(distant),...  33.8 us
    ppermute x23, waiting for transfers between devices, swap(): return lax.ppermute(x, axis, [(i, i ^ bits) for i in range(size)])  8.42 us
    ppermute x1, starting transfers between devices, plane_shift(): return lax.ppermute(x, 'ctx', [(i, (i + 8) % 32) for i in range(32)])  1.71 us
  transfers between devices with their start and end apart: 24, of which 7 were waited for; matrix products, arithmetic and copies ran while one was open for 0% of the time, Pallas kernels for 31%

profile of v5, /device:TPU:1, one launch (start us, length us, event | category | flops | bytes accessed | tf_op | source)
XLA Modules:
  0.0 81.0 jit_solution(13424596839648680648)
XLA Ops:
  0.6 2.0 %local_state.2 = (bf16[512,1024]{1,0:T(8,128)(2,1)S(1)}, bf16[512,1024]{1,0:T(8,128)(2,1)S(1)}, bf16[1040,128]{1,0:T(8,128)(2,1)S(1)}, f32[1024,128]{1,0:T(8,128...) custom-call(bf16[512,2048]{1,0:T(8,128)(2,1)} %refs_2_.2, bf16[512,2048]{1,0:T(8,128)(2,1)} %refs_3_.1, ...), custom_call_target="tpu_custom_call" | custom-call | flops 1000000000 | bytes 3333333 | tf_op jit(solution)/shard_map/local_state/pallas_call | solution.py:56
  2.6 1.5 %collective-permute-start = (bf16[1040,128]{1,0:T(8,128)(2,1)S(1)}, bf16[1040,128]{1,0:T(8,128)(2,1)S(1)}, u32[]{:S(2)}, u32[]{:S(2)}) collective-permute-start(bf16[1040,128]{1,0:T(8,128)(2,1)S(1)} %get-tuple-element.95), channel_id=1, source_target_pairs={{0,4},{4,0},{8,12},{12,8},{16,20},{20,16},{24,28},{28,24},{32,36},... | collective-permute-start | bytes 798728 | tf_op jit(solution)/shard_map/ppermute | solution.py:710
  4.1 2.0 %local_state.3 = (bf16[512,1024]{1,0:T(8,128)(2,1)S(1)}, bf16[512,1024]{1,0:T(8,128)(2,1)S(1)}, bf16[1040,128]{1,0:T(8,128)(2,1)S(1)}, f32[1024,128]{1,0:T(8,128)S(1)}) custom-call(s32[1,512]{1,0:T(1,128)S(1)} %get-tuple-element.90.refs_0_.refs_2_.refs_6_, bf16[512,128]{1,0:T(8,128)(2,1)S(1)} %get-tuple-element.91.refs_1_, bf16[512,2048]{1,0:T(8,128)(2,1)} %refs_2_.2, ...), custom_call_target="tpu_custom_call" | custom-call | flops 1000000000 | bytes 3333333 | tf_op jit(solution)/shard_map/local_state/pallas_call | solution.py:56
  6.1 0.0 collective-permute-done.refs_1_
  6.1 0.1 chip_sum.2
  6.2 1.4 %collective-permute-start.1 = (bf16[272,128]{1,0:T(8,128)(2,1)S(1)}, bf16[272,128]{1,0:T(8,128)(2,1)S(1)}, u32[]{:S(2)}, u32[]{:S(2)}) collective-permute-start(bf16[272,128]{1,0:T(8,128)(2,1)S(1)} %get-tuple-element.99), channel_id=1, source_target_pairs={{0,8},{4,12},{8,0},{12,4},{16,24},{20,28},{24,16},{28,20},{32,40},... | collective-permute-start | bytes 208904 | tf_op jit(solution)/shard_map/ppermute | solution.py:710
  7.6 2.4 %collective-permute-start.2 = (bf16[272,128]{1,0:T(8,128)(2,1)S(1)}, bf16[272,128]{1,0:T(8,128)(2,1)S(1)}, u32[]{:S(2)}, u32[]{:S(2)}) collective-permute-start(bf16[272,128]{1,0:T(8,128)(2,1)S(1)} %get-tuple-element.100), channel_id=1, source_target_pairs={{0,16},{4,20},{8,24},{12,28},{16,0},{20,4},{24,8},{28,12},{32,48},... | collective-permute-start | bytes 208904 | tf_op jit(solution)/shard_map/ppermute | solution.py:710
  10.0 0.1 collective-permute-start.3
  10.2 2.8 %intra.2 = (bf16[512,1024]{1,0:T(8,128)(2,1)S(1)}, f32[512,1024]{1,0:T(8,128)S(1)}, bf16[2048,256]{1,0:T(8,128)(2,1)S(1)}, bf16[2048,256]{1,0:T(8,128)(2,1)S(1)}...) custom-call(bf16[512,1024]{1,0:T(8,128)(2,1)S(1)} %get-tuple-element, ...), custom_call_target="tpu_custom_call" | custom-call | flops 3000000000 | bytes 10000000 | tf_op jit(solution)/shard_map/intra/pallas_call | solution.py:56
  13.0 0.0 collective-permute-done.1.refs_1_
  13.0 0.9 %collective-permute-done.2.refs_2_ = bf16[272,128]{1,0:T(8,128)(2,1)S(1)} collective-permute-done((bf16[272,128]{1,0:T(8,128)(2,1)S(1)}, bf16[272,128]{1,0:T(8,128)(2,1)S(1)}, u32[]{:S(2)}, u32[]{:S(2)}) %collective-permute-start.2) | collective-permute-done | bytes 69664 | tf_op jit(solution)/shard_map/ppermute | solution.py:710
  13.9 0.9 %collective-permute-done.3.refs_3_ = bf16[272,128]{1,0:T(8,128)(2,1)S(1)} collective-permute-done((bf16[272,128]{1,0:T(8,128)(2,1)S(1)}, bf16[272,128]{1,0:T(8,128)(2,1)S(1)}, u32[]{:S(2)}, u32[]{:S(2)}) %collective-permute-start.3) | collective-permute-done | bytes 69664 | tf_op jit(solution)/shard_map/ppermute | solution.py:710
  14.7 0.1 row_sum.2.refs_5_.refs_4_
  14.8 1.7 %collective-permute-start.4 = (bf16[272,128]{1,0:T(8,128)(2,1)S(1)}, bf16[272,128]{1,0:T(8,128)(2,1)S(1)}, u32[]{:S(2)}, u32[]{:S(2)}) collective-permute-start(bf16[272,128]{1,0:T(8,128)(2,1)S(1)} %row_sum.2.refs_5_.refs_4_), channel_id=1, source_target_pairs={{0,32},{4,36},{8,40},{12,44},{16,48},{20,52},{24,56},{28,60},{32,6... | collective-permute-start | bytes 208904 | tf_op jit(solution)/shard_map/ppermute | solution.py:726
  16.5 3.6 %collective-permute-start.5 = (bf16[272,128]{1,0:T(8,128)(2,1)S(1)}, bf16[272,128]{1,0:T(8,128)(2,1)S(1)}, u32[]{:S(2)}, u32[]{:S(2)}) collective-permute-start(bf16[272,128]{1,0:T(8,128)(2,1)S(1)} %row_sum.2.refs_5_.refs_4_), channel_id=1, source_target_pairs={{0,64},{4,68},{8,72},{12,76},{16,80},{20,84},{24,88},{28,92},{32,9... | collective-permute-start | bytes 208904 | tf_op jit(solution)/shard_map/ppermute | solution.py:710
  20.1 2.8 %intra.3 = (bf16[512,1024]{1,0:T(8,128)(2,1)S(1)}, f32[512,1024]{1,0:T(8,128)S(1)}, bf16[2048,256]{1,0:T(8,128)(2,1)S(1)}, bf16[2048,256]{1,0:T(8,128)(2,1)S(1)}...) custom-call(bf16[512,1024]{1,0:T(8,128)(2,1)S(1)} %get-tuple-element.103.refs_0_.refs_1_.refs_2_, ...), custom_call_target="tpu_custom_call" | custom-call | flops 3000000000 | bytes 10000000 | tf_op jit(solution)/shard_map/intra/pallas_call | solution.py:56
  22.9 0.0 collective-permute-done.4.refs_5_
  22.9 0.0 collective-permute-done.5.refs_6_
  22.9 0.3 entry.2
  23.2 0.2 collective-permute-start.6
  23.5 2.6 %collective-permute-start.7 = (bf16[256,128]{1,0:T(8,128)(2,1)S(1)}, bf16[256,128]{1,0:T(8,128)(2,1)S(1)}, u32[]{:S(2)}, u32[]{:S(2)}) collective-permute-start(bf16[256,128]{1,0:T(8,128)(2,1)S(1)} %get-tuple-element.111), channel_id=1, source_target_pairs={{0,16},{4,20},{8,24},{12,28},{16,0},{20,4},{24,8},{28,12},{32,48},... | collective-permute-start | bytes 196616 | tf_op jit(solution)/shard_map/ppermute | solution.py:710
  26.1 1.1 %collective-permute-start.8 = (bf16[256,128]{1,0:T(8,128)(2,1)S(1)}, bf16[256,128]{1,0:T(8,128)(2,1)S(1)}, u32[]{:S(2)}, u32[]{:S(2)}) collective-permute-start(bf16[256,128]{1,0:T(8,128)(2,1)S(1)} %get-tuple-element.112), channel_id=1, source_target_pairs={{0,24},{4,28},{8,16},{12,20},{16,8},{20,12},{24,0},{28,4},{32,56},... | collective-permute-start | bytes 196616 | tf_op jit(solution)/shard_map/ppermute | solution.py:710
  27.2 2.5 %prepare.1 = (f32[512,2048]{1,0:T(8,128)S(1)}, bf16[512,2048]{1,0:T(8,128)(2,1)S(1)}, f32[8,128]{1,0:T(8,128)S(1)}) custom-call(bf16[256,128]{1,0:T(8,128)(2,1)S(1)} %get-tuple-element.109.refs_0_.refs_2_, bf16[512,2048]{1,0:T(8,128)(2,1)} %refs_1_.3, bf16[512,2048]{1,0:T(8,128)(2,1)} %refs_2_.3), custom_call_target="tpu_custom_call" | custom-call | flops 3000000000 | bytes 10000000 | tf_op jit(solution)/shard_map/prepare/pallas_call | solution.py:56
  29.7 0.0 collective-permute-done.6.refs_3_
  29.7 0.0 collective-permute-done.7.refs_4_
  29.7 1.4 %collective-permute-done.8.refs_5_ = bf16[256,128]{1,0:T(8,128)(2,1)S(1)} collective-permute-done((bf16[256,128]{1,0:T(8,128)(2,1)S(1)}, bf16[256,128]{1,0:T(8,128)(2,1)S(1)}, u32[]{:S(2)}, u32[]{:S(2)}) %collective-permute-start.8) | collective-permute-done | bytes 65568 | tf_op jit(solution)/shard_map/ppermute | solution.py:710
  31.1 0.2 device_entry.2
  31.4 2.7 %collective-permute-start.9 = (bf16[1024,128]{1,0:T(8,128)(2,1)S(1)}, bf16[1024,128]{1,0:T(8,128)(2,1)S(1)}, u32[]{:S(2)}, u32[]{:S(2)}) collective-permute-start(bf16[1024,128]{1,0:T(8,128)(2,1)S(1)} %get-tuple-element.121), channel_id=1, source_target_pairs={{0,4},{4,0},{8,12},{12,8},{16,20},{20,16},{24,28},{28,24},{32,36},... | collective-permute-start | bytes 786440 | tf_op jit(solution)/shard_map/ppermute | solution.py:710
  34.1 1.4 %cross.2 = (f32[512,1024]{1,0:T(8,128)S(1)}, bf16[1024,128]{1,0:T(8,128)(2,1)S(1)}, f32[512,128]{1,0:T(8,128)S(1)}, f32[512,128]{1,0:T(8,128)S(1)}) custom-call(f32[512,1024]{1,0:T(8,128)S(1)} %get-tuple-element.97.refs_0_, bf16[512,1024]{1,0:T(8,128)(2,1)S(1)} %get-tuple-element.98.refs_1_.refs_0_, ...), custom_call_target="tpu_custom_call" | custom-call | flops 1200000000 | bytes 4000000 | tf_op jit(solution)/shard_map/cross/pallas_call | solution.py:56
  35.5 1.6 %cross.3 = (f32[512,1024]{1,0:T(8,128)S(1)}, bf16[1024,128]{1,0:T(8,128)(2,1)S(1)}, f32[8,512]{1,0:T(8,128)S(1)}) custom-call(f32[512,1024]{1,0:T(8,128)S(1)} %get-tuple-element.119.refs_0_, bf16[512,1024]{1,0:T(8,128)(2,1)S(1)} %get-tuple-element.120.refs_1_.refs_0_, bf16[1024,128]{1,0:T(8,128)(2,1)S(1)} %collective-permute-done.9.refs_2_.refs_4_, ...), custom_call_target="tpu_custom_call" | custom-call | flops 1200000000 | bytes 4000000 | tf_op jit(solution)/shard_map/cross/pallas_call | solution.py:56
  37.0 1.4 %collective-permute-start.10 = (f32[8,512]{1,0:T(8,128)S(1)}, f32[8,512]{1,0:T(8,128)S(1)}, u32[]{:S(2)}, u32[]{:S(2)}) collective-permute-start(f32[8,512]{1,0:T(8,128)S(1)} %get-tuple-element.128.refs_5_), channel_id=1, source_target_pairs={{0,1},{1,0},{2,3},{3,2},{4,5},{5,4},{6,7},{7,6},{8,9},{9,8},{10,11... | collective-permute-start | bytes 49160 | tf_op jit(solution)/shard_map/ppermute | solution.py:710
  38.4 2.6 %collective-permute-start.11 = (f32[8,512]{1,0:T(8,128)S(1)}, f32[8,512]{1,0:T(8,128)S(1)}, u32[]{:S(2)}, u32[]{:S(2)}) collective-permute-start(f32[8,512]{1,0:T(8,128)S(1)} %get-tuple-element.128.refs_5_), channel_id=1, source_target_pairs={{0,2},{1,3},{2,0},{3,1},{4,6},{5,7},{6,4},{7,5},{8,10},{9,11},{10,... | collective-permute-start | bytes 49160 | tf_op jit(solution)/shard_map/ppermute | solution.py:710
  41.0 0.0 collective-permute-start.12
  41.0 0.0 collective-permute-done.10.refs_6_
  41.0 1.5 %collective-permute-done.11.refs_7_ = f32[8,512]{1,0:T(8,128)S(1)} collective-permute-done((f32[8,512]{1,0:T(8,128)S(1)}, f32[8,512]{1,0:T(8,128)S(1)}, u32[]{:S(2)}, u32[]{:S(2)}) %collective-permute-start.11) | collective-permute-done | bytes 16416 | tf_op jit(solution)/shard_map/ppermute | solution.py:710
  42.5 2.3 %collective-permute-done.12.refs_8_ = f32[8,512]{1,0:T(8,128)S(1)} collective-permute-done((f32[8,512]{1,0:T(8,128)S(1)}, f32[8,512]{1,0:T(8,128)S(1)}, u32[]{:S(2)}, u32[]{:S(2)}) %collective-permute-start.12) | collective-permute-done | bytes 16416 | tf_op jit(solution)/shard_map/ppermute | solution.py:710
  44.8 1.9 %grad_attn.2 = (bf16[512,1024]{1,0:T(8,128)(2,1)S(1)}, bf16[1056,128]{1,0:T(8,128)(2,1)S(1)}, f32[1024,128]{1,0:T(8,128)S(1)}, f32[512,128]{1,0:T(8,128)S(1)}, f32[512,128]{1,0:T(8,128)S(1)}) custom-call(s32[1,512]{1,0:T(1,128)S(1)} %get-tuple-element.90.refs_0_.refs_2_.refs_6_, f32[512,1024]{1,0:T(8,128)S(1)} %get-tuple-element.125.refs_1_, ...), custom_call_target="tpu_custom_call" | custom-call | flops 1200000000 | bytes 4000000 | tf_op jit(solution)/shard_map/grad_attn/pallas_call | solution.py:56
  46.7 1.9 %collective-permute-start.13 = (bf16[1056,128]{1,0:T(8,128)(2,1)S(1)}, bf16[1056,128]{1,0:T(8,128)(2,1)S(1)}, u32[]{:S(2)}, u32[]{:S(2)}) collective-permute-start(bf16[1056,128]{1,0:T(8,128)(2,1)S(1)} %get-tuple-element.137), channel_id=1, source_target_pairs={{0,4},{4,0},{8,12},{12,8},{16,20},{20,16},{24,28},{28,24},{32,36},... | collective-permute-start | bytes 811016 | tf_op jit(solution)/shard_map/ppermute | solution.py:710
  48.7 1.7 %grad_attn.3 = (bf16[512,1024]{1,0:T(8,128)(2,1)S(1)}, bf16[1056,128]{1,0:T(8,128)(2,1)S(1)}, f32[1024,128]{1,0:T(8,128)S(1)}) custom-call(s32[1,512]{1,0:T(1,128)S(1)} %get-tuple-element.90.refs_0_.refs_2_.refs_6_, f32[512,1024]{1,0:T(8,128)S(1)} %get-tuple-element.118.refs_1_.refs_0_, f32[512,2048]{1,0:T(8,128)S(1)} %get-tuple-element.116.refs_4_.refs_2_.refs_3_, ...), custom_call_target="tpu_custom_call" | custom-call | flops 1200000000 | bytes 4000000 | tf_op jit(solution)/shard_map/grad_attn/pallas_call | solution.py:56
  50.3 0.1 chip_sum.3
  50.5 0.1 collective-permute-start.14
  50.6 2.5 %collective-permute-start.15 = (bf16[288,128]{1,0:T(8,128)(2,1)S(1)}, bf16[288,128]{1,0:T(8,128)(2,1)S(1)}, u32[]{:S(2)}, u32[]{:S(2)}) collective-permute-start(bf16[288,128]{1,0:T(8,128)(2,1)S(1)} %get-tuple-element.140), channel_id=1, source_target_pairs={{0,16},{4,20},{8,24},{12,28},{16,0},{20,4},{24,8},{28,12},{32,48},... | collective-permute-start | bytes 221192 | tf_op jit(solution)/shard_map/ppermute | solution.py:710
  53.0 1.4 %collective-permute-start.16 = (bf16[288,128]{1,0:T(8,128)(2,1)S(1)}, bf16[288,128]{1,0:T(8,128)(2,1)S(1)}, u32[]{:S(2)}, u32[]{:S(2)}) collective-permute-start(bf16[288,128]{1,0:T(8,128)(2,1)S(1)} %get-tuple-element.141), channel_id=1, source_target_pairs={{0,24},{4,28},{8,16},{12,20},{16,8},{20,12},{24,0},{28,4},{32,56},... | collective-permute-start | bytes 221192 | tf_op jit(solution)/shard_map/ppermute | solution.py:710
  54.4 3.2 %local_grads.2 = (bf16[512,1024]{1,0:T(8,128)(2,1)S(1)}, f32[512,1024]{1,0:T(8,128)S(1)}, f32[512,1024]{1,0:T(8,128)S(1)}, f32[8,128]{1,0:T(8,128)S(1)}) custom-call(bf16[512,1024]{1,0:T(8,128)(2,1)S(1)} %get-tuple-element.98.refs_1_.refs_0_, bf16[512,1024]{1,0:T(8,128)(2,1)S(1)} %get-tuple-element.92.refs_0_.refs_1_.refs_2_, ...), custom_call_target="tpu_custom_call" | custom-call | flops 5000000000 | bytes 16666666 | tf_op jit(solution)/shard_map/local_grads/pallas_call | solution.py:56
  57.7 0.0 collective-permute-done.14.refs_1_
  57.7 0.8 collective-permute-done.16.refs_3_
  58.5 0.1 row_sum.3.refs_11_.refs_4_
  58.5 0.9 %collective-permute-start.17 = (bf16[288,128]{1,0:T(8,128)(2,1)S(1)}, bf16[288,128]{1,0:T(8,128)(2,1)S(1)}, u32[]{:S(2)}, u32[]{:S(2)}) collective-permute-start(bf16[288,128]{1,0:T(8,128)(2,1)S(1)} %row_sum.3.refs_11_.refs_4_), channel_id=1, source_target_pairs={{0,32},{4,36},{8,40},{12,44},{16,48},{20,52},{24,56},{28,60},{32,0... | collective-permute-start | bytes 221192 | tf_op jit(solution)/shard_map/ppermute | solution.py:710
  59.4 1.8 %collective-permute-start.18 = (bf16[288,128]{1,0:T(8,128)(2,1)S(1)}, bf16[288,128]{1,0:T(8,128)(2,1)S(1)}, u32[]{:S(2)}, u32[]{:S(2)}) collective-permute-start(bf16[288,128]{1,0:T(8,128)(2,1)S(1)} %row_sum.3.refs_11_.refs_4_), channel_id=1, source_target_pairs={{0,64},{4,68},{8,72},{12,76},{16,80},{20,84},{24,88},{28,92},{32,9... | collective-permute-start | bytes 221192 | tf_op jit(solution)/shard_map/ppermute | solution.py:710
  61.2 1.3 %collective-permute-start.19 = (bf16[288,128]{1,0:T(8,128)(2,1)S(1)}, bf16[288,128]{1,0:T(8,128)(2,1)S(1)}, u32[]{:S(2)}, u32[]{:S(2)}) collective-permute-start(bf16[288,128]{1,0:T(8,128)(2,1)S(1)} %row_sum.3.refs_11_.refs_4_), channel_id=1, source_target_pairs={{0,96},{4,100},{8,104},{12,108},{16,112},{20,116},{24,120},{28,124... | collective-permute-start | bytes 221192 | tf_op jit(solution)/shard_map/ppermute | solution.py:710
  62.5 3.3 %local_grads.3 = (bf16[512,2048]{1,0:T(8,128)(2,1)}, bf16[512,1024]{1,0:T(8,128)(2,1)S(1)}, f32[512,1024]{1,0:T(8,128)S(1)}, f32[512,1024]{1,0:T(8,128)S(1)}, f32[8,128]{1,0:T(8,128)S(1)}) custom-call(bf16[512,1024]{1,0:T(8,128)(2,1)S(1)} %get-tuple-element.120.refs_1_.refs_0_, bf16[512,1024]{1,0:T(8,128)(2,1)S(1)} %get-tuple-element.103.refs_0_.refs_1_.refs_2_, ...), custom_call_target="tpu_custom_call" | custom-call | flops 5000000000 | bytes 16666666 | tf_op jit(solution)/shard_map/local_grads/pallas_call | solution.py:56
  65.7 0.0 collective-permute-done.18.refs_6_
  65.8 0.7 collective-permute-done.19.refs_7_
  66.4 0.3 entry.3
  66.8 0.1 collective-permute-start.20
  66.9 2.0 %collective-permute-start.21 = (bf16[256,128]{1,0:T(8,128)(2,1)S(1)}, bf16[256,128]{1,0:T(8,128)(2,1)S(1)}, u32[]{:S(2)}, u32[]{:S(2)}) collective-permute-start(bf16[256,128]{1,0:T(8,128)(2,1)S(1)} %get-tuple-element.157), channel_id=1, source_target_pairs={{0,16},{4,20},{8,24},{12,28},{16,0},{20,4},{24,8},{28,12},{32,48},... | collective-permute-start | bytes 196616 | tf_op jit(solution)/shard_map/ppermute | solution.py:710
  68.9 1.8 %collective-permute-start.22 = (bf16[256,128]{1,0:T(8,128)(2,1)S(1)}, bf16[256,128]{1,0:T(8,128)(2,1)S(1)}, u32[]{:S(2)}, u32[]{:S(2)}) collective-permute-start(bf16[256,128]{1,0:T(8,128)(2,1)S(1)} %get-tuple-element.158), channel_id=1, source_target_pairs={{0,24},{4,28},{8,16},{12,20},{16,8},{20,12},{24,0},{28,4},{32,56},... | collective-permute-start | bytes 196616 | tf_op jit(solution)/shard_map/ppermute | solution.py:710
  70.7 3.3 %gates.1 = (bf16[512,2048]{1,0:T(8,128)(2,1)}, bf16[512,2048]{1,0:T(8,128)(2,1)}, bf16[512,2048]{1,0:T(8,128)(2,1)}, f32[8,128]{1,0:T(8,128)S(1)}) custom-call(f32[512,1024]{1,0:T(8,128)S(1)} %get-tuple-element.118.refs_1_.refs_0_, f32[512,1024]{1,0:T(8,128)S(1)} %get-tuple-element.125.refs_1_, ...), custom_call_target="tpu_custom_call", output_to_operand_aliasing={{2}: (8, {})} | custom-call | flops 3000000000 | bytes 10000000 | tf_op jit(solution)/shard_map/gates/pallas_call | solution.py:56
  74.0 0.0 collective-permute-done.20.refs_3_
  74.0 0.0 collective-permute-done.21.refs_4_
  74.0 0.2 device_entry.3
  74.2 2.6 %collective-permute-start.23 = (bf16[1040,128]{1,0:T(8,128)(2,1)S(1)}, bf16[1040,128]{1,0:T(8,128)(2,1)S(1)}, u32[]{:S(2)}, u32[]{:S(2)}) collective-permute-start(bf16[1040,128]{1,0:T(8,128)(2,1)S(1)} %get-tuple-element.161), channel_id=1, source_target_pairs={{0,4},{4,0},{8,12},{12,8},{16,20},{20,16},{24,28},{28,24},{32,36},... | collective-permute-start | bytes 798728 | tf_op jit(solution)/shard_map/ppermute | solution.py:710
  76.9 2.0 %finish.2 = (bf16[512,2048]{1,0:T(8,128)(2,1)}, bf16[512,2048]{1,0:T(8,128)(2,1)}) custom-call(f32[512,1024]{1,0:T(8,128)S(1)} %get-tuple-element.164.refs_0_, f32[512,1024]{1,0:T(8,128)S(1)} %get-tuple-element.165.refs_1_, bf16[512,1024]{1,0:T(8,128)(2,1)S(1)} %get-tuple-element.92.refs_0_.refs_1_.refs_2_, ...), custom_call_target="tpu_custom_call" | custom-call | flops 1200000000 | bytes 4000000 | tf_op jit(solution)/shard_map/finish/pallas_call | solution.py:56
  78.9 2.0 %finish.3 = (bf16[512,2048]{1,0:T(8,128)(2,1)}, bf16[512,2048]{1,0:T(8,128)(2,1)}, f32[16,128]{1,0:T(8,128)}) custom-call(f32[512,1024]{1,0:T(8,128)S(1)} %get-tuple-element.154.refs_0_, f32[512,1024]{1,0:T(8,128)S(1)} %get-tuple-element.155.refs_1_, ...), custom_call_target="tpu_custom_call", output_to_operand_aliasing={{0}: (9, {}), {1}: (10, {})} | custom-call | flops 1200000000 | bytes 4000000 | tf_op jit(solution)/shard_map/finish/pallas_call | solution.py:56
  (8 shorter events, 0.0 us)
Async XLA Ops:
  2.6 3.5 %collective-permute-start = (bf16[1040,128]{1,0:T(8,128)(2,1)S(1)}, bf16[1040,128]{1,0:T(8,128)(2,1)S(1)}, u32[]{:S(2)}, u32[]{:S(2)}) collective-permute-start(bf16[1040,128]{1,0:T(8,128)(2,1)S(1)} %get-tuple-element.95), channel_id=1, source_target_pairs={{0,4},{4,0},{8,12},{12,8},{16,20},{20,16},{24,28},{28,24},{32,36},... | collective-permute-start | bytes 798728 | tf_op jit(solution)/shard_map/ppermute | solution.py:710
  6.2 6.8 %collective-permute-start.1 = (bf16[272,128]{1,0:T(8,128)(2,1)S(1)}, bf16[272,128]{1,0:T(8,128)(2,1)S(1)}, u32[]{:S(2)}, u32[]{:S(2)}) collective-permute-start(bf16[272,128]{1,0:T(8,128)(2,1)S(1)} %get-tuple-element.99), channel_id=1, source_target_pairs={{0,8},{4,12},{8,0},{12,4},{16,24},{20,28},{24,16},{28,20},{32,40},... | collective-permute-start | bytes 208904 | tf_op jit(solution)/shard_map/ppermute | solution.py:710
  7.6 6.3 %collective-permute-start.2 = (bf16[272,128]{1,0:T(8,128)(2,1)S(1)}, bf16[272,128]{1,0:T(8,128)(2,1)S(1)}, u32[]{:S(2)}, u32[]{:S(2)}) collective-permute-start(bf16[272,128]{1,0:T(8,128)(2,1)S(1)} %get-tuple-element.100), channel_id=1, source_target_pairs={{0,16},{4,20},{8,24},{12,28},{16,0},{20,4},{24,8},{28,12},{32,48},... | collective-permute-start | bytes 208904 | tf_op jit(solution)/shard_map/ppermute | solution.py:710
  10.0 4.7 %collective-permute-start.3 = (bf16[272,128]{1,0:T(8,128)(2,1)S(1)}, bf16[272,128]{1,0:T(8,128)(2,1)S(1)}, u32[]{:S(2)}, u32[]{:S(2)}) collective-permute-start(bf16[272,128]{1,0:T(8,128)(2,1)S(1)} %get-tuple-element.101), channel_id=1, source_target_pairs={{0,24},{4,28},{8,16},{12,20},{16,8},{20,12},{24,0},{28,4},{32,56},... | collective-permute-start | bytes 208904 | tf_op jit(solution)/shard_map/ppermute | solution.py:710
  14.8 8.2 %collective-permute-start.4 = (bf16[272,128]{1,0:T(8,128)(2,1)S(1)}, bf16[272,128]{1,0:T(8,128)(2,1)S(1)}, u32[]{:S(2)}, u32[]{:S(2)}) collective-permute-start(bf16[272,128]{1,0:T(8,128)(2,1)S(1)} %row_sum.2.refs_5_.refs_4_), channel_id=1, source_target_pairs={{0,32},{4,36},{8,40},{12,44},{16,48},{20,52},{24,56},{28,60},{32,6... | collective-permute-start | bytes 208904 | tf_op jit(solution)/shard_map/ppermute | solution.py:726
  16.5 6.5 %collective-permute-start.5 = (bf16[272,128]{1,0:T(8,128)(2,1)S(1)}, bf16[272,128]{1,0:T(8,128)(2,1)S(1)}, u32[]{:S(2)}, u32[]{:S(2)}) collective-permute-start(bf16[272,128]{1,0:T(8,128)(2,1)S(1)} %row_sum.2.refs_5_.refs_4_), channel_id=1, source_target_pairs={{0,64},{4,68},{8,72},{12,76},{16,80},{20,84},{24,88},{28,92},{32,9... | collective-permute-start | bytes 208904 | tf_op jit(solution)/shard_map/ppermute | solution.py:710
  23.2 6.5 %collective-permute-start.6 = (bf16[256,128]{1,0:T(8,128)(2,1)S(1)}, bf16[256,128]{1,0:T(8,128)(2,1)S(1)}, u32[]{:S(2)}, u32[]{:S(2)}) collective-permute-start(bf16[256,128]{1,0:T(8,128)(2,1)S(1)} %get-tuple-element.110), channel_id=1, source_target_pairs={{0,8},{4,12},{8,0},{12,4},{16,24},{20,28},{24,16},{28,20},{32,40},... | collective-permute-start | bytes 196616 | tf_op jit(solution)/shard_map/ppermute | solution.py:710
  23.5 6.3 %collective-permute-start.7 = (bf16[256,128]{1,0:T(8,128)(2,1)S(1)}, bf16[256,128]{1,0:T(8,128)(2,1)S(1)}, u32[]{:S(2)}, u32[]{:S(2)}) collective-permute-start(bf16[256,128]{1,0:T(8,128)(2,1)S(1)} %get-tuple-element.111), channel_id=1, source_target_pairs={{0,16},{4,20},{8,24},{12,28},{16,0},{20,4},{24,8},{28,12},{32,48},... | collective-permute-start | bytes 196616 | tf_op jit(solution)/shard_map/ppermute | solution.py:710
  26.1 5.0 %collective-permute-start.8 = (bf16[256,128]{1,0:T(8,128)(2,1)S(1)}, bf16[256,128]{1,0:T(8,128)(2,1)S(1)}, u32[]{:S(2)}, u32[]{:S(2)}) collective-permute-start(bf16[256,128]{1,0:T(8,128)(2,1)S(1)} %get-tuple-element.112), channel_id=1, source_target_pairs={{0,24},{4,28},{8,16},{12,20},{16,8},{20,12},{24,0},{28,4},{32,56},... | collective-permute-start | bytes 196616 | tf_op jit(solution)/shard_map/ppermute | solution.py:710
  27.2 6.9 %copy-start = (f32[2048]{0:T(1024)S(1)}, f32[2048]{0:T(1024)}, u32[]{:S(2)}) copy-start(f32[2048]{0:T(1024)} %param.12) | copy-start | bytes 24580
  31.4 4.1 %collective-permute-start.9 = (bf16[1024,128]{1,0:T(8,128)(2,1)S(1)}, bf16[1024,128]{1,0:T(8,128)(2,1)S(1)}, u32[]{:S(2)}, u32[]{:S(2)}) collective-permute-start(bf16[1024,128]{1,0:T(8,128)(2,1)S(1)} %get-tuple-element.121), channel_id=1, source_target_pairs={{0,4},{4,0},{8,12},{12,8},{16,20},{20,16},{24,28},{28,24},{32,36},... | collective-permute-start | bytes 786440 | tf_op jit(solution)/shard_map/ppermute | solution.py:710
  37.0 4.0 %collective-permute-start.10 = (f32[8,512]{1,0:T(8,128)S(1)}, f32[8,512]{1,0:T(8,128)S(1)}, u32[]{:S(2)}, u32[]{:S(2)}) collective-permute-start(f32[8,512]{1,0:T(8,128)S(1)} %get-tuple-element.128.refs_5_), channel_id=1, source_target_pairs={{0,1},{1,0},{2,3},{3,2},{4,5},{5,4},{6,7},{7,6},{8,9},{9,8},{10,11... | collective-permute-start | bytes 49160 | tf_op jit(solution)/shard_map/ppermute | solution.py:710
  38.4 4.1 %collective-permute-start.11 = (f32[8,512]{1,0:T(8,128)S(1)}, f32[8,512]{1,0:T(8,128)S(1)}, u32[]{:S(2)}, u32[]{:S(2)}) collective-permute-start(f32[8,512]{1,0:T(8,128)S(1)} %get-tuple-element.128.refs_5_), channel_id=1, source_target_pairs={{0,2},{1,3},{2,0},{3,1},{4,6},{5,7},{6,4},{7,5},{8,10},{9,11},{10,... | collective-permute-start | bytes 49160 | tf_op jit(solution)/shard_map/ppermute | solution.py:710
  41.0 3.8 %collective-permute-start.12 = (f32[8,512]{1,0:T(8,128)S(1)}, f32[8,512]{1,0:T(8,128)S(1)}, u32[]{:S(2)}, u32[]{:S(2)}) collective-permute-start(f32[8,512]{1,0:T(8,128)S(1)} %get-tuple-element.128.refs_5_), channel_id=1, source_target_pairs={{0,3},{1,2},{2,1},{3,0},{4,7},{5,6},{6,5},{7,4},{8,11},{9,10},{10,... | collective-permute-start | bytes 49160 | tf_op jit(solution)/shard_map/ppermute | solution.py:710
  46.7 3.6 %collective-permute-start.13 = (bf16[1056,128]{1,0:T(8,128)(2,1)S(1)}, bf16[1056,128]{1,0:T(8,128)(2,1)S(1)}, u32[]{:S(2)}, u32[]{:S(2)}) collective-permute-start(bf16[1056,128]{1,0:T(8,128)(2,1)S(1)} %get-tuple-element.137), channel_id=1, source_target_pairs={{0,4},{4,0},{8,12},{12,8},{16,20},{20,16},{24,28},{28,24},{32,36},... | collective-permute-start | bytes 811016 | tf_op jit(solution)/shard_map/ppermute | solution.py:710
  50.5 7.2 %collective-permute-start.14 = (bf16[288,128]{1,0:T(8,128)(2,1)S(1)}, bf16[288,128]{1,0:T(8,128)(2,1)S(1)}, u32[]{:S(2)}, u32[]{:S(2)}) collective-permute-start(bf16[288,128]{1,0:T(8,128)(2,1)S(1)} %get-tuple-element.139), channel_id=1, source_target_pairs={{0,8},{4,12},{8,0},{12,4},{16,24},{20,28},{24,16},{28,20},{32,40},... | collective-permute-start | bytes 221192 | tf_op jit(solution)/shard_map/ppermute | solution.py:710
  50.6 7.1 %collective-permute-start.15 = (bf16[288,128]{1,0:T(8,128)(2,1)S(1)}, bf16[288,128]{1,0:T(8,128)(2,1)S(1)}, u32[]{:S(2)}, u32[]{:S(2)}) collective-permute-start(bf16[288,128]{1,0:T(8,128)(2,1)S(1)} %get-tuple-element.140), channel_id=1, source_target_pairs={{0,16},{4,20},{8,24},{12,28},{16,0},{20,4},{24,8},{28,12},{32,48},... | collective-permute-start | bytes 221192 | tf_op jit(solution)/shard_map/ppermute | solution.py:710
  53.0 5.4 %collective-permute-start.16 = (bf16[288,128]{1,0:T(8,128)(2,1)S(1)}, bf16[288,128]{1,0:T(8,128)(2,1)S(1)}, u32[]{:S(2)}, u32[]{:S(2)}) collective-permute-start(bf16[288,128]{1,0:T(8,128)(2,1)S(1)} %get-tuple-element.141), channel_id=1, source_target_pairs={{0,24},{4,28},{8,16},{12,20},{16,8},{20,12},{24,0},{28,4},{32,56},... | collective-permute-start | bytes 221192 | tf_op jit(solution)/shard_map/ppermute | solution.py:710
  58.5 7.2 %collective-permute-start.17 = (bf16[288,128]{1,0:T(8,128)(2,1)S(1)}, bf16[288,128]{1,0:T(8,128)(2,1)S(1)}, u32[]{:S(2)}, u32[]{:S(2)}) collective-permute-start(bf16[288,128]{1,0:T(8,128)(2,1)S(1)} %row_sum.3.refs_11_.refs_4_), channel_id=1, source_target_pairs={{0,32},{4,36},{8,40},{12,44},{16,48},{20,52},{24,56},{28,60},{32,0... | collective-permute-start | bytes 221192 | tf_op jit(solution)/shard_map/ppermute | solution.py:710
  59.4 6.3 %collective-permute-start.18 = (bf16[288,128]{1,0:T(8,128)(2,1)S(1)}, bf16[288,128]{1,0:T(8,128)(2,1)S(1)}, u32[]{:S(2)}, u32[]{:S(2)}) collective-permute-start(bf16[288,128]{1,0:T(8,128)(2,1)S(1)} %row_sum.3.refs_11_.refs_4_), channel_id=1, source_target_pairs={{0,64},{4,68},{8,72},{12,76},{16,80},{20,84},{24,88},{28,92},{32,9... | collective-permute-start | bytes 221192 | tf_op jit(solution)/shard_map/ppermute | solution.py:710
  61.2 5.2 %collective-permute-start.19 = (bf16[288,128]{1,0:T(8,128)(2,1)S(1)}, bf16[288,128]{1,0:T(8,128)(2,1)S(1)}, u32[]{:S(2)}, u32[]{:S(2)}) collective-permute-start(bf16[288,128]{1,0:T(8,128)(2,1)S(1)} %row_sum.3.refs_11_.refs_4_), channel_id=1, source_target_pairs={{0,96},{4,100},{8,104},{12,108},{16,112},{20,116},{24,120},{28,124... | collective-permute-start | bytes 221192 | tf_op jit(solution)/shard_map/ppermute | solution.py:710
  66.8 7.2 %collective-permute-start.20 = (bf16[256,128]{1,0:T(8,128)(2,1)S(1)}, bf16[256,128]{1,0:T(8,128)(2,1)S(1)}, u32[]{:S(2)}, u32[]{:S(2)}) collective-permute-start(bf16[256,128]{1,0:T(8,128)(2,1)S(1)} %get-tuple-element.156), channel_id=1, source_target_pairs={{0,8},{4,12},{8,0},{12,4},{16,24},{20,28},{24,16},{28,20},{32,40},... | collective-permute-start | bytes 196616 | tf_op jit(solution)/shard_map/ppermute | solution.py:710
  66.9 7.1 %collective-permute-start.21 = (bf16[256,128]{1,0:T(8,128)(2,1)S(1)}, bf16[256,128]{1,0:T(8,128)(2,1)S(1)}, u32[]{:S(2)}, u32[]{:S(2)}) collective-permute-start(bf16[256,128]{1,0:T(8,128)(2,1)S(1)} %get-tuple-element.157), channel_id=1, source_target_pairs={{0,16},{4,20},{8,24},{12,28},{16,0},{20,4},{24,8},{28,12},{32,48},... | collective-permute-start | bytes 196616 | tf_op jit(solution)/shard_map/ppermute | solution.py:710
  68.9 5.1 %collective-permute-start.22 = (bf16[256,128]{1,0:T(8,128)(2,1)S(1)}, bf16[256,128]{1,0:T(8,128)(2,1)S(1)}, u32[]{:S(2)}, u32[]{:S(2)}) collective-permute-start(bf16[256,128]{1,0:T(8,128)(2,1)S(1)} %get-tuple-element.158), channel_id=1, source_target_pairs={{0,24},{4,28},{8,16},{12,20},{16,8},{20,12},{24,0},{28,4},{32,56},... | collective-permute-start | bytes 196616 | tf_op jit(solution)/shard_map/ppermute | solution.py:710
  74.2 4.6 %collective-permute-start.23 = (bf16[1040,128]{1,0:T(8,128)(2,1)S(1)}, bf16[1040,128]{1,0:T(8,128)(2,1)S(1)}, u32[]{:S(2)}, u32[]{:S(2)}) collective-permute-start(bf16[1040,128]{1,0:T(8,128)(2,1)S(1)} %get-tuple-element.161), channel_id=1, source_target_pairs={{0,4},{4,0},{8,12},{12,8},{16,20},{20,16},{24,28},{28,24},{32,36},... | collective-permute-start | bytes 798728 | tf_op jit(solution)/shard_map/ppermute | solution.py:710

commit v6 on v5

--- a/solution.py
+++ b/solution.py
@@ -32,6 +32,22 @@
     return lax.dot_general(a, b, (((da,), (db,)), ((), ())), preferred_element_type=F32)
 
 
+def pair_diagonal(a, b, da, db):
+    both = dot(a, b, da, db)
+    return both[0:HD, 0:HD], both[HD : 2 * HD, HD : 2 * HD]
+
+
+def diagonal(a, b):
+    zero = jnp.zeros_like(a)
+    return jnp.concatenate(
+        [jnp.concatenate([a, zero], axis=1), jnp.concatenate([zero, b], axis=1)], axis=0
+    )
+
+
+def pair_columns(p):
+    return pl.ds(pl.multiple_of(p * 2 * HD, 2 * HD), 2 * HD)
+
+
 def vmem(shape, dtype):
     return pltpu.VMEM(shape, dtype)
 
@@ -70,14 +86,6 @@
 
 def base_column(ids, flip):
     return pl.multiple_of((ids[0] ^ flip) * WIDE, WIDE)
-
-
-def each_group(body, groups=GROUPS):
-    def step(g, carry):
-        body(g)
-        return carry
-
-    lax.fori_loop(0, groups, step, 0)
 
 
 def head_columns(h):
@@ -183,8 +191,11 @@
     for n, t in BLOCKS:
         for c in copies[n]:
             c.wait()
-        rows = [(k[t, head_columns(h)] * last[t, :], v[t, head_columns(h)]) for h in range(HEADS)]
-        parts = [dot(kh, vh, 0, 0) for kh, vh in rows]
+        mask = jnp.concatenate([last[t, :]] * 2, axis=1)
+        rows = [
+            (k[t, pair_columns(p)] * mask, v[t, pair_columns(p)]) for p in range(HEADS // 2)
+        ]
+        parts = [part for kp, vp in rows for part in pair_diagonal(kp, vp, 0, 0)]
         if n == 1:
             parts = [two + early[head_rows(h), :] * join for h, two in enumerate(parts)]
         for h, part in enumerate(parts):
@@ -253,7 +264,8 @@
                 (w0, w1)[n][head_rows(h, BLOCK), :] = w[n]
                 attn[t, head_columns(h)] = a[n]
 
-    each_group(body)
+    for g in range(GROUPS):
+        body(g)
 
 
 TOKEN = vmem((8, HD), F32)
@@ -298,7 +310,8 @@
             c = head_columns(g * GROUP + j)
             w[:, c] = go[:, c].astype(F32) * sigmoid_parts(gi[:, c])[0]
 
-    each_group(body, 2 * GROUPS)
+    for g in range(2 * GROUPS):
+        body(g)
 
 
 def prepare(after, go, gi):
@@ -329,9 +342,14 @@
             (early[head_rows(h), :] + one.astype(F32) * join).astype(BF16)
             for h, one in zip(group, ones)
         ]
-        rows = [q[:, head_columns(h)] * before[...] for h in group]
+        mask = jnp.concatenate([before[...]] * 2, axis=1)
+        rows = [q[:, pair_columns(g * (GROUP // 2) + j)] * mask for j in range(GROUP // 2)]
         for n, t in BLOCKS:
-            hops = [dot(qh[t], pair[n], 1, 0) for qh, pair in zip(rows, zip(ones, twos))]
+            states = (ones, twos)[n]
+            hops = []
+            for j, qp in enumerate(rows):
+                hop = dot(qp[t], diagonal(states[2 * j], states[2 * j + 1]), 1, 0)
+                hops += [hop[:, 0:HD], hop[:, HD : 2 * HD]]
             sums = [attn_in[t, head_columns(h)] + hop for h, hop in zip(group, hops)]
             square, inner = squares[t, :], inners[t, :]
             for h, a in zip(group, sums):
@@ -345,7 +363,8 @@
         for h, two in zip(group, twos):
             second[head_rows(h), :] = two
 
-    each_group(body)
+    for g in range(GROUPS):
+        body(g)
     if flip:
         ones = jnp.ones((8, HD), BF16)
         totals = []
@@ -395,7 +414,7 @@
 
     def body(g):
         group = [g * GROUP + j for j in range(GROUP)]
-        turned = [qt[head_rows(h), :] for h in group]
+        turned = [qt[head_rows(g * (GROUP // 2) + j, 2 * HD), :] for j in range(GROUP // 2)]
         totals, rows = [], []
         for h in group:
             far_c = span(base + h * HD, HD)
@@ -403,14 +422,18 @@
             gated = w[:, far_c] * rinv[...]
             totals.append(jnp.sum(gated * a, axis=0, keepdims=True))
             rows.append((gated * gain[:, far_c] - a * back[...]).astype(BF16))
-        parts = [[dot(qh[:, t], x[t], 1, 0) for _, t in BLOCKS] for qh, x in zip(turned, rows)]
+        parts = []
+        for j, qp in enumerate(turned):
+            xp = jnp.concatenate(rows[2 * j : 2 * j + 2], axis=1)
+            parts += zip(*[pair_diagonal(qp[:, t], xp[t], 1, 0) for _, t in BLOCKS])
         for h, total, x, (one, two) in zip(group, totals, rows, parts):
             gains[pl.ds(h, 1), :] = total
             grad[:, head_columns(h)] = x
             late[head_rows(h), :] = two
             out[head_rows(h), :] = (one + two * join).astype(BF16)
 
-    each_group(body)
+    for g in range(GROUPS):
+        body(g)
     out[STATE_ROWS + TILE : STATE_ROWS + 2 * TILE, :] = split_tile(gains[...])
 
 
@@ -463,10 +486,11 @@
                 dq[t, c] = x.astype(BF16)
                 dk[t, c] = y
                 dv[t, c] = z
-        if flip:
-            pl.when(g == 0)(first_copy.start)
-
-    each_group(body)
+        if flip and g == 0:
+            first_copy.start()
+
+    for g in range(GROUPS):
+        body(g)
     if flip:
         first_copy.wait()
         keep_copy.wait()
@@ -505,7 +529,8 @@
             store(lo, at, to, lo_far, sems.at[0, flip, g]).start()
             store(gg, at, to, gg_far, sems.at[1, flip, g]).start()
 
-        each_group(body)
+        for g in range(GROUPS):
+            body(g)
         for g in range(GROUPS):
             at, to = flip * WIDE + g * SPAN, base + g * SPAN
             copies.append(store(lo, at, to, lo_far, sems.at[0, flip, g]))
@@ -551,13 +576,14 @@
             states.append(
                 ((late[head_rows(h), :] + one.astype(F32) * join).astype(BF16), one)
             )
-        rows = [
-            (k[:, head_columns(h)] * after[...], v[:, head_columns(h)] * after[...]) for h in group
-        ]
-        hops = [
-            [(dot(vh[t], state[n], 1, 1), dot(kh[t], state[n], 1, 0)) for n, t in BLOCKS]
-            for (kh, vh), state in zip(rows, states)
-        ]
+        mask = jnp.concatenate([after[...]] * 2, axis=1)
+        kp, vp = k[:, pair_columns(g)] * mask, v[:, pair_columns(g)] * mask
+        hops = ([], [])
+        for n, t in BLOCKS:
+            both = diagonal(states[0][n], states[1][n])
+            x, y = dot(vp[t], both, 1, 1), dot(kp[t], both, 1, 0)
+            hops[0].append((x[:, 0:HD], y[:, 0:HD]))
+            hops[1].append((x[:, HD : 2 * HD], y[:, HD : 2 * HD]))
         sums = [
             [
                 (dk_in[t, head_columns(h)] + hop[n][0], dv_in[t, head_columns(h)] + hop[n][1])

time: 81.2 us -> 79.4 us (0.978)
  Pallas kernels: 33.8 us -> 30.3 us
  starting transfers between devices: 37.7 us -> 39.1 us
    pallas_call x22, Pallas kernels: 33.8 us -> 30.3 us  [call(): pl.pallas_call(placed, in_specs=[VM] * len(near) + [ANY] * len(distant),...]
    ppermute x23, starting transfers between devices: 36 us -> 37.4 us  [swap(): return lax.ppermute(x, axis, [(i, i ^ bits) for i in range(size)])]
  transfers between devices with their start and end apart: 24 -> 24, of which waited for: 7 -> 9; matrix products, arithmetic and copies ran while one was open for 0% -> 0% of each run, Pallas kernels for 31% -> 29%
where the time goes in v6:
time: 79.4 us; the launch traced here: 79.2 us
  starting transfers between devices  39.1 us (49%)
  Pallas kernels  30.3 us (38%)
  waiting for transfers between devices  8.71 us (11%)
  between operations  1.06 us (1%)
    ppermute x23, starting transfers between devices, swap(): return lax.ppermute(x, axis, [(i, i ^ bits) for i in range(size)])  37.4 us
    pallas_call x22, Pallas kernels, call(): pl.pallas_call(placed, in_specs=[VM] * len(near) + [ANY] * len(distant),...  30.3 us
    ppermute x23, waiting for transfers between devices, swap(): return lax.ppermute(x, axis, [(i, i ^ bits) for i in range(size)])  8.71 us
    ppermute x1, starting transfers between devices, plane_shift(): return lax.ppermute(x, 'ctx', [(i, (i + 8) % 32) for i in range(32)])  1.71 us
  transfers between devices with their start and end apart: 24, of which 9 were waited for; matrix products, arithmetic and copies ran while one was open for 0% of the time, Pallas kernels for 29%

profile of v6, /device:TPU:1, one launch (start us, length us, event | category | flops | bytes accessed | tf_op | source)
XLA Modules:
  0.0 79.2 jit_solution(9591233711841622758)
XLA Ops:
  0.6 2.0 %local_state.2 = (bf16[512,1024]{1,0:T(8,128)(2,1)S(1)}, bf16[512,1024]{1,0:T(8,128)(2,1)S(1)}, bf16[1040,128]{1,0:T(8,128)(2,1)S(1)}, f32[1024,128]{1,0:T(8,128...) custom-call(bf16[512,2048]{1,0:T(8,128)(2,1)} %refs_2_.2, bf16[512,2048]{1,0:T(8,128)(2,1)} %refs_3_.1, ...), custom_call_target="tpu_custom_call" | custom-call | flops 1000000000 | bytes 3333333 | tf_op jit(solution)/shard_map/local_state/pallas_call | solution.py:72
  2.6 1.5 %collective-permute-start = (bf16[1040,128]{1,0:T(8,128)(2,1)S(1)}, bf16[1040,128]{1,0:T(8,128)(2,1)S(1)}, u32[]{:S(2)}, u32[]{:S(2)}) collective-permute-start(bf16[1040,128]{1,0:T(8,128)(2,1)S(1)} %get-tuple-element.95), channel_id=1, source_target_pairs={{0,4},{4,0},{8,12},{12,8},{16,20},{20,16},{24,28},{28,24},{32,36},... | collective-permute-start | bytes 798728 | tf_op jit(solution)/shard_map/ppermute | solution.py:736
  4.1 2.0 %local_state.3 = (bf16[512,1024]{1,0:T(8,128)(2,1)S(1)}, bf16[512,1024]{1,0:T(8,128)(2,1)S(1)}, bf16[1040,128]{1,0:T(8,128)(2,1)S(1)}, f32[1024,128]{1,0:T(8,128)S(1)}) custom-call(s32[1,512]{1,0:T(1,128)S(1)} %get-tuple-element.90.refs_0_.refs_2_.refs_6_, bf16[512,128]{1,0:T(8,128)(2,1)S(1)} %get-tuple-element.91.refs_1_, bf16[512,2048]{1,0:T(8,128)(2,1)} %refs_2_.2, ...), custom_call_target="tpu_custom_call" | custom-call | flops 1000000000 | bytes 3333333 | tf_op jit(solution)/shard_map/local_state/pallas_call | solution.py:72
  6.1 0.0 collective-permute-done.refs_1_
  6.2 0.1 chip_sum.2
  6.3 1.4 %collective-permute-start.1 = (bf16[272,128]{1,0:T(8,128)(2,1)S(1)}, bf16[272,128]{1,0:T(8,128)(2,1)S(1)}, u32[]{:S(2)}, u32[]{:S(2)}) collective-permute-start(bf16[272,128]{1,0:T(8,128)(2,1)S(1)} %get-tuple-element.99), channel_id=1, source_target_pairs={{0,8},{4,12},{8,0},{12,4},{16,24},{20,28},{24,16},{28,20},{32,40},... | collective-permute-start | bytes 208904 | tf_op jit(solution)/shard_map/ppermute | solution.py:736
  7.7 2.5 %collective-permute-start.2 = (bf16[272,128]{1,0:T(8,128)(2,1)S(1)}, bf16[272,128]{1,0:T(8,128)(2,1)S(1)}, u32[]{:S(2)}, u32[]{:S(2)}) collective-permute-start(bf16[272,128]{1,0:T(8,128)(2,1)S(1)} %get-tuple-element.100), channel_id=1, source_target_pairs={{0,16},{4,20},{8,24},{12,28},{16,0},{20,4},{24,8},{28,12},{32,48},... | collective-permute-start | bytes 208904 | tf_op jit(solution)/shard_map/ppermute | solution.py:736
  10.1 0.1 collective-permute-start.3
  10.2 2.7 %intra.2 = (bf16[512,1024]{1,0:T(8,128)(2,1)S(1)}, f32[512,1024]{1,0:T(8,128)S(1)}, bf16[2048,256]{1,0:T(8,128)(2,1)S(1)}, bf16[2048,256]{1,0:T(8,128)(2,1)S(1)}...) custom-call(bf16[512,1024]{1,0:T(8,128)(2,1)S(1)} %get-tuple-element, ...), custom_call_target="tpu_custom_call" | custom-call | flops 3000000000 | bytes 10000000 | tf_op jit(solution)/shard_map/intra/pallas_call | solution.py:72
  12.9 0.0 collective-permute-done.1.refs_1_
  12.9 1.0 %collective-permute-done.2.refs_2_ = bf16[272,128]{1,0:T(8,128)(2,1)S(1)} collective-permute-done((bf16[272,128]{1,0:T(8,128)(2,1)S(1)}, bf16[272,128]{1,0:T(8,128)(2,1)S(1)}, u32[]{:S(2)}, u32[]{:S(2)}) %collective-permute-start.2) | collective-permute-done | bytes 69664 | tf_op jit(solution)/shard_map/ppermute | solution.py:736
  13.9 1.2 %collective-permute-done.3.refs_3_ = bf16[272,128]{1,0:T(8,128)(2,1)S(1)} collective-permute-done((bf16[272,128]{1,0:T(8,128)(2,1)S(1)}, bf16[272,128]{1,0:T(8,128)(2,1)S(1)}, u32[]{:S(2)}, u32[]{:S(2)}) %collective-permute-start.3) | collective-permute-done | bytes 69664 | tf_op jit(solution)/shard_map/ppermute | solution.py:736
  15.1 0.1 row_sum.2.refs_5_.refs_4_
  15.1 1.7 %collective-permute-start.4 = (bf16[272,128]{1,0:T(8,128)(2,1)S(1)}, bf16[272,128]{1,0:T(8,128)(2,1)S(1)}, u32[]{:S(2)}, u32[]{:S(2)}) collective-permute-start(bf16[272,128]{1,0:T(8,128)(2,1)S(1)} %row_sum.2.refs_5_.refs_4_), channel_id=1, source_target_pairs={{0,32},{4,36},{8,40},{12,44},{16,48},{20,52},{24,56},{28,60},{32,6... | collective-permute-start | bytes 208904 | tf_op jit(solution)/shard_map/ppermute | solution.py:752
  16.8 3.3 %collective-permute-start.5 = (bf16[272,128]{1,0:T(8,128)(2,1)S(1)}, bf16[272,128]{1,0:T(8,128)(2,1)S(1)}, u32[]{:S(2)}, u32[]{:S(2)}) collective-permute-start(bf16[272,128]{1,0:T(8,128)(2,1)S(1)} %row_sum.2.refs_5_.refs_4_), channel_id=1, source_target_pairs={{0,64},{4,68},{8,72},{12,76},{16,80},{20,84},{24,88},{28,92},{32,9... | collective-permute-start | bytes 208904 | tf_op jit(solution)/shard_map/ppermute | solution.py:736
  20.1 2.7 %intra.3 = (bf16[512,1024]{1,0:T(8,128)(2,1)S(1)}, f32[512,1024]{1,0:T(8,128)S(1)}, bf16[2048,256]{1,0:T(8,128)(2,1)S(1)}, bf16[2048,256]{1,0:T(8,128)(2,1)S(1)}...) custom-call(bf16[512,1024]{1,0:T(8,128)(2,1)S(1)} %get-tuple-element.103.refs_0_.refs_1_.refs_2_, ...), custom_call_target="tpu_custom_call" | custom-call | flops 3000000000 | bytes 10000000 | tf_op jit(solution)/shard_map/intra/pallas_call | solution.py:72
  22.8 0.0 collective-permute-done.4.refs_5_
  22.9 0.0 collective-permute-done.5.refs_6_
  22.9 0.3 entry.2
  23.2 0.3 collective-permute-start.6
  23.4 2.8 %collective-permute-start.7 = (bf16[256,128]{1,0:T(8,128)(2,1)S(1)}, bf16[256,128]{1,0:T(8,128)(2,1)S(1)}, u32[]{:S(2)}, u32[]{:S(2)}) collective-permute-start(bf16[256,128]{1,0:T(8,128)(2,1)S(1)} %get-tuple-element.111), channel_id=1, source_target_pairs={{0,16},{4,20},{8,24},{12,28},{16,0},{20,4},{24,8},{28,12},{32,48},... | collective-permute-start | bytes 196616 | tf_op jit(solution)/shard_map/ppermute | solution.py:736
  26.2 0.9 %collective-permute-start.8 = (bf16[256,128]{1,0:T(8,128)(2,1)S(1)}, bf16[256,128]{1,0:T(8,128)(2,1)S(1)}, u32[]{:S(2)}, u32[]{:S(2)}) collective-permute-start(bf16[256,128]{1,0:T(8,128)(2,1)S(1)} %get-tuple-element.112), channel_id=1, source_target_pairs={{0,24},{4,28},{8,16},{12,20},{16,8},{20,12},{24,0},{28,4},{32,56},... | collective-permute-start | bytes 196616 | tf_op jit(solution)/shard_map/ppermute | solution.py:736
  27.1 2.5 %prepare.1 = (f32[512,2048]{1,0:T(8,128)S(1)}, bf16[512,2048]{1,0:T(8,128)(2,1)S(1)}, f32[8,128]{1,0:T(8,128)S(1)}) custom-call(bf16[256,128]{1,0:T(8,128)(2,1)S(1)} %get-tuple-element.109.refs_0_.refs_2_, bf16[512,2048]{1,0:T(8,128)(2,1)} %refs_1_.3, bf16[512,2048]{1,0:T(8,128)(2,1)} %refs_2_.3), custom_call_target="tpu_custom_call" | custom-call | flops 3000000000 | bytes 10000000 | tf_op jit(solution)/shard_map/prepare/pallas_call | solution.py:72
  29.6 0.0 collective-permute-done.7.refs_4_
  29.6 1.6 %collective-permute-done.8.refs_5_ = bf16[256,128]{1,0:T(8,128)(2,1)S(1)} collective-permute-done((bf16[256,128]{1,0:T(8,128)(2,1)S(1)}, bf16[256,128]{1,0:T(8,128)(2,1)S(1)}, u32[]{:S(2)}, u32[]{:S(2)}) %collective-permute-start.8) | collective-permute-done | bytes 65568 | tf_op jit(solution)/shard_map/ppermute | solution.py:736
  31.2 0.2 device_entry.2
  31.4 2.7 %collective-permute-start.9 = (bf16[1024,128]{1,0:T(8,128)(2,1)S(1)}, bf16[1024,128]{1,0:T(8,128)(2,1)S(1)}, u32[]{:S(2)}, u32[]{:S(2)}) collective-permute-start(bf16[1024,128]{1,0:T(8,128)(2,1)S(1)} %get-tuple-element.121), channel_id=1, source_target_pairs={{0,4},{4,0},{8,12},{12,8},{16,20},{20,16},{24,28},{28,24},{32,36},... | collective-permute-start | bytes 786440 | tf_op jit(solution)/shard_map/ppermute | solution.py:736
  34.2 0.9 %cross.2 = (f32[512,1024]{1,0:T(8,128)S(1)}, bf16[1024,128]{1,0:T(8,128)(2,1)S(1)}, f32[512,128]{1,0:T(8,128)S(1)}, f32[512,128]{1,0:T(8,128)S(1)}) custom-call(f32[512,1024]{1,0:T(8,128)S(1)} %get-tuple-element.97.refs_0_, bf16[512,1024]{1,0:T(8,128)(2,1)S(1)} %get-tuple-element.98.refs_1_.refs_0_, ...), custom_call_target="tpu_custom_call" | custom-call | flops 1200000000 | bytes 4000000 | tf_op jit(solution)/shard_map/cross/pallas_call | solution.py:72
  35.0 0.3 collective-permute-done.9.refs_2_.refs_4_
  35.3 1.1 %cross.3 = (f32[512,1024]{1,0:T(8,128)S(1)}, bf16[1024,128]{1,0:T(8,128)(2,1)S(1)}, f32[8,512]{1,0:T(8,128)S(1)}) custom-call(f32[512,1024]{1,0:T(8,128)S(1)} %get-tuple-element.119.refs_0_, bf16[512,1024]{1,0:T(8,128)(2,1)S(1)} %get-tuple-element.120.refs_1_.refs_0_, bf16[1024,128]{1,0:T(8,128)(2,1)S(1)} %collective-permute-done.9.refs_2_.refs_4_, ...), custom_call_target="tpu_custom_call" | custom-call | flops 1200000000 | bytes 4000000 | tf_op jit(solution)/shard_map/cross/pallas_call | solution.py:72
  36.4 1.4 %collective-permute-start.10 = (f32[8,512]{1,0:T(8,128)S(1)}, f32[8,512]{1,0:T(8,128)S(1)}, u32[]{:S(2)}, u32[]{:S(2)}) collective-permute-start(f32[8,512]{1,0:T(8,128)S(1)} %get-tuple-element.128.refs_5_), channel_id=1, source_target_pairs={{0,1},{1,0},{2,3},{3,2},{4,5},{5,4},{6,7},{7,6},{8,9},{9,8},{10,11... | collective-permute-start | bytes 49160 | tf_op jit(solution)/shard_map/ppermute | solution.py:736
  37.8 2.6 %collective-permute-start.11 = (f32[8,512]{1,0:T(8,128)S(1)}, f32[8,512]{1,0:T(8,128)S(1)}, u32[]{:S(2)}, u32[]{:S(2)}) collective-permute-start(f32[8,512]{1,0:T(8,128)S(1)} %get-tuple-element.128.refs_5_), channel_id=1, source_target_pairs={{0,2},{1,3},{2,0},{3,1},{4,6},{5,7},{6,4},{7,5},{8,10},{9,11},{10,... | collective-permute-start | bytes 49160 | tf_op jit(solution)/shard_map/ppermute | solution.py:736
  40.4 0.0 collective-permute-start.12
  40.4 1.5 %collective-permute-done.11.refs_7_ = f32[8,512]{1,0:T(8,128)S(1)} collective-permute-done((f32[8,512]{1,0:T(8,128)S(1)}, f32[8,512]{1,0:T(8,128)S(1)}, u32[]{:S(2)}, u32[]{:S(2)}) %collective-permute-start.11) | collective-permute-done | bytes 16416 | tf_op jit(solution)/shard_map/ppermute | solution.py:736
  41.9 2.3 %collective-permute-done.12.refs_8_ = f32[8,512]{1,0:T(8,128)S(1)} collective-permute-done((f32[8,512]{1,0:T(8,128)S(1)}, f32[8,512]{1,0:T(8,128)S(1)}, u32[]{:S(2)}, u32[]{:S(2)}) %collective-permute-start.12) | collective-permute-done | bytes 16416 | tf_op jit(solution)/shard_map/ppermute | solution.py:736
  44.2 1.2 %grad_attn.2 = (bf16[512,1024]{1,0:T(8,128)(2,1)S(1)}, bf16[1056,128]{1,0:T(8,128)(2,1)S(1)}, f32[1024,128]{1,0:T(8,128)S(1)}, f32[512,128]{1,0:T(8,128)S(1)}, f32[512,128]{1,0:T(8,128)S(1)}) custom-call(s32[1,512]{1,0:T(1,128)S(1)} %get-tuple-element.90.refs_0_.refs_2_.refs_6_, f32[512,1024]{1,0:T(8,128)S(1)} %get-tuple-element.125.refs_1_, ...), custom_call_target="tpu_custom_call" | custom-call | flops 1200000000 | bytes 4000000 | tf_op jit(solution)/shard_map/grad_attn/pallas_call | solution.py:72
  45.4 2.2 %collective-permute-start.13 = (bf16[1056,128]{1,0:T(8,128)(2,1)S(1)}, bf16[1056,128]{1,0:T(8,128)(2,1)S(1)}, u32[]{:S(2)}, u32[]{:S(2)}) collective-permute-start(bf16[1056,128]{1,0:T(8,128)(2,1)S(1)} %get-tuple-element.137), channel_id=1, source_target_pairs={{0,4},{4,0},{8,12},{12,8},{16,20},{20,16},{24,28},{28,24},{32,36},... | collective-permute-start | bytes 811016 | tf_op jit(solution)/shard_map/ppermute | solution.py:736
  47.6 1.0 %grad_attn.3 = (bf16[512,1024]{1,0:T(8,128)(2,1)S(1)}, bf16[1056,128]{1,0:T(8,128)(2,1)S(1)}, f32[1024,128]{1,0:T(8,128)S(1)}) custom-call(s32[1,512]{1,0:T(1,128)S(1)} %get-tuple-element.90.refs_0_.refs_2_.refs_6_, f32[512,1024]{1,0:T(8,128)S(1)} %get-tuple-element.118.refs_1_.refs_0_, f32[512,2048]{1,0:T(8,128)S(1)} %get-tuple-element.116.refs_4_.refs_2_.refs_3_, ...), custom_call_target="tpu_custom_call" | custom-call | flops 1200000000 | bytes 4000000 | tf_op jit(solution)/shard_map/grad_attn/pallas_call | solution.py:72
  48.5 0.2 collective-permute-done.13.refs_1_
  48.7 0.1 chip_sum.3
  48.8 0.1 collective-permute-start.14
  48.9 2.5 %collective-permute-start.15 = (bf16[288,128]{1,0:T(8,128)(2,1)S(1)}, bf16[288,128]{1,0:T(8,128)(2,1)S(1)}, u32[]{:S(2)}, u32[]{:S(2)}) collective-permute-start(bf16[288,128]{1,0:T(8,128)(2,1)S(1)} %get-tuple-element.140), channel_id=1, source_target_pairs={{0,16},{4,20},{8,24},{12,28},{16,0},{20,4},{24,8},{28,12},{32,48},... | collective-permute-start | bytes 221192 | tf_op jit(solution)/shard_map/ppermute | solution.py:736
  51.4 1.4 %collective-permute-start.16 = (bf16[288,128]{1,0:T(8,128)(2,1)S(1)}, bf16[288,128]{1,0:T(8,128)(2,1)S(1)}, u32[]{:S(2)}, u32[]{:S(2)}) collective-permute-start(bf16[288,128]{1,0:T(8,128)(2,1)S(1)} %get-tuple-element.141), channel_id=1, source_target_pairs={{0,24},{4,28},{8,16},{12,20},{16,8},{20,12},{24,0},{28,4},{32,56},... | collective-permute-start | bytes 221192 | tf_op jit(solution)/shard_map/ppermute | solution.py:736
  52.8 3.0 %local_grads.2 = (bf16[512,1024]{1,0:T(8,128)(2,1)S(1)}, f32[512,1024]{1,0:T(8,128)S(1)}, f32[512,1024]{1,0:T(8,128)S(1)}, f32[8,128]{1,0:T(8,128)S(1)}) custom-call(bf16[512,1024]{1,0:T(8,128)(2,1)S(1)} %get-tuple-element.98.refs_1_.refs_0_, bf16[512,1024]{1,0:T(8,128)(2,1)S(1)} %get-tuple-element.92.refs_0_.refs_1_.refs_2_, ...), custom_call_target="tpu_custom_call" | custom-call | flops 5000000000 | bytes 16666666 | tf_op jit(solution)/shard_map/local_grads/pallas_call | solution.py:72
  55.8 0.0 collective-permute-done.15.refs_2_
  55.8 0.5 collective-permute-done.16.refs_3_
  56.3 0.1 row_sum.3.refs_11_.refs_4_
  56.4 0.9 %collective-permute-start.17 = (bf16[288,128]{1,0:T(8,128)(2,1)S(1)}, bf16[288,128]{1,0:T(8,128)(2,1)S(1)}, u32[]{:S(2)}, u32[]{:S(2)}) collective-permute-start(bf16[288,128]{1,0:T(8,128)(2,1)S(1)} %row_sum.3.refs_11_.refs_4_), channel_id=1, source_target_pairs={{0,32},{4,36},{8,40},{12,44},{16,48},{20,52},{24,56},{28,60},{32,0... | collective-permute-start | bytes 221192 | tf_op jit(solution)/shard_map/ppermute | solution.py:736
  57.3 1.8 %collective-permute-start.18 = (bf16[288,128]{1,0:T(8,128)(2,1)S(1)}, bf16[288,128]{1,0:T(8,128)(2,1)S(1)}, u32[]{:S(2)}, u32[]{:S(2)}) collective-permute-start(bf16[288,128]{1,0:T(8,128)(2,1)S(1)} %row_sum.3.refs_11_.refs_4_), channel_id=1, source_target_pairs={{0,64},{4,68},{8,72},{12,76},{16,80},{20,84},{24,88},{28,92},{32,9... | collective-permute-start | bytes 221192 | tf_op jit(solution)/shard_map/ppermute | solution.py:736
  59.0 1.3 %collective-permute-start.19 = (bf16[288,128]{1,0:T(8,128)(2,1)S(1)}, bf16[288,128]{1,0:T(8,128)(2,1)S(1)}, u32[]{:S(2)}, u32[]{:S(2)}) collective-permute-start(bf16[288,128]{1,0:T(8,128)(2,1)S(1)} %row_sum.3.refs_11_.refs_4_), channel_id=1, source_target_pairs={{0,96},{4,100},{8,104},{12,108},{16,112},{20,116},{24,120},{28,124... | collective-permute-start | bytes 221192 | tf_op jit(solution)/shard_map/ppermute | solution.py:736
  60.3 3.0 %local_grads.3 = (bf16[512,2048]{1,0:T(8,128)(2,1)}, bf16[512,1024]{1,0:T(8,128)(2,1)S(1)}, f32[512,1024]{1,0:T(8,128)S(1)}, f32[512,1024]{1,0:T(8,128)S(1)}, f32[8,128]{1,0:T(8,128)S(1)}) custom-call(bf16[512,1024]{1,0:T(8,128)(2,1)S(1)} %get-tuple-element.120.refs_1_.refs_0_, bf16[512,1024]{1,0:T(8,128)(2,1)S(1)} %get-tuple-element.103.refs_0_.refs_1_.refs_2_, ...), custom_call_target="tpu_custom_call" | custom-call | flops 5000000000 | bytes 16666666 | tf_op jit(solution)/shard_map/local_grads/pallas_call | solution.py:72
  63.3 0.0 collective-permute-done.17.refs_5_
  63.3 0.0 collective-permute-done.18.refs_6_
  63.3 0.1 collective-permute-done.19.refs_7_
  63.5 0.3 entry.3
  63.8 0.8 %collective-permute-start.20 = (bf16[256,128]{1,0:T(8,128)(2,1)S(1)}, bf16[256,128]{1,0:T(8,128)(2,1)S(1)}, u32[]{:S(2)}, u32[]{:S(2)}) collective-permute-start(bf16[256,128]{1,0:T(8,128)(2,1)S(1)} %get-tuple-element.156), channel_id=1, source_target_pairs={{0,8},{4,12},{8,0},{12,4},{16,24},{20,28},{24,16},{28,20},{32,40},... | collective-permute-start | bytes 196616 | tf_op jit(solution)/shard_map/ppermute | solution.py:736
  64.6 1.7 %collective-permute-start.21 = (bf16[256,128]{1,0:T(8,128)(2,1)S(1)}, bf16[256,128]{1,0:T(8,128)(2,1)S(1)}, u32[]{:S(2)}, u32[]{:S(2)}) collective-permute-start(bf16[256,128]{1,0:T(8,128)(2,1)S(1)} %get-tuple-element.157), channel_id=1, source_target_pairs={{0,16},{4,20},{8,24},{12,28},{16,0},{20,4},{24,8},{28,12},{32,48},... | collective-permute-start | bytes 196616 | tf_op jit(solution)/shard_map/ppermute | solution.py:736
  66.3 1.4 %collective-permute-start.22 = (bf16[256,128]{1,0:T(8,128)(2,1)S(1)}, bf16[256,128]{1,0:T(8,128)(2,1)S(1)}, u32[]{:S(2)}, u32[]{:S(2)}) collective-permute-start(bf16[256,128]{1,0:T(8,128)(2,1)S(1)} %get-tuple-element.158), channel_id=1, source_target_pairs={{0,24},{4,28},{8,16},{12,20},{16,8},{20,12},{24,0},{28,4},{32,56},... | collective-permute-start | bytes 196616 | tf_op jit(solution)/shard_map/ppermute | solution.py:736
  67.7 3.3 %gates.1 = (bf16[512,2048]{1,0:T(8,128)(2,1)}, bf16[512,2048]{1,0:T(8,128)(2,1)}, bf16[512,2048]{1,0:T(8,128)(2,1)}, f32[8,128]{1,0:T(8,128)S(1)}) custom-call(f32[512,1024]{1,0:T(8,128)S(1)} %get-tuple-element.118.refs_1_.refs_0_, f32[512,1024]{1,0:T(8,128)S(1)} %get-tuple-element.125.refs_1_, ...), custom_call_target="tpu_custom_call", output_to_operand_aliasing={{2}: (8, {})} | custom-call | flops 3000000000 | bytes 10000000 | tf_op jit(solution)/shard_map/gates/pallas_call | solution.py:72
  71.0 0.0 collective-permute-done.20.refs_3_
  71.1 0.2 device_entry.3
  71.3 4.0 %collective-permute-start.23 = (bf16[1040,128]{1,0:T(8,128)(2,1)S(1)}, bf16[1040,128]{1,0:T(8,128)(2,1)S(1)}, u32[]{:S(2)}, u32[]{:S(2)}) collective-permute-start(bf16[1040,128]{1,0:T(8,128)(2,1)S(1)} %get-tuple-element.161), channel_id=1, source_target_pairs={{0,4},{4,0},{8,12},{12,8},{16,20},{20,16},{24,28},{28,24},{32,36},... | collective-permute-start | bytes 798728 | tf_op jit(solution)/shard_map/ppermute | solution.py:736
  75.3 1.8 %finish.2 = (bf16[512,2048]{1,0:T(8,128)(2,1)}, bf16[512,2048]{1,0:T(8,128)(2,1)}) custom-call(f32[512,1024]{1,0:T(8,128)S(1)} %get-tuple-element.164.refs_0_, f32[512,1024]{1,0:T(8,128)S(1)} %get-tuple-element.165.refs_1_, bf16[512,1024]{1,0:T(8,128)(2,1)S(1)} %get-tuple-element.92.refs_0_.refs_1_.refs_2_, ...), custom_call_target="tpu_custom_call" | custom-call | flops 1200000000 | bytes 4000000 | tf_op jit(solution)/shard_map/finish/pallas_call | solution.py:72
  77.1 1.9 %finish.3 = (bf16[512,2048]{1,0:T(8,128)(2,1)}, bf16[512,2048]{1,0:T(8,128)(2,1)}, f32[16,128]{1,0:T(8,128)}) custom-call(f32[512,1024]{1,0:T(8,128)S(1)} %get-tuple-element.154.refs_0_, f32[512,1024]{1,0:T(8,128)S(1)} %get-tuple-element.155.refs_1_, ...), custom_call_target="tpu_custom_call", output_to_operand_aliasing={{0}: (9, {}), {1}: (10, {})} | custom-call | flops 1200000000 | bytes 4000000 | tf_op jit(solution)/shard_map/finish/pallas_call | solution.py:72
  (8 shorter events, 0.0 us)
Async XLA Ops:
  2.6 3.5 %collective-permute-start = (bf16[1040,128]{1,0:T(8,128)(2,1)S(1)}, bf16[1040,128]{1,0:T(8,128)(2,1)S(1)}, u32[]{:S(2)}, u32[]{:S(2)}) collective-permute-start(bf16[1040,128]{1,0:T(8,128)(2,1)S(1)} %get-tuple-element.95), channel_id=1, source_target_pairs={{0,4},{4,0},{8,12},{12,8},{16,20},{20,16},{24,28},{28,24},{32,36},... | collective-permute-start | bytes 798728 | tf_op jit(solution)/shard_map/ppermute | solution.py:736
  6.3 6.6 %collective-permute-start.1 = (bf16[272,128]{1,0:T(8,128)(2,1)S(1)}, bf16[272,128]{1,0:T(8,128)(2,1)S(1)}, u32[]{:S(2)}, u32[]{:S(2)}) collective-permute-start(bf16[272,128]{1,0:T(8,128)(2,1)S(1)} %get-tuple-element.99), channel_id=1, source_target_pairs={{0,8},{4,12},{8,0},{12,4},{16,24},{20,28},{24,16},{28,20},{32,40},... | collective-permute-start | bytes 208904 | tf_op jit(solution)/shard_map/ppermute | solution.py:736
  7.7 6.3 %collective-permute-start.2 = (bf16[272,128]{1,0:T(8,128)(2,1)S(1)}, bf16[272,128]{1,0:T(8,128)(2,1)S(1)}, u32[]{:S(2)}, u32[]{:S(2)}) collective-permute-start(bf16[272,128]{1,0:T(8,128)(2,1)S(1)} %get-tuple-element.100), channel_id=1, source_target_pairs={{0,16},{4,20},{8,24},{12,28},{16,0},{20,4},{24,8},{28,12},{32,48},... | collective-permute-start | bytes 208904 | tf_op jit(solution)/shard_map/ppermute | solution.py:736
  10.1 5.0 %collective-permute-start.3 = (bf16[272,128]{1,0:T(8,128)(2,1)S(1)}, bf16[272,128]{1,0:T(8,128)(2,1)S(1)}, u32[]{:S(2)}, u32[]{:S(2)}) collective-permute-start(bf16[272,128]{1,0:T(8,128)(2,1)S(1)} %get-tuple-element.101), channel_id=1, source_target_pairs={{0,24},{4,28},{8,16},{12,20},{16,8},{20,12},{24,0},{28,4},{32,56},... | collective-permute-start | bytes 208904 | tf_op jit(solution)/shard_map/ppermute | solution.py:736
  15.1 7.7 %collective-permute-start.4 = (bf16[272,128]{1,0:T(8,128)(2,1)S(1)}, bf16[272,128]{1,0:T(8,128)(2,1)S(1)}, u32[]{:S(2)}, u32[]{:S(2)}) collective-permute-start(bf16[272,128]{1,0:T(8,128)(2,1)S(1)} %row_sum.2.refs_5_.refs_4_), channel_id=1, source_target_pairs={{0,32},{4,36},{8,40},{12,44},{16,48},{20,52},{24,56},{28,60},{32,6... | collective-permute-start | bytes 208904 | tf_op jit(solution)/shard_map/ppermute | solution.py:752
  16.8 6.0 %collective-permute-start.5 = (bf16[272,128]{1,0:T(8,128)(2,1)S(1)}, bf16[272,128]{1,0:T(8,128)(2,1)S(1)}, u32[]{:S(2)}, u32[]{:S(2)}) collective-permute-start(bf16[272,128]{1,0:T(8,128)(2,1)S(1)} %row_sum.2.refs_5_.refs_4_), channel_id=1, source_target_pairs={{0,64},{4,68},{8,72},{12,76},{16,80},{20,84},{24,88},{28,92},{32,9... | collective-permute-start | bytes 208904 | tf_op jit(solution)/shard_map/ppermute | solution.py:736
  23.2 6.5 %collective-permute-start.6 = (bf16[256,128]{1,0:T(8,128)(2,1)S(1)}, bf16[256,128]{1,0:T(8,128)(2,1)S(1)}, u32[]{:S(2)}, u32[]{:S(2)}) collective-permute-start(bf16[256,128]{1,0:T(8,128)(2,1)S(1)} %get-tuple-element.110), channel_id=1, source_target_pairs={{0,8},{4,12},{8,0},{12,4},{16,24},{20,28},{24,16},{28,20},{32,40},... | collective-permute-start | bytes 196616 | tf_op jit(solution)/shard_map/ppermute | solution.py:736
  23.4 6.2 %collective-permute-start.7 = (bf16[256,128]{1,0:T(8,128)(2,1)S(1)}, bf16[256,128]{1,0:T(8,128)(2,1)S(1)}, u32[]{:S(2)}, u32[]{:S(2)}) collective-permute-start(bf16[256,128]{1,0:T(8,128)(2,1)S(1)} %get-tuple-element.111), channel_id=1, source_target_pairs={{0,16},{4,20},{8,24},{12,28},{16,0},{20,4},{24,8},{28,12},{32,48},... | collective-permute-start | bytes 196616 | tf_op jit(solution)/shard_map/ppermute | solution.py:736
  26.2 5.0 %collective-permute-start.8 = (bf16[256,128]{1,0:T(8,128)(2,1)S(1)}, bf16[256,128]{1,0:T(8,128)(2,1)S(1)}, u32[]{:S(2)}, u32[]{:S(2)}) collective-permute-start(bf16[256,128]{1,0:T(8,128)(2,1)S(1)} %get-tuple-element.112), channel_id=1, source_target_pairs={{0,24},{4,28},{8,16},{12,20},{16,8},{20,12},{24,0},{28,4},{32,56},... | collective-permute-start | bytes 196616 | tf_op jit(solution)/shard_map/ppermute | solution.py:736
  27.1 7.1 %copy-start = (f32[2048]{0:T(1024)S(1)}, f32[2048]{0:T(1024)}, u32[]{:S(2)}) copy-start(f32[2048]{0:T(1024)} %param.12) | copy-start | bytes 24580
  31.4 3.9 %collective-permute-start.9 = (bf16[1024,128]{1,0:T(8,128)(2,1)S(1)}, bf16[1024,128]{1,0:T(8,128)(2,1)S(1)}, u32[]{:S(2)}, u32[]{:S(2)}) collective-permute-start(bf16[1024,128]{1,0:T(8,128)(2,1)S(1)} %get-tuple-element.121), channel_id=1, source_target_pairs={{0,4},{4,0},{8,12},{12,8},{16,20},{20,16},{24,28},{28,24},{32,36},... | collective-permute-start | bytes 786440 | tf_op jit(solution)/shard_map/ppermute | solution.py:736
  36.4 4.0 %collective-permute-start.10 = (f32[8,512]{1,0:T(8,128)S(1)}, f32[8,512]{1,0:T(8,128)S(1)}, u32[]{:S(2)}, u32[]{:S(2)}) collective-permute-start(f32[8,512]{1,0:T(8,128)S(1)} %get-tuple-element.128.refs_5_), channel_id=1, source_target_pairs={{0,1},{1,0},{2,3},{3,2},{4,5},{5,4},{6,7},{7,6},{8,9},{9,8},{10,11... | collective-permute-start | bytes 49160 | tf_op jit(solution)/shard_map/ppermute | solution.py:736
  37.8 4.1 %collective-permute-start.11 = (f32[8,512]{1,0:T(8,128)S(1)}, f32[8,512]{1,0:T(8,128)S(1)}, u32[]{:S(2)}, u32[]{:S(2)}) collective-permute-start(f32[8,512]{1,0:T(8,128)S(1)} %get-tuple-element.128.refs_5_), channel_id=1, source_target_pairs={{0,2},{1,3},{2,0},{3,1},{4,6},{5,7},{6,4},{7,5},{8,10},{9,11},{10,... | collective-permute-start | bytes 49160 | tf_op jit(solution)/shard_map/ppermute | solution.py:736
  40.4 3.8 %collective-permute-start.12 = (f32[8,512]{1,0:T(8,128)S(1)}, f32[8,512]{1,0:T(8,128)S(1)}, u32[]{:S(2)}, u32[]{:S(2)}) collective-permute-start(f32[8,512]{1,0:T(8,128)S(1)} %get-tuple-element.128.refs_5_), channel_id=1, source_target_pairs={{0,3},{1,2},{2,1},{3,0},{4,7},{5,6},{6,5},{7,4},{8,11},{9,10},{10,... | collective-permute-start | bytes 49160 | tf_op jit(solution)/shard_map/ppermute | solution.py:736
  45.4 3.3 %collective-permute-start.13 = (bf16[1056,128]{1,0:T(8,128)(2,1)S(1)}, bf16[1056,128]{1,0:T(8,128)(2,1)S(1)}, u32[]{:S(2)}, u32[]{:S(2)}) collective-permute-start(bf16[1056,128]{1,0:T(8,128)(2,1)S(1)} %get-tuple-element.137), channel_id=1, source_target_pairs={{0,4},{4,0},{8,12},{12,8},{16,20},{20,16},{24,28},{28,24},{32,36},... | collective-permute-start | bytes 811016 | tf_op jit(solution)/shard_map/ppermute | solution.py:736
  48.8 6.9 %collective-permute-start.14 = (bf16[288,128]{1,0:T(8,128)(2,1)S(1)}, bf16[288,128]{1,0:T(8,128)(2,1)S(1)}, u32[]{:S(2)}, u32[]{:S(2)}) collective-permute-start(bf16[288,128]{1,0:T(8,128)(2,1)S(1)} %get-tuple-element.139), channel_id=1, source_target_pairs={{0,8},{4,12},{8,0},{12,4},{16,24},{20,28},{24,16},{28,20},{32,40},... | collective-permute-start | bytes 221192 | tf_op jit(solution)/shard_map/ppermute | solution.py:736
  48.9 6.8 %collective-permute-start.15 = (bf16[288,128]{1,0:T(8,128)(2,1)S(1)}, bf16[288,128]{1,0:T(8,128)(2,1)S(1)}, u32[]{:S(2)}, u32[]{:S(2)}) collective-permute-start(bf16[288,128]{1,0:T(8,128)(2,1)S(1)} %get-tuple-element.140), channel_id=1, source_target_pairs={{0,16},{4,20},{8,24},{12,28},{16,0},{20,4},{24,8},{28,12},{32,48},... | collective-permute-start | bytes 221192 | tf_op jit(solution)/shard_map/ppermute | solution.py:736
  51.4 4.9 %collective-permute-start.16 = (bf16[288,128]{1,0:T(8,128)(2,1)S(1)}, bf16[288,128]{1,0:T(8,128)(2,1)S(1)}, u32[]{:S(2)}, u32[]{:S(2)}) collective-permute-start(bf16[288,128]{1,0:T(8,128)(2,1)S(1)} %get-tuple-element.141), channel_id=1, source_target_pairs={{0,24},{4,28},{8,16},{12,20},{16,8},{20,12},{24,0},{28,4},{32,56},... | collective-permute-start | bytes 221192 | tf_op jit(solution)/shard_map/ppermute | solution.py:736
  56.4 6.9 %collective-permute-start.17 = (bf16[288,128]{1,0:T(8,128)(2,1)S(1)}, bf16[288,128]{1,0:T(8,128)(2,1)S(1)}, u32[]{:S(2)}, u32[]{:S(2)}) collective-permute-start(bf16[288,128]{1,0:T(8,128)(2,1)S(1)} %row_sum.3.refs_11_.refs_4_), channel_id=1, source_target_pairs={{0,32},{4,36},{8,40},{12,44},{16,48},{20,52},{24,56},{28,60},{32,0... | collective-permute-start | bytes 221192 | tf_op jit(solution)/shard_map/ppermute | solution.py:736
  57.3 6.0 %collective-permute-start.18 = (bf16[288,128]{1,0:T(8,128)(2,1)S(1)}, bf16[288,128]{1,0:T(8,128)(2,1)S(1)}, u32[]{:S(2)}, u32[]{:S(2)}) collective-permute-start(bf16[288,128]{1,0:T(8,128)(2,1)S(1)} %row_sum.3.refs_11_.refs_4_), channel_id=1, source_target_pairs={{0,64},{4,68},{8,72},{12,76},{16,80},{20,84},{24,88},{28,92},{32,9... | collective-permute-start | bytes 221192 | tf_op jit(solution)/shard_map/ppermute | solution.py:736
  59.0 4.4 %collective-permute-start.19 = (bf16[288,128]{1,0:T(8,128)(2,1)S(1)}, bf16[288,128]{1,0:T(8,128)(2,1)S(1)}, u32[]{:S(2)}, u32[]{:S(2)}) collective-permute-start(bf16[288,128]{1,0:T(8,128)(2,1)S(1)} %row_sum.3.refs_11_.refs_4_), channel_id=1, source_target_pairs={{0,96},{4,100},{8,104},{12,108},{16,112},{20,116},{24,120},{28,124... | collective-permute-start | bytes 221192 | tf_op jit(solution)/shard_map/ppermute | solution.py:736
  63.8 7.2 %collective-permute-start.20 = (bf16[256,128]{1,0:T(8,128)(2,1)S(1)}, bf16[256,128]{1,0:T(8,128)(2,1)S(1)}, u32[]{:S(2)}, u32[]{:S(2)}) collective-permute-start(bf16[256,128]{1,0:T(8,128)(2,1)S(1)} %get-tuple-element.156), channel_id=1, source_target_pairs={{0,8},{4,12},{8,0},{12,4},{16,24},{20,28},{24,16},{28,20},{32,40},... | collective-permute-start | bytes 196616 | tf_op jit(solution)/shard_map/ppermute | solution.py:736
  64.6 6.4 %collective-permute-start.21 = (bf16[256,128]{1,0:T(8,128)(2,1)S(1)}, bf16[256,128]{1,0:T(8,128)(2,1)S(1)}, u32[]{:S(2)}, u32[]{:S(2)}) collective-permute-start(bf16[256,128]{1,0:T(8,128)(2,1)S(1)} %get-tuple-element.157), channel_id=1, source_target_pairs={{0,16},{4,20},{8,24},{12,28},{16,0},{20,4},{24,8},{28,12},{32,48},... | collective-permute-start | bytes 196616 | tf_op jit(solution)/shard_map/ppermute | solution.py:736
  66.3 4.7 %collective-permute-start.22 = (bf16[256,128]{1,0:T(8,128)(2,1)S(1)}, bf16[256,128]{1,0:T(8,128)(2,1)S(1)}, u32[]{:S(2)}, u32[]{:S(2)}) collective-permute-start(bf16[256,128]{1,0:T(8,128)(2,1)S(1)} %get-tuple-element.158), channel_id=1, source_target_pairs={{0,24},{4,28},{8,16},{12,20},{16,8},{20,12},{24,0},{28,4},{32,56},... | collective-permute-start | bytes 196616 | tf_op jit(solution)/shard_map/ppermute | solution.py:736
  71.3 5.8 %collective-permute-start.23 = (bf16[1040,128]{1,0:T(8,128)(2,1)S(1)}, bf16[1040,128]{1,0:T(8,128)(2,1)S(1)}, u32[]{:S(2)}, u32[]{:S(2)}) collective-permute-start(bf16[1040,128]{1,0:T(8,128)(2,1)S(1)} %get-tuple-element.161), channel_id=1, source_target_pairs={{0,4},{4,0},{8,12},{12,8},{16,20},{20,16},{24,28},{28,24},{32,36},... | collective-permute-start | bytes 798728 | tf_op jit(solution)/shard_map/ppermute | solution.py:736

commit v7 on v6

--- a/solution.py
+++ b/solution.py
@@ -372,8 +372,11 @@
             high = x.astype(BF16)
             low = (x - high.astype(F32)).astype(BF16)
             totals.append(dot(ones, high, 1, 1) + dot(ones, low, 1, 1))
-        row = lax.broadcasted_iota(jnp.int32, (8, TOK), 0)
-        sums[...] = jnp.where(row < 4, totals[0], totals[1])
+        row = lax.broadcasted_iota(jnp.int32, (8, HD), 0)
+        for n in range(8):
+            total = totals[n // 4][:, (n % 4) * HD : (n % 4 + 1) * HD]
+            packed = total if n == 0 else jnp.where(row == n, total, packed)
+        sums[...] = packed
 
 
 def cross(flip, attn, q, state, early, w, before, seg, gain, previous=()):
@@ -382,23 +385,20 @@
     return call(
         functools.partial(cross_kernel, flip), "cross", 1.2e9,
         [attn, q, state, early, w, before, seg, gain, *previous],
-        outs + ([vmem((8, TOK), F32)] if flip else [total, total]), (),
+        outs + ([vmem((8, HD), F32)] if flip else [total, total]), (),
         [pltpu.VMEM((TOK, HD), F32)] * 2 if flip else [],
     )
 
 
 def scales(sums, rinv_ref, back_ref):
-    own, one, two, three = [r[...] for r in sums]
+    own, two, one, three = [r[...] for r in sums]
     total = (own + one) + (two + three)
-    rinv = lax.rsqrt(total[0:1] * (1.0 / ATT) + EPSILON)
-    back = rinv * rinv * rinv * total[4:5] * (1.0 / ATT)
-    row = lax.broadcasted_iota(jnp.int32, (8, TOK), 0)
-    both = jnp.where(
-        row < 4, jnp.broadcast_to(rinv, (8, TOK)), jnp.broadcast_to(back, (8, TOK))
-    )
-    cols = jnp.transpose(both)
-    rinv_ref[...] = jnp.broadcast_to(cols[:, 0:1], (TOK, HD))
-    back_ref[...] = jnp.broadcast_to(cols[:, 4:5], (TOK, HD))
+    rinv = lax.rsqrt(total[0:4] * (1.0 / ATT) + EPSILON)
+    back = rinv * rinv * rinv * total[4:8] * (1.0 / ATT)
+    cols = jnp.transpose(jnp.concatenate([rinv, back], axis=0))
+    for n in range(4):
+        rinv_ref[n * HD : (n + 1) * HD, :] = jnp.broadcast_to(cols[:, n : n + 1], (HD, HD))
+        back_ref[n * HD : (n + 1) * HD, :] = jnp.broadcast_to(cols[:, n + 4 : n + 5], (HD, HD))
 
 
 def grad_kernel(flip, ids, seg, attn, w, qt, gain, *rest):
@@ -663,7 +663,7 @@
             out[QUARTER + TILE : QUARTER + 2 * TILE, :] = split_tile(both)
 
 
-def row_kernel(gain, ids, p0, p1, p2, p3, _, out):
+def row_kernel(gain, ids, p0, p2, p1, p3, _, out):
     parts = (p0, p1, p2, p3)
     info = [info_rows(p, QUARTER) for p in parts]
     low = jnp.minimum(jnp.minimum(info[0][0], info[1][0]), jnp.minimum(info[2][0], info[3][0]))
@@ -679,16 +679,16 @@
         out[QUARTER + TILE : QUARTER + 2 * TILE, :] = split_tile((g[0] + g[1]) + (g[2] + g[3]))
 
 
-def entry_kernel(reverse, gain, ids, p0, p1, p2, p3, *rest):
+def entry_kernel(reverse, gain, ids, p0, p2, p1, p3, *rest):
     _, vx, vz = place(ids, reverse)
     parts = (p0, p1, p2, p3)
     outs = rest[-5 if gain else -4 :]
     if gain:
         rows = rest[1:4]
-        earlier = [(vz ^ n) < vz for n in range(1, 4)]
+        earlier = [(vz ^ n) < vz for n in FAR_FIRST[1:]]
     else:
         rows = rest[1:3]
-        earlier = [vz >= 1, vz >= 2]
+        earlier = [vz >= 2, vz >= 1]
     info = [info_rows(p, QUARTER) for p in parts]
     row_high = [info_rows(t, QUARTER)[1] for t in rows]
     for m in range(4):
@@ -703,11 +703,12 @@
             total = total + row[0:QUARTER, :].astype(F32) * weight
         outs[m][...] = total.astype(BF16)
     if gain:
-        g = [joined_tile(t[QUARTER + TILE : QUARTER + 2 * TILE, :]) for t in rest[0:4]]
+        tiles = [joined_tile(t[QUARTER + TILE : QUARTER + 2 * TILE, :]) for t in rest[0:4]]
+        g = [tiles[m] for m in FAR_FIRST]
         outs[4][...] = split_tile((g[0] + g[1]) + (g[2] + g[3]))
 
 
-def device_kernel(reverse, gain, ids, own_ref, other_ref, e0, e1, e2, e3, _, *rest):
+def device_kernel(reverse, gain, ids, own_ref, other_ref, e0, e2, e1, e3, _, *rest):
     keep, send = rest[-2:]
     vcore, _, _ = place(ids, reverse)
     first_core = vcore == 0
@@ -736,6 +737,13 @@
     return lax.ppermute(x, axis, [(i, i ^ bits) for i in range(size)])
 
 
+FAR_FIRST = (0, 2, 1, 3)
+
+
+def swap_all(arrays, send):
+    return [arrays[0]] + [send(arrays[m], m) for m in FAR_FIRST[1:]]
+
+
 def chip_swap(x):
     return swap(x, "ctx", 32, 1)
 
@@ -758,13 +766,14 @@
     sent = glue(
         functools.partial(chip_kernel, reverse, gain), "chip_sum", [rows] * 4, own, other
     )
-    parts = [sent[0]] + [row_swap(sent[m], m) for m in range(1, 4)]
+    parts = swap_all(sent, row_swap)
     token = beside_x(sent[0])
     total = glue(functools.partial(row_kernel, gain), "row_sum", [rows], *parts, token)[0]
     if gain:
-        totals = [total] + [plane_swap(total, m) for m in range(1, 4)]
+        totals = swap_all([total] * 4, plane_swap)
     else:
-        totals = [total, plane_shift(total), plane_swap(total, 2)]
+        second = plane_swap(total, 2)
+        totals = [total, second, plane_shift(total)]
     token = beside_z(total)
     entries = glue(
         functools.partial(entry_kernel, reverse, gain),
@@ -775,7 +784,7 @@
         token,
     )
     tail = entries[4:]
-    back = [entries[0]] + [row_swap(entries[m], m) for m in range(1, 4)]
+    back = swap_all(entries, row_swap)
     token = beside_back(entries[0])
     keep, send = glue(
         functools.partial(device_kernel, reverse, gain),
@@ -824,7 +833,7 @@
     attn_send, second_send, sums = cross(
         1, attn_send, q_send, state_send, early_send, gated, before, seg, gain, sums
     )
-    sums = [sums] + [swap(sums, "tp", 4, m) for m in range(1, 4)]
+    sums = swap_all([sums] * 4, lambda x, m: swap(x, "tp", 4, m))
 
     g_send, sent, late_send, rinv, back = grad_attn(
         1, seg, attn_send, gated, qt_send, gain, sums

time: 79.4 us -> 75.8 us (0.955)
  starting transfers between devices: 39.1 us -> 36.5 us
  waiting for transfers between devices: 8.71 us -> 7.66 us
    ppermute x23, waiting for transfers between devices: 8.71 us -> 6.36 us  [swap(): return lax.ppermute(x, axis, [(i, i ^ bits) for i in range(size)])]
    ppermute x23, starting transfers between devices: 37.4 us -> 35.8 us  [swap(): return lax.ppermute(x, axis, [(i, i ^ bits) for i in range(size)])]
    ppermute x1, waiting for transfers between devices: 0.01 us -> 1.3 us  [plane_shift(): return lax.ppermute(x, 'ctx', [(i, (i + 8) % 32) for i in range(32)])]
    ppermute x1, starting transfers between devices: 1.71 us -> 0.74 us  [plane_shift(): return lax.ppermute(x, 'ctx', [(i, (i + 8) % 32) for i in range(32)])]
  transfers between devices with their start and end apart: 24 -> 24, of which waited for: 9 -> 10; matrix products, arithmetic and copies ran while one was open for 0% -> 0% of each run, Pallas kernels for 29% -> 30%
where the time goes in v7:
time: 75.8 us; the launch traced here: 75.6 us
  starting transfers between devices  36.5 us (48%)
  Pallas kernels  30.4 us (40%)
  waiting for transfers between devices  7.66 us (10%)
  between operations  1.06 us (1%)
    ppermute x23, starting transfers between devices, swap(): return lax.ppermute(x, axis, [(i, i ^ bits) for i in range(size)])  35.8 us
    pallas_call x22, Pallas kernels, call(): pl.pallas_call(placed, in_specs=[VM] * len(near) + [ANY] * len(distant),...  30.4 us
    ppermute x23, waiting for transfers between devices, swap(): return lax.ppermute(x, axis, [(i, i ^ bits) for i in range(size)])  6.36 us
  transfers between devices with their start and end apart: 24, of which 10 were waited for; matrix products, arithmetic and copies ran while one was open for 0% of the time, Pallas kernels for 30%

profile of v7, /device:TPU:1, one launch (start us, length us, event | category | flops | bytes accessed | tf_op | source)
XLA Modules:
  0.0 75.6 jit_solution(14557140721874952217)
XLA Ops:
  0.6 2.0 %local_state.2 = (bf16[512,1024]{1,0:T(8,128)(2,1)S(1)}, bf16[512,1024]{1,0:T(8,128)(2,1)S(1)}, bf16[1040,128]{1,0:T(8,128)(2,1)S(1)}, f32[1024,128]{1,0:T(8,128...) custom-call(bf16[512,2048]{1,0:T(8,128)(2,1)} %refs_2_.2, bf16[512,2048]{1,0:T(8,128)(2,1)} %refs_3_.1, ...), custom_call_target="tpu_custom_call" | custom-call | flops 1000000000 | bytes 3333333 | tf_op jit(solution)/shard_map/local_state/pallas_call | solution.py:72
  2.6 1.5 %collective-permute-start = (bf16[1040,128]{1,0:T(8,128)(2,1)S(1)}, bf16[1040,128]{1,0:T(8,128)(2,1)S(1)}, u32[]{:S(2)}, u32[]{:S(2)}) collective-permute-start(bf16[1040,128]{1,0:T(8,128)(2,1)S(1)} %get-tuple-element.95), channel_id=1, source_target_pairs={{0,4},{4,0},{8,12},{12,8},{16,20},{20,16},{24,28},{28,24},{32,36},... | collective-permute-start | bytes 798728 | tf_op jit(solution)/shard_map/ppermute | solution.py:737
  4.1 2.0 %local_state.3 = (bf16[512,1024]{1,0:T(8,128)(2,1)S(1)}, bf16[512,1024]{1,0:T(8,128)(2,1)S(1)}, bf16[1040,128]{1,0:T(8,128)(2,1)S(1)}, f32[1024,128]{1,0:T(8,128)S(1)}) custom-call(s32[1,512]{1,0:T(1,128)S(1)} %get-tuple-element.90.refs_0_.refs_2_.refs_6_, bf16[512,128]{1,0:T(8,128)(2,1)S(1)} %get-tuple-element.91.refs_1_, bf16[512,2048]{1,0:T(8,128)(2,1)} %refs_2_.2, ...), custom_call_target="tpu_custom_call" | custom-call | flops 1000000000 | bytes 3333333 | tf_op jit(solution)/shard_map/local_state/pallas_call | solution.py:72
  6.1 0.0 collective-permute-done.refs_1_
  6.2 0.1 chip_sum.2
  6.3 2.9 %collective-permute-start.1 = (bf16[272,128]{1,0:T(8,128)(2,1)S(1)}, bf16[272,128]{1,0:T(8,128)(2,1)S(1)}, u32[]{:S(2)}, u32[]{:S(2)}) collective-permute-start(bf16[272,128]{1,0:T(8,128)(2,1)S(1)} %get-tuple-element.99), channel_id=1, source_target_pairs={{0,16},{4,20},{8,24},{12,28},{16,0},{20,4},{24,8},{28,12},{32,48},... | collective-permute-start | bytes 208904 | tf_op jit(solution)/shard_map/ppermute | solution.py:737
  9.2 0.3 collective-permute-start.2
  9.5 0.6 collective-permute-start.3
  10.0 2.7 %intra.2 = (bf16[512,1024]{1,0:T(8,128)(2,1)S(1)}, f32[512,1024]{1,0:T(8,128)S(1)}, bf16[2048,256]{1,0:T(8,128)(2,1)S(1)}, bf16[2048,256]{1,0:T(8,128)(2,1)S(1)}...) custom-call(bf16[512,1024]{1,0:T(8,128)(2,1)S(1)} %get-tuple-element, ...), custom_call_target="tpu_custom_call" | custom-call | flops 3000000000 | bytes 10000000 | tf_op jit(solution)/shard_map/intra/pallas_call | solution.py:72
  12.7 0.0 collective-permute-done.1.refs_1_
  12.7 0.6 collective-permute-done.2.refs_2_
  13.3 0.5 collective-permute-done.3.refs_3_
  13.9 0.1 row_sum.2.refs_5_.refs_4_
  13.9 3.7 %collective-permute-start.4 = (bf16[272,128]{1,0:T(8,128)(2,1)S(1)}, bf16[272,128]{1,0:T(8,128)(2,1)S(1)}, u32[]{:S(2)}, u32[]{:S(2)}) collective-permute-start(bf16[272,128]{1,0:T(8,128)(2,1)S(1)} %row_sum.2.refs_5_.refs_4_), channel_id=1, source_target_pairs={{0,64},{4,68},{8,72},{12,76},{16,80},{20,84},{24,88},{28,92},{32,9... | collective-permute-start | bytes 208904 | tf_op jit(solution)/shard_map/ppermute | solution.py:737
  17.6 0.7 collective-permute-start.5
  18.3 2.7 %intra.3 = (bf16[512,1024]{1,0:T(8,128)(2,1)S(1)}, f32[512,1024]{1,0:T(8,128)S(1)}, bf16[2048,256]{1,0:T(8,128)(2,1)S(1)}, bf16[2048,256]{1,0:T(8,128)(2,1)S(1)}...) custom-call(bf16[512,1024]{1,0:T(8,128)(2,1)S(1)} %get-tuple-element.103.refs_0_.refs_1_.refs_2_, ...), custom_call_target="tpu_custom_call" | custom-call | flops 3000000000 | bytes 10000000 | tf_op jit(solution)/shard_map/intra/pallas_call | solution.py:72
  21.0 0.0 collective-permute-done.4.refs_5_
  21.0 1.3 %collective-permute-done.5.refs_6_ = bf16[272,128]{1,0:T(8,128)(2,1)S(1)} collective-permute-done((bf16[272,128]{1,0:T(8,128)(2,1)S(1)}, bf16[272,128]{1,0:T(8,128)(2,1)S(1)}, u32[]{:S(2)}, u32[]{:S(2)}) %collective-permute-start.5) | collective-permute-done | bytes 69664 | tf_op jit(solution)/shard_map/ppermute | solution.py:760
  22.3 0.3 entry.2
  22.6 2.0 %collective-permute-start.6 = (bf16[256,128]{1,0:T(8,128)(2,1)S(1)}, bf16[256,128]{1,0:T(8,128)(2,1)S(1)}, u32[]{:S(2)}, u32[]{:S(2)}) collective-permute-start(bf16[256,128]{1,0:T(8,128)(2,1)S(1)} %get-tuple-element.110), channel_id=1, source_target_pairs={{0,16},{4,20},{8,24},{12,28},{16,0},{20,4},{24,8},{28,12},{32,48},... | collective-permute-start | bytes 196616 | tf_op jit(solution)/shard_map/ppermute | solution.py:737
  24.6 0.3 collective-permute-start.7
  24.9 1.0 %collective-permute-start.8 = (bf16[256,128]{1,0:T(8,128)(2,1)S(1)}, bf16[256,128]{1,0:T(8,128)(2,1)S(1)}, u32[]{:S(2)}, u32[]{:S(2)}) collective-permute-start(bf16[256,128]{1,0:T(8,128)(2,1)S(1)} %get-tuple-element.112), channel_id=1, source_target_pairs={{0,24},{4,28},{8,16},{12,20},{16,8},{20,12},{24,0},{28,4},{32,56},... | collective-permute-start | bytes 196616 | tf_op jit(solution)/shard_map/ppermute | solution.py:737
  26.0 2.5 %prepare.1 = (f32[512,2048]{1,0:T(8,128)S(1)}, bf16[512,2048]{1,0:T(8,128)(2,1)S(1)}, f32[8,128]{1,0:T(8,128)S(1)}) custom-call(bf16[256,128]{1,0:T(8,128)(2,1)S(1)} %get-tuple-element.109.refs_0_.refs_2_, bf16[512,2048]{1,0:T(8,128)(2,1)} %refs_1_.3, bf16[512,2048]{1,0:T(8,128)(2,1)} %refs_2_.3), custom_call_target="tpu_custom_call" | custom-call | flops 3000000000 | bytes 10000000 | tf_op jit(solution)/shard_map/prepare/pallas_call | solution.py:72
  28.5 0.7 collective-permute-done.8.refs_5_
  29.2 0.2 device_entry.2
  29.5 3.9 %collective-permute-start.9 = (bf16[1024,128]{1,0:T(8,128)(2,1)S(1)}, bf16[1024,128]{1,0:T(8,128)(2,1)S(1)}, u32[]{:S(2)}, u32[]{:S(2)}) collective-permute-start(bf16[1024,128]{1,0:T(8,128)(2,1)S(1)} %get-tuple-element.121), channel_id=1, source_target_pairs={{0,4},{4,0},{8,12},{12,8},{16,20},{20,16},{24,28},{28,24},{32,36},... | collective-permute-start | bytes 786440 | tf_op jit(solution)/shard_map/ppermute | solution.py:737
  33.4 0.9 %cross.2 = (f32[512,1024]{1,0:T(8,128)S(1)}, bf16[1024,128]{1,0:T(8,128)(2,1)S(1)}, f32[512,128]{1,0:T(8,128)S(1)}, f32[512,128]{1,0:T(8,128)S(1)}) custom-call(f32[512,1024]{1,0:T(8,128)S(1)} %get-tuple-element.97.refs_0_, bf16[512,1024]{1,0:T(8,128)(2,1)S(1)} %get-tuple-element.98.refs_1_.refs_0_, ...), custom_call_target="tpu_custom_call" | custom-call | flops 1200000000 | bytes 4000000 | tf_op jit(solution)/shard_map/cross/pallas_call | solution.py:72
  34.2 0.3 collective-permute-done.9.refs_2_.refs_4_
  34.5 1.1 %cross.3 = (f32[512,1024]{1,0:T(8,128)S(1)}, bf16[1024,128]{1,0:T(8,128)(2,1)S(1)}, f32[8,128]{1,0:T(8,128)S(1)}) custom-call(f32[512,1024]{1,0:T(8,128)S(1)} %get-tuple-element.119.refs_0_, bf16[512,1024]{1,0:T(8,128)(2,1)S(1)} %get-tuple-element.120.refs_1_.refs_0_, bf16[1024,128]{1,0:T(8,128)(2,1)S(1)} %collective-permute-done.9.refs_2_.refs_4_, ...), custom_call_target="tpu_custom_call" | custom-call | flops 1200000000 | bytes 4000000 | tf_op jit(solution)/shard_map/cross/pallas_call | solution.py:72
  35.6 2.9 %collective-permute-start.10 = (f32[8,128]{1,0:T(8,128)S(1)}, f32[8,128]{1,0:T(8,128)S(1)}, u32[]{:S(2)}, u32[]{:S(2)}) collective-permute-start(f32[8,128]{1,0:T(8,128)S(1)} %get-tuple-element.128.refs_5_), channel_id=1, source_target_pairs={{0,2},{1,3},{2,0},{3,1},{4,6},{5,7},{6,4},{7,5},{8,10},{9,11},{10,... | collective-permute-start | bytes 12296 | tf_op jit(solution)/shard_map/ppermute | solution.py:737
  38.6 0.4 collective-permute-start.11
  39.0 0.4 collective-permute-start.12
  39.3 0.3 collective-permute-done.10.refs_6_
  39.6 1.4 %collective-permute-done.11.refs_7_ = f32[8,128]{1,0:T(8,128)S(1)} collective-permute-done((f32[8,128]{1,0:T(8,128)S(1)}, f32[8,128]{1,0:T(8,128)S(1)}, u32[]{:S(2)}, u32[]{:S(2)}) %collective-permute-start.11) | collective-permute-done | bytes 4128 | tf_op jit(solution)/shard_map/ppermute | solution.py:737
  41.0 1.6 %collective-permute-done.12.refs_8_ = f32[8,128]{1,0:T(8,128)S(1)} collective-permute-done((f32[8,128]{1,0:T(8,128)S(1)}, f32[8,128]{1,0:T(8,128)S(1)}, u32[]{:S(2)}, u32[]{:S(2)}) %collective-permute-start.12) | collective-permute-done | bytes 4128 | tf_op jit(solution)/shard_map/ppermute | solution.py:737
  42.6 1.1 %grad_attn.2 = (bf16[512,1024]{1,0:T(8,128)(2,1)S(1)}, bf16[1056,128]{1,0:T(8,128)(2,1)S(1)}, f32[1024,128]{1,0:T(8,128)S(1)}, f32[512,128]{1,0:T(8,128)S(1)}, f32[512,128]{1,0:T(8,128)S(1)}) custom-call(s32[1,512]{1,0:T(1,128)S(1)} %get-tuple-element.90.refs_0_.refs_2_.refs_6_, f32[512,1024]{1,0:T(8,128)S(1)} %get-tuple-element.125.refs_1_, ...), custom_call_target="tpu_custom_call" | custom-call | flops 1200000000 | bytes 4000000 | tf_op jit(solution)/shard_map/grad_attn/pallas_call | solution.py:72
  43.8 2.2 %collective-permute-start.13 = (bf16[1056,128]{1,0:T(8,128)(2,1)S(1)}, bf16[1056,128]{1,0:T(8,128)(2,1)S(1)}, u32[]{:S(2)}, u32[]{:S(2)}) collective-permute-start(bf16[1056,128]{1,0:T(8,128)(2,1)S(1)} %get-tuple-element.137), channel_id=1, source_target_pairs={{0,4},{4,0},{8,12},{12,8},{16,20},{20,16},{24,28},{28,24},{32,36},... | collective-permute-start | bytes 811016 | tf_op jit(solution)/shard_map/ppermute | solution.py:737
  45.9 1.0 %grad_attn.3 = (bf16[512,1024]{1,0:T(8,128)(2,1)S(1)}, bf16[1056,128]{1,0:T(8,128)(2,1)S(1)}, f32[1024,128]{1,0:T(8,128)S(1)}) custom-call(s32[1,512]{1,0:T(1,128)S(1)} %get-tuple-element.90.refs_0_.refs_2_.refs_6_, f32[512,1024]{1,0:T(8,128)S(1)} %get-tuple-element.118.refs_1_.refs_0_, f32[512,2048]{1,0:T(8,128)S(1)} %get-tuple-element.116.refs_4_.refs_2_.refs_3_, ...), custom_call_target="tpu_custom_call" | custom-call | flops 1200000000 | bytes 4000000 | tf_op jit(solution)/shard_map/grad_attn/pallas_call | solution.py:72
  46.9 0.2 collective-permute-done.13.refs_1_
  47.1 0.1 chip_sum.3
  47.2 0.9 %collective-permute-start.14 = (bf16[288,128]{1,0:T(8,128)(2,1)S(1)}, bf16[288,128]{1,0:T(8,128)(2,1)S(1)}, u32[]{:S(2)}, u32[]{:S(2)}) collective-permute-start(bf16[288,128]{1,0:T(8,128)(2,1)S(1)} %get-tuple-element.139), channel_id=1, source_target_pairs={{0,16},{4,20},{8,24},{12,28},{16,0},{20,4},{24,8},{28,12},{32,48},... | collective-permute-start | bytes 221192 | tf_op jit(solution)/shard_map/ppermute | solution.py:737
  48.1 1.5 %collective-permute-start.15 = (bf16[288,128]{1,0:T(8,128)(2,1)S(1)}, bf16[288,128]{1,0:T(8,128)(2,1)S(1)}, u32[]{:S(2)}, u32[]{:S(2)}) collective-permute-start(bf16[288,128]{1,0:T(8,128)(2,1)S(1)} %get-tuple-element.140), channel_id=1, source_target_pairs={{0,8},{4,12},{8,0},{12,4},{16,24},{20,28},{24,16},{28,20},{32,40},... | collective-permute-start | bytes 221192 | tf_op jit(solution)/shard_map/ppermute | solution.py:737
  49.7 0.9 %collective-permute-start.16 = (bf16[288,128]{1,0:T(8,128)(2,1)S(1)}, bf16[288,128]{1,0:T(8,128)(2,1)S(1)}, u32[]{:S(2)}, u32[]{:S(2)}) collective-permute-start(bf16[288,128]{1,0:T(8,128)(2,1)S(1)} %get-tuple-element.141), channel_id=1, source_target_pairs={{0,24},{4,28},{8,16},{12,20},{16,8},{20,12},{24,0},{28,4},{32,56},... | collective-permute-start | bytes 221192 | tf_op jit(solution)/shard_map/ppermute | solution.py:737
  50.6 3.0 %local_grads.2 = (bf16[512,1024]{1,0:T(8,128)(2,1)S(1)}, f32[512,1024]{1,0:T(8,128)S(1)}, f32[512,1024]{1,0:T(8,128)S(1)}, f32[8,128]{1,0:T(8,128)S(1)}) custom-call(bf16[512,1024]{1,0:T(8,128)(2,1)S(1)} %get-tuple-element.98.refs_1_.refs_0_, bf16[512,1024]{1,0:T(8,128)(2,1)S(1)} %get-tuple-element.92.refs_0_.refs_1_.refs_2_, ...), custom_call_target="tpu_custom_call" | custom-call | flops 5000000000 | bytes 16666666 | tf_op jit(solution)/shard_map/local_grads/pallas_call | solution.py:72
  53.5 0.0 collective-permute-done.15.refs_2_
  53.6 0.7 collective-permute-done.16.refs_3_
  54.2 0.1 row_sum.3.refs_11_.refs_4_
  54.3 0.6 collective-permute-start.17
  54.9 0.2 collective-permute-start.18
  55.1 2.5 %collective-permute-start.19 = (bf16[288,128]{1,0:T(8,128)(2,1)S(1)}, bf16[288,128]{1,0:T(8,128)(2,1)S(1)}, u32[]{:S(2)}, u32[]{:S(2)}) collective-permute-start(bf16[288,128]{1,0:T(8,128)(2,1)S(1)} %row_sum.3.refs_11_.refs_4_), channel_id=1, source_target_pairs={{0,96},{4,100},{8,104},{12,108},{16,112},{20,116},{24,120},{28,124... | collective-permute-start | bytes 221192 | tf_op jit(solution)/shard_map/ppermute | solution.py:737
  57.6 3.0 %local_grads.3 = (bf16[512,2048]{1,0:T(8,128)(2,1)}, bf16[512,1024]{1,0:T(8,128)(2,1)S(1)}, f32[512,1024]{1,0:T(8,128)S(1)}, f32[512,1024]{1,0:T(8,128)S(1)}, f32[8,128]{1,0:T(8,128)S(1)}) custom-call(bf16[512,1024]{1,0:T(8,128)(2,1)S(1)} %get-tuple-element.120.refs_1_.refs_0_, bf16[512,1024]{1,0:T(8,128)(2,1)S(1)} %get-tuple-element.103.refs_0_.refs_1_.refs_2_, ...), custom_call_target="tpu_custom_call" | custom-call | flops 5000000000 | bytes 16666666 | tf_op jit(solution)/shard_map/local_grads/pallas_call | solution.py:72
  60.7 0.0 collective-permute-done.17.refs_5_
  60.7 0.0 collective-permute-done.19.refs_7_
  60.7 0.3 entry.3
  61.0 0.6 collective-permute-start.20
  61.6 1.5 %collective-permute-start.21 = (bf16[256,128]{1,0:T(8,128)(2,1)S(1)}, bf16[256,128]{1,0:T(8,128)(2,1)S(1)}, u32[]{:S(2)}, u32[]{:S(2)}) collective-permute-start(bf16[256,128]{1,0:T(8,128)(2,1)S(1)} %get-tuple-element.157), channel_id=1, source_target_pairs={{0,8},{4,12},{8,0},{12,4},{16,24},{20,28},{24,16},{28,20},{32,40},... | collective-permute-start | bytes 196616 | tf_op jit(solution)/shard_map/ppermute | solution.py:737
  63.1 1.3 %collective-permute-start.22 = (bf16[256,128]{1,0:T(8,128)(2,1)S(1)}, bf16[256,128]{1,0:T(8,128)(2,1)S(1)}, u32[]{:S(2)}, u32[]{:S(2)}) collective-permute-start(bf16[256,128]{1,0:T(8,128)(2,1)S(1)} %get-tuple-element.158), channel_id=1, source_target_pairs={{0,24},{4,28},{8,16},{12,20},{16,8},{20,12},{24,0},{28,4},{32,56},... | collective-permute-start | bytes 196616 | tf_op jit(solution)/shard_map/ppermute | solution.py:737
  64.4 3.3 %gates.1 = (bf16[512,2048]{1,0:T(8,128)(2,1)}, bf16[512,2048]{1,0:T(8,128)(2,1)}, bf16[512,2048]{1,0:T(8,128)(2,1)}, f32[8,128]{1,0:T(8,128)S(1)}) custom-call(f32[512,1024]{1,0:T(8,128)S(1)} %get-tuple-element.118.refs_1_.refs_0_, f32[512,1024]{1,0:T(8,128)S(1)} %get-tuple-element.125.refs_1_, ...), custom_call_target="tpu_custom_call", output_to_operand_aliasing={{2}: (8, {})} | custom-call | flops 3000000000 | bytes 10000000 | tf_op jit(solution)/shard_map/gates/pallas_call | solution.py:72
  67.7 0.0 collective-permute-done.21.refs_4_
  67.7 0.0 collective-permute-done.22.refs_5_
  67.7 0.2 device_entry.3
  67.9 3.8 %collective-permute-start.23 = (bf16[1040,128]{1,0:T(8,128)(2,1)S(1)}, bf16[1040,128]{1,0:T(8,128)(2,1)S(1)}, u32[]{:S(2)}, u32[]{:S(2)}) collective-permute-start(bf16[1040,128]{1,0:T(8,128)(2,1)S(1)} %get-tuple-element.161), channel_id=1, source_target_pairs={{0,4},{4,0},{8,12},{12,8},{16,20},{20,16},{24,28},{28,24},{32,36},... | collective-permute-start | bytes 798728 | tf_op jit(solution)/shard_map/ppermute | solution.py:737
  71.7 1.9 %finish.2 = (bf16[512,2048]{1,0:T(8,128)(2,1)}, bf16[512,2048]{1,0:T(8,128)(2,1)}) custom-call(f32[512,1024]{1,0:T(8,128)S(1)} %get-tuple-element.164.refs_0_, f32[512,1024]{1,0:T(8,128)S(1)} %get-tuple-element.165.refs_1_, bf16[512,1024]{1,0:T(8,128)(2,1)S(1)} %get-tuple-element.92.refs_0_.refs_1_.refs_2_, ...), custom_call_target="tpu_custom_call" | custom-call | flops 1200000000 | bytes 4000000 | tf_op jit(solution)/shard_map/finish/pallas_call | solution.py:72
  73.6 1.9 %finish.3 = (bf16[512,2048]{1,0:T(8,128)(2,1)}, bf16[512,2048]{1,0:T(8,128)(2,1)}, f32[16,128]{1,0:T(8,128)}) custom-call(f32[512,1024]{1,0:T(8,128)S(1)} %get-tuple-element.154.refs_0_, f32[512,1024]{1,0:T(8,128)S(1)} %get-tuple-element.155.refs_1_, ...), custom_call_target="tpu_custom_call", output_to_operand_aliasing={{0}: (9, {}), {1}: (10, {})} | custom-call | flops 1200000000 | bytes 4000000 | tf_op jit(solution)/shard_map/finish/pallas_call | solution.py:72
  (8 shorter events, 0.0 us)
Async XLA Ops:
  2.6 3.5 %collective-permute-start = (bf16[1040,128]{1,0:T(8,128)(2,1)S(1)}, bf16[1040,128]{1,0:T(8,128)(2,1)S(1)}, u32[]{:S(2)}, u32[]{:S(2)}) collective-permute-start(bf16[1040,128]{1,0:T(8,128)(2,1)S(1)} %get-tuple-element.95), channel_id=1, source_target_pairs={{0,4},{4,0},{8,12},{12,8},{16,20},{20,16},{24,28},{28,24},{32,36},... | collective-permute-start | bytes 798728 | tf_op jit(solution)/shard_map/ppermute | solution.py:737
  6.3 6.5 %collective-permute-start.1 = (bf16[272,128]{1,0:T(8,128)(2,1)S(1)}, bf16[272,128]{1,0:T(8,128)(2,1)S(1)}, u32[]{:S(2)}, u32[]{:S(2)}) collective-permute-start(bf16[272,128]{1,0:T(8,128)(2,1)S(1)} %get-tuple-element.99), channel_id=1, source_target_pairs={{0,16},{4,20},{8,24},{12,28},{16,0},{20,4},{24,8},{28,12},{32,48},... | collective-permute-start | bytes 208904 | tf_op jit(solution)/shard_map/ppermute | solution.py:737
  9.2 4.2 %collective-permute-start.2 = (bf16[272,128]{1,0:T(8,128)(2,1)S(1)}, bf16[272,128]{1,0:T(8,128)(2,1)S(1)}, u32[]{:S(2)}, u32[]{:S(2)}) collective-permute-start(bf16[272,128]{1,0:T(8,128)(2,1)S(1)} %get-tuple-element.100), channel_id=1, source_target_pairs={{0,8},{4,12},{8,0},{12,4},{16,24},{20,28},{24,16},{28,20},{32,40},... | collective-permute-start | bytes 208904 | tf_op jit(solution)/shard_map/ppermute | solution.py:737
  9.5 4.4 %collective-permute-start.3 = (bf16[272,128]{1,0:T(8,128)(2,1)S(1)}, bf16[272,128]{1,0:T(8,128)(2,1)S(1)}, u32[]{:S(2)}, u32[]{:S(2)}) collective-permute-start(bf16[272,128]{1,0:T(8,128)(2,1)S(1)} %get-tuple-element.101), channel_id=1, source_target_pairs={{0,24},{4,28},{8,16},{12,20},{16,8},{20,12},{24,0},{28,4},{32,56},... | collective-permute-start | bytes 208904 | tf_op jit(solution)/shard_map/ppermute | solution.py:737
  13.9 7.1 %collective-permute-start.4 = (bf16[272,128]{1,0:T(8,128)(2,1)S(1)}, bf16[272,128]{1,0:T(8,128)(2,1)S(1)}, u32[]{:S(2)}, u32[]{:S(2)}) collective-permute-start(bf16[272,128]{1,0:T(8,128)(2,1)S(1)} %row_sum.2.refs_5_.refs_4_), channel_id=1, source_target_pairs={{0,64},{4,68},{8,72},{12,76},{16,80},{20,84},{24,88},{28,92},{32,9... | collective-permute-start | bytes 208904 | tf_op jit(solution)/shard_map/ppermute | solution.py:737
  17.6 4.7 %collective-permute-start.5 = (bf16[272,128]{1,0:T(8,128)(2,1)S(1)}, bf16[272,128]{1,0:T(8,128)(2,1)S(1)}, u32[]{:S(2)}, u32[]{:S(2)}) collective-permute-start(bf16[272,128]{1,0:T(8,128)(2,1)S(1)} %row_sum.2.refs_5_.refs_4_), channel_id=1, source_target_pairs={{0,32},{4,36},{8,40},{12,44},{16,48},{20,52},{24,56},{28,60},{32,6... | collective-permute-start | bytes 208904 | tf_op jit(solution)/shard_map/ppermute | solution.py:760
  22.6 5.9 %collective-permute-start.6 = (bf16[256,128]{1,0:T(8,128)(2,1)S(1)}, bf16[256,128]{1,0:T(8,128)(2,1)S(1)}, u32[]{:S(2)}, u32[]{:S(2)}) collective-permute-start(bf16[256,128]{1,0:T(8,128)(2,1)S(1)} %get-tuple-element.110), channel_id=1, source_target_pairs={{0,16},{4,20},{8,24},{12,28},{16,0},{20,4},{24,8},{28,12},{32,48},... | collective-permute-start | bytes 196616 | tf_op jit(solution)/shard_map/ppermute | solution.py:737
  24.6 3.9 %collective-permute-start.7 = (bf16[256,128]{1,0:T(8,128)(2,1)S(1)}, bf16[256,128]{1,0:T(8,128)(2,1)S(1)}, u32[]{:S(2)}, u32[]{:S(2)}) collective-permute-start(bf16[256,128]{1,0:T(8,128)(2,1)S(1)} %get-tuple-element.111), channel_id=1, source_target_pairs={{0,8},{4,12},{8,0},{12,4},{16,24},{20,28},{24,16},{28,20},{32,40},... | collective-permute-start | bytes 196616 | tf_op jit(solution)/shard_map/ppermute | solution.py:737
  24.9 4.3 %collective-permute-start.8 = (bf16[256,128]{1,0:T(8,128)(2,1)S(1)}, bf16[256,128]{1,0:T(8,128)(2,1)S(1)}, u32[]{:S(2)}, u32[]{:S(2)}) collective-permute-start(bf16[256,128]{1,0:T(8,128)(2,1)S(1)} %get-tuple-element.112), channel_id=1, source_target_pairs={{0,24},{4,28},{8,16},{12,20},{16,8},{20,12},{24,0},{28,4},{32,56},... | collective-permute-start | bytes 196616 | tf_op jit(solution)/shard_map/ppermute | solution.py:737
  26.0 7.4 %copy-start = (f32[2048]{0:T(1024)S(1)}, f32[2048]{0:T(1024)}, u32[]{:S(2)}) copy-start(f32[2048]{0:T(1024)} %param.12) | copy-start | bytes 24580
  29.5 5.0 %collective-permute-start.9 = (bf16[1024,128]{1,0:T(8,128)(2,1)S(1)}, bf16[1024,128]{1,0:T(8,128)(2,1)S(1)}, u32[]{:S(2)}, u32[]{:S(2)}) collective-permute-start(bf16[1024,128]{1,0:T(8,128)(2,1)S(1)} %get-tuple-element.121), channel_id=1, source_target_pairs={{0,4},{4,0},{8,12},{12,8},{16,20},{20,16},{24,28},{28,24},{32,36},... | collective-permute-start | bytes 786440 | tf_op jit(solution)/shard_map/ppermute | solution.py:737
  35.6 4.0 %collective-permute-start.10 = (f32[8,128]{1,0:T(8,128)S(1)}, f32[8,128]{1,0:T(8,128)S(1)}, u32[]{:S(2)}, u32[]{:S(2)}) collective-permute-start(f32[8,128]{1,0:T(8,128)S(1)} %get-tuple-element.128.refs_5_), channel_id=1, source_target_pairs={{0,2},{1,3},{2,0},{3,1},{4,6},{5,7},{6,4},{7,5},{8,10},{9,11},{10,... | collective-permute-start | bytes 12296 | tf_op jit(solution)/shard_map/ppermute | solution.py:737
  38.6 2.5 %collective-permute-start.11 = (f32[8,128]{1,0:T(8,128)S(1)}, f32[8,128]{1,0:T(8,128)S(1)}, u32[]{:S(2)}, u32[]{:S(2)}) collective-permute-start(f32[8,128]{1,0:T(8,128)S(1)} %get-tuple-element.128.refs_5_), channel_id=1, source_target_pairs={{0,1},{1,0},{2,3},{3,2},{4,5},{5,4},{6,7},{7,6},{8,9},{9,8},{10,11... | collective-permute-start | bytes 12296 | tf_op jit(solution)/shard_map/ppermute | solution.py:737
  39.0 3.7 %collective-permute-start.12 = (f32[8,128]{1,0:T(8,128)S(1)}, f32[8,128]{1,0:T(8,128)S(1)}, u32[]{:S(2)}, u32[]{:S(2)}) collective-permute-start(f32[8,128]{1,0:T(8,128)S(1)} %get-tuple-element.128.refs_5_), channel_id=1, source_target_pairs={{0,3},{1,2},{2,1},{3,0},{4,7},{5,6},{6,5},{7,4},{8,11},{9,10},{10,... | collective-permute-start | bytes 12296 | tf_op jit(solution)/shard_map/ppermute | solution.py:737
  43.8 3.3 %collective-permute-start.13 = (bf16[1056,128]{1,0:T(8,128)(2,1)S(1)}, bf16[1056,128]{1,0:T(8,128)(2,1)S(1)}, u32[]{:S(2)}, u32[]{:S(2)}) collective-permute-start(bf16[1056,128]{1,0:T(8,128)(2,1)S(1)} %get-tuple-element.137), channel_id=1, source_target_pairs={{0,4},{4,0},{8,12},{12,8},{16,20},{20,16},{24,28},{28,24},{32,36},... | collective-permute-start | bytes 811016 | tf_op jit(solution)/shard_map/ppermute | solution.py:737
  47.2 6.3 %collective-permute-start.14 = (bf16[288,128]{1,0:T(8,128)(2,1)S(1)}, bf16[288,128]{1,0:T(8,128)(2,1)S(1)}, u32[]{:S(2)}, u32[]{:S(2)}) collective-permute-start(bf16[288,128]{1,0:T(8,128)(2,1)S(1)} %get-tuple-element.139), channel_id=1, source_target_pairs={{0,16},{4,20},{8,24},{12,28},{16,0},{20,4},{24,8},{28,12},{32,48},... | collective-permute-start | bytes 221192 | tf_op jit(solution)/shard_map/ppermute | solution.py:737
  48.1 5.4 %collective-permute-start.15 = (bf16[288,128]{1,0:T(8,128)(2,1)S(1)}, bf16[288,128]{1,0:T(8,128)(2,1)S(1)}, u32[]{:S(2)}, u32[]{:S(2)}) collective-permute-start(bf16[288,128]{1,0:T(8,128)(2,1)S(1)} %get-tuple-element.140), channel_id=1, source_target_pairs={{0,8},{4,12},{8,0},{12,4},{16,24},{20,28},{24,16},{28,20},{32,40},... | collective-permute-start | bytes 221192 | tf_op jit(solution)/shard_map/ppermute | solution.py:737
  49.7 4.6 %collective-permute-start.16 = (bf16[288,128]{1,0:T(8,128)(2,1)S(1)}, bf16[288,128]{1,0:T(8,128)(2,1)S(1)}, u32[]{:S(2)}, u32[]{:S(2)}) collective-permute-start(bf16[288,128]{1,0:T(8,128)(2,1)S(1)} %get-tuple-element.141), channel_id=1, source_target_pairs={{0,24},{4,28},{8,16},{12,20},{16,8},{20,12},{24,0},{28,4},{32,56},... | collective-permute-start | bytes 221192 | tf_op jit(solution)/shard_map/ppermute | solution.py:737
  54.3 6.4 %collective-permute-start.17 = (bf16[288,128]{1,0:T(8,128)(2,1)S(1)}, bf16[288,128]{1,0:T(8,128)(2,1)S(1)}, u32[]{:S(2)}, u32[]{:S(2)}) collective-permute-start(bf16[288,128]{1,0:T(8,128)(2,1)S(1)} %row_sum.3.refs_11_.refs_4_), channel_id=1, source_target_pairs={{0,64},{4,68},{8,72},{12,76},{16,80},{20,84},{24,88},{28,92},{32,9... | collective-permute-start | bytes 221192 | tf_op jit(solution)/shard_map/ppermute | solution.py:737
  54.9 5.8 %collective-permute-start.18 = (bf16[288,128]{1,0:T(8,128)(2,1)S(1)}, bf16[288,128]{1,0:T(8,128)(2,1)S(1)}, u32[]{:S(2)}, u32[]{:S(2)}) collective-permute-start(bf16[288,128]{1,0:T(8,128)(2,1)S(1)} %row_sum.3.refs_11_.refs_4_), channel_id=1, source_target_pairs={{0,32},{4,36},{8,40},{12,44},{16,48},{20,52},{24,56},{28,60},{32,0... | collective-permute-start | bytes 221192 | tf_op jit(solution)/shard_map/ppermute | solution.py:737
  55.1 5.5 %collective-permute-start.19 = (bf16[288,128]{1,0:T(8,128)(2,1)S(1)}, bf16[288,128]{1,0:T(8,128)(2,1)S(1)}, u32[]{:S(2)}, u32[]{:S(2)}) collective-permute-start(bf16[288,128]{1,0:T(8,128)(2,1)S(1)} %row_sum.3.refs_11_.refs_4_), channel_id=1, source_target_pairs={{0,96},{4,100},{8,104},{12,108},{16,112},{20,116},{24,120},{28,124... | collective-permute-start | bytes 221192 | tf_op jit(solution)/shard_map/ppermute | solution.py:737
  61.0 6.6 %collective-permute-start.20 = (bf16[256,128]{1,0:T(8,128)(2,1)S(1)}, bf16[256,128]{1,0:T(8,128)(2,1)S(1)}, u32[]{:S(2)}, u32[]{:S(2)}) collective-permute-start(bf16[256,128]{1,0:T(8,128)(2,1)S(1)} %get-tuple-element.156), channel_id=1, source_target_pairs={{0,16},{4,20},{8,24},{12,28},{16,0},{20,4},{24,8},{28,12},{32,48},... | collective-permute-start | bytes 196616 | tf_op jit(solution)/shard_map/ppermute | solution.py:737
  61.6 6.0 %collective-permute-start.21 = (bf16[256,128]{1,0:T(8,128)(2,1)S(1)}, bf16[256,128]{1,0:T(8,128)(2,1)S(1)}, u32[]{:S(2)}, u32[]{:S(2)}) collective-permute-start(bf16[256,128]{1,0:T(8,128)(2,1)S(1)} %get-tuple-element.157), channel_id=1, source_target_pairs={{0,8},{4,12},{8,0},{12,4},{16,24},{20,28},{24,16},{28,20},{32,40},... | collective-permute-start | bytes 196616 | tf_op jit(solution)/shard_map/ppermute | solution.py:737
  63.1 4.6 %collective-permute-start.22 = (bf16[256,128]{1,0:T(8,128)(2,1)S(1)}, bf16[256,128]{1,0:T(8,128)(2,1)S(1)}, u32[]{:S(2)}, u32[]{:S(2)}) collective-permute-start(bf16[256,128]{1,0:T(8,128)(2,1)S(1)} %get-tuple-element.158), channel_id=1, source_target_pairs={{0,24},{4,28},{8,16},{12,20},{16,8},{20,12},{24,0},{28,4},{32,56},... | collective-permute-start | bytes 196616 | tf_op jit(solution)/shard_map/ppermute | solution.py:737
  67.9 5.7 %collective-permute-start.23 = (bf16[1040,128]{1,0:T(8,128)(2,1)S(1)}, bf16[1040,128]{1,0:T(8,128)(2,1)S(1)}, u32[]{:S(2)}, u32[]{:S(2)}) collective-permute-start(bf16[1040,128]{1,0:T(8,128)(2,1)S(1)} %get-tuple-element.161), channel_id=1, source_target_pairs={{0,4},{4,0},{8,12},{12,8},{16,20},{20,16},{24,28},{28,24},{32,36},... | collective-permute-start | bytes 798728 | tf_op jit(solution)/shard_map/ppermute | solution.py:737

commit v8 on v7

--- a/solution.py
+++ b/solution.py
@@ -391,7 +391,7 @@
 
 
 def scales(sums, rinv_ref, back_ref):
-    own, two, one, three = [r[...] for r in sums]
+    own, two, three, one = [r[...] for r in sums]
     total = (own + one) + (two + three)
     rinv = lax.rsqrt(total[0:4] * (1.0 / ATT) + EPSILON)
     back = rinv * rinv * rinv * total[4:8] * (1.0 / ATT)
@@ -663,7 +663,7 @@
             out[QUARTER + TILE : QUARTER + 2 * TILE, :] = split_tile(both)
 
 
-def row_kernel(gain, ids, p0, p2, p1, p3, _, out):
+def row_kernel(gain, ids, p0, p2, p3, p1, _, out):
     parts = (p0, p1, p2, p3)
     info = [info_rows(p, QUARTER) for p in parts]
     low = jnp.minimum(jnp.minimum(info[0][0], info[1][0]), jnp.minimum(info[2][0], info[3][0]))
@@ -679,7 +679,7 @@
         out[QUARTER + TILE : QUARTER + 2 * TILE, :] = split_tile((g[0] + g[1]) + (g[2] + g[3]))
 
 
-def entry_kernel(reverse, gain, ids, p0, p2, p1, p3, *rest):
+def entry_kernel(reverse, gain, ids, p0, p2, p3, p1, *rest):
     _, vx, vz = place(ids, reverse)
     parts = (p0, p1, p2, p3)
     outs = rest[-5 if gain else -4 :]
@@ -704,11 +704,11 @@
         outs[m][...] = total.astype(BF16)
     if gain:
         tiles = [joined_tile(t[QUARTER + TILE : QUARTER + 2 * TILE, :]) for t in rest[0:4]]
-        g = [tiles[m] for m in FAR_FIRST]
+        g = [tiles[FAR_FIRST.index(m)] for m in range(4)]
         outs[4][...] = split_tile((g[0] + g[1]) + (g[2] + g[3]))
 
 
-def device_kernel(reverse, gain, ids, own_ref, other_ref, e0, e2, e1, e3, _, *rest):
+def device_kernel(reverse, gain, ids, own_ref, other_ref, e0, e2, e3, e1, _, *rest):
     keep, send = rest[-2:]
     vcore, _, _ = place(ids, reverse)
     first_core = vcore == 0
@@ -737,7 +737,7 @@
     return lax.ppermute(x, axis, [(i, i ^ bits) for i in range(size)])
 
 
-FAR_FIRST = (0, 2, 1, 3)
+FAR_FIRST = (0, 2, 3, 1)
 
 
 def swap_all(arrays, send):

time: 75.8 us -> 73.4 us (0.968)
  starting transfers between devices: 36.5 us -> 33.4 us
  waiting for transfers between devices: 7.66 us -> 8.48 us
    ppermute x23, starting transfers between devices: 35.8 us -> 32.6 us  [swap(): return lax.ppermute(x, axis, [(i, i ^ bits) for i in range(size)])]
    ppermute x23, waiting for transfers between devices: 6.36 us -> 7.32 us  [swap(): return lax.ppermute(x, axis, [(i, i ^ bits) for i in range(size)])]
  transfers between devices with their start and end apart: 24 -> 24, of which waited for: 10 -> 11; matrix products, arithmetic and copies ran while one was open for 0% -> 0% of each run, Pallas kernels for 30% -> 31%
where the time goes in v8:
time: 73.4 us; the launch traced here: 73.2 us
  starting transfers between devices  33.4 us (46%)
  Pallas kernels  30.4 us (41%)
  waiting for transfers between devices  8.48 us (12%)
  between operations  1.02 us (1%)
    ppermute x23, starting transfers between devices, swap(): return lax.ppermute(x, axis, [(i, i ^ bits) for i in range(size)])  32.6 us
    pallas_call x22, Pallas kernels, call(): pl.pallas_call(placed, in_specs=[VM] * len(near) + [ANY] * len(distant),...  30.4 us
    ppermute x23, waiting for transfers between devices, swap(): return lax.ppermute(x, axis, [(i, i ^ bits) for i in range(size)])  7.32 us
  transfers between devices with their start and end apart: 24, of which 11 were waited for; matrix products, arithmetic and copies ran while one was open for 0% of the time, Pallas kernels for 31%

profile of v8, /device:TPU:1, one launch (start us, length us, event | category | flops | bytes accessed | tf_op | source)
XLA Modules:
  0.0 73.2 jit_solution(10116630127202451358)
XLA Ops:
  0.6 2.0 %local_state.2 = (bf16[512,1024]{1,0:T(8,128)(2,1)S(1)}, bf16[512,1024]{1,0:T(8,128)(2,1)S(1)}, bf16[1040,128]{1,0:T(8,128)(2,1)S(1)}, f32[1024,128]{1,0:T(8,128...) custom-call(bf16[512,2048]{1,0:T(8,128)(2,1)} %refs_2_.2, bf16[512,2048]{1,0:T(8,128)(2,1)} %refs_3_.1, ...), custom_call_target="tpu_custom_call" | custom-call | flops 1000000000 | bytes 3333333 | tf_op jit(solution)/shard_map/local_state/pallas_call | solution.py:72
  2.6 1.5 %collective-permute-start = (bf16[1040,128]{1,0:T(8,128)(2,1)S(1)}, bf16[1040,128]{1,0:T(8,128)(2,1)S(1)}, u32[]{:S(2)}, u32[]{:S(2)}) collective-permute-start(bf16[1040,128]{1,0:T(8,128)(2,1)S(1)} %get-tuple-element.95), channel_id=1, source_target_pairs={{0,4},{4,0},{8,12},{12,8},{16,20},{20,16},{24,28},{28,24},{32,36},... | collective-permute-start | bytes 798728 | tf_op jit(solution)/shard_map/ppermute | solution.py:737
  4.1 2.0 %local_state.3 = (bf16[512,1024]{1,0:T(8,128)(2,1)S(1)}, bf16[512,1024]{1,0:T(8,128)(2,1)S(1)}, bf16[1040,128]{1,0:T(8,128)(2,1)S(1)}, f32[1024,128]{1,0:T(8,128)S(1)}) custom-call(s32[1,512]{1,0:T(1,128)S(1)} %get-tuple-element.90.refs_0_.refs_2_.refs_6_, bf16[512,128]{1,0:T(8,128)(2,1)S(1)} %get-tuple-element.91.refs_1_, bf16[512,2048]{1,0:T(8,128)(2,1)} %refs_2_.2, ...), custom_call_target="tpu_custom_call" | custom-call | flops 1000000000 | bytes 3333333 | tf_op jit(solution)/shard_map/local_state/pallas_call | solution.py:72
  6.1 0.0 collective-permute-done.refs_1_
  6.2 0.1 chip_sum.2
  6.3 2.9 %collective-permute-start.1 = (bf16[272,128]{1,0:T(8,128)(2,1)S(1)}, bf16[272,128]{1,0:T(8,128)(2,1)S(1)}, u32[]{:S(2)}, u32[]{:S(2)}) collective-permute-start(bf16[272,128]{1,0:T(8,128)(2,1)S(1)} %get-tuple-element.99), channel_id=1, source_target_pairs={{0,16},{4,20},{8,24},{12,28},{16,0},{20,4},{24,8},{28,12},{32,48},... | collective-permute-start | bytes 208904 | tf_op jit(solution)/shard_map/ppermute | solution.py:737
  9.2 0.9 %collective-permute-start.2 = (bf16[272,128]{1,0:T(8,128)(2,1)S(1)}, bf16[272,128]{1,0:T(8,128)(2,1)S(1)}, u32[]{:S(2)}, u32[]{:S(2)}) collective-permute-start(bf16[272,128]{1,0:T(8,128)(2,1)S(1)} %get-tuple-element.100), channel_id=1, source_target_pairs={{0,24},{4,28},{8,16},{12,20},{16,8},{20,12},{24,0},{28,4},{32,56},... | collective-permute-start | bytes 208904 | tf_op jit(solution)/shard_map/ppermute | solution.py:737
  10.0 0.0 collective-permute-start.3
  10.0 2.7 %intra.2 = (bf16[512,1024]{1,0:T(8,128)(2,1)S(1)}, f32[512,1024]{1,0:T(8,128)S(1)}, bf16[2048,256]{1,0:T(8,128)(2,1)S(1)}, bf16[2048,256]{1,0:T(8,128)(2,1)S(1)}...) custom-call(bf16[512,1024]{1,0:T(8,128)(2,1)S(1)} %get-tuple-element, ...), custom_call_target="tpu_custom_call" | custom-call | flops 3000000000 | bytes 10000000 | tf_op jit(solution)/shard_map/intra/pallas_call | solution.py:72
  12.7 0.0 collective-permute-done.1.refs_1_
  12.7 0.8 %collective-permute-done.2.refs_2_ = bf16[272,128]{1,0:T(8,128)(2,1)S(1)} collective-permute-done((bf16[272,128]{1,0:T(8,128)(2,1)S(1)}, bf16[272,128]{1,0:T(8,128)(2,1)S(1)}, u32[]{:S(2)}, u32[]{:S(2)}) %collective-permute-start.2) | collective-permute-done | bytes 69664 | tf_op jit(solution)/shard_map/ppermute | solution.py:737
  13.6 0.0 collective-permute-done.3.refs_3_
  13.6 0.1 row_sum.2.refs_5_.refs_4_
  13.6 3.7 %collective-permute-start.4 = (bf16[272,128]{1,0:T(8,128)(2,1)S(1)}, bf16[272,128]{1,0:T(8,128)(2,1)S(1)}, u32[]{:S(2)}, u32[]{:S(2)}) collective-permute-start(bf16[272,128]{1,0:T(8,128)(2,1)S(1)} %row_sum.2.refs_5_.refs_4_), channel_id=1, source_target_pairs={{0,64},{4,68},{8,72},{12,76},{16,80},{20,84},{24,88},{28,92},{32,9... | collective-permute-start | bytes 208904 | tf_op jit(solution)/shard_map/ppermute | solution.py:737
  17.3 0.7 %collective-permute-start.5 = (bf16[272,128]{1,0:T(8,128)(2,1)S(1)}, bf16[272,128]{1,0:T(8,128)(2,1)S(1)}, u32[]{:S(2)}, u32[]{:S(2)}) collective-permute-start(bf16[272,128]{1,0:T(8,128)(2,1)S(1)} %row_sum.2.refs_5_.refs_4_), channel_id=1, source_target_pairs={{0,32},{4,36},{8,40},{12,44},{16,48},{20,52},{24,56},{28,60},{32,6... | collective-permute-start | bytes 208904 | tf_op jit(solution)/shard_map/ppermute | solution.py:760
  18.0 2.7 %intra.3 = (bf16[512,1024]{1,0:T(8,128)(2,1)S(1)}, f32[512,1024]{1,0:T(8,128)S(1)}, bf16[2048,256]{1,0:T(8,128)(2,1)S(1)}, bf16[2048,256]{1,0:T(8,128)(2,1)S(1)}...) custom-call(bf16[512,1024]{1,0:T(8,128)(2,1)S(1)} %get-tuple-element.103.refs_0_.refs_1_.refs_2_, ...), custom_call_target="tpu_custom_call" | custom-call | flops 3000000000 | bytes 10000000 | tf_op jit(solution)/shard_map/intra/pallas_call | solution.py:72
  20.7 1.2 %collective-permute-done.5.refs_6_ = bf16[272,128]{1,0:T(8,128)(2,1)S(1)} collective-permute-done((bf16[272,128]{1,0:T(8,128)(2,1)S(1)}, bf16[272,128]{1,0:T(8,128)(2,1)S(1)}, u32[]{:S(2)}, u32[]{:S(2)}) %collective-permute-start.5) | collective-permute-done | bytes 69664 | tf_op jit(solution)/shard_map/ppermute | solution.py:760
  21.9 0.3 entry.2
  22.2 2.1 %collective-permute-start.6 = (bf16[256,128]{1,0:T(8,128)(2,1)S(1)}, bf16[256,128]{1,0:T(8,128)(2,1)S(1)}, u32[]{:S(2)}, u32[]{:S(2)}) collective-permute-start(bf16[256,128]{1,0:T(8,128)(2,1)S(1)} %get-tuple-element.110), channel_id=1, source_target_pairs={{0,16},{4,20},{8,24},{12,28},{16,0},{20,4},{24,8},{28,12},{32,48},... | collective-permute-start | bytes 196616 | tf_op jit(solution)/shard_map/ppermute | solution.py:737
  24.2 1.4 %collective-permute-start.7 = (bf16[256,128]{1,0:T(8,128)(2,1)S(1)}, bf16[256,128]{1,0:T(8,128)(2,1)S(1)}, u32[]{:S(2)}, u32[]{:S(2)}) collective-permute-start(bf16[256,128]{1,0:T(8,128)(2,1)S(1)} %get-tuple-element.111), channel_id=1, source_target_pairs={{0,24},{4,28},{8,16},{12,20},{16,8},{20,12},{24,0},{28,4},{32,56},... | collective-permute-start | bytes 196616 | tf_op jit(solution)/shard_map/ppermute | solution.py:737
  25.7 2.5 %prepare.1 = (f32[512,2048]{1,0:T(8,128)S(1)}, bf16[512,2048]{1,0:T(8,128)(2,1)S(1)}, f32[8,128]{1,0:T(8,128)S(1)}) custom-call(bf16[256,128]{1,0:T(8,128)(2,1)S(1)} %get-tuple-element.109.refs_0_.refs_2_, bf16[512,2048]{1,0:T(8,128)(2,1)} %refs_1_.3, bf16[512,2048]{1,0:T(8,128)(2,1)} %refs_2_.3), custom_call_target="tpu_custom_call" | custom-call | flops 3000000000 | bytes 10000000 | tf_op jit(solution)/shard_map/prepare/pallas_call | solution.py:72
  28.2 0.0 collective-permute-done.6.refs_3_
  28.2 0.4 collective-permute-done.7.refs_4_
  28.6 0.4 collective-permute-done.8.refs_5_
  28.9 0.2 device_entry.2
  29.2 3.6 %collective-permute-start.9 = (bf16[1024,128]{1,0:T(8,128)(2,1)S(1)}, bf16[1024,128]{1,0:T(8,128)(2,1)S(1)}, u32[]{:S(2)}, u32[]{:S(2)}) collective-permute-start(bf16[1024,128]{1,0:T(8,128)(2,1)S(1)} %get-tuple-element.121), channel_id=1, source_target_pairs={{0,4},{4,0},{8,12},{12,8},{16,20},{20,16},{24,28},{28,24},{32,36},... | collective-permute-start | bytes 786440 | tf_op jit(solution)/shard_map/ppermute | solution.py:737
  32.8 0.9 %cross.2 = (f32[512,1024]{1,0:T(8,128)S(1)}, bf16[1024,128]{1,0:T(8,128)(2,1)S(1)}, f32[512,128]{1,0:T(8,128)S(1)}, f32[512,128]{1,0:T(8,128)S(1)}) custom-call(f32[512,1024]{1,0:T(8,128)S(1)} %get-tuple-element.97.refs_0_, bf16[512,1024]{1,0:T(8,128)(2,1)S(1)} %get-tuple-element.98.refs_1_.refs_0_, ...), custom_call_target="tpu_custom_call" | custom-call | flops 1200000000 | bytes 4000000 | tf_op jit(solution)/shard_map/cross/pallas_call | solution.py:72
  33.6 0.3 collective-permute-done.9.refs_2_.refs_4_
  33.9 1.1 %cross.3 = (f32[512,1024]{1,0:T(8,128)S(1)}, bf16[1024,128]{1,0:T(8,128)(2,1)S(1)}, f32[8,128]{1,0:T(8,128)S(1)}) custom-call(f32[512,1024]{1,0:T(8,128)S(1)} %get-tuple-element.119.refs_0_, bf16[512,1024]{1,0:T(8,128)(2,1)S(1)} %get-tuple-element.120.refs_1_.refs_0_, bf16[1024,128]{1,0:T(8,128)(2,1)S(1)} %collective-permute-done.9.refs_2_.refs_4_, ...), custom_call_target="tpu_custom_call" | custom-call | flops 1200000000 | bytes 4000000 | tf_op jit(solution)/shard_map/cross/pallas_call | solution.py:72
  35.0 3.0 %collective-permute-start.10 = (f32[8,128]{1,0:T(8,128)S(1)}, f32[8,128]{1,0:T(8,128)S(1)}, u32[]{:S(2)}, u32[]{:S(2)}) collective-permute-start(f32[8,128]{1,0:T(8,128)S(1)} %get-tuple-element.128.refs_5_), channel_id=1, source_target_pairs={{0,2},{1,3},{2,0},{3,1},{4,6},{5,7},{6,4},{7,5},{8,10},{9,11},{10,... | collective-permute-start | bytes 12296 | tf_op jit(solution)/shard_map/ppermute | solution.py:737
  38.0 0.8 %collective-permute-start.11 = (f32[8,128]{1,0:T(8,128)S(1)}, f32[8,128]{1,0:T(8,128)S(1)}, u32[]{:S(2)}, u32[]{:S(2)}) collective-permute-start(f32[8,128]{1,0:T(8,128)S(1)} %get-tuple-element.128.refs_5_), channel_id=1, source_target_pairs={{0,3},{1,2},{2,1},{3,0},{4,7},{5,6},{6,5},{7,4},{8,11},{9,10},{10,... | collective-permute-start | bytes 12296 | tf_op jit(solution)/shard_map/ppermute | solution.py:737
  38.8 0.0 collective-permute-start.12
  38.8 0.3 collective-permute-done.10.refs_6_
  39.0 2.6 %collective-permute-done.11.refs_7_ = f32[8,128]{1,0:T(8,128)S(1)} collective-permute-done((f32[8,128]{1,0:T(8,128)S(1)}, f32[8,128]{1,0:T(8,128)S(1)}, u32[]{:S(2)}, u32[]{:S(2)}) %collective-permute-start.11) | collective-permute-done | bytes 4128 | tf_op jit(solution)/shard_map/ppermute | solution.py:737
  41.7 1.1 %grad_attn.2 = (bf16[512,1024]{1,0:T(8,128)(2,1)S(1)}, bf16[1056,128]{1,0:T(8,128)(2,1)S(1)}, f32[1024,128]{1,0:T(8,128)S(1)}, f32[512,128]{1,0:T(8,128)S(1)}, f32[512,128]{1,0:T(8,128)S(1)}) custom-call(s32[1,512]{1,0:T(1,128)S(1)} %get-tuple-element.90.refs_0_.refs_2_.refs_6_, f32[512,1024]{1,0:T(8,128)S(1)} %get-tuple-element.125.refs_1_, ...), custom_call_target="tpu_custom_call" | custom-call | flops 1200000000 | bytes 4000000 | tf_op jit(solution)/shard_map/grad_attn/pallas_call | solution.py:72
  42.8 1.9 %collective-permute-start.13 = (bf16[1056,128]{1,0:T(8,128)(2,1)S(1)}, bf16[1056,128]{1,0:T(8,128)(2,1)S(1)}, u32[]{:S(2)}, u32[]{:S(2)}) collective-permute-start(bf16[1056,128]{1,0:T(8,128)(2,1)S(1)} %get-tuple-element.137), channel_id=1, source_target_pairs={{0,4},{4,0},{8,12},{12,8},{16,20},{20,16},{24,28},{28,24},{32,36},... | collective-permute-start | bytes 811016 | tf_op jit(solution)/shard_map/ppermute | solution.py:737
  44.7 1.0 %grad_attn.3 = (bf16[512,1024]{1,0:T(8,128)(2,1)S(1)}, bf16[1056,128]{1,0:T(8,128)(2,1)S(1)}, f32[1024,128]{1,0:T(8,128)S(1)}) custom-call(s32[1,512]{1,0:T(1,128)S(1)} %get-tuple-element.90.refs_0_.refs_2_.refs_6_, f32[512,1024]{1,0:T(8,128)S(1)} %get-tuple-element.118.refs_1_.refs_0_, f32[512,2048]{1,0:T(8,128)S(1)} %get-tuple-element.116.refs_4_.refs_2_.refs_3_, ...), custom_call_target="tpu_custom_call" | custom-call | flops 1200000000 | bytes 4000000 | tf_op jit(solution)/shard_map/grad_attn/pallas_call | solution.py:72
  45.7 0.2 collective-permute-done.13.refs_1_
  45.9 0.1 chip_sum.3
  46.0 1.5 %collective-permute-start.14 = (bf16[288,128]{1,0:T(8,128)(2,1)S(1)}, bf16[288,128]{1,0:T(8,128)(2,1)S(1)}, u32[]{:S(2)}, u32[]{:S(2)}) collective-permute-start(bf16[288,128]{1,0:T(8,128)(2,1)S(1)} %get-tuple-element.139), channel_id=1, source_target_pairs={{0,16},{4,20},{8,24},{12,28},{16,0},{20,4},{24,8},{28,12},{32,48},... | collective-permute-start | bytes 221192 | tf_op jit(solution)/shard_map/ppermute | solution.py:737
  47.5 1.0 %collective-permute-start.15 = (bf16[288,128]{1,0:T(8,128)(2,1)S(1)}, bf16[288,128]{1,0:T(8,128)(2,1)S(1)}, u32[]{:S(2)}, u32[]{:S(2)}) collective-permute-start(bf16[288,128]{1,0:T(8,128)(2,1)S(1)} %get-tuple-element.140), channel_id=1, source_target_pairs={{0,24},{4,28},{8,16},{12,20},{16,8},{20,12},{24,0},{28,4},{32,56},... | collective-permute-start | bytes 221192 | tf_op jit(solution)/shard_map/ppermute | solution.py:737
  48.5 0.2 collective-permute-start.16
  48.7 3.0 %local_grads.2 = (bf16[512,1024]{1,0:T(8,128)(2,1)S(1)}, f32[512,1024]{1,0:T(8,128)S(1)}, f32[512,1024]{1,0:T(8,128)S(1)}, f32[8,128]{1,0:T(8,128)S(1)}) custom-call(bf16[512,1024]{1,0:T(8,128)(2,1)S(1)} %get-tuple-element.98.refs_1_.refs_0_, bf16[512,1024]{1,0:T(8,128)(2,1)S(1)} %get-tuple-element.92.refs_0_.refs_1_.refs_2_, ...), custom_call_target="tpu_custom_call" | custom-call | flops 5000000000 | bytes 16666666 | tf_op jit(solution)/shard_map/local_grads/pallas_call | solution.py:72
  51.7 1.2 %collective-permute-done.15.refs_2_ = bf16[288,128]{1,0:T(8,128)(2,1)S(1)} collective-permute-done((bf16[288,128]{1,0:T(8,128)(2,1)S(1)}, bf16[288,128]{1,0:T(8,128)(2,1)S(1)}, u32[]{:S(2)}, u32[]{:S(2)}) %collective-permute-start.15) | collective-permute-done | bytes 73760 | tf_op jit(solution)/shard_map/ppermute | solution.py:737
  52.8 0.0 collective-permute-done.16.refs_3_
  52.8 0.1 row_sum.3.refs_11_.refs_4_
  52.9 1.1 %collective-permute-start.17 = (bf16[288,128]{1,0:T(8,128)(2,1)S(1)}, bf16[288,128]{1,0:T(8,128)(2,1)S(1)}, u32[]{:S(2)}, u32[]{:S(2)}) collective-permute-start(bf16[288,128]{1,0:T(8,128)(2,1)S(1)} %row_sum.3.refs_11_.refs_4_), channel_id=1, source_target_pairs={{0,64},{4,68},{8,72},{12,76},{16,80},{20,84},{24,88},{28,92},{32,9... | collective-permute-start | bytes 221192 | tf_op jit(solution)/shard_map/ppermute | solution.py:737
  54.0 1.3 %collective-permute-start.18 = (bf16[288,128]{1,0:T(8,128)(2,1)S(1)}, bf16[288,128]{1,0:T(8,128)(2,1)S(1)}, u32[]{:S(2)}, u32[]{:S(2)}) collective-permute-start(bf16[288,128]{1,0:T(8,128)(2,1)S(1)} %row_sum.3.refs_11_.refs_4_), channel_id=1, source_target_pairs={{0,96},{4,100},{8,104},{12,108},{16,112},{20,116},{24,120},{28,124... | collective-permute-start | bytes 221192 | tf_op jit(solution)/shard_map/ppermute | solution.py:737
  55.4 0.3 collective-permute-start.19
  55.6 3.0 %local_grads.3 = (bf16[512,2048]{1,0:T(8,128)(2,1)}, bf16[512,1024]{1,0:T(8,128)(2,1)S(1)}, f32[512,1024]{1,0:T(8,128)S(1)}, f32[512,1024]{1,0:T(8,128)S(1)}, f32[8,128]{1,0:T(8,128)S(1)}) custom-call(bf16[512,1024]{1,0:T(8,128)(2,1)S(1)} %get-tuple-element.120.refs_1_.refs_0_, bf16[512,1024]{1,0:T(8,128)(2,1)S(1)} %get-tuple-element.103.refs_0_.refs_1_.refs_2_, ...), custom_call_target="tpu_custom_call" | custom-call | flops 5000000000 | bytes 16666666 | tf_op jit(solution)/shard_map/local_grads/pallas_call | solution.py:72
  58.7 0.0 collective-permute-done.17.refs_5_
  58.7 0.6 collective-permute-done.18.refs_6_
  59.2 0.0 collective-permute-done.19.refs_7_
  59.2 0.3 entry.3
  59.6 2.2 %collective-permute-start.20 = (bf16[256,128]{1,0:T(8,128)(2,1)S(1)}, bf16[256,128]{1,0:T(8,128)(2,1)S(1)}, u32[]{:S(2)}, u32[]{:S(2)}) collective-permute-start(bf16[256,128]{1,0:T(8,128)(2,1)S(1)} %get-tuple-element.156), channel_id=1, source_target_pairs={{0,16},{4,20},{8,24},{12,28},{16,0},{20,4},{24,8},{28,12},{32,48},... | collective-permute-start | bytes 196616 | tf_op jit(solution)/shard_map/ppermute | solution.py:737
  61.8 0.8 %collective-permute-start.21 = (bf16[256,128]{1,0:T(8,128)(2,1)S(1)}, bf16[256,128]{1,0:T(8,128)(2,1)S(1)}, u32[]{:S(2)}, u32[]{:S(2)}) collective-permute-start(bf16[256,128]{1,0:T(8,128)(2,1)S(1)} %get-tuple-element.157), channel_id=1, source_target_pairs={{0,24},{4,28},{8,16},{12,20},{16,8},{20,12},{24,0},{28,4},{32,56},... | collective-permute-start | bytes 196616 | tf_op jit(solution)/shard_map/ppermute | solution.py:737
  62.7 0.3 collective-permute-start.22
  63.0 3.3 %gates.1 = (bf16[512,2048]{1,0:T(8,128)(2,1)}, bf16[512,2048]{1,0:T(8,128)(2,1)}, bf16[512,2048]{1,0:T(8,128)(2,1)}, f32[8,128]{1,0:T(8,128)S(1)}) custom-call(f32[512,1024]{1,0:T(8,128)S(1)} %get-tuple-element.118.refs_1_.refs_0_, f32[512,1024]{1,0:T(8,128)S(1)} %get-tuple-element.125.refs_1_, ...), custom_call_target="tpu_custom_call", output_to_operand_aliasing={{2}: (8, {})} | custom-call | flops 3000000000 | bytes 10000000 | tf_op jit(solution)/shard_map/gates/pallas_call | solution.py:72
  66.3 0.0 collective-permute-done.20.refs_3_
  66.3 0.6 collective-permute-done.21.refs_4_
  66.9 0.2 device_entry.3
  67.1 2.2 %collective-permute-start.23 = (bf16[1040,128]{1,0:T(8,128)(2,1)S(1)}, bf16[1040,128]{1,0:T(8,128)(2,1)S(1)}, u32[]{:S(2)}, u32[]{:S(2)}) collective-permute-start(bf16[1040,128]{1,0:T(8,128)(2,1)S(1)} %get-tuple-element.161), channel_id=1, source_target_pairs={{0,4},{4,0},{8,12},{12,8},{16,20},{20,16},{24,28},{28,24},{32,36},... | collective-permute-start | bytes 798728 | tf_op jit(solution)/shard_map/ppermute | solution.py:737
  69.3 1.9 %finish.2 = (bf16[512,2048]{1,0:T(8,128)(2,1)}, bf16[512,2048]{1,0:T(8,128)(2,1)}) custom-call(f32[512,1024]{1,0:T(8,128)S(1)} %get-tuple-element.164.refs_0_, f32[512,1024]{1,0:T(8,128)S(1)} %get-tuple-element.165.refs_1_, bf16[512,1024]{1,0:T(8,128)(2,1)S(1)} %get-tuple-element.92.refs_0_.refs_1_.refs_2_, ...), custom_call_target="tpu_custom_call" | custom-call | flops 1200000000 | bytes 4000000 | tf_op jit(solution)/shard_map/finish/pallas_call | solution.py:72
  71.2 1.9 %finish.3 = (bf16[512,2048]{1,0:T(8,128)(2,1)}, bf16[512,2048]{1,0:T(8,128)(2,1)}, f32[16,128]{1,0:T(8,128)}) custom-call(f32[512,1024]{1,0:T(8,128)S(1)} %get-tuple-element.154.refs_0_, f32[512,1024]{1,0:T(8,128)S(1)} %get-tuple-element.155.refs_1_, ...), custom_call_target="tpu_custom_call", output_to_operand_aliasing={{0}: (9, {}), {1}: (10, {})} | custom-call | flops 1200000000 | bytes 4000000 | tf_op jit(solution)/shard_map/finish/pallas_call | solution.py:72
  (8 shorter events, 0.0 us)
Async XLA Ops:
  2.6 3.5 %collective-permute-start = (bf16[1040,128]{1,0:T(8,128)(2,1)S(1)}, bf16[1040,128]{1,0:T(8,128)(2,1)S(1)}, u32[]{:S(2)}, u32[]{:S(2)}) collective-permute-start(bf16[1040,128]{1,0:T(8,128)(2,1)S(1)} %get-tuple-element.95), channel_id=1, source_target_pairs={{0,4},{4,0},{8,12},{12,8},{16,20},{20,16},{24,28},{28,24},{32,36},... | collective-permute-start | bytes 798728 | tf_op jit(solution)/shard_map/ppermute | solution.py:737
  6.3 6.5 %collective-permute-start.1 = (bf16[272,128]{1,0:T(8,128)(2,1)S(1)}, bf16[272,128]{1,0:T(8,128)(2,1)S(1)}, u32[]{:S(2)}, u32[]{:S(2)}) collective-permute-start(bf16[272,128]{1,0:T(8,128)(2,1)S(1)} %get-tuple-element.99), channel_id=1, source_target_pairs={{0,16},{4,20},{8,24},{12,28},{16,0},{20,4},{24,8},{28,12},{32,48},... | collective-permute-start | bytes 208904 | tf_op jit(solution)/shard_map/ppermute | solution.py:737
  9.2 4.4 %collective-permute-start.2 = (bf16[272,128]{1,0:T(8,128)(2,1)S(1)}, bf16[272,128]{1,0:T(8,128)(2,1)S(1)}, u32[]{:S(2)}, u32[]{:S(2)}) collective-permute-start(bf16[272,128]{1,0:T(8,128)(2,1)S(1)} %get-tuple-element.100), channel_id=1, source_target_pairs={{0,24},{4,28},{8,16},{12,20},{16,8},{20,12},{24,0},{28,4},{32,56},... | collective-permute-start | bytes 208904 | tf_op jit(solution)/shard_map/ppermute | solution.py:737
  10.0 3.5 %collective-permute-start.3 = (bf16[272,128]{1,0:T(8,128)(2,1)S(1)}, bf16[272,128]{1,0:T(8,128)(2,1)S(1)}, u32[]{:S(2)}, u32[]{:S(2)}) collective-permute-start(bf16[272,128]{1,0:T(8,128)(2,1)S(1)} %get-tuple-element.101), channel_id=1, source_target_pairs={{0,8},{4,12},{8,0},{12,4},{16,24},{20,28},{24,16},{28,20},{32,40},... | collective-permute-start | bytes 208904 | tf_op jit(solution)/shard_map/ppermute | solution.py:737
  13.6 7.1 %collective-permute-start.4 = (bf16[272,128]{1,0:T(8,128)(2,1)S(1)}, bf16[272,128]{1,0:T(8,128)(2,1)S(1)}, u32[]{:S(2)}, u32[]{:S(2)}) collective-permute-start(bf16[272,128]{1,0:T(8,128)(2,1)S(1)} %row_sum.2.refs_5_.refs_4_), channel_id=1, source_target_pairs={{0,64},{4,68},{8,72},{12,76},{16,80},{20,84},{24,88},{28,92},{32,9... | collective-permute-start | bytes 208904 | tf_op jit(solution)/shard_map/ppermute | solution.py:737
  17.3 4.6 %collective-permute-start.5 = (bf16[272,128]{1,0:T(8,128)(2,1)S(1)}, bf16[272,128]{1,0:T(8,128)(2,1)S(1)}, u32[]{:S(2)}, u32[]{:S(2)}) collective-permute-start(bf16[272,128]{1,0:T(8,128)(2,1)S(1)} %row_sum.2.refs_5_.refs_4_), channel_id=1, source_target_pairs={{0,32},{4,36},{8,40},{12,44},{16,48},{20,52},{24,56},{28,60},{32,6... | collective-permute-start | bytes 208904 | tf_op jit(solution)/shard_map/ppermute | solution.py:760
  22.2 6.0 %collective-permute-start.6 = (bf16[256,128]{1,0:T(8,128)(2,1)S(1)}, bf16[256,128]{1,0:T(8,128)(2,1)S(1)}, u32[]{:S(2)}, u32[]{:S(2)}) collective-permute-start(bf16[256,128]{1,0:T(8,128)(2,1)S(1)} %get-tuple-element.110), channel_id=1, source_target_pairs={{0,16},{4,20},{8,24},{12,28},{16,0},{20,4},{24,8},{28,12},{32,48},... | collective-permute-start | bytes 196616 | tf_op jit(solution)/shard_map/ppermute | solution.py:737
  24.2 4.3 %collective-permute-start.7 = (bf16[256,128]{1,0:T(8,128)(2,1)S(1)}, bf16[256,128]{1,0:T(8,128)(2,1)S(1)}, u32[]{:S(2)}, u32[]{:S(2)}) collective-permute-start(bf16[256,128]{1,0:T(8,128)(2,1)S(1)} %get-tuple-element.111), channel_id=1, source_target_pairs={{0,24},{4,28},{8,16},{12,20},{16,8},{20,12},{24,0},{28,4},{32,56},... | collective-permute-start | bytes 196616 | tf_op jit(solution)/shard_map/ppermute | solution.py:737
  25.6 3.3 %collective-permute-start.8 = (bf16[256,128]{1,0:T(8,128)(2,1)S(1)}, bf16[256,128]{1,0:T(8,128)(2,1)S(1)}, u32[]{:S(2)}, u32[]{:S(2)}) collective-permute-start(bf16[256,128]{1,0:T(8,128)(2,1)S(1)} %get-tuple-element.112), channel_id=1, source_target_pairs={{0,8},{4,12},{8,0},{12,4},{16,24},{20,28},{24,16},{28,20},{32,40},... | collective-permute-start | bytes 196616 | tf_op jit(solution)/shard_map/ppermute | solution.py:737
  25.6 7.1 %copy-start = (f32[2048]{0:T(1024)S(1)}, f32[2048]{0:T(1024)}, u32[]{:S(2)}) copy-start(f32[2048]{0:T(1024)} %param.12) | copy-start | bytes 24580
  29.2 4.7 %collective-permute-start.9 = (bf16[1024,128]{1,0:T(8,128)(2,1)S(1)}, bf16[1024,128]{1,0:T(8,128)(2,1)S(1)}, u32[]{:S(2)}, u32[]{:S(2)}) collective-permute-start(bf16[1024,128]{1,0:T(8,128)(2,1)S(1)} %get-tuple-element.121), channel_id=1, source_target_pairs={{0,4},{4,0},{8,12},{12,8},{16,20},{20,16},{24,28},{28,24},{32,36},... | collective-permute-start | bytes 786440 | tf_op jit(solution)/shard_map/ppermute | solution.py:737
  35.0 4.0 %collective-permute-start.10 = (f32[8,128]{1,0:T(8,128)S(1)}, f32[8,128]{1,0:T(8,128)S(1)}, u32[]{:S(2)}, u32[]{:S(2)}) collective-permute-start(f32[8,128]{1,0:T(8,128)S(1)} %get-tuple-element.128.refs_5_), channel_id=1, source_target_pairs={{0,2},{1,3},{2,0},{3,1},{4,6},{5,7},{6,4},{7,5},{8,10},{9,11},{10,... | collective-permute-start | bytes 12296 | tf_op jit(solution)/shard_map/ppermute | solution.py:737
  38.0 3.7 %collective-permute-start.11 = (f32[8,128]{1,0:T(8,128)S(1)}, f32[8,128]{1,0:T(8,128)S(1)}, u32[]{:S(2)}, u32[]{:S(2)}) collective-permute-start(f32[8,128]{1,0:T(8,128)S(1)} %get-tuple-element.128.refs_5_), channel_id=1, source_target_pairs={{0,3},{1,2},{2,1},{3,0},{4,7},{5,6},{6,5},{7,4},{8,11},{9,10},{10,... | collective-permute-start | bytes 12296 | tf_op jit(solution)/shard_map/ppermute | solution.py:737
  38.8 2.9 %collective-permute-start.12 = (f32[8,128]{1,0:T(8,128)S(1)}, f32[8,128]{1,0:T(8,128)S(1)}, u32[]{:S(2)}, u32[]{:S(2)}) collective-permute-start(f32[8,128]{1,0:T(8,128)S(1)} %get-tuple-element.128.refs_5_), channel_id=1, source_target_pairs={{0,1},{1,0},{2,3},{3,2},{4,5},{5,4},{6,7},{7,6},{8,9},{9,8},{10,11... | collective-permute-start | bytes 12296 | tf_op jit(solution)/shard_map/ppermute | solution.py:737
  42.8 3.0 %collective-permute-start.13 = (bf16[1056,128]{1,0:T(8,128)(2,1)S(1)}, bf16[1056,128]{1,0:T(8,128)(2,1)S(1)}, u32[]{:S(2)}, u32[]{:S(2)}) collective-permute-start(bf16[1056,128]{1,0:T(8,128)(2,1)S(1)} %get-tuple-element.137), channel_id=1, source_target_pairs={{0,4},{4,0},{8,12},{12,8},{16,20},{20,16},{24,28},{28,24},{32,36},... | collective-permute-start | bytes 811016 | tf_op jit(solution)/shard_map/ppermute | solution.py:737
  46.0 5.7 %collective-permute-start.14 = (bf16[288,128]{1,0:T(8,128)(2,1)S(1)}, bf16[288,128]{1,0:T(8,128)(2,1)S(1)}, u32[]{:S(2)}, u32[]{:S(2)}) collective-permute-start(bf16[288,128]{1,0:T(8,128)(2,1)S(1)} %get-tuple-element.139), channel_id=1, source_target_pairs={{0,16},{4,20},{8,24},{12,28},{16,0},{20,4},{24,8},{28,12},{32,48},... | collective-permute-start | bytes 221192 | tf_op jit(solution)/shard_map/ppermute | solution.py:737
  47.5 5.4 %collective-permute-start.15 = (bf16[288,128]{1,0:T(8,128)(2,1)S(1)}, bf16[288,128]{1,0:T(8,128)(2,1)S(1)}, u32[]{:S(2)}, u32[]{:S(2)}) collective-permute-start(bf16[288,128]{1,0:T(8,128)(2,1)S(1)} %get-tuple-element.140), channel_id=1, source_target_pairs={{0,24},{4,28},{8,16},{12,20},{16,8},{20,12},{24,0},{28,4},{32,56},... | collective-permute-start | bytes 221192 | tf_op jit(solution)/shard_map/ppermute | solution.py:737
  48.5 4.4 %collective-permute-start.16 = (bf16[288,128]{1,0:T(8,128)(2,1)S(1)}, bf16[288,128]{1,0:T(8,128)(2,1)S(1)}, u32[]{:S(2)}, u32[]{:S(2)}) collective-permute-start(bf16[288,128]{1,0:T(8,128)(2,1)S(1)} %get-tuple-element.141), channel_id=1, source_target_pairs={{0,8},{4,12},{8,0},{12,4},{16,24},{20,28},{24,16},{28,20},{32,40},... | collective-permute-start | bytes 221192 | tf_op jit(solution)/shard_map/ppermute | solution.py:737
  52.9 5.8 %collective-permute-start.17 = (bf16[288,128]{1,0:T(8,128)(2,1)S(1)}, bf16[288,128]{1,0:T(8,128)(2,1)S(1)}, u32[]{:S(2)}, u32[]{:S(2)}) collective-permute-start(bf16[288,128]{1,0:T(8,128)(2,1)S(1)} %row_sum.3.refs_11_.refs_4_), channel_id=1, source_target_pairs={{0,64},{4,68},{8,72},{12,76},{16,80},{20,84},{24,88},{28,92},{32,9... | collective-permute-start | bytes 221192 | tf_op jit(solution)/shard_map/ppermute | solution.py:737
  54.0 5.2 %collective-permute-start.18 = (bf16[288,128]{1,0:T(8,128)(2,1)S(1)}, bf16[288,128]{1,0:T(8,128)(2,1)S(1)}, u32[]{:S(2)}, u32[]{:S(2)}) collective-permute-start(bf16[288,128]{1,0:T(8,128)(2,1)S(1)} %row_sum.3.refs_11_.refs_4_), channel_id=1, source_target_pairs={{0,96},{4,100},{8,104},{12,108},{16,112},{20,116},{24,120},{28,124... | collective-permute-start | bytes 221192 | tf_op jit(solution)/shard_map/ppermute | solution.py:737
  55.4 3.9 %collective-permute-start.19 = (bf16[288,128]{1,0:T(8,128)(2,1)S(1)}, bf16[288,128]{1,0:T(8,128)(2,1)S(1)}, u32[]{:S(2)}, u32[]{:S(2)}) collective-permute-start(bf16[288,128]{1,0:T(8,128)(2,1)S(1)} %row_sum.3.refs_11_.refs_4_), channel_id=1, source_target_pairs={{0,32},{4,36},{8,40},{12,44},{16,48},{20,52},{24,56},{28,60},{32,0... | collective-permute-start | bytes 221192 | tf_op jit(solution)/shard_map/ppermute | solution.py:737
  59.6 6.7 %collective-permute-start.20 = (bf16[256,128]{1,0:T(8,128)(2,1)S(1)}, bf16[256,128]{1,0:T(8,128)(2,1)S(1)}, u32[]{:S(2)}, u32[]{:S(2)}) collective-permute-start(bf16[256,128]{1,0:T(8,128)(2,1)S(1)} %get-tuple-element.156), channel_id=1, source_target_pairs={{0,16},{4,20},{8,24},{12,28},{16,0},{20,4},{24,8},{28,12},{32,48},... | collective-permute-start | bytes 196616 | tf_op jit(solution)/shard_map/ppermute | solution.py:737
  61.8 5.0 %collective-permute-start.21 = (bf16[256,128]{1,0:T(8,128)(2,1)S(1)}, bf16[256,128]{1,0:T(8,128)(2,1)S(1)}, u32[]{:S(2)}, u32[]{:S(2)}) collective-permute-start(bf16[256,128]{1,0:T(8,128)(2,1)S(1)} %get-tuple-element.157), channel_id=1, source_target_pairs={{0,24},{4,28},{8,16},{12,20},{16,8},{20,12},{24,0},{28,4},{32,56},... | collective-permute-start | bytes 196616 | tf_op jit(solution)/shard_map/ppermute | solution.py:737
  62.7 4.2 %collective-permute-start.22 = (bf16[256,128]{1,0:T(8,128)(2,1)S(1)}, bf16[256,128]{1,0:T(8,128)(2,1)S(1)}, u32[]{:S(2)}, u32[]{:S(2)}) collective-permute-start(bf16[256,128]{1,0:T(8,128)(2,1)S(1)} %get-tuple-element.158), channel_id=1, source_target_pairs={{0,8},{4,12},{8,0},{12,4},{16,24},{20,28},{24,16},{28,20},{32,40},... | collective-permute-start | bytes 196616 | tf_op jit(solution)/shard_map/ppermute | solution.py:737
  67.1 4.1 %collective-permute-start.23 = (bf16[1040,128]{1,0:T(8,128)(2,1)S(1)}, bf16[1040,128]{1,0:T(8,128)(2,1)S(1)}, u32[]{:S(2)}, u32[]{:S(2)}) collective-permute-start(bf16[1040,128]{1,0:T(8,128)(2,1)S(1)} %get-tuple-element.161), channel_id=1, source_target_pairs={{0,4},{4,0},{8,12},{12,8},{16,20},{20,16},{24,28},{28,24},{32,36},... | collective-permute-start | bytes 798728 | tf_op jit(solution)/shard_map/ppermute | solution.py:737
